TPU v7x, 32 devices: a whole 2x2x4 slice. The times are simulated.
32 devices in a mesh: gen: 8 (over z, x), tm: 4 (over y, core).
Axes of the slice: x: 2, y: 2, z: 4, core: 2. Of those that a mesh axis runs over, the one named last changes fastest.
Arguments:
- relation: bfloat16 [6400, 6400], P('gen', 'tm'), may hold values from -1 to 3
- effects: float32 [6400, 1024], P('tm', 'gen'), may hold values from -6 to 6
- phi_one: float32 [1024], replicated, may hold values from 0.3 to 1.2
- phi_two: float32 [1024], replicated, may hold values from -0.7 to 0.3
- innov_scale: float32 [1024], replicated, may hold values from 0.4 to 2.5
Outputs:
- applied: float32 [6400, 1024], P('gen', 'tm')
All inputs are finite; a program needn't handle non-finite values.
Results may differ from a plain program's by a relative error of at most 0.0003.
Values sent between devices are 32-bit elements; how exact they have to be, the bound alone decides.
No kernel may reach another device: no remote copies, remote signals or barrier semaphores. Data moves between devices by JAX's collectives and lax.ppermute only.
A program may use at most 64 MiB of HBM per device.

v0:
```python
import jax
import jax.numpy as jnp
from jax import lax
from jax.sharding import PartitionSpec as P


def extended(cells, sides, width):
    for axis, dim in sides:
        count = lax.axis_size(axis)
        ends = count - 1
        head = lax.slice_in_dim(cells, 0, width, axis=dim)
        tail = lax.slice_in_dim(cells, cells.shape[dim] - width, cells.shape[dim], axis=dim)
        cells = jnp.concatenate(
            [
                lax.ppermute(tail, axis, [(i, (i + 1) % count) for i in range(ends)]),
                cells,
                lax.ppermute(head, axis, [((i + 1) % count, i) for i in range(ends)]),
            ],
            axis=dim,
        )
    return cells


def temporal_block(widened, first_time, phi_one, phi_two, innov_scale):
    block = widened.shape[1] - 4
    zero_pair = jnp.zeros((2,), jnp.float32)
    first_pad = jnp.concatenate([phi_one, zero_pair])
    second_pad = jnp.concatenate([phi_two, zero_pair])
    scale_pad = jnp.concatenate([innov_scale, zero_pair])
    first_win = lax.dynamic_slice_in_dim(first_pad, first_time, block + 2)
    second_win = lax.dynamic_slice_in_dim(second_pad, first_time, block + 2)
    scale_win = lax.dynamic_slice_in_dim(scale_pad, first_time, block + 2)
    innov = (
        widened[:, 2:]
        - first_win[None, :] * widened[:, 1:-1]
        - second_win[None, :] * widened[:, :-2]
    )
    weighted = scale_win[None, :] * innov
    first_next = lax.dynamic_slice_in_dim(first_pad, first_time + 1, block)
    second_next = lax.dynamic_slice_in_dim(second_pad, first_time + 2, block)
    return (
        weighted[:, :block]
        - first_next[None, :] * weighted[:, 1 : block + 1]
        - second_next[None, :] * weighted[:, 2 : block + 2]
    )


def on_device(relation, effects, phi_one, phi_two, innov_scale):
    relation_wide = relation.astype(jnp.float32)
    partial_sums = jnp.dot(
        relation_wide,
        lax.all_gather(effects, "gen", axis=1, tiled=True),
        precision=lax.Precision.HIGHEST,
        preferred_element_type=jnp.float32,
    )
    genetic = lax.psum_scatter(partial_sums, "tm", scatter_dimension=1, tiled=True)
    widened_time = extended(genetic, (("tm", 1),), 2)
    start_tm = lax.axis_index("tm") * genetic.shape[1]
    applied = temporal_block(widened_time, start_tm, phi_one, phi_two, innov_scale)
    return applied


def solution(mesh):
    placed = (P("gen", "tm"), P("tm", "gen"), P(), P(), P())
    return jax.shard_map(
        on_device, mesh=mesh, in_specs=placed, out_specs=P("gen", "tm"), check_vma=False
    )
```

profile of v0, /device:TPU:1, one launch (start us, length us, event | category | flops | bytes accessed | tf_op | source)
XLA Modules:
  0.0 185.2 jit_solution(5339196339845183569)
XLA Ops:
  6.5 0.0 copy-start
  6.5 0.0 all-gather.2.cloned.1.call-start
  6.5 0.7 all-gather.2.cloned.1.call-update
  7.3 0.0 reduce-scatter.2.cloned.1.call-start
  7.3 106.9 %all-gather.2.cloned.1.call-done = f32[1600,1024]{1,0:T(8,128)} async-done(((f32[1600,128]{1,0:T(8,128)}), f32[1600,1024]{1,0:T(8,128)}) %all-gather.2.cloned.1.call-update) | async-done | bytes 6553616 | tf_op jit(solution)/shard_map/all_gather | solution.py:52
  114.2 0.0 copy-done
  114.2 12.5 %fusion.7 = f32[800,1024]{1,0:T(8,128)} fusion(bf16[800,1600]{1,0:T(8,128)(2,1)S(1)} %copy-done, f32[1600,1024]{1,0:T(8,128)} %all-gather.2.cloned.1.call-done), kind=kOutput, calls=%fused_computation.17 | convolution fusion | flops 15728640000 | bytes 12390400 | tf_op jit(solution)/shard_map/dot_general | solution.py:50
  126.7 0.0 copy-start.4
  126.7 0.0 copy-start.2
  126.7 0.0 copy-start.3
  126.7 0.0 reduce-scatter.2.cloned.1.call-update
  126.7 0.7 copy-done.4
  127.4 0.1 pad_dynamic-slice_fusion.4
  127.5 0.0 copy-done.2
  127.5 0.0 copy-done.3
  127.5 0.1 pad_dynamic-slice_fusion.1
  127.5 36.7 %reduce-scatter.2.cloned.1.call-done = f32[800,256]{1,0:T(8,128)} async-done(((f32[800,1024]{1,0:T(8,128)}), f32[800,256]{1,0:T(8,128)}) %reduce-scatter.2.cloned.1.call-update) | async-done | bytes 819216 | tf_op jit(solution)/shard_map/reduce_scatter | solution.py:56
  164.3 0.0 copy-start.1
  164.3 1.4 fusion.6
  165.6 2.6 %collective-permute-start = (f32[800,2]{1,0:T(8,128)S(1)}, f32[800,2]{1,0:T(8,128)S(1)}, u32[]{:S(2)}, u32[]{:S(2)}) collective-permute-start(f32[800,2]{1,0:T(8,128)S(1)} %get-tuple-element.6), channel_id=1, source_target_pairs={{1,0},{2,1},{3,2},{5,4},{6,5},{7,6},{9,8},{10,9},{11,10},{13,12},{... | collective-permute-start | bytes 19208 | tf_op jit(solution)/shard_map/ppermute | solution.py:17
  168.2 3.0 %collective-permute-start.1 = (f32[800,2]{1,0:T(8,128)S(1)}, f32[800,2]{1,0:T(8,128)S(1)}, u32[]{:S(2)}, u32[]{:S(2)}) collective-permute-start(f32[800,2]{1,0:T(8,128)S(1)} %get-tuple-element.5), channel_id=1, source_target_pairs={{0,1},{1,2},{2,3},{4,5},{5,6},{6,7},{8,9},{9,10},{10,11},{12,13},{... | collective-permute-start | bytes 19208 | tf_op jit(solution)/shard_map/ppermute | solution.py:15
  171.2 0.1 pad_dynamic-slice_fusion
  171.3 3.6 %collective-permute-done = f32[800,2]{1,0:T(8,128)S(1)} collective-permute-done((f32[800,2]{1,0:T(8,128)S(1)}, f32[800,2]{1,0:T(8,128)S(1)}, u32[]{:S(2)}, u32[]{:S(2)}) %collective-permute-start) | collective-permute-done | bytes 6432 | tf_op jit(solution)/shard_map/ppermute | solution.py:17
  174.9 1.2 collective-permute-done.1
  176.1 0.0 copy-done.1
  176.1 0.9 fusion.3
  177.0 1.4 fusion.4
Async XLA Ops:
  6.5 107.6 %copy-start = (bf16[800,1600]{1,0:T(8,128)(2,1)S(1)}, bf16[800,1600]{1,0:T(8,128)(2,1)}, u32[]{:S(2)}) copy-start(bf16[800,1600]{1,0:T(8,128)(2,1)} %param.5) | copy-start | bytes 7680004
  6.5 107.6 %all-gather.2.cloned.1.call-start = ((), (), s32[]{:S(2)}) async-start(), calls=%async_computation.1 | async-start | bytes 7372800 | tf_op jit(solution)/shard_map/all_gather | solution.py:52
  7.3 157.0 %reduce-scatter.2.cloned.1.call-start = ((), (), s32[]{:S(2)}) async-start(), calls=%async_computation.2 | async-start | bytes 4096000 | tf_op jit(solution)/shard_map/reduce_scatter | solution.py:56
  126.7 0.7 copy-start.4
  126.7 0.8 copy-start.2
  126.7 0.8 copy-start.3
  164.3 11.8 %copy-start.1 = (f32[800,256]{1,0:T(8,128)S(1)}, f32[800,256]{1,0:T(8,128)}, u32[]{:S(2)}) copy-start(f32[800,256]{1,0:T(8,128)} %reduce-scatter.2.cloned.1.call-done) | copy-start | bytes 2457604
  165.6 9.3 %collective-permute-start = (f32[800,2]{1,0:T(8,128)S(1)}, f32[800,2]{1,0:T(8,128)S(1)}, u32[]{:S(2)}, u32[]{:S(2)}) collective-permute-start(f32[800,2]{1,0:T(8,128)S(1)} %get-tuple-element.6), channel_id=1, source_target_pairs={{1,0},{2,1},{3,2},{5,4},{6,5},{7,6},{9,8},{10,9},{11,10},{13,12},{... | collective-permute-start | bytes 19208 | tf_op jit(solution)/shard_map/ppermute | solution.py:17
  168.2 7.8 %collective-permute-start.1 = (f32[800,2]{1,0:T(8,128)S(1)}, f32[800,2]{1,0:T(8,128)S(1)}, u32[]{:S(2)}, u32[]{:S(2)}) collective-permute-start(f32[800,2]{1,0:T(8,128)S(1)} %get-tuple-element.5), channel_id=1, source_target_pairs={{0,1},{1,2},{2,3},{4,5},{5,6},{6,7},{8,9},{9,10},{10,11},{12,13},{... | collective-permute-start | bytes 19208 | tf_op jit(solution)/shard_map/ppermute | solution.py:15
Sparse Core Ops, SparseCore 0:
  9.4 104.7 all-gather.1
  126.8 37.3 reduce-scatter.1
where the time goes:
time: 185 us
  waiting for transfers between devices  149 us (81%)
  between operations  13.4 us (7%)
  matrix products  12.5 us (7%)
  starting transfers between devices  5.6 us (3%)
  other arithmetic  2.3 us (1%)
  local copies, waits for them, and re-layouts  2.28 us (1%)
    all_gather x1, waiting for transfers between devices, on_device(): lax.all_gather(effects, 'gen', axis=1, tiled=True)  107 us
    reduce_scatter x1, waiting for transfers between devices, on_device(): lax.psum_scatter(partial_sums, 'tm', scatter_dimension=1, tiled=True)  36.7 us
    dot_general x1, matrix products, on_device(): jnp.dot(relation_wide, lax.all_gather(effects, 'gen', axis=1, tiled=True)...  12.5 us
  transfers between devices with their start and end apart: 4, of which 4 were waited for; matrix products, arithmetic and copies ran while one was open for 0% of the time, Pallas kernels for 0%

commit v1 on v0

--- a/solution.py
+++ b/solution.py
@@ -1,7 +1,164 @@
 import jax
 import jax.numpy as jnp
 from jax import lax
+from jax.experimental import pallas as pl
+from jax.experimental.pallas import tpu as pltpu
 from jax.sharding import PartitionSpec as P
+
+VMEM_LIMIT = 40 * 1024 * 1024
+
+
+def bands(phi_one, phi_two, innov_scale):
+    zero_pair = jnp.zeros((2,), jnp.float32)
+    first = jnp.concatenate([phi_one, zero_pair])
+    second = jnp.concatenate([phi_two, zero_pair])
+    scale = jnp.concatenate([innov_scale, zero_pair])
+    count = phi_one.shape[0]
+    first_0, first_1, first_2 = first[:count], first[1 : count + 1], first[2:]
+    second_0, second_1, second_2 = second[:count], second[1 : count + 1], second[2:]
+    scale_0, scale_1, scale_2 = scale[:count], scale[1 : count + 1], scale[2:]
+    return jnp.stack(
+        [
+            -scale_0 * second_0,
+            first_1 * scale_1 * second_1 - scale_0 * first_0,
+            scale_0 + first_1 * first_1 * scale_1 + second_2 * second_2 * scale_2,
+            second_2 * scale_2 * first_2 - first_1 * scale_1,
+            -second_2 * scale_2,
+        ]
+    )
+
+
+def edge(cells, pairs):
+    flat = lax.ppermute(cells.T.reshape(-1), "gen", pairs)
+    return flat.reshape(2, cells.shape[0]).T
+
+
+def banded(effects, weights):
+    gens = lax.axis_size("gen")
+    rows, width = effects.shape
+    before = edge(effects[:, width - 2 :], [(i, i + 1) for i in range(gens - 1)])
+    after = edge(effects[:, :2], [(i + 1, i) for i in range(gens - 1)])
+    start = lax.axis_index("gen") * width
+    mine = lax.dynamic_slice_in_dim(weights, start, width, axis=1)
+    widened = jnp.concatenate([before, effects, after], axis=1)
+    return sum(mine[j][None, :] * widened[:, j : j + width] for j in range(5))
+
+
+def product_of(relation_ref, halves):
+    block = jnp.concatenate([half[...] for half in halves], axis=0)
+    high = block.astype(jnp.bfloat16)
+    low = (block - high.astype(jnp.float32)).astype(jnp.bfloat16)
+    both = jnp.dot(
+        relation_ref[...],
+        jnp.concatenate([high, low], axis=1),
+        preferred_element_type=jnp.float32,
+    )
+    width = block.shape[1]
+    return both[:, :width] + both[:, width:]
+
+
+def one_kernel(relation_ref, top_ref, bottom_ref, out_ref):
+    out_ref[...] = product_of(relation_ref, (top_ref, bottom_ref))
+
+
+def pair_kernel(flag_ref, relation_ref, top_ref, bottom_ref, other_ref, send_ref, keep_ref):
+    made = product_of(relation_ref, (top_ref, bottom_ref))
+    other = other_ref[...]
+    keep_other = flag_ref[0] == 1
+    send_ref[...] = jnp.where(keep_other, made, other)
+    keep_ref[...] = jnp.where(keep_other, other, made)
+
+
+def call(kernel, outs, relation, operands, scalars=()):
+    rows, depth = relation.shape
+    width = operands[0].shape[1]
+    whole = pl.BlockSpec(memory_space=pltpu.VMEM)
+    return pl.pallas_call(
+        kernel,
+        out_shape=[jax.ShapeDtypeStruct((rows, width), jnp.float32)] * outs,
+        in_specs=[pl.BlockSpec(memory_space=pltpu.SMEM)] * len(scalars)
+        + [whole] * (1 + len(operands)),
+        out_specs=[whole] * outs,
+        compiler_params=pltpu.CompilerParams(vmem_limit_bytes=VMEM_LIMIT),
+        cost_estimate=pl.CostEstimate(
+            flops=4 * rows * depth * width, bytes_accessed=4 * rows * width, transcendentals=0
+        ),
+    )(*scalars, relation, *operands)
+
+
+def ring_plan(gens, tms):
+    order = list(range(0, gens, 2)) + list(range(gens - 1, 0, -2))
+    place = {g: p for p, g in enumerate(order)}
+    share = gens // tms
+    return order, place, share
+
+
+def by_ring(relation, effects, phi_one, phi_two, innov_scale):
+    gens, tms = lax.axis_size("gen"), lax.axis_size("tm")
+    order, place, share = ring_plan(gens, tms)
+    half = gens // 2
+    forward = [(order[p], order[(p + 1) % gens]) for p in range(gens)]
+    backward = [(b, a) for a, b in forward]
+    swap = [(t, t ^ 1) for t in range(tms)]
+
+    gen, tm = lax.axis_index("gen"), lax.axis_index("tm")
+    own = banded(effects, bands(phi_one, phi_two, innov_scale))
+    depth = own.shape[0]
+    cut = depth // 256 * 128
+    top, bottom = own[:cut], own[cut:]
+
+    blocks = {0: (top, bottom)}
+    for step in range(1, half):
+        behind, ahead = blocks[1 - step], blocks[step - 1]
+        behind_top = lax.ppermute(behind[0], "gen", forward)
+        ahead_bottom = lax.ppermute(ahead[1], "gen", backward)
+        behind_bottom = lax.ppermute(behind[1], "gen", forward)
+        ahead_top = lax.ppermute(ahead[0], "gen", backward)
+        blocks[-step] = (behind_top, behind_bottom)
+        blocks[step] = (ahead_top, ahead_bottom)
+    last = half - 1
+    blocks[-half] = (
+        lax.ppermute(blocks[-last][0], "gen", forward),
+        lax.ppermute(blocks[last][1], "gen", backward),
+    )
+
+    products = {}
+    for far in [0] + [s for n in range(1, half // 2 + 1) for s in (n, -n)]:
+        if far != -(half // 2):
+            products[far] = call(one_kernel, 1, relation, blocks[far])[0]
+
+    first_block = {}
+    summed = {}
+    for near, far in ((2, -2), (1, -3), (-1, 3), (0, -4)):
+        owner = {
+            d: [order[(place[g] + d) % gens] // share for g in range(gens)] for d in (near, far)
+        }
+        keep_near = (jnp.asarray([t % 2 for t in owner[near]])[gen] == tm % 2).astype(jnp.int32)
+        send, keep = call(
+            pair_kernel, 2, relation, (*blocks[far], products[near]), (keep_near.reshape(1),)
+        )
+        chip_sum = keep + lax.ppermute(send, "tm", swap)
+        across = [
+            (g * tms + (t ^ 2), g * tms + t)
+            for d in (near, far)
+            for g, t in enumerate(owner[d])
+        ]
+        total = chip_sum + lax.ppermute(chip_sum, ("gen", "tm"), across)
+        for d in (near, far):
+            for j in range(share):
+                holds = jnp.asarray(
+                    [order[(place[g] + d) % gens] % share == j for g in range(gens)]
+                )[gen]
+                mine = holds & (jnp.asarray(owner[d])[gen] == tm)
+                summed.setdefault(j, []).append((mine, total))
+        first_block[near] = keep_near
+    columns = []
+    for j in range(share):
+        column = summed[j][0][1]
+        for mine, total in summed[j][1:]:
+            column = jnp.where(mine, total, column)
+        columns.append(column)
+    return jnp.concatenate(columns, axis=1)
 
 
 def extended(cells, sides, width):
@@ -45,7 +202,7 @@
     )
 
 
-def on_device(relation, effects, phi_one, phi_two, innov_scale):
+def by_gather(relation, effects, phi_one, phi_two, innov_scale):
     relation_wide = relation.astype(jnp.float32)
     partial_sums = jnp.dot(
         relation_wide,
@@ -56,8 +213,14 @@
     genetic = lax.psum_scatter(partial_sums, "tm", scatter_dimension=1, tiled=True)
     widened_time = extended(genetic, (("tm", 1),), 2)
     start_tm = lax.axis_index("tm") * genetic.shape[1]
-    applied = temporal_block(widened_time, start_tm, phi_one, phi_two, innov_scale)
-    return applied
+    return temporal_block(widened_time, start_tm, phi_one, phi_two, innov_scale)
+
+
+def on_device(relation, effects, phi_one, phi_two, innov_scale):
+    gens, tms = lax.axis_size("gen"), lax.axis_size("tm")
+    fits = gens == 8 and tms == 4 and effects.shape[1] % 128 == 0 and effects.shape[0] % 8 == 0
+    way = by_ring if fits else by_gather
+    return way(relation, effects, phi_one, phi_two, innov_scale)
 
 
 def solution(mesh):

time: 185 us -> 119 us (0.64)
  the two profiles are of different devices: /device:TPU:1 before, /device:TPU:28 now
where the time goes in v1:
time: 119 us; the launch traced here: 118 us
  waiting for transfers between devices  36.4 us (31%)
  starting transfers between devices  31.7 us (27%)
  local copies, waits for them, and re-layouts  18.2 us (15%)
  between operations  14.9 us (13%)
  Pallas kernels  11.9 us (10%)
  other arithmetic  5.16 us (4%)
    ppermute x3, waiting for transfers between devices, by_ring(): behind_bottom = lax.ppermute(behind[1], 'gen', forward)  12.1 us
    pallas_call x8, Pallas kernels, call(): pl.pallas_call(kernel, out_shape=[jax.ShapeDtypeStruct((rows, width), jnp...  11.9 us
    ppermute x4, starting transfers between devices, by_ring(): total = chip_sum + lax.ppermute(chip_sum, ('gen', 'tm'), across)  11.8 us
    ppermute x3, waiting for transfers between devices, by_ring(): ahead_top = lax.ppermute(ahead[0], 'gen', backward)  11.7 us
    ppermute x3, waiting for transfers between devices, by_ring(): ahead_bottom = lax.ppermute(ahead[1], 'gen', backward)  7.96 us
    ppermute x2, starting transfers between devices, edge(): flat = lax.ppermute(cells.T.reshape(-1), 'gen', pairs)  5.83 us
    ppermute x3, starting transfers between devices, by_ring(): behind_top = lax.ppermute(behind[0], 'gen', forward)  4.78 us
    ppermute x2, waiting for transfers between devices, edge(): flat = lax.ppermute(cells.T.reshape(-1), 'gen', pairs)  3.77 us
  transfers between devices with their start and end apart: 24, of which 7 were waited for; matrix products, arithmetic and copies ran while one was open for 10% of the time, Pallas kernels for 10%

profile of v1, /device:TPU:28, one launch (start us, length us, event | category | flops | bytes accessed | tf_op | source)
XLA Modules:
  0.0 118.2 jit_solution(2956565476013776082)
XLA Ops:
  0.0 1.7 %slice_bitcast_fusion.1 = (f32[2,1600]{0,1:T(8,128)S(1)}, f32[2,1600]{0,1:T(8,128)S(1)}) fusion(f32[1600,128]{1,0:T(8,128)} %param.34), kind=kLoop, calls=%fused_computation.18 | loop fusion | bytes 51200 | tf_op jit(solution)/shard_map/transpose | solution.py:32
  2.1 3.3 %collective-permute-start.1 = (f32[3200]{0:T(1024)S(1)}, f32[3200]{0:T(1024)S(1)}, u32[]{:S(2)}, u32[]{:S(2)}) collective-permute-start(f32[3200]{0:T(1024)S(1)} %reshape.36), channel_id=1, source_target_pairs={{4,0},{8,4},{12,8},{16,12},{20,16},{24,20},{28,24},{5,1},{9,5},{13... | collective-permute-start | bytes 38408 | tf_op jit(solution)/shard_map/ppermute | solution.py:32
  5.8 2.5 %collective-permute-start = (f32[3200]{0:T(1024)S(1)}, f32[3200]{0:T(1024)S(1)}, u32[]{:S(2)}, u32[]{:S(2)}) collective-permute-start(f32[3200]{0:T(1024)S(1)} %reshape.34), channel_id=1, source_target_pairs={{0,4},{4,8},{8,12},{12,16},{16,20},{20,24},{24,28},{1,5},{5,9},{9,... | collective-permute-start | bytes 38408 | tf_op jit(solution)/shard_map/ppermute | solution.py:32
  8.5 3.8 %collective-permute-done = f32[3200]{0:T(1024)S(1)} collective-permute-done((f32[3200]{0:T(1024)S(1)}, f32[3200]{0:T(1024)S(1)}, u32[]{:S(2)}, u32[]{:S(2)}) %collective-permute-start) | collective-permute-done | bytes 12832 | tf_op jit(solution)/shard_map/ppermute | solution.py:32
  12.4 1.2 %copy.35 = f32[2,1600]{0,1:T(8,128)} copy(f32[2,1600]{1,0:T(2,128)S(1)} %reshape.35) | data formatting | bytes 25600 | tf_op jit(solution)/shard_map/reshape | solution.py:33
  13.7 1.2 %copy.37 = f32[2,1600]{0,1:T(8,128)} copy(f32[2,1600]{1,0:T(2,128)S(1)} %reshape.37) | data formatting | bytes 25600 | tf_op jit(solution)/shard_map/reshape | solution.py:33
  14.9 3.6 %fusion.3 = f32[1600,128]{1,0:T(8,128)S(1)} fusion(f32[1600,128]{1,0:T(8,128)S(1)} %copy-done.9, f32[1600,2]{1,0:T(8,128)} %bitcast.42, f32[1600,2]{1,0:T(8,128)} %bitcast.41, f32[128]{0:T(128)S(1)} %get-tuple-element.29, f32[128]{0:T(128)S(1)} %get-tuple-element.30, f32[128]{0:T(128)S(1)} %get-tuple-element.31, f32[128]{0:T(128)S(1)} %get-tuple-element.32, ...), kind=kLoop, calls=%fused_computation.7 | loop fusion | flops 2662400 | bytes 1666560 | tf_op jit(solution)/shard_map/add | solution.py:44
  19.1 1.6 %collective-permute-start.2 = (f32[768,128]{1,0:T(8,128)S(1)}, f32[768,128]{1,0:T(8,128)S(1)}, u32[]{:S(2)}, u32[]{:S(2)}) collective-permute-start(f32[768,128]{1,0:T(8,128)S(1)} %slice.84.top_ref), channel_id=1, source_target_pairs={{0,8},{8,16},{16,24},{24,28},{28,20},{20,12},{12,4},{4,0},{1,9},{9... | collective-permute-start | bytes 1179656 | tf_op jit(solution)/shard_map/ppermute | solution.py:113
  20.8 8.0 %collective-permute-done.6.bottom_ref = f32[832,128]{1,0:T(8,128)S(1)} collective-permute-done((f32[832,128]{1,0:T(8,128)S(1)}, f32[832,128]{1,0:T(8,128)S(1)}, u32[]{:S(2)}, u32[]{:S(2)}) %collective-permute-start.6) | collective-permute-done | bytes 426016 | tf_op jit(solution)/shard_map/ppermute | solution.py:114
  29.2 0.8 copy-done.1
  30.4 0.8 collective-permute-done.2.top_ref
  31.2 1.6 %collective-permute-start.3 = (f32[768,128]{1,0:T(8,128)S(1)}, f32[768,128]{1,0:T(8,128)}, u32[]{:S(2)}, u32[]{:S(2)}) collective-permute-start(f32[768,128]{1,0:T(8,128)S(1)} %collective-permute-done.2.top_ref), channel_id=1, source_target_pairs={{0,8},{8,16},{16,24},{24,28},{28,20},{20,12},{12,4},{4,0},{1,9},{9... | collective-permute-start | bytes 1179656 | tf_op jit(solution)/shard_map/ppermute | solution.py:113
  32.8 0.8 copy-done.5
  33.6 6.8 %collective-permute-done.15.bottom_ref = f32[832,128]{1,0:T(8,128)S(1)} collective-permute-done((f32[832,128]{1,0:T(8,128)S(1)}, f32[832,128]{1,0:T(8,128)S(1)}, u32[]{:S(2)}, u32[]{:S(2)}) %collective-permute-start.15) | collective-permute-done | bytes 426016 | tf_op jit(solution)/shard_map/ppermute | solution.py:115
  40.4 1.6 %collective-permute-start.18 = (f32[832,128]{1,0:T(8,128)S(1)}, f32[832,128]{1,0:T(8,128)}, u32[]{:S(2)}, u32[]{:S(2)}) collective-permute-start(f32[832,128]{1,0:T(8,128)S(1)} %collective-permute-done.15.bottom_ref), channel_id=1, source_target_pairs={{0,8},{8,16},{16,24},{24,28},{28,20},{20,12},{12,4},{4,0},{1,9},{9... | collective-permute-start | bytes 1277960 | tf_op jit(solution)/shard_map/ppermute | solution.py:115
  41.9 0.8 copy-done.3
  43.2 6.8 %collective-permute-done.12.top_ref = f32[768,128]{1,0:T(8,128)S(1)} collective-permute-done((f32[768,128]{1,0:T(8,128)S(1)}, f32[768,128]{1,0:T(8,128)S(1)}, u32[]{:S(2)}, u32[]{:S(2)}) %collective-permute-start.12) | collective-permute-done | bytes 393248 | tf_op jit(solution)/shard_map/ppermute | solution.py:116
  50.4 0.7 copy-done.7
  51.1 1.6 %collective-permute-start.4 = (f32[768,128]{1,0:T(8,128)}, f32[768,128]{1,0:T(8,128)}, u32[]{:S(2)}, u32[]{:S(2)}) collective-permute-start(f32[768,128]{1,0:T(8,128)} %collective-permute-done.3.top_ref), channel_id=1, source_target_pairs={{0,8},{8,16},{16,24},{24,28},{28,20},{20,12},{12,4},{4,0},{1,9},{9... | collective-permute-start | bytes 1179656 | tf_op jit(solution)/shard_map/ppermute | solution.py:113
  52.7 5.3 %collective-permute-done.18.bottom_ref = f32[832,128]{1,0:T(8,128)} collective-permute-done((f32[832,128]{1,0:T(8,128)S(1)}, f32[832,128]{1,0:T(8,128)}, u32[]{:S(2)}, u32[]{:S(2)}) %collective-permute-start.18) | collective-permute-done | bytes 426016 | tf_op jit(solution)/shard_map/ppermute | solution.py:115
  58.0 1.6 %collective-permute-start.19 = (f32[832,128]{1,0:T(8,128)}, f32[832,128]{1,0:T(8,128)}, u32[]{:S(2)}, u32[]{:S(2)}) collective-permute-start(f32[832,128]{1,0:T(8,128)} %collective-permute-done.18.bottom_ref), channel_id=1, source_target_pairs={{0,8},{8,16},{16,24},{24,28},{28,20},{20,12},{12,4},{4,0},{1,9},{9... | collective-permute-start | bytes 1277960 | tf_op jit(solution)/shard_map/ppermute | solution.py:115
  59.6 4.9 %collective-permute-done.13.top_ref = f32[768,128]{1,0:T(8,128)} collective-permute-done((f32[768,128]{1,0:T(8,128)S(1)}, f32[768,128]{1,0:T(8,128)}, u32[]{:S(2)}, u32[]{:S(2)}) %collective-permute-start.13) | collective-permute-done | bytes 393248 | tf_op jit(solution)/shard_map/ppermute | solution.py:116
  65.0 0.6 dynamic_slice.93
  66.2 0.6 dynamic_slice.99
  68.6 0.7 dynamic_slice.107
  70.0 1.6 %collective-permute-start.5 = (f32[768,128]{1,0:T(8,128)}, f32[768,128]{1,0:T(8,128)S(1)}, u32[]{:S(2)}, u32[]{:S(2)}) collective-permute-start(f32[768,128]{1,0:T(8,128)} %collective-permute-done.4.top_ref), channel_id=1, source_target_pairs={{0,8},{8,16},{16,24},{24,28},{28,20},{20,12},{12,4},{4,0},{1,9},{9... | collective-permute-start | bytes 1179656 | tf_op jit(solution)/shard_map/ppermute | solution.py:121
  72.1 0.9 shard_map.327.other_ref
  73.0 0.9 shard_map.329.other_ref
  74.1 0.9 shard_map.331.other_ref
  75.1 2.0 %shard_map.333.other_ref = f32[800,128]{1,0:T(8,128)S(1)} custom-call(bf16[800,1600]{1,0:T(8,128)(2,1)S(1)} %copy-done, f32[768,128]{1,0:T(8,128)} %collective-permute-done.13.top_ref, f32[832,128]{1,0:T(8,128)} %collective-permute-done.7.bottom_ref), custom_call_target="tpu_custom_call" | custom-call | flops 655360000 | bytes 409600 | tf_op jit(solution)/shard_map/pallas_call | solution.py:76
  77.1 2.0 %shard_map.334 = (f32[800,128]{1,0:T(8,128)S(1)}, f32[800,128]{1,0:T(8,128)S(1)}) custom-call(s32[1]{0:T(128)} %bitcast.33.flag_ref, bf16[800,1600]{1,0:T(8,128)(2,1)S(1)} %copy-done, f32[768,128]{1,0:T(8,128)} %collective-permute-done.3.top_ref, f32[832,128]{1,0:T(8,128)} %collective-permute-done.18.bottom_ref, f32[800,128]{1,0:T(8,128)S(1)} %shard_map.333.other_ref), custom_call_target="tpu_custom_call" | custom-call | flops 655360000 | bytes 409600 | tf_op jit(solution)/shard_map/pallas_call | solution.py:76
  79.2 2.1 %shard_map.332 = (f32[800,128]{1,0:T(8,128)S(1)}, f32[800,128]{1,0:T(8,128)S(1)}) custom-call(s32[1]{0:T(128)} %bitcast.29.flag_ref, bf16[800,1600]{1,0:T(8,128)(2,1)S(1)} %copy-done, f32[768,128]{1,0:T(8,128)} %collective-permute-done.4.top_ref, f32[832,128]{1,0:T(8,128)} %collective-permute-done.19.bottom_ref, f32[800,128]{1,0:T(8,128)S(1)} %shard_map.331.other_ref), custom_call_target="tpu_custom_call" | custom-call | flops 655360000 | bytes 409600 | tf_op jit(solution)/shard_map/pallas_call | solution.py:76
  81.9 2.0 %shard_map.330 = (f32[800,128]{1,0:T(8,128)S(1)}, f32[800,128]{1,0:T(8,128)S(1)}) custom-call(s32[1]{0:T(128)} %bitcast.23.flag_ref, bf16[800,1600]{1,0:T(8,128)(2,1)S(1)} %copy-done, f32[768,128]{1,0:T(8,128)} %collective-permute-done.14.top_ref, f32[832,128]{1,0:T(8,128)} %collective-permute-done.8.bottom_ref, f32[800,128]{1,0:T(8,128)S(1)} %shard_map.329.other_ref), custom_call_target="tpu_custom_call" | custom-call | flops 655360000 | bytes 409600 | tf_op jit(solution)/shard_map/pallas_call | solution.py:76
  84.0 0.9 shard_map.328
  85.5 1.3 %collective-permute-start.23 = (f32[800,128]{1,0:T(8,128)S(1)}, f32[800,128]{1,0:T(8,128)S(1)}, u32[]{:S(2)}, u32[]{:S(2)}) collective-permute-start(f32[800,128]{1,0:T(8,128)S(1)} %add.107), channel_id=1, source_target_pairs={{0,2},{7,5},{9,11},{14,12},{17,19},{22,20},{24,26},{31,29},{3,1},{... | collective-permute-start | bytes 1228808 | tf_op jit(solution)/shard_map/ppermute | solution.py:146
  87.1 4.6 %collective-permute-start.21 = (f32[800,128]{1,0:T(8,128)S(1)}, f32[800,128]{1,0:T(8,128)S(1)}, u32[]{:S(2)}, u32[]{:S(2)}) collective-permute-start(f32[800,128]{1,0:T(8,128)S(1)} %add.105), channel_id=1, source_target_pairs={{3,1},{6,4},{8,10},{14,12},{17,19},{23,21},{25,27},{28,30},{0,2},{... | collective-permute-start | bytes 1228808 | tf_op jit(solution)/shard_map/ppermute | solution.py:146
  91.7 1.3 %collective-permute-start.17 = (f32[800,128]{1,0:T(8,128)S(1)}, f32[800,128]{1,0:T(8,128)S(1)}, u32[]{:S(2)}, u32[]{:S(2)}) collective-permute-start(f32[800,128]{1,0:T(8,128)S(1)} %add.103), channel_id=1, source_target_pairs={{2,0},{7,5},{10,8},{12,14},{19,17},{21,23},{24,26},{29,31},{1,3},{... | collective-permute-start | bytes 1228808 | tf_op jit(solution)/shard_map/ppermute | solution.py:146
  93.1 4.6 %collective-permute-start.11 = (f32[800,128]{1,0:T(8,128)S(1)}, f32[800,128]{1,0:T(8,128)S(1)}, u32[]{:S(2)}, u32[]{:S(2)}) collective-permute-start(f32[800,128]{1,0:T(8,128)S(1)} %add.101), channel_id=1, source_target_pairs={{2,0},{6,4},{11,9},{15,13},{16,18},{20,22},{25,27},{29,31},{1,3},{... | collective-permute-start | bytes 1228808 | tf_op jit(solution)/shard_map/ppermute | solution.py:146
  99.0 0.6 dynamic_slice.91
  99.6 0.6 dynamic_slice.96
  102.2 0.6 dynamic_slice.95
  105.4 0.6 dynamic_slice.97
  106.0 0.6 dynamic_slice.101
  108.6 0.6 dynamic_slice.100
  111.7 0.6 dynamic_slice.102
  112.3 0.6 dynamic_slice.106
  115.0 0.6 dynamic_slice.105
  117.2 0.9 pad_maximum_fusion.2
  (105 shorter events, 8.9 us)
Async XLA Ops:
  1.7 6.7 %copy-start.10 = (f32[1024]{0:T(1024)S(1)}, f32[1024]{0:T(1024)}, u32[]{:S(2)}) copy-start(f32[1024]{0:T(1024)} %param.35) | copy-start | bytes 12292
  1.7 6.7 %copy-start.11 = (f32[1024]{0:T(1024)S(1)}, f32[1024]{0:T(1024)}, u32[]{:S(2)}) copy-start(f32[1024]{0:T(1024)} %param.37) | copy-start | bytes 12292
  1.7 6.7 %copy-start.12 = (f32[1024]{0:T(1024)S(1)}, f32[1024]{0:T(1024)}, u32[]{:S(2)}) copy-start(f32[1024]{0:T(1024)} %param.36) | copy-start | bytes 12292
  1.7 13.2 %copy-start.9 = (f32[1600,128]{1,0:T(8,128)S(1)}, f32[1600,128]{1,0:T(8,128)}, u32[]{:S(2)}) copy-start(f32[1600,128]{1,0:T(8,128)} %param.34) | copy-start | bytes 2457604
  2.1 11.5 %collective-permute-start.1 = (f32[3200]{0:T(1024)S(1)}, f32[3200]{0:T(1024)S(1)}, u32[]{:S(2)}, u32[]{:S(2)}) collective-permute-start(f32[3200]{0:T(1024)S(1)} %reshape.36), channel_id=1, source_target_pairs={{4,0},{8,4},{12,8},{16,12},{20,16},{24,20},{28,24},{5,1},{9,5},{13... | collective-permute-start | bytes 38408 | tf_op jit(solution)/shard_map/ppermute | solution.py:32
  5.8 6.5 %collective-permute-start = (f32[3200]{0:T(1024)S(1)}, f32[3200]{0:T(1024)S(1)}, u32[]{:S(2)}, u32[]{:S(2)}) collective-permute-start(f32[3200]{0:T(1024)S(1)} %reshape.34), channel_id=1, source_target_pairs={{0,4},{4,8},{8,12},{12,16},{16,20},{20,24},{24,28},{1,5},{5,9},{9,... | collective-permute-start | bytes 38408 | tf_op jit(solution)/shard_map/ppermute | solution.py:32
  14.9 57.1 %copy-start = (bf16[800,1600]{1,0:T(8,128)(2,1)S(1)}, bf16[800,1600]{1,0:T(8,128)(2,1)}, u32[]{:S(2)}) copy-start(bf16[800,1600]{1,0:T(8,128)(2,1)} %relation_ref.15) | copy-start | bytes 7680004
  18.5 46.5 %copy-start.28 = (s32[8]{0:T(128)S(1)}, s32[8]{0:T(128)}, u32[]{:S(2)}) copy-start(s32[8]{0:T(128)} %constant.86.clone) | copy-start | bytes 100
  18.5 47.7 %copy-start.27 = (s32[8]{0:T(128)S(1)}, s32[8]{0:T(128)}, u32[]{:S(2)}) copy-start(s32[8]{0:T(128)} %constant.81.clone) | copy-start | bytes 100
  18.5 49.0 %copy-start.26 = (s32[8]{0:T(128)S(1)}, s32[8]{0:T(128)}, u32[]{:S(2)}) copy-start(s32[8]{0:T(128)} %constant.76.clone) | copy-start | bytes 100
  18.5 50.1 %copy-start.25 = (s32[8]{0:T(128)S(1)}, s32[8]{0:T(128)}, u32[]{:S(2)}) copy-start(s32[8]{0:T(128)} %constant.75.clone) | copy-start | bytes 100
  18.6 10.2 %collective-permute-start.6 = (f32[832,128]{1,0:T(8,128)S(1)}, f32[832,128]{1,0:T(8,128)S(1)}, u32[]{:S(2)}, u32[]{:S(2)}) collective-permute-start(f32[832,128]{1,0:T(8,128)S(1)} %slice.85.bottom_ref), channel_id=1, source_target_pairs={{8,0},{16,8},{24,16},{28,24},{20,28},{12,20},{4,12},{0,4},{9,1},{1... | collective-permute-start | bytes 1277960 | tf_op jit(solution)/shard_map/ppermute | solution.py:114
  19.1 12.1 %collective-permute-start.2 = (f32[768,128]{1,0:T(8,128)S(1)}, f32[768,128]{1,0:T(8,128)S(1)}, u32[]{:S(2)}, u32[]{:S(2)}) collective-permute-start(f32[768,128]{1,0:T(8,128)S(1)} %slice.84.top_ref), channel_id=1, source_target_pairs={{0,8},{8,16},{16,24},{24,28},{28,20},{20,12},{12,4},{4,0},{1,9},{9... | collective-permute-start | bytes 1179656 | tf_op jit(solution)/shard_map/ppermute | solution.py:113
  20.7 19.6 %collective-permute-start.15 = (f32[832,128]{1,0:T(8,128)S(1)}, f32[832,128]{1,0:T(8,128)S(1)}, u32[]{:S(2)}, u32[]{:S(2)}) collective-permute-start(f32[832,128]{1,0:T(8,128)S(1)} %slice.85.bottom_ref), channel_id=1, source_target_pairs={{0,8},{8,16},{16,24},{24,28},{28,20},{20,12},{12,4},{4,0},{1,9},{9... | collective-permute-start | bytes 1277960 | tf_op jit(solution)/shard_map/ppermute | solution.py:115
  28.8 13.9 %collective-permute-start.7 = (f32[832,128]{1,0:T(8,128)S(1)}, f32[832,128]{1,0:T(8,128)}, u32[]{:S(2)}, u32[]{:S(2)}) collective-permute-start(f32[832,128]{1,0:T(8,128)S(1)} %collective-permute-done.6.bottom_ref), channel_id=1, source_target_pairs={{8,0},{16,8},{24,16},{28,24},{20,28},{12,20},{4,12},{0,4},{9,1},{1... | collective-permute-start | bytes 1277960 | tf_op jit(solution)/shard_map/ppermute | solution.py:114
  30.0 20.0 %collective-permute-start.12 = (f32[768,128]{1,0:T(8,128)S(1)}, f32[768,128]{1,0:T(8,128)S(1)}, u32[]{:S(2)}, u32[]{:S(2)}) collective-permute-start(f32[768,128]{1,0:T(8,128)S(1)} %slice.84.top_ref), channel_id=1, source_target_pairs={{8,0},{16,8},{24,16},{28,24},{20,28},{12,20},{4,12},{0,4},{9,1},{1... | collective-permute-start | bytes 1179656 | tf_op jit(solution)/shard_map/ppermute | solution.py:116
  31.2 19.9 %collective-permute-start.3 = (f32[768,128]{1,0:T(8,128)S(1)}, f32[768,128]{1,0:T(8,128)}, u32[]{:S(2)}, u32[]{:S(2)}) collective-permute-start(f32[768,128]{1,0:T(8,128)S(1)} %collective-permute-done.2.top_ref), channel_id=1, source_target_pairs={{0,8},{8,16},{16,24},{24,28},{28,20},{20,12},{12,4},{4,0},{1,9},{9... | collective-permute-start | bytes 1179656 | tf_op jit(solution)/shard_map/ppermute | solution.py:113
  40.4 17.7 %collective-permute-start.18 = (f32[832,128]{1,0:T(8,128)S(1)}, f32[832,128]{1,0:T(8,128)}, u32[]{:S(2)}, u32[]{:S(2)}) collective-permute-start(f32[832,128]{1,0:T(8,128)S(1)} %collective-permute-done.15.bottom_ref), channel_id=1, source_target_pairs={{0,8},{8,16},{16,24},{24,28},{28,20},{20,12},{12,4},{4,0},{1,9},{9... | collective-permute-start | bytes 1277960 | tf_op jit(solution)/shard_map/ppermute | solution.py:115
  42.7 28.9 %collective-permute-start.8 = (f32[832,128]{1,0:T(8,128)}, f32[832,128]{1,0:T(8,128)}, u32[]{:S(2)}, u32[]{:S(2)}) collective-permute-start(f32[832,128]{1,0:T(8,128)} %collective-permute-done.7.bottom_ref), channel_id=1, source_target_pairs={{8,0},{16,8},{24,16},{28,24},{20,28},{12,20},{4,12},{0,4},{9,1},{1... | collective-permute-start | bytes 1277960 | tf_op jit(solution)/shard_map/ppermute | solution.py:114
  49.9 14.6 %collective-permute-start.13 = (f32[768,128]{1,0:T(8,128)S(1)}, f32[768,128]{1,0:T(8,128)}, u32[]{:S(2)}, u32[]{:S(2)}) collective-permute-start(f32[768,128]{1,0:T(8,128)S(1)} %collective-permute-done.12.top_ref), channel_id=1, source_target_pairs={{8,0},{16,8},{24,16},{28,24},{20,28},{12,20},{4,12},{0,4},{9,1},{1... | collective-permute-start | bytes 1179656 | tf_op jit(solution)/shard_map/ppermute | solution.py:116
  51.1 18.8 %collective-permute-start.4 = (f32[768,128]{1,0:T(8,128)}, f32[768,128]{1,0:T(8,128)}, u32[]{:S(2)}, u32[]{:S(2)}) collective-permute-start(f32[768,128]{1,0:T(8,128)} %collective-permute-done.3.top_ref), channel_id=1, source_target_pairs={{0,8},{8,16},{16,24},{24,28},{28,20},{20,12},{12,4},{4,0},{1,9},{9... | collective-permute-start | bytes 1179656 | tf_op jit(solution)/shard_map/ppermute | solution.py:113
  58.0 21.2 %collective-permute-start.19 = (f32[832,128]{1,0:T(8,128)}, f32[832,128]{1,0:T(8,128)}, u32[]{:S(2)}, u32[]{:S(2)}) collective-permute-start(f32[832,128]{1,0:T(8,128)} %collective-permute-done.18.bottom_ref), channel_id=1, source_target_pairs={{0,8},{8,16},{16,24},{24,28},{28,20},{20,12},{12,4},{4,0},{1,9},{9... | collective-permute-start | bytes 1277960 | tf_op jit(solution)/shard_map/ppermute | solution.py:115
  64.5 17.3 %collective-permute-start.14 = (f32[768,128]{1,0:T(8,128)}, f32[768,128]{1,0:T(8,128)}, u32[]{:S(2)}, u32[]{:S(2)}) collective-permute-start(f32[768,128]{1,0:T(8,128)} %collective-permute-done.13.top_ref), channel_id=1, source_target_pairs={{8,0},{16,8},{24,16},{28,24},{20,28},{12,20},{4,12},{0,4},{9,1},{1... | collective-permute-start | bytes 1179656 | tf_op jit(solution)/shard_map/ppermute | solution.py:116
  69.9 3.0 %copy-start.4 = (f32[832,128]{1,0:T(8,128)S(1)}, f32[832,128]{1,0:T(8,128)}, u32[]{:S(2)}) copy-start(f32[832,128]{1,0:T(8,128)} %copy-done.3) | copy-start | bytes 1277956
  70.0 3.0 %copy-start.6 = (f32[768,128]{1,0:T(8,128)S(1)}, f32[768,128]{1,0:T(8,128)}, u32[]{:S(2)}) copy-start(f32[768,128]{1,0:T(8,128)} %copy-done.5) | copy-start | bytes 1179652
  70.0 14.0 %collective-permute-start.5 = (f32[768,128]{1,0:T(8,128)}, f32[768,128]{1,0:T(8,128)S(1)}, u32[]{:S(2)}, u32[]{:S(2)}) collective-permute-start(f32[768,128]{1,0:T(8,128)} %collective-permute-done.4.top_ref), channel_id=1, source_target_pairs={{0,8},{8,16},{16,24},{24,28},{28,20},{20,12},{12,4},{4,0},{1,9},{9... | collective-permute-start | bytes 1179656 | tf_op jit(solution)/shard_map/ppermute | solution.py:121
  71.6 12.4 %collective-permute-start.9 = (f32[832,128]{1,0:T(8,128)}, f32[832,128]{1,0:T(8,128)S(1)}, u32[]{:S(2)}, u32[]{:S(2)}) collective-permute-start(f32[832,128]{1,0:T(8,128)} %collective-permute-done.8.bottom_ref), channel_id=1, source_target_pairs={{8,0},{16,8},{24,16},{28,24},{20,28},{12,20},{4,12},{0,4},{9,1},{1... | collective-permute-start | bytes 1277960 | tf_op jit(solution)/shard_map/ppermute | solution.py:122
  73.0 1.1 copy-start.8
  79.2 6.3 %collective-permute-start.22 = (f32[800,128]{1,0:T(8,128)S(1)}, f32[800,128]{1,0:T(8,128)S(1)}, u32[]{:S(2)}, u32[]{:S(2)}) collective-permute-start(f32[800,128]{1,0:T(8,128)S(1)} %get-tuple-element.20), channel_id=1, source_target_pairs={{0,1},{1,0},{2,3},{3,2},{4,5},{5,4},{6,7},{7,6},{8,9},{9,8},{10,11... | collective-permute-start | bytes 1228808 | tf_op jit(solution)/shard_map/ppermute | solution.py:140
  81.3 5.5 %collective-permute-start.20 = (f32[800,128]{1,0:T(8,128)S(1)}, f32[800,128]{1,0:T(8,128)S(1)}, u32[]{:S(2)}, u32[]{:S(2)}) collective-permute-start(f32[800,128]{1,0:T(8,128)S(1)} %get-tuple-element.18), channel_id=1, source_target_pairs={{0,1},{1,0},{2,3},{3,2},{4,5},{5,4},{6,7},{7,6},{8,9},{9,8},{10,11... | collective-permute-start | bytes 1228808 | tf_op jit(solution)/shard_map/ppermute | solution.py:140
  83.9 7.8 %collective-permute-start.16 = (f32[800,128]{1,0:T(8,128)S(1)}, f32[800,128]{1,0:T(8,128)S(1)}, u32[]{:S(2)}, u32[]{:S(2)}) collective-permute-start(f32[800,128]{1,0:T(8,128)S(1)} %get-tuple-element.16), channel_id=1, source_target_pairs={{0,1},{1,0},{2,3},{3,2},{4,5},{5,4},{6,7},{7,6},{8,9},{9,8},{10,11... | collective-permute-start | bytes 1228808 | tf_op jit(solution)/shard_map/ppermute | solution.py:140
  84.9 8.1 %collective-permute-start.10 = (f32[800,128]{1,0:T(8,128)S(1)}, f32[800,128]{1,0:T(8,128)S(1)}, u32[]{:S(2)}, u32[]{:S(2)}) collective-permute-start(f32[800,128]{1,0:T(8,128)S(1)} %get-tuple-element.14), channel_id=1, source_target_pairs={{0,1},{1,0},{2,3},{3,2},{4,5},{5,4},{6,7},{7,6},{8,9},{9,8},{10,11... | collective-permute-start | bytes 1228808 | tf_op jit(solution)/shard_map/ppermute | solution.py:140
  85.5 31.3 %collective-permute-start.23 = (f32[800,128]{1,0:T(8,128)S(1)}, f32[800,128]{1,0:T(8,128)S(1)}, u32[]{:S(2)}, u32[]{:S(2)}) collective-permute-start(f32[800,128]{1,0:T(8,128)S(1)} %add.107), channel_id=1, source_target_pairs={{0,2},{7,5},{9,11},{14,12},{17,19},{22,20},{24,26},{31,29},{3,1},{... | collective-permute-start | bytes 1228808 | tf_op jit(solution)/shard_map/ppermute | solution.py:146
  86.9 10.9 %copy-start.24 = (s32[8]{0:T(128)S(1)}, s32[8]{0:T(128)}, u32[]{:S(2)}) copy-start(s32[8]{0:T(128)} %constant.90.clone) | copy-start | bytes 100
  86.9 12.1 %copy-start.23 = (pred[8]{0:T(512)(128)(4,1)S(1)}, pred[8]{0:T(512)(128)(4,1)}, u32[]{:S(2)}) copy-start(pred[8]{0:T(512)(128)(4,1)} %constant.89.clone) | copy-start | bytes 28
  86.9 12.7 %copy-start.22 = (s32[8]{0:T(128)S(1)}, s32[8]{0:T(128)}, u32[]{:S(2)}) copy-start(s32[8]{0:T(128)} %constant.88.clone) | copy-start | bytes 100
  86.9 15.3 %copy-start.21 = (pred[8]{0:T(512)(128)(4,1)S(1)}, pred[8]{0:T(512)(128)(4,1)}, u32[]{:S(2)}) copy-start(pred[8]{0:T(512)(128)(4,1)} %constant.87.clone) | copy-start | bytes 28
  86.9 17.2 %copy-start.20 = (s32[8]{0:T(128)S(1)}, s32[8]{0:T(128)}, u32[]{:S(2)}) copy-start(s32[8]{0:T(128)} %constant.85.clone) | copy-start | bytes 100
  86.9 18.4 %copy-start.19 = (pred[8]{0:T(512)(128)(4,1)S(1)}, pred[8]{0:T(512)(128)(4,1)}, u32[]{:S(2)}) copy-start(pred[8]{0:T(512)(128)(4,1)} %constant.84.clone) | copy-start | bytes 28
  86.9 19.0 %copy-start.18 = (s32[8]{0:T(128)S(1)}, s32[8]{0:T(128)}, u32[]{:S(2)}) copy-start(s32[8]{0:T(128)} %constant.83.clone) | copy-start | bytes 100
  86.9 21.6 %copy-start.17 = (pred[8]{0:T(512)(128)(4,1)S(1)}, pred[8]{0:T(512)(128)(4,1)}, u32[]{:S(2)}) copy-start(pred[8]{0:T(512)(128)(4,1)} %constant.82.clone) | copy-start | bytes 28
  87.0 23.5 %copy-start.16 = (s32[8]{0:T(128)S(1)}, s32[8]{0:T(128)}, u32[]{:S(2)}) copy-start(s32[8]{0:T(128)} %constant.80.clone) | copy-start | bytes 100
  87.0 24.8 %copy-start.15 = (pred[8]{0:T(512)(128)(4,1)S(1)}, pred[8]{0:T(512)(128)(4,1)}, u32[]{:S(2)}) copy-start(pred[8]{0:T(512)(128)(4,1)} %constant.79.clone) | copy-start | bytes 28
  87.0 25.3 %copy-start.14 = (s32[8]{0:T(128)S(1)}, s32[8]{0:T(128)}, u32[]{:S(2)}) copy-start(s32[8]{0:T(128)} %constant.78.clone) | copy-start | bytes 100
  87.0 28.0 %copy-start.13 = (pred[8]{0:T(512)(128)(4,1)S(1)}, pred[8]{0:T(512)(128)(4,1)}, u32[]{:S(2)}) copy-start(pred[8]{0:T(512)(128)(4,1)} %constant.77.clone) | copy-start | bytes 28
  87.1 29.8 %collective-permute-start.21 = (f32[800,128]{1,0:T(8,128)S(1)}, f32[800,128]{1,0:T(8,128)S(1)}, u32[]{:S(2)}, u32[]{:S(2)}) collective-permute-start(f32[800,128]{1,0:T(8,128)S(1)} %add.105), channel_id=1, source_target_pairs={{3,1},{6,4},{8,10},{14,12},{17,19},{23,21},{25,27},{28,30},{0,2},{... | collective-permute-start | bytes 1228808 | tf_op jit(solution)/shard_map/ppermute | solution.py:146
  91.7 25.1 %collective-permute-start.17 = (f32[800,128]{1,0:T(8,128)S(1)}, f32[800,128]{1,0:T(8,128)S(1)}, u32[]{:S(2)}, u32[]{:S(2)}) collective-permute-start(f32[800,128]{1,0:T(8,128)S(1)} %add.103), channel_id=1, source_target_pairs={{2,0},{7,5},{10,8},{12,14},{19,17},{21,23},{24,26},{29,31},{1,3},{... | collective-permute-start | bytes 1228808 | tf_op jit(solution)/shard_map/ppermute | solution.py:146
  93.1 23.8 %collective-permute-start.11 = (f32[800,128]{1,0:T(8,128)S(1)}, f32[800,128]{1,0:T(8,128)S(1)}, u32[]{:S(2)}, u32[]{:S(2)}) collective-permute-start(f32[800,128]{1,0:T(8,128)S(1)} %add.101), channel_id=1, source_target_pairs={{2,0},{6,4},{11,9},{15,13},{16,18},{20,22},{25,27},{29,31},{1,3},{... | collective-permute-start | bytes 1228808 | tf_op jit(solution)/shard_map/ppermute | solution.py:146
  (5 other events, 4.0 us)

commit v2 on v0

--- a/solution.py
+++ b/solution.py
@@ -1,7 +1,379 @@
 import jax
 import jax.numpy as jnp
 from jax import lax
+from jax.experimental import pallas as pl
+from jax.experimental.pallas import tpu as pltpu
 from jax.sharding import PartitionSpec as P
+
+VMEM_LIMIT = 12 * 1024 * 1024
+WIDTH = 128
+CORE_PIECES = 2
+LAST_COST = 1
+KERNEL_FLOPS = 10**8
+
+WHOLE = pl.BlockSpec(memory_space=pltpu.VMEM)
+SCALAR = pl.BlockSpec(memory_space=pltpu.SMEM)
+ANYWHERE = pl.BlockSpec(memory_space=pl.ANY)
+
+
+def call(kernel, shapes, operands, scratch=(), scalars=(), places=None, into=WHOLE, flops=0):
+    return pl.pallas_call(
+        kernel,
+        out_shape=[jax.ShapeDtypeStruct(shape, jnp.float32) for shape in shapes],
+        in_specs=[SCALAR] * len(scalars) + (places or [WHOLE] * len(operands)),
+        out_specs=[into] * len(shapes),
+        scratch_shapes=scratch,
+        compiler_params=pltpu.CompilerParams(vmem_limit_bytes=VMEM_LIMIT),
+        cost_estimate=pl.CostEstimate(flops=flops, bytes_accessed=0, transcendentals=0),
+    )(*scalars, *operands)
+
+
+def bands(phi_one, phi_two, innov_scale):
+    count = phi_one.shape[1]
+    row = lax.broadcasted_iota(jnp.int32, (8, count), 0)
+    lane = lax.broadcasted_iota(jnp.int32, (8, count), 1)
+
+    def rows(*values):
+        out = jnp.zeros((8, count), jnp.float32)
+        for n, value in enumerate(values):
+            out = jnp.where(row == n, value, out)
+        return out
+
+    now = rows(phi_one, phi_two, innov_scale)
+    next_1 = jnp.where(lane < count - 1, pltpu.roll(now, count - 1, 1), 0.0)
+    next_2 = jnp.where(lane < count - 2, pltpu.roll(now, count - 2, 1), 0.0)
+    first_0, second_0, scale_0 = (now[n : n + 1] for n in range(3))
+    first_1, second_1, scale_1 = (next_1[n : n + 1] for n in range(3))
+    first_2, second_2, scale_2 = (next_2[n : n + 1] for n in range(3))
+    return rows(
+        -scale_0 * second_0,
+        first_1 * scale_1 * second_1 - scale_0 * first_0,
+        scale_0 + first_1 * first_1 * scale_1 + second_2 * second_2 * scale_2,
+        second_2 * scale_2 * first_2 - first_1 * scale_1,
+        -second_2 * scale_2,
+    )
+
+
+def weights_kernel(one_ref, two_ref, scale_ref, weights_ref):
+    weights_ref[...] = bands(one_ref[...][None], two_ref[...][None], scale_ref[...][None])
+
+
+def products_kernel(relation_ref, *refs):
+    both_ref, padded_ref = refs[-2:]
+    count = (len(refs) - 2) // 4
+    rows = relation_ref.shape[0]
+    padded_ref[rows:] = jnp.zeros((padded_ref.shape[0] - rows, WIDTH), jnp.float32)
+    for n in range(count):
+        block = jnp.concatenate([refs[2 * n][...], refs[2 * n + 1][...]], axis=0)
+        high = block.astype(jnp.bfloat16)
+        low = (block - high.astype(jnp.float32)).astype(jnp.bfloat16)
+        both_ref[...] = jnp.dot(
+            relation_ref[...],
+            jnp.concatenate([high, low], axis=1),
+            preferred_element_type=jnp.float32,
+        )
+        made = both_ref[:, :WIDTH] + both_ref[:, WIDTH:]
+        refs[2 * count + 2 * n][...] = made
+        padded_ref[:rows] = made
+        turned = padded_ref[...].T
+        edges_ref = refs[2 * count + 2 * n + 1]
+        edges_ref[0:2] = turned[0:2]
+        edges_ref[2:4] = turned[WIDTH - 2 :]
+
+
+def pairs_kernel(flag_ref, *refs):
+    send_ref, keep_ref = refs[-2:]
+    rows = refs[0].shape[0]
+    for n in range((len(refs) - 2) // 2):
+        here = pl.ds(n * rows, rows)
+        for near in range(2):
+
+            @pl.when(flag_ref[n] == near)
+            def _():
+                send_ref[here] = refs[2 * n + near][...]
+                keep_ref[here] = refs[2 * n + 1 - near][...]
+
+
+def borders_kernel(flag_ref, *refs):
+    send_ref, keep_ref, edges_ref = refs[-3:]
+    count = len(refs) - 3
+    for n in range(count):
+        edges_ref[n] = refs[n][...]
+    edges_ref[count] = jnp.zeros_like(refs[0])
+    for out_ref, first in ((send_ref, 0), (keep_ref, 2)):
+        for n in range(2):
+            before, after = flag_ref[2 * (first + n)], flag_ref[2 * (first + n) + 1]
+            out_ref[4 * n : 4 * n + 2] = edges_ref[before][2:4]
+            out_ref[4 * n + 2 : 4 * n + 4] = edges_ref[after][0:2]
+
+
+def part_sums_kernel(flag_ref, keep_ref, *refs):
+    send_ref, mine_ref = refs[-2:]
+    rows = mine_ref.shape[0]
+    pieces = (len(refs) - 2) // 2
+    piece = rows // pieces
+    for n in range(2):
+
+        @pl.when(flag_ref[0] == n)
+        def _():
+            for sums_ref, first in ((mine_ref, n), (send_ref, 1 - n)):
+                for m in range(pieces):
+                    here = pl.ds(m * piece, piece)
+                    there = pl.ds(first * rows + m * piece, piece)
+                    sums_ref[here] = keep_ref[there] + refs[first * pieces + m][...]
+
+
+def border_sums_kernel(flag_ref, keep_ref, got_ref, send_ref, mine_ref):
+    rows = mine_ref.shape[0]
+    for n in range(2):
+
+        @pl.when(flag_ref[0] == n)
+        def _():
+            for sums_ref, first in ((mine_ref, n), (send_ref, 1 - n)):
+                here = slice(first * rows, first * rows + rows)
+                sums_ref[...] = keep_ref[here] + got_ref[here]
+
+
+def last_kernel(
+    flag_ref,
+    odd_any,
+    odd_got_any,
+    two_any,
+    two_got_any,
+    zero_ref,
+    zero_got_ref,
+    mine_ref,
+    got_ref,
+    weights_ref,
+    out_any,
+    sums_ref,
+    sides_ref,
+    out_ref,
+    sems,
+    out_sems,
+):
+    odd, is_two = flag_ref[0], flag_ref[1]
+    rows = out_any.shape[0]
+    span = sides_ref.shape[1]
+    copies = [
+        pltpu.make_async_copy(odd_any, sums_ref.at[0], sems.at[0]),
+        pltpu.make_async_copy(odd_got_any, sums_ref.at[1], sems.at[1]),
+    ]
+    two_copies = [
+        pltpu.make_async_copy(two_any, sums_ref.at[2], sems.at[2]),
+        pltpu.make_async_copy(two_got_any, sums_ref.at[3], sems.at[3]),
+    ]
+    for copy in copies:
+        copy.start()
+
+    @pl.when(is_two == 1)
+    def _():
+        for copy in two_copies:
+            copy.start()
+
+    start = pl.multiple_of(flag_ref[2] * (2 * WIDTH), 2 * WIDTH)
+    weights = weights_ref[:, pl.ds(start, 2 * WIDTH)]
+    row = lax.broadcasted_iota(jnp.int32, (8, span), 0)
+    nothing = jnp.zeros((WIDTH - 8, span), jnp.float32)
+    border = mine_ref[...] + got_ref[...]
+    end = 2 * WIDTH - 1
+    first = weights[0:1, 0:1] * border[0:1] + weights[1:2, 0:1] * border[1:2]
+    second = weights[0:1, 1:2] * border[1:2]
+    above = jnp.where(row == 0, first, jnp.where(row == 1, second, 0.0))
+    last = weights[3:4, end:] * border[2:3] + weights[4:5, end:] * border[3:4]
+    but_last = weights[4:5, end - 1 : end] * border[2:3]
+    below = jnp.where(row == 7, last, jnp.where(row == 6, but_last, 0.0))
+    sides_ref[0] = jnp.concatenate([above, nothing], axis=0).T
+    sides_ref[1] = jnp.concatenate([nothing, below], axis=0).T
+    lane = lax.broadcasted_iota(jnp.int32, (1, WIDTH), 1)
+    inner = [weights[:, :WIDTH], weights[:, WIDTH:]]
+    for copy in copies:
+        copy.wait()
+
+    @pl.when(is_two == 1)
+    def _():
+        for copy in two_copies:
+            copy.wait()
+
+    step = rows // 5
+    for n in range(5):
+        here = slice(n * step, (n + 1) * step)
+        odd_sum = sums_ref[0, here] + sums_ref[1, here]
+        even_sum = jnp.where(
+            is_two == 1, sums_ref[2, here] + sums_ref[3, here], zero_ref[here] + zero_got_ref[here]
+        )
+        left = jnp.where(odd == 0, odd_sum, even_sum)
+        right = jnp.where(odd == 0, even_sum, odd_sum)
+        made = [sides_ref[0, here] + inner[0][2:3] * left, sides_ref[1, here] + inner[1][2:3] * right]
+        for far in (1, 2):
+            left_back, right_back = pltpu.roll(left, far, 1), pltpu.roll(right, far, 1)
+            left_on, right_on = pltpu.roll(left, WIDTH - far, 1), pltpu.roll(right, WIDTH - far, 1)
+            back, on = [w[2 - far : 3 - far] for w in inner], [w[2 + far : 3 + far] for w in inner]
+            made[0] += jnp.where(lane >= far, back[0], 0.0) * left_back
+            made[0] += on[0] * jnp.where(lane < WIDTH - far, left_on, right_on)
+            made[1] += back[1] * jnp.where(lane >= far, right_back, left_back)
+            made[1] += jnp.where(lane < WIDTH - far, on[1], 0.0) * right_on
+        out_ref[here, :WIDTH] = made[0]
+        out_ref[here, WIDTH:] = made[1]
+        pltpu.make_async_copy(out_ref.at[here], out_any.at[here], out_sems.at[n]).start()
+    for n in range(5):
+        here = slice(n * step, (n + 1) * step)
+        pltpu.make_async_copy(out_ref.at[here], out_any.at[here], out_sems.at[n]).wait()
+
+
+def flags_of(*values):
+    return jnp.stack([jnp.asarray(v, jnp.int32) for v in values])
+
+
+def tied(value, *others):
+    return lax.optimization_barrier((value, *others))[0]
+
+
+def by_ring(relation, effects, phi_one, phi_two, innov_scale):
+    gens, tms = lax.axis_size("gen"), lax.axis_size("tm")
+    share = gens // tms
+    half = gens // 2
+    rows, depth = relation.shape
+    cut = depth // 256 * 128
+    wide = pl.cdiv(rows, 128) * 128
+    order = list(range(0, gens, 2)) + list(range(gens - 1, 0, -2))
+    forward = [(order[p], order[(p + 1) % gens]) for p in range(gens)]
+    backward = [(b, a) for a, b in forward]
+    swap = [(t, t ^ 1) for t in range(tms)]
+    gen, tm = lax.axis_index("gen"), lax.axis_index("tm")
+
+    def place_of(g):
+        return jnp.where(g % 2 == 0, g // 2, gens - 1 - g // 2)
+
+    place = place_of(gen)
+
+    def block_at(far):
+        p = (place + far + gens) % gens
+        return jnp.where(p < half, 2 * p, 2 * (gens - 1 - p) + 1)
+
+    def owner_of(far):
+        return block_at(far) // share
+
+    def ahead_of(x):
+        return lax.ppermute(x, "gen", backward)
+
+    def behind_of(x):
+        return lax.ppermute(x, "gen", forward)
+
+    def multiplied(*fars, after=(), cost=1):
+        parts = [tied(x, *after) for far in fars for x in blocks[far]]
+        made = call(
+            products_kernel,
+            [(rows, WIDTH), (4, wide)] * len(fars),
+            (relation, *parts),
+            [pltpu.VMEM((rows, 2 * WIDTH), jnp.float32), pltpu.VMEM((wide, WIDTH), jnp.float32)],
+            flops=cost * len(fars) * KERNEL_FLOPS,
+        )
+        for n, far in enumerate(fars):
+            products[far], edges[far] = made[2 * n : 2 * n + 2]
+
+    def over_cores(x, pieces=1):
+        piece = x.shape[0] // pieces
+        return [lax.ppermute(x[n * piece : (n + 1) * piece], "tm", swap) for n in range(pieces)]
+
+    def keeps(far):
+        return owner_of(far) % 2 == tm % 2
+
+    def paired(*fars):
+        return call(
+            pairs_kernel,
+            [(len(fars) * rows, WIDTH)] * 2,
+            [products[f] for far in fars for f in (far, far + half if far <= 0 else far - half)],
+            (),
+            (flags_of(*[keeps(far) for far in fars]),),
+            flops=KERNEL_FLOPS // 2,
+        )
+
+    def over_y_of(fars, x):
+        across = [
+            (g * tms + (t ^ 2), g * tms + t)
+            for far in fars
+            for p, g in enumerate(order)
+            for t in [order[(p + far) % gens] // share]
+        ]
+        return lax.ppermute(x, ("gen", "tm"), across)
+
+    def over_y(x):
+        return lax.ppermute(x, "tm", [(t, t ^ 2) for t in range(tms)])
+
+    top, bottom = effects[:cut], effects[cut:]
+    blocks, products, edges = {0: (top, bottom)}, {}, {}
+    behind, ahead = blocks[0], blocks[0]
+    multiplied(0)
+    for n in range(1, half):
+        behind_top = behind_of(behind[0] if n < 3 else tied(behind[0], products[n - 2]))
+        ahead_bottom = ahead_of(ahead[1])
+        behind_bottom = behind_of(behind[1])
+        ahead_top = ahead_of(ahead[0])
+        behind, ahead = (behind_top, behind_bottom), (ahead_top, ahead_bottom)
+        blocks[-n], blocks[n] = behind, ahead
+        if n < half - 1:
+            multiplied(-n, n)
+    blocks[half] = (behind_of(behind[0]), ahead_of(ahead[1]))
+    send, keep = paired(-2)
+    two_sum = keep + over_cores(send)[0]
+    two_got = over_y_of((-2, 2), two_sum)
+    multiplied(1 - half, half - 1)
+    send, keep = paired(-1, 1)
+    odd_owner = jnp.where(keeps(-1), owner_of(-1), owner_of(3))
+    odd_send, odd_sum = call(
+        part_sums_kernel,
+        [(rows, WIDTH)] * 2,
+        (keep, *over_cores(send, CORE_PIECES)),
+        scalars=(flags_of(odd_owner // 2 != tm // 2),),
+        flops=KERNEL_FLOPS // 2,
+    )
+    odd_got = over_y(odd_send)
+    multiplied(half, cost=LAST_COST)
+    products[-half] = products[half]
+    send, keep = paired(0)
+    fars = sorted(edges)
+    at = []
+    for owner in (1 - tm % 2, 3 - tm % 2, tm % 2, 2 + tm % 2):
+        for g, there in ((share * owner - 1, owner > 0), (share * owner + share, owner < tms - 1)):
+            index = (place_of(g) - place + gens + half - 1) % gens
+            at.append(jnp.where(there, index, len(fars)))
+    border_send, border_keep = call(
+        borders_kernel,
+        [(8, wide)] * 2,
+        [edges[far] for far in fars],
+        [pltpu.VMEM((len(fars) + 1, 4, wide), jnp.float32)],
+        (flags_of(*at),),
+        flops=KERNEL_FLOPS // 10,
+    )
+    border_send, border_sum = call(
+        border_sums_kernel,
+        [(4, wide)] * 2,
+        (border_keep, over_cores(border_send)[0]),
+        scalars=(flags_of(tm // 2),),
+        flops=KERNEL_FLOPS // 10,
+    )
+    border_got = over_y(border_send)
+    zero_sum = tied(keep, two_got) + over_cores(send)[0]
+    zero_got = over_y_of((0, half), zero_sum)
+    weights = call(weights_kernel, [(8, phi_one.shape[0])], (phi_one, phi_two, innov_scale))[0]
+    odd_column = (place_of(share * tm) - place) % 2 == 0
+    is_two = (owner_of(2) == tm) | (owner_of(-2) == tm)
+    return call(
+        last_kernel,
+        [(rows, share * WIDTH)],
+        (odd_sum, odd_got, two_sum, two_got, zero_sum, zero_got, border_sum, border_got, weights),
+        [
+            pltpu.VMEM((4, rows, WIDTH), jnp.float32),
+            pltpu.VMEM((2, wide, WIDTH), jnp.float32),
+            pltpu.VMEM((rows, share * WIDTH), jnp.float32),
+            pltpu.SemaphoreType.DMA((4,)),
+            pltpu.SemaphoreType.DMA((5,)),
+        ],
+        (flags_of(odd_column, is_two, tm),),
+        [ANYWHERE] * 4 + [WHOLE] * 5,
+        ANYWHERE,
+    )[0]
 
 
 def extended(cells, sides, width):
@@ -45,7 +417,7 @@
     )
 
 
-def on_device(relation, effects, phi_one, phi_two, innov_scale):
+def by_gather(relation, effects, phi_one, phi_two, innov_scale):
     relation_wide = relation.astype(jnp.float32)
     partial_sums = jnp.dot(
         relation_wide,
@@ -56,8 +428,14 @@
     genetic = lax.psum_scatter(partial_sums, "tm", scatter_dimension=1, tiled=True)
     widened_time = extended(genetic, (("tm", 1),), 2)
     start_tm = lax.axis_index("tm") * genetic.shape[1]
-    applied = temporal_block(widened_time, start_tm, phi_one, phi_two, innov_scale)
-    return applied
+    return temporal_block(widened_time, start_tm, phi_one, phi_two, innov_scale)
+
+
+def on_device(relation, effects, phi_one, phi_two, innov_scale):
+    gens, tms = lax.axis_size("gen"), lax.axis_size("tm")
+    fits = gens == 8 and tms == 4 and effects.shape[1] == WIDTH and effects.shape[0] % 64 == 0 and relation.shape[0] % 40 == 0
+    way = by_ring if fits else by_gather
+    return way(relation, effects, phi_one, phi_two, innov_scale)
 
 
 def solution(mesh):

time: 185 us -> 98.7 us (0.53)
  the two profiles are of different devices: /device:TPU:1 before, /device:TPU:0 now
where the time goes in v2:
time: 98.7 us; the launch traced here: 98.3 us
  waiting for transfers between devices  40.6 us (41%)
  starting transfers between devices  24.9 us (25%)
  Pallas kernels  19 us (19%)
  local copies, waits for them, and re-layouts  11.7 us (12%)
  other arithmetic  1.44 us (1%)
    pallas_call x13, Pallas kernels, call(): pl.pallas_call(kernel, out_shape=[jax.ShapeDtypeStruct(shape, jnp.float32...  19 us
    ppermute x7, waiting for transfers between devices, ahead_of(): return lax.ppermute(x, 'gen', backward)  17.4 us
    ppermute x7, starting transfers between devices, ahead_of(): return lax.ppermute(x, 'gen', backward)  12.4 us
    ppermute x7, waiting for transfers between devices, behind_of(): return lax.ppermute(x, 'gen', forward)  12.4 us
    ppermute x2, waiting for transfers between devices, over_y(): return lax.ppermute(x, 'tm', [(t, t ^ 2) for t in range(tms)])  9.88 us
    unnamed x44, local copies, waits for them, and re-layouts  8.57 us
    ppermute x2, starting transfers between devices, over_y_of(): return lax.ppermute(x, ('gen', 'tm'), across)  5.86 us
    ppermute x5, starting transfers between devices, over_cores(): lax.ppermute(x[n * piece:(n + 1) * piece], 'tm', swap)  3.14 us
  transfers between devices with their start and end apart: 23, of which 8 were waited for; matrix products, arithmetic and copies ran while one was open for 4% of the time, Pallas kernels for 16%

profile of v2, /device:TPU:0, one launch (start us, length us, event | category | flops | bytes accessed | tf_op | source)
XLA Modules:
  0.0 98.3 jit_solution(10777122656188243348)
XLA Ops:
  0.0 1.0 %slice.13.refs_1_ = f32[832,128]{1,0:T(8,128)S(1)} slice(f32[1600,128]{1,0:T(8,128)} %param.6), slice={[768:1600], [0:128]} | slice | bytes 851968 | tf_op jit(solution)/shard_map/slice | solution.py:304
  1.0 3.0 %collective-permute-start.3 = (f32[832,128]{1,0:T(8,128)S(1)}, f32[832,128]{1,0:T(8,128)S(1)}, u32[]{:S(2)}, u32[]{:S(2)}) collective-permute-start(f32[832,128]{1,0:T(8,128)S(1)} %slice.13.refs_1_), channel_id=1, source_target_pairs={{8,0},{16,8},{24,16},{28,24},{20,28},{12,20},{4,12},{0,4},{9,1},{1... | collective-permute-start | bytes 1277960 | tf_op jit(solution)/shard_map/ppermute | solution.py:258
  4.0 1.0 %slice.12.refs_0_ = f32[768,128]{1,0:T(8,128)S(1)} slice(f32[1600,128]{1,0:T(8,128)} %param.6), slice={[0:768], [0:128]} | slice | bytes 786432 | tf_op jit(solution)/shard_map/slice | solution.py:304
  5.1 0.2 collective-permute-start
  5.2 2.0 %collective-permute-start.1 = (f32[832,128]{1,0:T(8,128)S(1)}, f32[832,128]{1,0:T(8,128)}, u32[]{:S(2)}, u32[]{:S(2)}) collective-permute-start(f32[832,128]{1,0:T(8,128)S(1)} %slice.13.refs_1_), channel_id=1, source_target_pairs={{0,8},{8,16},{16,24},{24,28},{28,20},{20,12},{12,4},{4,0},{1,9},{9... | collective-permute-start | bytes 1277960 | tf_op jit(solution)/shard_map/ppermute | solution.py:261
  7.2 7.5 %collective-permute-done.3.refs_3_ = f32[832,128]{1,0:T(8,128)S(1)} collective-permute-done((f32[832,128]{1,0:T(8,128)S(1)}, f32[832,128]{1,0:T(8,128)S(1)}, u32[]{:S(2)}, u32[]{:S(2)}) %collective-permute-start.3) | collective-permute-done | bytes 426016 | tf_op jit(solution)/shard_map/ppermute | solution.py:258
  14.8 2.0 %collective-permute-start.10 = (f32[832,128]{1,0:T(8,128)S(1)}, f32[832,128]{1,0:T(8,128)}, u32[]{:S(2)}, u32[]{:S(2)}) collective-permute-start(f32[832,128]{1,0:T(8,128)S(1)} %collective-permute-done.3.refs_3_), channel_id=1, source_target_pairs={{8,0},{16,8},{24,16},{28,24},{20,28},{12,20},{4,12},{0,4},{9,1},{1... | collective-permute-start | bytes 1277960 | tf_op jit(solution)/shard_map/ppermute | solution.py:258
  16.7 0.4 collective-permute-done.refs_0_
  17.2 9.2 %collective-permute-done.1.refs_1_ = f32[832,128]{1,0:T(8,128)} collective-permute-done((f32[832,128]{1,0:T(8,128)S(1)}, f32[832,128]{1,0:T(8,128)}, u32[]{:S(2)}, u32[]{:S(2)}) %collective-permute-start.1) | collective-permute-done | bytes 426016 | tf_op jit(solution)/shard_map/ppermute | solution.py:261
  26.4 2.0 %collective-permute-start.8 = (f32[768,128]{1,0:T(8,128)}, f32[768,128]{1,0:T(8,128)}, u32[]{:S(2)}, u32[]{:S(2)}) collective-permute-start(f32[768,128]{1,0:T(8,128)} %collective-permute-done.2.refs_2_), channel_id=1, source_target_pairs={{8,0},{16,8},{24,16},{28,24},{20,28},{12,20},{4,12},{0,4},{9,1},{1... | collective-permute-start | bytes 1179656 | tf_op jit(solution)/shard_map/ppermute | solution.py:258
  28.4 4.0 %collective-permute-done.10.refs_3_ = f32[832,128]{1,0:T(8,128)} collective-permute-done((f32[832,128]{1,0:T(8,128)S(1)}, f32[832,128]{1,0:T(8,128)}, u32[]{:S(2)}, u32[]{:S(2)}) %collective-permute-start.10) | collective-permute-done | bytes 426016 | tf_op jit(solution)/shard_map/ppermute | solution.py:258
  32.4 2.0 %collective-permute-start.11 = (f32[832,128]{1,0:T(8,128)}, f32[832,128]{1,0:T(8,128)}, u32[]{:S(2)}, u32[]{:S(2)}) collective-permute-start(f32[832,128]{1,0:T(8,128)} %collective-permute-done.10.refs_3_), channel_id=1, source_target_pairs={{8,0},{16,8},{24,16},{28,24},{20,28},{12,20},{4,12},{0,4},{9,1},{1... | collective-permute-start | bytes 1277960 | tf_op jit(solution)/shard_map/ppermute | solution.py:258
  34.4 1.7 %copy-done = bf16[800,1600]{1,0:T(8,128)(2,1)S(1)} copy-done((bf16[800,1600]{1,0:T(8,128)(2,1)S(1)}, bf16[800,1600]{1,0:T(8,128)(2,1)}, u32[]{:S(2)}) %copy-start) | copy-done | bytes 2560024
  36.1 3.0 %shard_map.55 = (f32[800,128]{1,0:T(8,128)S(1)}, f32[4,896]{1,0:T(4,128)S(1)}, f32[800,128]{1,0:T(8,128)S(1)}, f32[4,896]{1,0:T(4,128)S(1)}) custom-call(bf16[800,1600]{1,0:T(8,128)(2,1)S(1)} %copy-done, f32[768,128]{1,0:T(8,128)S(1)} %collective-permute-done.refs_0_, f32[832,128]{1,0:T(8,128)} %collective-permute-done.1.refs_1_, ...), custom_call_target="tpu_custom_call" | custom-call | flops 200000000 | tf_op jit(solution)/shard_map/pallas_call | solution.py:20
  39.2 0.8 copy-done.4
  40.0 0.8 copy-done.6
  40.7 0.1 collective-permute-start.5
  40.8 2.8 %collective-permute-done.6.refs_1_ = f32[832,128]{1,0:T(8,128)} collective-permute-done((f32[832,128]{1,0:T(8,128)}, f32[832,128]{1,0:T(8,128)}, u32[]{:S(2)}, u32[]{:S(2)}) %collective-permute-start.6) | collective-permute-done | bytes 426016 | tf_op jit(solution)/shard_map/ppermute | solution.py:261
  43.8 3.1 %shard_map.59 = (f32[800,128]{1,0:T(8,128)S(1)}, f32[4,896]{1,0:T(4,128)S(1)}, f32[800,128]{1,0:T(8,128)S(1)}, f32[4,896]{1,0:T(4,128)S(1)}) custom-call(bf16[800,1600]{1,0:T(8,128)(2,1)S(1)} %copy-done.1, f32[768,128]{1,0:T(8,128)} %collective-permute-done.4.refs_0_, f32[832,128]{1,0:T(8,128)} %collective-permute-done.6.refs_1_, ...), custom_call_target="tpu_custom_call" | custom-call | flops 200000000 | tf_op jit(solution)/shard_map/pallas_call | solution.py:20
  46.9 0.8 shard_map.60
  47.7 0.8 copy-done.8
  48.5 1.9 %collective-permute-start.9 = (f32[768,128]{1,0:T(8,128)}, f32[768,128]{1,0:T(8,128)}, u32[]{:S(2)}, u32[]{:S(2)}) collective-permute-start(f32[768,128]{1,0:T(8,128)} %collective-permute-done.8.refs_2_), channel_id=1, source_target_pairs={{8,0},{16,8},{24,16},{28,24},{20,28},{12,20},{4,12},{0,4},{9,1},{1... | collective-permute-start | bytes 1179656 | tf_op jit(solution)/shard_map/ppermute | solution.py:258
  50.5 1.6 %collective-permute-start.18 = (f32[832,128]{1,0:T(8,128)}, f32[832,128]{1,0:T(8,128)}, u32[]{:S(2)}, u32[]{:S(2)}) collective-permute-start(f32[832,128]{1,0:T(8,128)} %collective-permute-done.11.refs_3_), channel_id=1, source_target_pairs={{8,0},{16,8},{24,16},{28,24},{20,28},{12,20},{4,12},{0,4},{9,1},{1... | collective-permute-start | bytes 1277960 | tf_op jit(solution)/shard_map/ppermute | solution.py:258
  52.0 1.0 %shard_map.61 = (f32[800,128]{1,0:T(8,128)S(1)}, f32[4,896]{1,0:T(4,128)S(1)}) custom-call(bf16[800,1600]{1,0:T(8,128)(2,1)S(1)} %copy-done.1, f32[768,128]{1,0:T(8,128)S(1)} %slice.12.refs_0_, f32[832,128]{1,0:T(8,128)S(1)} %slice.13.refs_1_), custom_call_target="tpu_custom_call" | custom-call | flops 100000000 | tf_op jit(solution)/shard_map/pallas_call | solution.py:20
  53.0 0.8 copy-done.9
  53.8 0.6 copy-done.11
  54.4 0.4 collective-permute-start.17
  55.0 5.9 %collective-permute-done.9.refs_2_ = f32[768,128]{1,0:T(8,128)} collective-permute-done((f32[768,128]{1,0:T(8,128)}, f32[768,128]{1,0:T(8,128)}, u32[]{:S(2)}, u32[]{:S(2)}) %collective-permute-start.9) | collective-permute-done | bytes 393248 | tf_op jit(solution)/shard_map/ppermute | solution.py:258
  60.8 1.2 %add.284.two_any = f32[800,128]{1,0:T(8,128)S(1)} add(f32[800,128]{1,0:T(8,128)} %copy-done.8, f32[800,128]{1,0:T(8,128)} %collective-permute-done.15) | non-fusion elementwise | flops 102400 | bytes 1228800 | tf_op jit(solution)/shard_map/add | solution.py:319
  62.1 4.6 %collective-permute-start.16 = (f32[800,128]{1,0:T(8,128)S(1)}, f32[800,128]{1,0:T(8,128)}, u32[]{:S(2)}, u32[]{:S(2)}) collective-permute-start(f32[800,128]{1,0:T(8,128)S(1)} %add.284.two_any), channel_id=1, source_target_pairs={{3,1},{10,8},{18,16},{27,25},{28,30},{21,23},{13,15},{4,6},{0,2},{... | collective-permute-start | bytes 1228808 | tf_op jit(solution)/shard_map/ppermute | solution.py:299
  66.6 3.1 %shard_map.56 = (f32[800,128]{1,0:T(8,128)S(1)}, f32[4,896]{1,0:T(4,128)S(1)}, f32[800,128]{1,0:T(8,128)S(1)}, f32[4,896]{1,0:T(4,128)S(1)}) custom-call(bf16[800,1600]{1,0:T(8,128)(2,1)S(1)} %copy-done.1, f32[768,128]{1,0:T(8,128)} %collective-permute-done.5.refs_0_, f32[832,128]{1,0:T(8,128)} %collective-permute-done.7.refs_1_, ...), custom_call_target="tpu_custom_call" | custom-call | flops 200000000 | tf_op jit(solution)/shard_map/pallas_call | solution.py:20
  69.8 0.6 copy-done.13
  70.4 0.7 shard_map.57
  71.1 0.9 copy-done.2
  72.0 1.0 fusion
  73.0 0.5 collective-permute-start.12
  73.5 2.1 %shard_map.62 = (f32[800,128]{1,0:T(8,128)S(1)}, f32[4,896]{1,0:T(4,128)S(1)}) custom-call(bf16[800,1600]{1,0:T(8,128)(2,1)S(1)} %copy-done.1, f32[768,128]{1,0:T(8,128)} %collective-permute-done.17.refs_0_, f32[832,128]{1,0:T(8,128)} %collective-permute-done.18.refs_1_), custom_call_target="tpu_custom_call" | custom-call | flops 100000000 | tf_op jit(solution)/shard_map/pallas_call | solution.py:20
  75.8 0.5 copy-done.17
  76.2 1.1 %copy-done.3 = f32[1600,128]{1,0:T(8,128)S(1)} copy-done((f32[1600,128]{1,0:T(8,128)S(1)}, f32[1600,128]{1,0:T(8,128)}, u32[]{:S(2)}) %copy-start.3) | copy-done | bytes 819224
  77.4 1.2 %shard_map.58 = (f32[800,128]{1,0:T(8,128)S(1)}, f32[800,128]{1,0:T(8,128)S(1)}) custom-call(s32[1]{0:T(128)} %bitcast.3.flag_ref, f32[1600,128]{1,0:T(8,128)S(1)} %copy-done.3, f32[800,128]{1,0:T(8,128)} %collective-permute-done.12.refs_0_, f32[800,128]{1,0:T(8,128)} %collective-permute-done.13.refs_1_), custom_call_target="tpu_custom_call" | custom-call | flops 50000000 | tf_op jit(solution)/shard_map/pallas_call | solution.py:20
  78.8 1.3 %collective-permute-start.20 = (f32[800,128]{1,0:T(8,128)S(1)}, f32[800,128]{1,0:T(8,128)S(1)}, u32[]{:S(2)}, u32[]{:S(2)}) collective-permute-start(f32[800,128]{1,0:T(8,128)S(1)} %add.289.zero_ref), channel_id=1, source_target_pairs={{2,0},{11,9},{16,18},{25,27},{29,31},{20,22},{15,13},{6,4},{1,3},{... | collective-permute-start | bytes 1228808 | tf_op jit(solution)/shard_map/ppermute | solution.py:299
  80.6 0.6 shard_map.64
  81.1 2.6 %collective-permute-start.21 = (f32[8,896]{1,0:T(8,128)S(1)}, f32[8,896]{1,0:T(8,128)S(1)}, u32[]{:S(2)}, u32[]{:S(2)}) collective-permute-start(f32[8,896]{1,0:T(8,128)S(1)} %get-tuple-element.62), channel_id=1, source_target_pairs={{0,1},{1,0},{2,3},{3,2},{4,5},{5,4},{6,7},{7,6},{8,9},{9,8},{10,11... | collective-permute-start | bytes 86024 | tf_op jit(solution)/shard_map/ppermute | solution.py:277
  83.8 0.9 collective-permute-done.21.got_ref
  84.6 0.5 collective-permute-start.22
  85.2 0.1 shard_map.66.weights_ref
  85.3 9.9 %collective-permute-done.22.got_ref = f32[4,896]{1,0:T(4,128)S(1)} collective-permute-done((f32[4,896]{1,0:T(4,128)S(1)}, f32[4,896]{1,0:T(4,128)S(1)}, u32[]{:S(2)}, u32[]{:S(2)}) %collective-permute-start.22) | collective-permute-done | bytes 14368 | tf_op jit(solution)/shard_map/ppermute | solution.py:302
  95.2 3.1 %shard_map.67 = f32[800,256]{1,0:T(8,128)} custom-call(s32[3]{0:T(128)S(1)} %pad_add_fusion.flag_ref, f32[800,128]{1,0:T(8,128)S(1)} %get-tuple-element.42.odd_any, f32[800,128]{1,0:T(8,128)S(1)} %collective-permute-done.14.odd_got_any, f32[800,128]{1,0:T(8,128)S(1)} %add.284.two_any, f32[800,128]{1,0:T(8,128)} %collective-permute-done.16.two_got_any, ...), custom_call_target="tpu_custom_call" | custom-call | tf_op jit(solution)/shard_map/pallas_call | solution.py:20
  (63 shorter events, 0.8 us)
Async XLA Ops:
  1.0 13.7 %collective-permute-start.3 = (f32[832,128]{1,0:T(8,128)S(1)}, f32[832,128]{1,0:T(8,128)S(1)}, u32[]{:S(2)}, u32[]{:S(2)}) collective-permute-start(f32[832,128]{1,0:T(8,128)S(1)} %slice.13.refs_1_), channel_id=1, source_target_pairs={{8,0},{16,8},{24,16},{28,24},{20,28},{12,20},{4,12},{0,4},{9,1},{1... | collective-permute-start | bytes 1277960 | tf_op jit(solution)/shard_map/ppermute | solution.py:258
  5.1 12.1 %collective-permute-start = (f32[768,128]{1,0:T(8,128)S(1)}, f32[768,128]{1,0:T(8,128)S(1)}, u32[]{:S(2)}, u32[]{:S(2)}) collective-permute-start(f32[768,128]{1,0:T(8,128)S(1)} %slice.12.refs_0_), channel_id=1, source_target_pairs={{0,8},{8,16},{16,24},{24,28},{28,20},{20,12},{12,4},{4,0},{1,9},{9... | collective-permute-start | bytes 1179656 | tf_op jit(solution)/shard_map/ppermute | solution.py:261
  5.2 21.2 %collective-permute-start.1 = (f32[832,128]{1,0:T(8,128)S(1)}, f32[832,128]{1,0:T(8,128)}, u32[]{:S(2)}, u32[]{:S(2)}) collective-permute-start(f32[832,128]{1,0:T(8,128)S(1)} %slice.13.refs_1_), channel_id=1, source_target_pairs={{0,8},{8,16},{16,24},{24,28},{28,20},{20,12},{12,4},{4,0},{1,9},{9... | collective-permute-start | bytes 1277960 | tf_op jit(solution)/shard_map/ppermute | solution.py:261
  7.2 19.2 %collective-permute-start.2 = (f32[768,128]{1,0:T(8,128)S(1)}, f32[768,128]{1,0:T(8,128)}, u32[]{:S(2)}, u32[]{:S(2)}) collective-permute-start(f32[768,128]{1,0:T(8,128)S(1)} %slice.12.refs_0_), channel_id=1, source_target_pairs={{8,0},{16,8},{24,16},{28,24},{20,28},{12,20},{4,12},{0,4},{9,1},{1... | collective-permute-start | bytes 1179656 | tf_op jit(solution)/shard_map/ppermute | solution.py:258
  14.8 17.7 %collective-permute-start.10 = (f32[832,128]{1,0:T(8,128)S(1)}, f32[832,128]{1,0:T(8,128)}, u32[]{:S(2)}, u32[]{:S(2)}) collective-permute-start(f32[832,128]{1,0:T(8,128)S(1)} %collective-permute-done.3.refs_3_), channel_id=1, source_target_pairs={{8,0},{16,8},{24,16},{28,24},{20,28},{12,20},{4,12},{0,4},{9,1},{1... | collective-permute-start | bytes 1277960 | tf_op jit(solution)/shard_map/ppermute | solution.py:258
  17.1 23.6 %collective-permute-start.4 = (f32[768,128]{1,0:T(8,128)S(1)}, f32[768,128]{1,0:T(8,128)}, u32[]{:S(2)}, u32[]{:S(2)}) collective-permute-start(f32[768,128]{1,0:T(8,128)S(1)} %collective-permute-done.refs_0_), channel_id=1, source_target_pairs={{0,8},{8,16},{16,24},{24,28},{28,20},{20,12},{12,4},{4,0},{1,9},{9... | collective-permute-start | bytes 1179656 | tf_op jit(solution)/shard_map/ppermute | solution.py:261
  26.4 17.3 %collective-permute-start.6 = (f32[832,128]{1,0:T(8,128)}, f32[832,128]{1,0:T(8,128)}, u32[]{:S(2)}, u32[]{:S(2)}) collective-permute-start(f32[832,128]{1,0:T(8,128)} %collective-permute-done.1.refs_1_), channel_id=1, source_target_pairs={{0,8},{8,16},{16,24},{24,28},{28,20},{20,12},{12,4},{4,0},{1,9},{9... | collective-permute-start | bytes 1277960 | tf_op jit(solution)/shard_map/ppermute | solution.py:261
  26.4 14.4 %collective-permute-start.8 = (f32[768,128]{1,0:T(8,128)}, f32[768,128]{1,0:T(8,128)}, u32[]{:S(2)}, u32[]{:S(2)}) collective-permute-start(f32[768,128]{1,0:T(8,128)} %collective-permute-done.2.refs_2_), channel_id=1, source_target_pairs={{8,0},{16,8},{24,16},{28,24},{20,28},{12,20},{4,12},{0,4},{9,1},{1... | collective-permute-start | bytes 1179656 | tf_op jit(solution)/shard_map/ppermute | solution.py:258
  32.4 18.0 %collective-permute-start.11 = (f32[832,128]{1,0:T(8,128)}, f32[832,128]{1,0:T(8,128)}, u32[]{:S(2)}, u32[]{:S(2)}) collective-permute-start(f32[832,128]{1,0:T(8,128)} %collective-permute-done.10.refs_3_), channel_id=1, source_target_pairs={{8,0},{16,8},{24,16},{28,24},{20,28},{12,20},{4,12},{0,4},{9,1},{1... | collective-permute-start | bytes 1277960 | tf_op jit(solution)/shard_map/ppermute | solution.py:258
  34.4 1.8 %copy-start = (bf16[800,1600]{1,0:T(8,128)(2,1)S(1)}, bf16[800,1600]{1,0:T(8,128)(2,1)}, u32[]{:S(2)}) copy-start(bf16[800,1600]{1,0:T(8,128)(2,1)} %relation_ref.9) | copy-start | bytes 7680004
  36.1 7.6 %copy-start.1 = (bf16[800,1600]{1,0:T(8,128)(2,1)S(1)}, bf16[800,1600]{1,0:T(8,128)(2,1)}, u32[]{:S(2)}) copy-start(bf16[800,1600]{1,0:T(8,128)(2,1)} %relation_ref.9) | copy-start | bytes 7680004
  39.2 0.8 copy-start.4
  40.0 0.8 copy-start.6
  40.7 13.7 %collective-permute-start.5 = (f32[768,128]{1,0:T(8,128)}, f32[768,128]{1,0:T(8,128)}, u32[]{:S(2)}, u32[]{:S(2)}) collective-permute-start(f32[768,128]{1,0:T(8,128)} %collective-permute-done.4.refs_0_), channel_id=1, source_target_pairs={{0,8},{8,16},{16,24},{24,28},{28,20},{20,12},{12,4},{4,0},{1,9},{9... | collective-permute-start | bytes 1179656 | tf_op jit(solution)/shard_map/ppermute | solution.py:261
  43.7 22.9 %collective-permute-start.7 = (f32[832,128]{1,0:T(8,128)}, f32[832,128]{1,0:T(8,128)}, u32[]{:S(2)}, u32[]{:S(2)}) collective-permute-start(f32[832,128]{1,0:T(8,128)} %collective-permute-done.6.refs_1_), channel_id=1, source_target_pairs={{0,8},{8,16},{16,24},{24,28},{28,20},{20,12},{12,4},{4,0},{1,9},{9... | collective-permute-start | bytes 1277960 | tf_op jit(solution)/shard_map/ppermute | solution.py:261
  47.7 0.8 copy-start.8
  48.5 12.3 %collective-permute-start.15 = (f32[800,128]{1,0:T(8,128)}, f32[800,128]{1,0:T(8,128)}, u32[]{:S(2)}, u32[]{:S(2)}) collective-permute-start(f32[800,128]{1,0:T(8,128)} %get-tuple-element.47), channel_id=1, source_target_pairs={{0,1},{1,0},{2,3},{3,2},{4,5},{5,4},{6,7},{7,6},{8,9},{9,8},{10,11... | collective-permute-start | bytes 1228808 | tf_op jit(solution)/shard_map/ppermute | solution.py:277
  48.5 12.3 %collective-permute-start.9 = (f32[768,128]{1,0:T(8,128)}, f32[768,128]{1,0:T(8,128)}, u32[]{:S(2)}, u32[]{:S(2)}) collective-permute-start(f32[768,128]{1,0:T(8,128)} %collective-permute-done.8.refs_2_), channel_id=1, source_target_pairs={{8,0},{16,8},{24,16},{28,24},{20,28},{12,20},{4,12},{0,4},{9,1},{1... | collective-permute-start | bytes 1179656 | tf_op jit(solution)/shard_map/ppermute | solution.py:258
  50.5 23.0 %collective-permute-start.18 = (f32[832,128]{1,0:T(8,128)}, f32[832,128]{1,0:T(8,128)}, u32[]{:S(2)}, u32[]{:S(2)}) collective-permute-start(f32[832,128]{1,0:T(8,128)} %collective-permute-done.11.refs_3_), channel_id=1, source_target_pairs={{8,0},{16,8},{24,16},{28,24},{20,28},{12,20},{4,12},{0,4},{9,1},{1... | collective-permute-start | bytes 1277960 | tf_op jit(solution)/shard_map/ppermute | solution.py:258
  53.0 0.8 copy-start.9
  53.8 0.6 copy-start.11
  54.4 19.0 %collective-permute-start.17 = (f32[768,128]{1,0:T(8,128)}, f32[768,128]{1,0:T(8,128)}, u32[]{:S(2)}, u32[]{:S(2)}) collective-permute-start(f32[768,128]{1,0:T(8,128)} %collective-permute-done.5.refs_0_), channel_id=1, source_target_pairs={{0,8},{8,16},{16,24},{24,28},{28,20},{20,12},{12,4},{4,0},{1,9},{9... | collective-permute-start | bytes 1179656 | tf_op jit(solution)/shard_map/ppermute | solution.py:261
  60.8 9.6 %copy-start.5 = (f32[800,128]{1,0:T(8,128)S(1)}, f32[800,128]{1,0:T(8,128)}, u32[]{:S(2)}) copy-start(f32[800,128]{1,0:T(8,128)} %copy-done.4) | copy-start | bytes 1228804
  60.8 9.6 %copy-start.7 = (f32[800,128]{1,0:T(8,128)S(1)}, f32[800,128]{1,0:T(8,128)}, u32[]{:S(2)}) copy-start(f32[800,128]{1,0:T(8,128)} %copy-done.6) | copy-start | bytes 1228804
  62.1 16.6 %collective-permute-start.16 = (f32[800,128]{1,0:T(8,128)S(1)}, f32[800,128]{1,0:T(8,128)}, u32[]{:S(2)}, u32[]{:S(2)}) collective-permute-start(f32[800,128]{1,0:T(8,128)S(1)} %add.284.two_any), channel_id=1, source_target_pairs={{3,1},{10,8},{18,16},{27,25},{28,30},{21,23},{13,15},{4,6},{0,2},{... | collective-permute-start | bytes 1228808 | tf_op jit(solution)/shard_map/ppermute | solution.py:299
  69.8 0.6 copy-start.13
  70.4 0.7 copy-start.15
  71.1 0.9 copy-start.2
  72.0 3.7 %copy-start.10 = (f32[800,128]{1,0:T(8,128)S(1)}, f32[800,128]{1,0:T(8,128)}, u32[]{:S(2)}) copy-start(f32[800,128]{1,0:T(8,128)} %copy-done.9) | copy-start | bytes 1228804
  73.0 3.3 %collective-permute-start.13 = (f32[800,128]{1,0:T(8,128)}, f32[800,128]{1,0:T(8,128)}, u32[]{:S(2)}, u32[]{:S(2)}) collective-permute-start(f32[800,128]{1,0:T(8,128)} %get-tuple-element.65), channel_id=1, source_target_pairs={{0,1},{1,0},{2,3},{3,2},{4,5},{5,4},{6,7},{7,6},{8,9},{9,8},{10,11... | collective-permute-start | bytes 1228808 | tf_op jit(solution)/shard_map/ppermute | solution.py:277
  73.0 3.3 %collective-permute-start.12 = (f32[800,128]{1,0:T(8,128)}, f32[800,128]{1,0:T(8,128)}, u32[]{:S(2)}, u32[]{:S(2)}) collective-permute-start(f32[800,128]{1,0:T(8,128)} %get-tuple-element.66), channel_id=1, source_target_pairs={{0,1},{1,0},{2,3},{3,2},{4,5},{5,4},{6,7},{7,6},{8,9},{9,8},{10,11... | collective-permute-start | bytes 1228808 | tf_op jit(solution)/shard_map/ppermute | solution.py:277
  75.6 0.6 copy-start.17
  75.6 4.9 %copy-start.12 = (f32[4,896]{1,0:T(4,128)S(1)}, f32[4,896]{1,0:T(4,128)}, u32[]{:S(2)}) copy-start(f32[4,896]{1,0:T(4,128)} %copy-done.11) | copy-start | bytes 43012
  75.6 4.9 %copy-start.14 = (f32[4,896]{1,0:T(4,128)S(1)}, f32[4,896]{1,0:T(4,128)}, u32[]{:S(2)}) copy-start(f32[4,896]{1,0:T(4,128)} %copy-done.13) | copy-start | bytes 43012
  75.6 4.9 %copy-start.16 = (f32[4,896]{1,0:T(4,128)S(1)}, f32[4,896]{1,0:T(4,128)}, u32[]{:S(2)}) copy-start(f32[4,896]{1,0:T(4,128)} %copy-done.15) | copy-start | bytes 43012
  75.6 9.6 %copy-start.19 = (f32[1024]{0:T(1024)S(1)}, f32[1024]{0:T(1024)}, u32[]{:S(2)}) copy-start(f32[1024]{0:T(1024)} %one_ref.1) | copy-start | bytes 12292
  75.7 9.6 %copy-start.20 = (f32[1024]{0:T(1024)S(1)}, f32[1024]{0:T(1024)}, u32[]{:S(2)}) copy-start(f32[1024]{0:T(1024)} %two_ref.1) | copy-start | bytes 12292
  75.7 9.6 %copy-start.21 = (f32[1024]{0:T(1024)S(1)}, f32[1024]{0:T(1024)}, u32[]{:S(2)}) copy-start(f32[1024]{0:T(1024)} %scale_ref.1) | copy-start | bytes 12292
  76.2 4.3 %copy-start.18 = (f32[4,896]{1,0:T(4,128)S(1)}, f32[4,896]{1,0:T(4,128)}, u32[]{:S(2)}) copy-start(f32[4,896]{1,0:T(4,128)} %copy-done.17) | copy-start | bytes 43012
  76.2 2.5 %collective-permute-start.19 = (f32[800,128]{1,0:T(8,128)S(1)}, f32[800,128]{1,0:T(8,128)S(1)}, u32[]{:S(2)}, u32[]{:S(2)}) collective-permute-start(f32[800,128]{1,0:T(8,128)S(1)} %get-tuple-element.52), channel_id=1, source_target_pairs={{0,1},{1,0},{2,3},{3,2},{4,5},{5,4},{6,7},{7,6},{8,9},{9,8},{10,11... | collective-permute-start | bytes 1228808 | tf_op jit(solution)/shard_map/ppermute | solution.py:277
  76.2 1.1 %copy-start.3 = (f32[1600,128]{1,0:T(8,128)S(1)}, f32[1600,128]{1,0:T(8,128)}, u32[]{:S(2)}) copy-start(f32[1600,128]{1,0:T(8,128)} %copy-done.2) | copy-start | bytes 2457604
  78.6 16.6 %collective-permute-start.14 = (f32[800,128]{1,0:T(8,128)S(1)}, f32[800,128]{1,0:T(8,128)S(1)}, u32[]{:S(2)}, u32[]{:S(2)}) collective-permute-start(f32[800,128]{1,0:T(8,128)S(1)} %get-tuple-element.43), channel_id=1, source_target_pairs={{0,2},{1,3},{2,0},{3,1},{4,6},{5,7},{6,4},{7,5},{8,10},{9,11},{10,... | collective-permute-start | bytes 1228808 | tf_op jit(solution)/shard_map/ppermute | solution.py:302
  78.8 16.5 %collective-permute-start.20 = (f32[800,128]{1,0:T(8,128)S(1)}, f32[800,128]{1,0:T(8,128)S(1)}, u32[]{:S(2)}, u32[]{:S(2)}) collective-permute-start(f32[800,128]{1,0:T(8,128)S(1)} %add.289.zero_ref), channel_id=1, source_target_pairs={{2,0},{11,9},{16,18},{25,27},{29,31},{20,22},{15,13},{6,4},{1,3},{... | collective-permute-start | bytes 1228808 | tf_op jit(solution)/shard_map/ppermute | solution.py:299
  81.1 3.5 %collective-permute-start.21 = (f32[8,896]{1,0:T(8,128)S(1)}, f32[8,896]{1,0:T(8,128)S(1)}, u32[]{:S(2)}, u32[]{:S(2)}) collective-permute-start(f32[8,896]{1,0:T(8,128)S(1)} %get-tuple-element.62), channel_id=1, source_target_pairs={{0,1},{1,0},{2,3},{3,2},{4,5},{5,4},{6,7},{7,6},{8,9},{9,8},{10,11... | collective-permute-start | bytes 86024 | tf_op jit(solution)/shard_map/ppermute | solution.py:277
  84.6 10.6 %collective-permute-start.22 = (f32[4,896]{1,0:T(4,128)S(1)}, f32[4,896]{1,0:T(4,128)S(1)}, u32[]{:S(2)}, u32[]{:S(2)}) collective-permute-start(f32[4,896]{1,0:T(4,128)S(1)} %get-tuple-element.64), channel_id=1, source_target_pairs={{0,2},{1,3},{2,0},{3,1},{4,6},{5,7},{6,4},{7,5},{8,10},{9,11},{10,... | collective-permute-start | bytes 43016 | tf_op jit(solution)/shard_map/ppermute | solution.py:302

commit v3 on v0

--- a/solution.py
+++ b/solution.py
@@ -1,7 +1,278 @@
+import functools
+
 import jax
 import jax.numpy as jnp
 from jax import lax
+from jax.experimental import pallas as pl
+from jax.experimental.pallas import tpu as pltpu
 from jax.sharding import PartitionSpec as P
+
+VMEM_LIMIT = 12 * 1024 * 1024
+WIDTH = 128
+KERNEL_FLOPS = 10**8
+
+WHOLE = pl.BlockSpec(memory_space=pltpu.VMEM)
+
+
+def call(kernel, shapes, operands, scratch=(), flops=0):
+    return pl.pallas_call(
+        kernel,
+        out_shape=[jax.ShapeDtypeStruct(shape, jnp.float32) for shape in shapes],
+        in_specs=[WHOLE] * len(operands),
+        out_specs=[WHOLE] * len(shapes),
+        scratch_shapes=scratch,
+        compiler_params=pltpu.CompilerParams(vmem_limit_bytes=VMEM_LIMIT),
+        cost_estimate=pl.CostEstimate(flops=flops, bytes_accessed=0, transcendentals=0),
+    )(*operands)
+
+
+def bands(phi_one, phi_two, innov_scale):
+    count = phi_one.shape[1]
+    row = lax.broadcasted_iota(jnp.int32, (8, count), 0)
+    lane = lax.broadcasted_iota(jnp.int32, (8, count), 1)
+
+    def rows(*values):
+        out = jnp.zeros((8, count), jnp.float32)
+        for n, value in enumerate(values):
+            out = jnp.where(row == n, value, out)
+        return out
+
+    now = rows(phi_one, phi_two, innov_scale)
+    next_1 = jnp.where(lane < count - 1, pltpu.roll(now, count - 1, 1), 0.0)
+    next_2 = jnp.where(lane < count - 2, pltpu.roll(now, count - 2, 1), 0.0)
+    first_0, second_0, scale_0 = (now[n : n + 1] for n in range(3))
+    first_1, second_1, scale_1 = (next_1[n : n + 1] for n in range(3))
+    first_2, second_2, scale_2 = (next_2[n : n + 1] for n in range(3))
+    return rows(
+        -scale_0 * second_0,
+        first_1 * scale_1 * second_1 - scale_0 * first_0,
+        scale_0 + first_1 * first_1 * scale_1 + second_2 * second_2 * scale_2,
+        second_2 * scale_2 * first_2 - first_1 * scale_1,
+        -second_2 * scale_2,
+    )
+
+
+class Spot:
+    def __init__(self, gens, tms):
+        self.gens, self.share, self.half = gens, gens // tms, gens // 2
+        self.gen, self.tm = lax.axis_index("gen"), lax.axis_index("tm")
+        self.place = self.place_of(self.gen)
+
+    def place_of(self, gen):
+        return jnp.where(gen % 2 == 0, gen // 2, self.gens - 1 - gen // 2)
+
+    def block_at(self, far):
+        p = (self.place + (far + self.gens)) % self.gens
+        return jnp.where(p < self.half, 2 * p, 2 * (self.gens - 1 - p) + 1)
+
+    def owner_of(self, far):
+        return self.block_at(far) // self.share
+
+    def keeps(self, far):
+        return jnp.where(self.owner_of(far) % 2 == self.tm % 2, 1, 0)
+
+    def border_of(self, far, fars):
+        there = (2 * self.gens - 2 * self.place - far) % self.gens
+        at = jnp.int32(len(fars))
+        for m, other in enumerate(fars):
+            if other != far:
+                at = jnp.where(there == other % self.gens, m, at)
+        return at
+
+
+def weights_kernel(one_ref, two_ref, scale_ref, weights_ref):
+    weights_ref[...] = bands(one_ref[...][None], two_ref[...][None], scale_ref[...][None])
+
+
+def products_kernel(relation_ref, *refs):
+    both_ref, padded_ref = refs[-2:]
+    count = (len(refs) - 2) // 4
+    rows = relation_ref.shape[0]
+    padded_ref[...] = jnp.zeros_like(padded_ref)
+    for n in range(count):
+        block = jnp.concatenate([refs[2 * n][...], refs[2 * n + 1][...]], axis=0)
+        high = block.astype(jnp.bfloat16)
+        low = (block - high.astype(jnp.float32)).astype(jnp.bfloat16)
+        both_ref[...] = jnp.dot(
+            relation_ref[...],
+            jnp.concatenate([high, low], axis=1),
+            preferred_element_type=jnp.float32,
+        )
+        padded_ref[:rows] = both_ref[:, :WIDTH] + both_ref[:, WIDTH:]
+        refs[2 * count + 2 * n][...] = padded_ref[:rows]
+        turned = padded_ref[...].T
+        edges_ref = refs[2 * count + 2 * n + 1]
+        edges_ref[0:2] = turned[0:2]
+        edges_ref[2:4] = turned[WIDTH - 2 :]
+
+
+def class_kernel(spot_of, fars, *refs):
+    send_ref, keep_ref, edges_ref, message_ref = refs[-4:]
+    spot = spot_of()
+    rows, long = refs[0].shape[0], message_ref.shape[1]
+    for m in range(4):
+        edges_ref[m] = refs[2 * m + 1][...]
+    edges_ref[4] = jnp.zeros_like(refs[1])
+    for m in range(4):
+        there = edges_ref[spot.border_of(fars[m], fars)]
+        border = jnp.where(spot.block_at(fars[m]) % spot.share == 0, there[2:4], there[0:2])
+        message_ref[m % 2, :rows] = refs[2 * m][...]
+        message_ref[m % 2, rows:] = jnp.zeros((long - rows, WIDTH), jnp.float32)
+        for k in range(border.shape[1] // WIDTH):
+            message_ref[m % 2, rows + 2 * k : rows + 2 * k + 2] = border[:, k * WIDTH : (k + 1) * WIDTH]
+        if m % 2:
+            here = pl.ds(m // 2 * long, long)
+            near = spot.keeps(fars[m - 1])
+            keep_ref[here] = message_ref[1 - near]
+            send_ref[here] = message_ref[near]
+
+
+def part_sums_kernel(spot_of, fars, keep_ref, got_ref, send_ref, mine_ref):
+    spot = spot_of()
+    owner = jnp.where(spot.keeps(fars[0]) == 1, spot.owner_of(fars[0]), spot.owner_of(fars[1]))
+    mine = jnp.where(owner // 2 == spot.tm // 2, 0, 1)
+    rows = mine_ref.shape[0]
+    for n in range(2):
+
+        @pl.when(mine == n)
+        def _():
+            here, there = slice(n * rows, (n + 1) * rows), slice((1 - n) * rows, (2 - n) * rows)
+            send_ref[...] = keep_ref[there] + got_ref[there]
+            mine_ref[...] = keep_ref[here] + got_ref[here]
+
+
+def last_kernel(
+    spot_of, mine_odd, got_odd, mine_even, got_even, weights_ref, out_ref, sums_ref, sides_ref
+):
+    spot = spot_of()
+    odd = jnp.where((spot.place_of(spot.share * spot.tm) + spot.place) % 2 == 0, 1, 0)
+    rows = out_ref.shape[0]
+    span = sides_ref.shape[1]
+    sums_ref[odd] = mine_odd[...] + got_odd[...]
+    sums_ref[1 - odd] = mine_even[...] + got_even[...]
+    start = pl.multiple_of(spot.tm * (2 * WIDTH), 2 * WIDTH)
+    weights = weights_ref[:, pl.ds(start, 2 * WIDTH)]
+    row = lax.broadcasted_iota(jnp.int32, (8, span), 0)
+    nothing = jnp.zeros((WIDTH - 8, span), jnp.float32)
+
+    def border(column):
+        return jnp.concatenate(
+            [sums_ref[column, rows + 2 * k : rows + 2 * k + 2] for k in range(span // WIDTH)], axis=1
+        )
+
+    before, after = border(0), border(1)
+    end = 2 * WIDTH - 1
+    first = weights[0:1, 0:1] * before[0:1] + weights[1:2, 0:1] * before[1:2]
+    second = weights[0:1, 1:2] * before[1:2]
+    above = jnp.where(row == 0, first, jnp.where(row == 1, second, 0.0))
+    last = weights[3:4, end:] * after[0:1] + weights[4:5, end:] * after[1:2]
+    but_last = weights[4:5, end - 1 : end] * after[0:1]
+    below = jnp.where(row == 7, last, jnp.where(row == 6, but_last, 0.0))
+    sides_ref[0] = jnp.concatenate([above, nothing], axis=0).T
+    sides_ref[1] = jnp.concatenate([nothing, below], axis=0).T
+    lane = lax.broadcasted_iota(jnp.int32, (1, WIDTH), 1)
+    inner = [weights[:, :WIDTH], weights[:, WIDTH:]]
+    step = rows // 5
+
+    @pl.loop(0, 5)
+    def _(n):
+        here = pl.ds(pl.multiple_of(n * step, 8), step)
+        left, right = sums_ref[0, here], sums_ref[1, here]
+        made = [sides_ref[0, here] + inner[0][2:3] * left, sides_ref[1, here] + inner[1][2:3] * right]
+        for far in (1, 2):
+            left_back, right_back = pltpu.roll(left, far, 1), pltpu.roll(right, far, 1)
+            left_on, right_on = pltpu.roll(left, WIDTH - far, 1), pltpu.roll(right, WIDTH - far, 1)
+            back, on = [w[2 - far : 3 - far] for w in inner], [w[2 + far : 3 + far] for w in inner]
+            made[0] += jnp.where(lane >= far, back[0], 0.0) * left_back
+            made[0] += on[0] * jnp.where(lane < WIDTH - far, left_on, right_on)
+            made[1] += back[1] * jnp.where(lane >= far, right_back, left_back)
+            made[1] += jnp.where(lane < WIDTH - far, on[1], 0.0) * right_on
+        out_ref[here, :WIDTH] = made[0]
+        out_ref[here, WIDTH:] = made[1]
+
+
+def tied(value, *others):
+    return lax.optimization_barrier((value, *others))[0]
+
+
+def by_ring(relation, effects, phi_one, phi_two, innov_scale):
+    gens, tms = lax.axis_size("gen"), lax.axis_size("tm")
+    share = gens // tms
+    half = gens // 2
+    rows, depth = relation.shape
+    cut = depth // 256 * 128
+    wide = pl.cdiv(rows, 128) * 128
+    long = rows + pl.cdiv(2 * wide // 128, 8) * 8
+    order = list(range(0, gens, 2)) + list(range(gens - 1, 0, -2))
+    forward = [(order[p], order[(p + 1) % gens]) for p in range(gens)]
+    backward = [(b, a) for a, b in forward]
+    swap = [(t, t ^ 1) for t in range(tms)]
+    def spot_of():
+        return Spot(gens, tms)
+
+    def ahead_of(x):
+        return lax.ppermute(x, "gen", backward)
+
+    def behind_of(x):
+        return lax.ppermute(x, "gen", forward)
+
+    def multiplied(*fars, after=()):
+        parts = [tied(x, *after) for far in fars for x in blocks[far]]
+        made = call(
+            products_kernel,
+            [(rows, WIDTH), (4, wide)] * len(fars),
+            (relation, *parts),
+            [pltpu.VMEM((rows, 2 * WIDTH), jnp.float32), pltpu.VMEM((wide, WIDTH), jnp.float32)],
+            flops=len(fars) * KERNEL_FLOPS,
+        )
+        for n, far in enumerate(fars):
+            products[far] = made[2 * n : 2 * n + 2]
+
+    def core_sums(fars):
+        send, keep = call(
+            functools.partial(class_kernel, spot_of, fars),
+            [(2 * long, WIDTH)] * 2,
+            [x for far in fars for x in products[far]],
+            [pltpu.VMEM((5, 4, wide), jnp.float32), pltpu.VMEM((2, long, WIDTH), jnp.float32)],
+            flops=KERNEL_FLOPS // 2,
+        )
+        return call(
+            functools.partial(part_sums_kernel, spot_of, fars),
+            [(long, WIDTH)] * 2,
+            (keep, lax.ppermute(send, "tm", swap)),
+            flops=KERNEL_FLOPS // 2,
+        )
+
+    def over_y(x):
+        return lax.ppermute(x, "tm", [(t, t ^ 2) for t in range(tms)])
+
+    top, bottom = effects[:cut], effects[cut:]
+    blocks, products = {0: (top, bottom)}, {}
+    behind, ahead = blocks[0], blocks[0]
+    multiplied(0)
+    for n in range(1, half):
+        behind_top = behind_of(behind[0] if n < 3 else tied(behind[0], *products[n - 2]))
+        ahead_bottom = ahead_of(ahead[1])
+        behind_bottom = behind_of(behind[1])
+        ahead_top = ahead_of(ahead[0])
+        behind, ahead = (behind_top, behind_bottom), (ahead_top, ahead_bottom)
+        blocks[-n], blocks[n] = behind, ahead
+        if n < half - 1:
+            multiplied(-n, n)
+    blocks[half] = (behind_of(behind[0]), ahead_of(ahead[1]))
+    multiplied(1 - half, half - 1, after=(*products[half - 2],))
+    odd_send, odd_mine = core_sums((-1, 3, 1, -3))
+    odd_got = over_y(odd_send)
+    multiplied(half, after=(odd_got,))
+    even_send, even_mine = core_sums((0, 4, 2, -2))
+    even_got = over_y(even_send)
+    weights = call(weights_kernel, [(8, phi_one.shape[0])], (phi_one, phi_two, innov_scale))[0]
+    return call(
+        functools.partial(last_kernel, spot_of),
+        [(rows, share * WIDTH)],
+        (odd_mine, odd_got, even_mine, even_got, weights),
+        [pltpu.VMEM((2, long, WIDTH), jnp.float32), pltpu.VMEM((2, wide, WIDTH), jnp.float32)],
+    )[0]
 
 
 def extended(cells, sides, width):
@@ -45,7 +316,7 @@
     )
 
 
-def on_device(relation, effects, phi_one, phi_two, innov_scale):
+def by_gather(relation, effects, phi_one, phi_two, innov_scale):
     relation_wide = relation.astype(jnp.float32)
     partial_sums = jnp.dot(
         relation_wide,
@@ -56,8 +327,14 @@
     genetic = lax.psum_scatter(partial_sums, "tm", scatter_dimension=1, tiled=True)
     widened_time = extended(genetic, (("tm", 1),), 2)
     start_tm = lax.axis_index("tm") * genetic.shape[1]
-    applied = temporal_block(widened_time, start_tm, phi_one, phi_two, innov_scale)
-    return applied
+    return temporal_block(widened_time, start_tm, phi_one, phi_two, innov_scale)
+
+
+def on_device(relation, effects, phi_one, phi_two, innov_scale):
+    gens, tms = lax.axis_size("gen"), lax.axis_size("tm")
+    fits = gens == 8 and tms == 4 and effects.shape[1] == WIDTH and effects.shape[0] % 64 == 0 and relation.shape[0] % 40 == 0
+    way = by_ring if fits else by_gather
+    return way(relation, effects, phi_one, phi_two, innov_scale)
 
 
 def solution(mesh):

time: 185 us -> 94.3 us (0.51)
  the two profiles are of different devices: /device:TPU:1 before, /device:TPU:0 now
where the time goes in v3:
time: 94.3 us; the launch traced here: 94 us
  waiting for transfers between devices  61 us (65%)
  starting transfers between devices  18.3 us (19%)
  Pallas kernels  10.7 us (11%)
  local copies, waits for them, and re-layouts  3.83 us (4%)
    ppermute x7, waiting for transfers between devices, ahead_of(): return lax.ppermute(x, 'gen', backward)  43 us
    ppermute x7, starting transfers between devices, ahead_of(): return lax.ppermute(x, 'gen', backward)  14.4 us
    ppermute x2, waiting for transfers between devices, over_y(): return lax.ppermute(x, 'tm', [(t, t ^ 2) for t in range(tms)])  12.7 us
    pallas_call x11, Pallas kernels, call(): pl.pallas_call(kernel, out_shape=[jax.ShapeDtypeStruct(shape, jnp.float32...  10.7 us
    ppermute x2, waiting for transfers between devices, core_sums(): lax.ppermute(send, 'tm', swap)  3.06 us
    ppermute x2, starting transfers between devices, over_y(): return lax.ppermute(x, 'tm', [(t, t ^ 2) for t in range(tms)])  2.45 us
    ppermute x7, waiting for transfers between devices, behind_of(): return lax.ppermute(x, 'gen', forward)  2.25 us
    slice x2, local copies, waits for them, and re-layouts, by_ring(): top, bottom = (effects[:cut], effects[cut:])  2.06 us
  transfers between devices with their start and end apart: 18, of which 12 were waited for; matrix products, arithmetic and copies ran while one was open for 1% of the time, Pallas kernels for 5%

profile of v3, /device:TPU:0, one launch (start us, length us, event | category | flops | bytes accessed | tf_op | source)
XLA Modules:
  0.0 94.0 jit_solution(4987154964640576278)
XLA Ops:
  0.0 1.0 %slice.7.refs_1_ = f32[832,128]{1,0:T(8,128)S(1)} slice(f32[1600,128]{1,0:T(8,128)} %param.6), slice={[768:1600], [0:128]} | slice | bytes 851968 | tf_op jit(solution)/shard_map/slice | solution.py:249
  1.0 3.0 %collective-permute-start.3 = (f32[832,128]{1,0:T(8,128)S(1)}, f32[832,128]{1,0:T(8,128)S(1)}, u32[]{:S(2)}, u32[]{:S(2)}) collective-permute-start(f32[832,128]{1,0:T(8,128)S(1)} %slice.7.refs_1_), channel_id=1, source_target_pairs={{8,0},{16,8},{24,16},{28,24},{20,28},{12,20},{4,12},{0,4},{9,1},{1... | collective-permute-start | bytes 1277960 | tf_op jit(solution)/shard_map/ppermute | solution.py:214
  4.0 0.2 collective-permute-start.1
  4.2 1.0 %slice.6.refs_0_ = f32[768,128]{1,0:T(8,128)S(1)} slice(f32[1600,128]{1,0:T(8,128)} %param.6), slice={[0:768], [0:128]} | slice | bytes 786432 | tf_op jit(solution)/shard_map/slice | solution.py:249
  5.2 1.9 %collective-permute-start.2 = (f32[768,128]{1,0:T(8,128)S(1)}, f32[768,128]{1,0:T(8,128)S(1)}, u32[]{:S(2)}, u32[]{:S(2)}) collective-permute-start(f32[768,128]{1,0:T(8,128)S(1)} %slice.6.refs_0_), channel_id=1, source_target_pairs={{8,0},{16,8},{24,16},{28,24},{20,28},{12,20},{4,12},{0,4},{9,1},{1... | collective-permute-start | bytes 1179656 | tf_op jit(solution)/shard_map/ppermute | solution.py:214
  7.1 0.2 collective-permute-start
  7.3 7.5 %collective-permute-done.3.refs_3_ = f32[832,128]{1,0:T(8,128)S(1)} collective-permute-done((f32[832,128]{1,0:T(8,128)S(1)}, f32[832,128]{1,0:T(8,128)S(1)}, u32[]{:S(2)}, u32[]{:S(2)}) %collective-permute-start.3) | collective-permute-done | bytes 426016 | tf_op jit(solution)/shard_map/ppermute | solution.py:214
  14.8 2.0 %collective-permute-start.8 = (f32[832,128]{1,0:T(8,128)S(1)}, f32[832,128]{1,0:T(8,128)S(1)}, u32[]{:S(2)}, u32[]{:S(2)}) collective-permute-start(f32[832,128]{1,0:T(8,128)S(1)} %collective-permute-done.3.refs_3_), channel_id=1, source_target_pairs={{8,0},{16,8},{24,16},{28,24},{20,28},{12,20},{4,12},{0,4},{9,1},{1... | collective-permute-start | bytes 1277960 | tf_op jit(solution)/shard_map/ppermute | solution.py:214
  16.7 0.0 collective-permute-done.1.refs_1_
  16.8 0.1 collective-permute-start.6
  16.9 6.3 %collective-permute-done.2.refs_2_ = f32[768,128]{1,0:T(8,128)S(1)} collective-permute-done((f32[768,128]{1,0:T(8,128)S(1)}, f32[768,128]{1,0:T(8,128)S(1)}, u32[]{:S(2)}, u32[]{:S(2)}) %collective-permute-start.2) | collective-permute-done | bytes 393248 | tf_op jit(solution)/shard_map/ppermute | solution.py:214
  23.2 2.0 %collective-permute-start.7 = (f32[768,128]{1,0:T(8,128)S(1)}, f32[768,128]{1,0:T(8,128)S(1)}, u32[]{:S(2)}, u32[]{:S(2)}) collective-permute-start(f32[768,128]{1,0:T(8,128)S(1)} %collective-permute-done.2.refs_2_), channel_id=1, source_target_pairs={{8,0},{16,8},{24,16},{28,24},{20,28},{12,20},{4,12},{0,4},{9,1},{1... | collective-permute-start | bytes 1179656 | tf_op jit(solution)/shard_map/ppermute | solution.py:214
  25.2 0.0 collective-permute-done.refs_0_
  25.2 0.1 collective-permute-start.4
  25.3 7.0 %collective-permute-done.8.refs_3_ = f32[832,128]{1,0:T(8,128)S(1)} collective-permute-done((f32[832,128]{1,0:T(8,128)S(1)}, f32[832,128]{1,0:T(8,128)S(1)}, u32[]{:S(2)}, u32[]{:S(2)}) %collective-permute-start.8) | collective-permute-done | bytes 426016 | tf_op jit(solution)/shard_map/ppermute | solution.py:214
  32.3 2.0 %collective-permute-start.11 = (f32[832,128]{1,0:T(8,128)S(1)}, f32[832,128]{1,0:T(8,128)S(1)}, u32[]{:S(2)}, u32[]{:S(2)}) collective-permute-start(f32[832,128]{1,0:T(8,128)S(1)} %collective-permute-done.8.refs_3_), channel_id=1, source_target_pairs={{8,0},{16,8},{24,16},{28,24},{20,28},{12,20},{4,12},{0,4},{9,1},{1... | collective-permute-start | bytes 1277960 | tf_op jit(solution)/shard_map/ppermute | solution.py:214
  34.3 0.0 collective-permute-done.6.refs_1_
  34.3 0.1 collective-permute-start.9
  34.4 1.7 %copy-done = bf16[800,1600]{1,0:T(8,128)(2,1)S(1)} copy-done((bf16[800,1600]{1,0:T(8,128)(2,1)S(1)}, bf16[800,1600]{1,0:T(8,128)(2,1)}, u32[]{:S(2)}) %copy-start) | copy-done | bytes 2560024
  36.2 1.8 %shard_map.55 = (f32[800,128]{1,0:T(8,128)S(1)}, f32[4,896]{1,0:T(4,128)S(1)}, f32[800,128]{1,0:T(8,128)S(1)}, f32[4,896]{1,0:T(4,128)S(1)}) custom-call(bf16[800,1600]{1,0:T(8,128)(2,1)S(1)} %copy-done, f32[768,128]{1,0:T(8,128)S(1)} %collective-permute-done.refs_0_, f32[832,128]{1,0:T(8,128)S(1)} %collective-permute-done.1.refs_1_, ...), custom_call_target="tpu_custom_call" | custom-call | flops 200000000 | tf_op jit(solution)/shard_map/pallas_call | solution.py:18
  38.0 2.8 %collective-permute-done.7.refs_2_ = f32[768,128]{1,0:T(8,128)S(1)} collective-permute-done((f32[768,128]{1,0:T(8,128)S(1)}, f32[768,128]{1,0:T(8,128)S(1)}, u32[]{:S(2)}, u32[]{:S(2)}) %collective-permute-start.7) | collective-permute-done | bytes 393248 | tf_op jit(solution)/shard_map/ppermute | solution.py:214
  40.7 2.0 %collective-permute-start.10 = (f32[768,128]{1,0:T(8,128)S(1)}, f32[768,128]{1,0:T(8,128)S(1)}, u32[]{:S(2)}, u32[]{:S(2)}) collective-permute-start(f32[768,128]{1,0:T(8,128)S(1)} %collective-permute-done.7.refs_2_), channel_id=1, source_target_pairs={{8,0},{16,8},{24,16},{28,24},{20,28},{12,20},{4,12},{0,4},{9,1},{1... | collective-permute-start | bytes 1179656 | tf_op jit(solution)/shard_map/ppermute | solution.py:214
  42.7 0.0 collective-permute-done.4.refs_0_
  42.8 0.1 collective-permute-start.5
  42.9 1.8 %shard_map.56 = (f32[800,128]{1,0:T(8,128)S(1)}, f32[4,896]{1,0:T(4,128)S(1)}, f32[800,128]{1,0:T(8,128)S(1)}, f32[4,896]{1,0:T(4,128)S(1)}) custom-call(bf16[800,1600]{1,0:T(8,128)(2,1)S(1)} %copy-done, f32[768,128]{1,0:T(8,128)S(1)} %collective-permute-done.4.refs_0_, f32[832,128]{1,0:T(8,128)S(1)} %collective-permute-done.6.refs_1_, ...), custom_call_target="tpu_custom_call" | custom-call | flops 200000000 | tf_op jit(solution)/shard_map/pallas_call | solution.py:18
  44.6 12.8 %collective-permute-done.10.refs_2_ = f32[768,128]{1,0:T(8,128)S(1)} collective-permute-done((f32[768,128]{1,0:T(8,128)S(1)}, f32[768,128]{1,0:T(8,128)S(1)}, u32[]{:S(2)}, u32[]{:S(2)}) %collective-permute-start.10) | collective-permute-done | bytes 393248 | tf_op jit(solution)/shard_map/ppermute | solution.py:214
  57.5 1.4 %collective-permute-done.5.refs_0_ = f32[768,128]{1,0:T(8,128)S(1)} collective-permute-done((f32[768,128]{1,0:T(8,128)S(1)}, f32[768,128]{1,0:T(8,128)S(1)}, u32[]{:S(2)}, u32[]{:S(2)}) %collective-permute-start.5) | collective-permute-done | bytes 393248 | tf_op jit(solution)/shard_map/ppermute | solution.py:217
  58.9 1.8 %shard_map.57 = (f32[800,128]{1,0:T(8,128)S(1)}, f32[4,896]{1,0:T(4,128)S(1)}, f32[800,128]{1,0:T(8,128)S(1)}, f32[4,896]{1,0:T(4,128)S(1)}) custom-call(bf16[800,1600]{1,0:T(8,128)(2,1)S(1)} %copy-done, f32[768,128]{1,0:T(8,128)S(1)} %collective-permute-done.5.refs_0_, f32[832,128]{1,0:T(8,128)S(1)} %collective-permute-done.9.refs_1_, ...), custom_call_target="tpu_custom_call" | custom-call | flops 200000000 | tf_op jit(solution)/shard_map/pallas_call | solution.py:18
  60.6 0.3 shard_map.58
  60.9 0.1 collective-permute-start.12
  61.0 1.6 %collective-permute-start.15 = (f32[832,128]{1,0:T(8,128)S(1)}, f32[832,128]{1,0:T(8,128)S(1)}, u32[]{:S(2)}, u32[]{:S(2)}) collective-permute-start(f32[832,128]{1,0:T(8,128)S(1)} %collective-permute-done.11.refs_3_), channel_id=1, source_target_pairs={{8,0},{16,8},{24,16},{28,24},{20,28},{12,20},{4,12},{0,4},{9,1},{1... | collective-permute-start | bytes 1277960 | tf_op jit(solution)/shard_map/ppermute | solution.py:214
  62.6 0.7 collective-permute-done.12.got_ref
  63.4 0.1 shard_map.59
  63.4 1.6 %collective-permute-start.13 = (f32[816,128]{1,0:T(8,128)S(1)}, f32[816,128]{1,0:T(8,128)S(1)}, u32[]{:S(2)}, u32[]{:S(2)}) collective-permute-start(f32[816,128]{1,0:T(8,128)S(1)} %get-tuple-element.54), channel_id=1, source_target_pairs={{0,2},{1,3},{2,0},{3,1},{4,6},{5,7},{6,4},{7,5},{8,10},{9,11},{10,... | collective-permute-start | bytes 1253384 | tf_op jit(solution)/shard_map/ppermute | solution.py:247
  65.0 0.5 collective-permute-start.14
  65.6 1.0 %shard_map.60 = (f32[800,128]{1,0:T(8,128)S(1)}, f32[4,896]{1,0:T(4,128)S(1)}) custom-call(bf16[800,1600]{1,0:T(8,128)(2,1)S(1)} %copy-done.1, f32[768,128]{1,0:T(8,128)S(1)} %slice.6.refs_0_, f32[832,128]{1,0:T(8,128)S(1)} %slice.7.refs_1_), custom_call_target="tpu_custom_call" | custom-call | flops 100000000 | tf_op jit(solution)/shard_map/pallas_call | solution.py:18
  66.6 6.6 %collective-permute-done.15.refs_1_ = f32[832,128]{1,0:T(8,128)S(1)} collective-permute-done((f32[832,128]{1,0:T(8,128)S(1)}, f32[832,128]{1,0:T(8,128)S(1)}, u32[]{:S(2)}, u32[]{:S(2)}) %collective-permute-start.15) | collective-permute-done | bytes 426016 | tf_op jit(solution)/shard_map/ppermute | solution.py:214
  73.2 2.0 %collective-permute-done.13.got_odd = f32[816,128]{1,0:T(8,128)S(1)} collective-permute-done((f32[816,128]{1,0:T(8,128)S(1)}, f32[816,128]{1,0:T(8,128)S(1)}, u32[]{:S(2)}, u32[]{:S(2)}) %collective-permute-start.13) | collective-permute-done | bytes 417824 | tf_op jit(solution)/shard_map/ppermute | solution.py:247
  75.2 0.7 collective-permute-done.14.refs_0_
  75.9 1.0 %shard_map.61 = (f32[800,128]{1,0:T(8,128)S(1)}, f32[4,896]{1,0:T(4,128)S(1)}) custom-call(bf16[800,1600]{1,0:T(8,128)(2,1)S(1)} %copy-done.1, f32[768,128]{1,0:T(8,128)S(1)} %collective-permute-done.14.refs_0_, f32[832,128]{1,0:T(8,128)S(1)} %collective-permute-done.15.refs_1_), custom_call_target="tpu_custom_call" | custom-call | flops 100000000 | tf_op jit(solution)/shard_map/pallas_call | solution.py:18
  76.9 0.3 shard_map.62
  77.2 0.1 collective-permute-start.16
  77.3 2.3 %collective-permute-done.16.got_ref = f32[1632,128]{1,0:T(8,128)S(1)} collective-permute-done((f32[1632,128]{1,0:T(8,128)S(1)}, f32[1632,128]{1,0:T(8,128)S(1)}, u32[]{:S(2)}, u32[]{:S(2)}) %collective-permute-start.16) | collective-permute-done | bytes 835616 | tf_op jit(solution)/shard_map/ppermute | solution.py:242
  79.6 0.1 shard_map.63
  79.7 0.9 collective-permute-start.17
  80.6 0.1 shard_map.64.weights_ref
  80.7 10.8 %collective-permute-done.17.got_even = f32[816,128]{1,0:T(8,128)S(1)} collective-permute-done((f32[816,128]{1,0:T(8,128)S(1)}, f32[816,128]{1,0:T(8,128)S(1)}, u32[]{:S(2)}, u32[]{:S(2)}) %collective-permute-start.17) | collective-permute-done | bytes 417824 | tf_op jit(solution)/shard_map/ppermute | solution.py:247
  91.5 2.6 %shard_map.65 = f32[800,256]{1,0:T(8,128)} custom-call(f32[816,128]{1,0:T(8,128)S(1)} %get-tuple-element.53.mine_odd, f32[816,128]{1,0:T(8,128)S(1)} %collective-permute-done.13.got_odd, f32[816,128]{1,0:T(8,128)S(1)} %get-tuple-element.65.mine_even, f32[816,128]{1,0:T(8,128)S(1)} %collective-permute-done.17.got_even, f32[8,1024]{1,0:T(8,128)S(1)} %shard_map.64.weights_ref), custom_call_target="tpu_custom_call" | custom-call | tf_op jit(solution)/shard_map/pallas_call | solution.py:18
  (11 shorter events, 0.0 us)
Async XLA Ops:
  1.0 13.7 %collective-permute-start.3 = (f32[832,128]{1,0:T(8,128)S(1)}, f32[832,128]{1,0:T(8,128)S(1)}, u32[]{:S(2)}, u32[]{:S(2)}) collective-permute-start(f32[832,128]{1,0:T(8,128)S(1)} %slice.7.refs_1_), channel_id=1, source_target_pairs={{8,0},{16,8},{24,16},{28,24},{20,28},{12,20},{4,12},{0,4},{9,1},{1... | collective-permute-start | bytes 1277960 | tf_op jit(solution)/shard_map/ppermute | solution.py:214
  4.0 12.7 %collective-permute-start.1 = (f32[832,128]{1,0:T(8,128)S(1)}, f32[832,128]{1,0:T(8,128)S(1)}, u32[]{:S(2)}, u32[]{:S(2)}) collective-permute-start(f32[832,128]{1,0:T(8,128)S(1)} %slice.7.refs_1_), channel_id=1, source_target_pairs={{0,8},{8,16},{16,24},{24,28},{28,20},{20,12},{12,4},{4,0},{1,9},{9... | collective-permute-start | bytes 1277960 | tf_op jit(solution)/shard_map/ppermute | solution.py:217
  5.2 18.0 %collective-permute-start.2 = (f32[768,128]{1,0:T(8,128)S(1)}, f32[768,128]{1,0:T(8,128)S(1)}, u32[]{:S(2)}, u32[]{:S(2)}) collective-permute-start(f32[768,128]{1,0:T(8,128)S(1)} %slice.6.refs_0_), channel_id=1, source_target_pairs={{8,0},{16,8},{24,16},{28,24},{20,28},{12,20},{4,12},{0,4},{9,1},{1... | collective-permute-start | bytes 1179656 | tf_op jit(solution)/shard_map/ppermute | solution.py:214
  7.1 18.1 %collective-permute-start = (f32[768,128]{1,0:T(8,128)S(1)}, f32[768,128]{1,0:T(8,128)S(1)}, u32[]{:S(2)}, u32[]{:S(2)}) collective-permute-start(f32[768,128]{1,0:T(8,128)S(1)} %slice.6.refs_0_), channel_id=1, source_target_pairs={{0,8},{8,16},{16,24},{24,28},{28,20},{20,12},{12,4},{4,0},{1,9},{9... | collective-permute-start | bytes 1179656 | tf_op jit(solution)/shard_map/ppermute | solution.py:217
  14.8 17.6 %collective-permute-start.8 = (f32[832,128]{1,0:T(8,128)S(1)}, f32[832,128]{1,0:T(8,128)S(1)}, u32[]{:S(2)}, u32[]{:S(2)}) collective-permute-start(f32[832,128]{1,0:T(8,128)S(1)} %collective-permute-done.3.refs_3_), channel_id=1, source_target_pairs={{8,0},{16,8},{24,16},{28,24},{20,28},{12,20},{4,12},{0,4},{9,1},{1... | collective-permute-start | bytes 1277960 | tf_op jit(solution)/shard_map/ppermute | solution.py:214
  16.8 17.6 %collective-permute-start.6 = (f32[832,128]{1,0:T(8,128)S(1)}, f32[832,128]{1,0:T(8,128)S(1)}, u32[]{:S(2)}, u32[]{:S(2)}) collective-permute-start(f32[832,128]{1,0:T(8,128)S(1)} %collective-permute-done.1.refs_1_), channel_id=1, source_target_pairs={{0,8},{8,16},{16,24},{24,28},{28,20},{20,12},{12,4},{4,0},{1,9},{9... | collective-permute-start | bytes 1277960 | tf_op jit(solution)/shard_map/ppermute | solution.py:217
  23.2 17.6 %collective-permute-start.7 = (f32[768,128]{1,0:T(8,128)S(1)}, f32[768,128]{1,0:T(8,128)S(1)}, u32[]{:S(2)}, u32[]{:S(2)}) collective-permute-start(f32[768,128]{1,0:T(8,128)S(1)} %collective-permute-done.2.refs_2_), channel_id=1, source_target_pairs={{8,0},{16,8},{24,16},{28,24},{20,28},{12,20},{4,12},{0,4},{9,1},{1... | collective-permute-start | bytes 1179656 | tf_op jit(solution)/shard_map/ppermute | solution.py:214
  25.2 17.6 %collective-permute-start.4 = (f32[768,128]{1,0:T(8,128)S(1)}, f32[768,128]{1,0:T(8,128)S(1)}, u32[]{:S(2)}, u32[]{:S(2)}) collective-permute-start(f32[768,128]{1,0:T(8,128)S(1)} %collective-permute-done.refs_0_), channel_id=1, source_target_pairs={{0,8},{8,16},{16,24},{24,28},{28,20},{20,12},{12,4},{4,0},{1,9},{9... | collective-permute-start | bytes 1179656 | tf_op jit(solution)/shard_map/ppermute | solution.py:217
  32.3 26.5 %collective-permute-start.11 = (f32[832,128]{1,0:T(8,128)S(1)}, f32[832,128]{1,0:T(8,128)S(1)}, u32[]{:S(2)}, u32[]{:S(2)}) collective-permute-start(f32[832,128]{1,0:T(8,128)S(1)} %collective-permute-done.8.refs_3_), channel_id=1, source_target_pairs={{8,0},{16,8},{24,16},{28,24},{20,28},{12,20},{4,12},{0,4},{9,1},{1... | collective-permute-start | bytes 1277960 | tf_op jit(solution)/shard_map/ppermute | solution.py:214
  34.3 24.5 %collective-permute-start.9 = (f32[832,128]{1,0:T(8,128)S(1)}, f32[832,128]{1,0:T(8,128)S(1)}, u32[]{:S(2)}, u32[]{:S(2)}) collective-permute-start(f32[832,128]{1,0:T(8,128)S(1)} %collective-permute-done.6.refs_1_), channel_id=1, source_target_pairs={{0,8},{8,16},{16,24},{24,28},{28,20},{20,12},{12,4},{4,0},{1,9},{9... | collective-permute-start | bytes 1277960 | tf_op jit(solution)/shard_map/ppermute | solution.py:217
  34.4 1.8 %copy-start = (bf16[800,1600]{1,0:T(8,128)(2,1)S(1)}, bf16[800,1600]{1,0:T(8,128)(2,1)}, u32[]{:S(2)}) copy-start(bf16[800,1600]{1,0:T(8,128)(2,1)} %relation_ref.9) | copy-start | bytes 7680004
  40.7 16.7 %collective-permute-start.10 = (f32[768,128]{1,0:T(8,128)S(1)}, f32[768,128]{1,0:T(8,128)S(1)}, u32[]{:S(2)}, u32[]{:S(2)}) collective-permute-start(f32[768,128]{1,0:T(8,128)S(1)} %collective-permute-done.7.refs_2_), channel_id=1, source_target_pairs={{8,0},{16,8},{24,16},{28,24},{20,28},{12,20},{4,12},{0,4},{9,1},{1... | collective-permute-start | bytes 1179656 | tf_op jit(solution)/shard_map/ppermute | solution.py:214
  42.8 16.1 %collective-permute-start.5 = (f32[768,128]{1,0:T(8,128)S(1)}, f32[768,128]{1,0:T(8,128)S(1)}, u32[]{:S(2)}, u32[]{:S(2)}) collective-permute-start(f32[768,128]{1,0:T(8,128)S(1)} %collective-permute-done.4.refs_0_), channel_id=1, source_target_pairs={{0,8},{8,16},{16,24},{24,28},{28,20},{20,12},{12,4},{4,0},{1,9},{9... | collective-permute-start | bytes 1179656 | tf_op jit(solution)/shard_map/ppermute | solution.py:217
  60.6 4.9 %copy-start.1 = (bf16[800,1600]{1,0:T(8,128)(2,1)S(1)}, bf16[800,1600]{1,0:T(8,128)(2,1)}, u32[]{:S(2)}) copy-start(bf16[800,1600]{1,0:T(8,128)(2,1)} %relation_ref.9) | copy-start | bytes 7680004
  60.9 2.4 %collective-permute-start.12 = (f32[1632,128]{1,0:T(8,128)S(1)}, f32[1632,128]{1,0:T(8,128)S(1)}, u32[]{:S(2)}, u32[]{:S(2)}) collective-permute-start(f32[1632,128]{1,0:T(8,128)S(1)} %get-tuple-element.52), channel_id=1, source_target_pairs={{0,1},{1,0},{2,3},{3,2},{4,5},{5,4},{6,7},{7,6},{8,9},{9,8},{10,11... | collective-permute-start | bytes 2506760 | tf_op jit(solution)/shard_map/ppermute | solution.py:242
  61.0 12.2 %collective-permute-start.15 = (f32[832,128]{1,0:T(8,128)S(1)}, f32[832,128]{1,0:T(8,128)S(1)}, u32[]{:S(2)}, u32[]{:S(2)}) collective-permute-start(f32[832,128]{1,0:T(8,128)S(1)} %collective-permute-done.11.refs_3_), channel_id=1, source_target_pairs={{8,0},{16,8},{24,16},{28,24},{20,28},{12,20},{4,12},{0,4},{9,1},{1... | collective-permute-start | bytes 1277960 | tf_op jit(solution)/shard_map/ppermute | solution.py:214
  63.4 11.7 %collective-permute-start.13 = (f32[816,128]{1,0:T(8,128)S(1)}, f32[816,128]{1,0:T(8,128)S(1)}, u32[]{:S(2)}, u32[]{:S(2)}) collective-permute-start(f32[816,128]{1,0:T(8,128)S(1)} %get-tuple-element.54), channel_id=1, source_target_pairs={{0,2},{1,3},{2,0},{3,1},{4,6},{5,7},{6,4},{7,5},{8,10},{9,11},{10,... | collective-permute-start | bytes 1253384 | tf_op jit(solution)/shard_map/ppermute | solution.py:247
  65.0 10.9 %collective-permute-start.14 = (f32[768,128]{1,0:T(8,128)S(1)}, f32[768,128]{1,0:T(8,128)S(1)}, u32[]{:S(2)}, u32[]{:S(2)}) collective-permute-start(f32[768,128]{1,0:T(8,128)S(1)} %collective-permute-done.5.refs_0_), channel_id=1, source_target_pairs={{0,8},{8,16},{16,24},{24,28},{28,20},{20,12},{12,4},{4,0},{1,9},{9... | collective-permute-start | bytes 1179656 | tf_op jit(solution)/shard_map/ppermute | solution.py:217
  66.6 14.0 %copy-start.2 = (f32[1024]{0:T(1024)S(1)}, f32[1024]{0:T(1024)}, u32[]{:S(2)}) copy-start(f32[1024]{0:T(1024)} %one_ref.1) | copy-start | bytes 12292
  66.6 14.0 %copy-start.3 = (f32[1024]{0:T(1024)S(1)}, f32[1024]{0:T(1024)}, u32[]{:S(2)}) copy-start(f32[1024]{0:T(1024)} %two_ref.1) | copy-start | bytes 12292
  66.6 14.0 %copy-start.4 = (f32[1024]{0:T(1024)S(1)}, f32[1024]{0:T(1024)}, u32[]{:S(2)}) copy-start(f32[1024]{0:T(1024)} %scale_ref.1) | copy-start | bytes 12292
  77.2 2.4 %collective-permute-start.16 = (f32[1632,128]{1,0:T(8,128)S(1)}, f32[1632,128]{1,0:T(8,128)S(1)}, u32[]{:S(2)}, u32[]{:S(2)}) collective-permute-start(f32[1632,128]{1,0:T(8,128)S(1)} %get-tuple-element.64), channel_id=1, source_target_pairs={{0,1},{1,0},{2,3},{3,2},{4,5},{5,4},{6,7},{7,6},{8,9},{9,8},{10,11... | collective-permute-start | bytes 2506760 | tf_op jit(solution)/shard_map/ppermute | solution.py:242
  79.7 11.7 %collective-permute-start.17 = (f32[816,128]{1,0:T(8,128)S(1)}, f32[816,128]{1,0:T(8,128)S(1)}, u32[]{:S(2)}, u32[]{:S(2)}) collective-permute-start(f32[816,128]{1,0:T(8,128)S(1)} %get-tuple-element.66), channel_id=1, source_target_pairs={{0,2},{1,3},{2,0},{3,1},{4,6},{5,7},{6,4},{7,5},{8,10},{9,11},{10,... | collective-permute-start | bytes 1253384 | tf_op jit(solution)/shard_map/ppermute | solution.py:247

commit v4 on v3

--- a/solution.py
+++ b/solution.py
@@ -14,12 +14,12 @@
 WHOLE = pl.BlockSpec(memory_space=pltpu.VMEM)
 
 
-def call(kernel, shapes, operands, scratch=(), flops=0):
+def call(kernel, shapes, operands, scratch=(), flops=0, into=WHOLE):
     return pl.pallas_call(
         kernel,
         out_shape=[jax.ShapeDtypeStruct(shape, jnp.float32) for shape in shapes],
         in_specs=[WHOLE] * len(operands),
-        out_specs=[WHOLE] * len(shapes),
+        out_specs=[into] * len(shapes),
         scratch_shapes=scratch,
         compiler_params=pltpu.CompilerParams(vmem_limit_bytes=VMEM_LIMIT),
         cost_estimate=pl.CostEstimate(flops=flops, bytes_accessed=0, transcendentals=0),
@@ -106,7 +106,7 @@
         edges_ref[2:4] = turned[WIDTH - 2 :]
 
 
-def class_kernel(spot_of, fars, *refs):
+def odd_kernel(spot_of, fars, *refs):
     send_ref, keep_ref, edges_ref, message_ref = refs[-4:]
     spot = spot_of()
     rows, long = refs[0].shape[0], message_ref.shape[1]
@@ -127,6 +127,73 @@
             send_ref[here] = message_ref[near]
 
 
+def halves_kernel(spot_of, near, near_ref, far_ref, send_ref, keep_ref):
+    spot = spot_of()
+    rows = near_ref.shape[0] // 2
+    core = spot.tm % 2
+    mine = spot.owner_of(near) // 2 == spot.tm // 2
+    for ours in (True, False):
+
+        @pl.when(mine == ours)
+        def _():
+            for n, ref in enumerate((near_ref, far_ref) if ours else (far_ref, near_ref)):
+                here = pl.ds(n * rows, rows)
+                send_ref[here] = ref[pl.ds(pl.multiple_of((1 - core) * rows, 8), rows)]
+                keep_ref[here] = ref[pl.ds(pl.multiple_of(core * rows, 8), rows)]
+
+
+def half_sums_kernel(keep_ref, got_ref, send_ref, mine_ref):
+    rows = mine_ref.shape[0]
+    mine_ref[...] = keep_ref[:rows] + got_ref[:rows]
+    send_ref[...] = keep_ref[rows:] + got_ref[rows:]
+
+
+def chip_pair_kernel(spot_of, near, near_ref, far_ref, send_ref, keep_ref):
+    spot = spot_of()
+    mine = spot.owner_of(near) // 2 == spot.tm // 2
+
+    @pl.when(mine)
+    def _():
+        keep_ref[...] = near_ref[...]
+        send_ref[...] = far_ref[...]
+
+    @pl.when(jnp.logical_not(mine))
+    def _():
+        keep_ref[...] = far_ref[...]
+        send_ref[...] = near_ref[...]
+
+
+def borders_kernel(spot_of, fars, *refs):
+    send_ref, keep_ref, edges_ref = refs[-3:]
+    spot = spot_of()
+    for m in range(4):
+        edges_ref[m] = refs[m][...]
+    edges_ref[4] = jnp.zeros_like(refs[0])
+    chip, core = spot.tm // 2, spot.tm % 2
+    send_ref[...] = jnp.zeros_like(send_ref)
+    keep_ref[...] = jnp.zeros_like(keep_ref)
+    for m, far in enumerate(fars):
+        owner = spot.owner_of(far)
+        there = edges_ref[spot.border_of(far, fars)]
+        border = jnp.where(spot.block_at(far) % spot.share == 0, there[2:4], there[0:2])
+        for n in range(2):
+            for out_ref, whose in ((send_ref, 1 - core), (keep_ref, core)):
+                wanted = 2 * jnp.where(n == 0, chip, 1 - chip) + whose
+
+                @pl.when(owner == wanted)
+                def _():
+                    out_ref[2 * n : 2 * n + 2] = border
+
+
+def border_sums_kernel(keep_ref, got_ref, send_ref, mine_ref):
+    mine_ref[...] = keep_ref[0:2] + got_ref[0:2]
+    send_ref[...] = keep_ref[2:4] + got_ref[2:4]
+
+
+def sum_kernel(one_ref, other_ref, out_ref):
+    out_ref[...] = one_ref[...] + other_ref[...]
+
+
 def part_sums_kernel(spot_of, fars, keep_ref, got_ref, send_ref, mine_ref):
     spot = spot_of()
     owner = jnp.where(spot.keeps(fars[0]) == 1, spot.owner_of(fars[0]), spot.owner_of(fars[1]))
@@ -142,25 +209,49 @@
 
 
 def last_kernel(
-    spot_of, mine_odd, got_odd, mine_even, got_even, weights_ref, out_ref, sums_ref, sides_ref
+    spot_of,
+    mine_odd,
+    got_odd,
+    two_sum,
+    two_got,
+    zero_sum,
+    zero_got,
+    border_mine,
+    border_got,
+    weights_ref,
+    out_any,
+    sums_ref,
+    sides_ref,
+    made_ref,
+    sems,
 ):
     spot = spot_of()
     odd = jnp.where((spot.place_of(spot.share * spot.tm) + spot.place) % 2 == 0, 1, 0)
-    rows = out_ref.shape[0]
+    rows = out_any.shape[0]
     span = sides_ref.shape[1]
-    sums_ref[odd] = mine_odd[...] + got_odd[...]
-    sums_ref[1 - odd] = mine_even[...] + got_even[...]
+    is_two = (spot.owner_of(2) == spot.tm) | (spot.owner_of(-2) == spot.tm)
+    sums_ref[odd] = mine_odd[:rows] + got_odd[:rows]
+
+    @pl.when(is_two)
+    def _():
+        sums_ref[1 - odd] = two_sum[...] + two_got[...]
+
+    @pl.when(jnp.logical_not(is_two))
+    def _():
+        half, core = rows // 2, spot.tm % 2
+        sums_ref[1 - odd, pl.ds(pl.multiple_of(core * half, 8), half)] = zero_sum[...]
+        sums_ref[1 - odd, pl.ds(pl.multiple_of((1 - core) * half, 8), half)] = zero_got[...]
+
     start = pl.multiple_of(spot.tm * (2 * WIDTH), 2 * WIDTH)
     weights = weights_ref[:, pl.ds(start, 2 * WIDTH)]
     row = lax.broadcasted_iota(jnp.int32, (8, span), 0)
     nothing = jnp.zeros((WIDTH - 8, span), jnp.float32)
 
-    def border(column):
-        return jnp.concatenate(
-            [sums_ref[column, rows + 2 * k : rows + 2 * k + 2] for k in range(span // WIDTH)], axis=1
-        )
-
-    before, after = border(0), border(1)
+    extra = mine_odd[rows:] + got_odd[rows:]
+    odd_border = jnp.concatenate([extra[2 * k : 2 * k + 2] for k in range(span // WIDTH)], axis=1)
+    even_border = border_mine[...] + border_got[...]
+    before = jnp.where(odd == 0, odd_border, even_border)
+    after = jnp.where(odd == 0, even_border, odd_border)
     end = 2 * WIDTH - 1
     first = weights[0:1, 0:1] * before[0:1] + weights[1:2, 0:1] * before[1:2]
     second = weights[0:1, 1:2] * before[1:2]
@@ -172,23 +263,29 @@
     sides_ref[1] = jnp.concatenate([nothing, below], axis=0).T
     lane = lax.broadcasted_iota(jnp.int32, (1, WIDTH), 1)
     inner = [weights[:, :WIDTH], weights[:, WIDTH:]]
-    step = rows // 5
-
-    @pl.loop(0, 5)
-    def _(n):
-        here = pl.ds(pl.multiple_of(n * step, 8), step)
+    near = [jnp.where(lane >= far, inner[0][2 - far : 3 - far], 0.0) for far in (1, 2)]
+    beyond = [jnp.where(lane < WIDTH - far, inner[1][2 + far : 3 + far], 0.0) for far in (1, 2)]
+    pieces = 5
+    step = rows // pieces
+    copies = []
+    for n in range(pieces):
+        here = slice(n * step, (n + 1) * step)
         left, right = sums_ref[0, here], sums_ref[1, here]
-        made = [sides_ref[0, here] + inner[0][2:3] * left, sides_ref[1, here] + inner[1][2:3] * right]
+        made_left = sides_ref[0, here] + inner[0][2:3] * left
+        made_right = sides_ref[1, here] + inner[1][2:3] * right
         for far in (1, 2):
             left_back, right_back = pltpu.roll(left, far, 1), pltpu.roll(right, far, 1)
             left_on, right_on = pltpu.roll(left, WIDTH - far, 1), pltpu.roll(right, WIDTH - far, 1)
-            back, on = [w[2 - far : 3 - far] for w in inner], [w[2 + far : 3 + far] for w in inner]
-            made[0] += jnp.where(lane >= far, back[0], 0.0) * left_back
-            made[0] += on[0] * jnp.where(lane < WIDTH - far, left_on, right_on)
-            made[1] += back[1] * jnp.where(lane >= far, right_back, left_back)
-            made[1] += jnp.where(lane < WIDTH - far, on[1], 0.0) * right_on
-        out_ref[here, :WIDTH] = made[0]
-        out_ref[here, WIDTH:] = made[1]
+            on = jnp.where(lane < WIDTH - far, left_on, right_on)
+            back = jnp.where(lane >= far, right_back, left_back)
+            made_left += near[far - 1] * left_back + inner[0][2 + far : 3 + far] * on
+            made_right += inner[1][2 - far : 3 - far] * back + beyond[far - 1] * right_on
+        made_ref[here, :WIDTH] = made_left
+        made_ref[here, WIDTH:] = made_right
+        copies.append(pltpu.make_async_copy(made_ref.at[here], out_any.at[here], sems.at[n]))
+        copies[n].start()
+    for copy in copies:
+        copy.wait()
 
 
 def tied(value, *others):
@@ -216,32 +313,20 @@
     def behind_of(x):
         return lax.ppermute(x, "gen", forward)
 
-    def multiplied(*fars, after=()):
+    def multiplied(*fars, after=(), cost=1):
         parts = [tied(x, *after) for far in fars for x in blocks[far]]
         made = call(
             products_kernel,
             [(rows, WIDTH), (4, wide)] * len(fars),
             (relation, *parts),
             [pltpu.VMEM((rows, 2 * WIDTH), jnp.float32), pltpu.VMEM((wide, WIDTH), jnp.float32)],
-            flops=len(fars) * KERNEL_FLOPS,
+            flops=cost * len(fars) * KERNEL_FLOPS,
         )
         for n, far in enumerate(fars):
             products[far] = made[2 * n : 2 * n + 2]
 
-    def core_sums(fars):
-        send, keep = call(
-            functools.partial(class_kernel, spot_of, fars),
-            [(2 * long, WIDTH)] * 2,
-            [x for far in fars for x in products[far]],
-            [pltpu.VMEM((5, 4, wide), jnp.float32), pltpu.VMEM((2, long, WIDTH), jnp.float32)],
-            flops=KERNEL_FLOPS // 2,
-        )
-        return call(
-            functools.partial(part_sums_kernel, spot_of, fars),
-            [(long, WIDTH)] * 2,
-            (keep, lax.ppermute(send, "tm", swap)),
-            flops=KERNEL_FLOPS // 2,
-        )
+    def over_cores(x):
+        return lax.ppermute(x, "tm", swap)
 
     def over_y(x):
         return lax.ppermute(x, "tm", [(t, t ^ 2) for t in range(tms)])
@@ -251,7 +336,7 @@
     behind, ahead = blocks[0], blocks[0]
     multiplied(0)
     for n in range(1, half):
-        behind_top = behind_of(behind[0] if n < 3 else tied(behind[0], *products[n - 2]))
+        behind_top = behind_of(behind[0] if n < 2 else tied(behind[0], *products[n - 2]))
         ahead_bottom = ahead_of(ahead[1])
         behind_bottom = behind_of(behind[1])
         ahead_top = ahead_of(ahead[0])
@@ -260,18 +345,77 @@
         if n < half - 1:
             multiplied(-n, n)
     blocks[half] = (behind_of(behind[0]), ahead_of(ahead[1]))
-    multiplied(1 - half, half - 1, after=(*products[half - 2],))
-    odd_send, odd_mine = core_sums((-1, 3, 1, -3))
+    two_send, two_keep = call(
+        functools.partial(chip_pair_kernel, spot_of, 2),
+        [(rows, WIDTH)] * 2,
+        (products[2][0], products[-2][0]),
+        flops=KERNEL_FLOPS // 2,
+    )
+    two_sum = call(sum_kernel, [(rows, WIDTH)], (two_keep, over_y(two_send)), flops=KERNEL_FLOPS // 10)[0]
+    two_got = over_cores(two_sum)
+    multiplied(1 - half, half - 1, cost=10)
+    odd_fars = (-1, 3, 1, -3)
+    send, keep = call(
+        functools.partial(odd_kernel, spot_of, odd_fars),
+        [(2 * long, WIDTH)] * 2,
+        [tied(x, two_sum) for far in odd_fars for x in products[far]],
+        [pltpu.VMEM((5, 4, wide), jnp.float32), pltpu.VMEM((2, long, WIDTH), jnp.float32)],
+        flops=KERNEL_FLOPS // 2,
+    )
+    odd_send, odd_mine = call(
+        functools.partial(part_sums_kernel, spot_of, odd_fars),
+        [(long, WIDTH)] * 2,
+        (keep, over_cores(send)),
+        flops=KERNEL_FLOPS // 2,
+    )
     odd_got = over_y(odd_send)
-    multiplied(half, after=(odd_got,))
-    even_send, even_mine = core_sums((0, 4, 2, -2))
-    even_got = over_y(even_send)
+    multiplied(half, cost=20)
+    even_fars = (0, half, 2, -2)
+    border_send, border_keep = call(
+        functools.partial(borders_kernel, spot_of, even_fars),
+        [(4, wide)] * 2,
+        [products[far][1] for far in even_fars],
+        [pltpu.VMEM((5, 4, wide), jnp.float32)],
+        flops=KERNEL_FLOPS // 10,
+    )
+    border_send, border_mine = call(
+        border_sums_kernel,
+        [(2, wide)] * 2,
+        (border_keep, over_cores(border_send)),
+        flops=KERNEL_FLOPS // 10,
+    )
+    border_got = over_y(border_send)
+    send, keep = call(
+        functools.partial(halves_kernel, spot_of, 0),
+        [(rows, WIDTH)] * 2,
+        [tied(products[far][0], odd_got) for far in (0, half)],
+        flops=KERNEL_FLOPS // 2,
+    )
+    zero_send, zero_mine = call(
+        half_sums_kernel,
+        [(rows // 2, WIDTH)] * 2,
+        (keep, over_cores(send)),
+        flops=KERNEL_FLOPS // 10,
+    )
+    zero_sum = call(
+        sum_kernel,
+        [(rows // 2, WIDTH)],
+        (tied(zero_mine, border_got), over_y(zero_send)),
+        flops=KERNEL_FLOPS // 10,
+    )[0]
+    zero_got = over_cores(zero_sum)
     weights = call(weights_kernel, [(8, phi_one.shape[0])], (phi_one, phi_two, innov_scale))[0]
     return call(
         functools.partial(last_kernel, spot_of),
         [(rows, share * WIDTH)],
-        (odd_mine, odd_got, even_mine, even_got, weights),
-        [pltpu.VMEM((2, long, WIDTH), jnp.float32), pltpu.VMEM((2, wide, WIDTH), jnp.float32)],
+        (odd_mine, odd_got, two_sum, two_got, zero_sum, zero_got, border_mine, border_got, weights),
+        [
+            pltpu.VMEM((2, rows, WIDTH), jnp.float32),
+            pltpu.VMEM((2, wide, WIDTH), jnp.float32),
+            pltpu.VMEM((rows, share * WIDTH), jnp.float32),
+            pltpu.SemaphoreType.DMA((5,)),
+        ],
+        into=pl.BlockSpec(memory_space=pl.ANY),
     )[0]
 
 
@@ -332,7 +476,7 @@
 
 def on_device(relation, effects, phi_one, phi_two, innov_scale):
     gens, tms = lax.axis_size("gen"), lax.axis_size("tm")
-    fits = gens == 8 and tms == 4 and effects.shape[1] == WIDTH and effects.shape[0] % 64 == 0 and relation.shape[0] % 40 == 0
+    fits = gens == 8 and tms == 4 and effects.shape[1] == WIDTH and effects.shape[0] % 64 == 0 and relation.shape[0] % 80 == 0
     way = by_ring if fits else by_gather
     return way(relation, effects, phi_one, phi_two, innov_scale)
 

time: 94.3 us -> 91.1 us (0.966)
  waiting for transfers between devices: 61 us -> 54.7 us
  starting transfers between devices: 18.3 us -> 21.7 us
    ppermute x7, waiting for transfers between devices: 2.25 us -> 42.6 us  [behind_of(): return lax.ppermute(x, 'gen', forward)]
    ppermute x7, waiting for transfers between devices: 43 us -> 3.46 us  [ahead_of(): return lax.ppermute(x, 'gen', backward)]
    ppermute x7, starting transfers between devices: 14.4 us -> 1.4 us  [ahead_of(): return lax.ppermute(x, 'gen', backward)]
    ppermute x7, starting transfers between devices: 1.28 us -> 14.2 us  [behind_of(): return lax.ppermute(x, 'gen', forward)]
    ppermute x2 -> x4, waiting for transfers between devices: 12.7 us -> 4.4 us  [over_y(): return lax.ppermute(x, 'tm', [(t, t ^ 2) for t in range(tms)])]
    ppermute x2 -> x4, starting transfers between devices: 2.45 us -> 5.32 us  [over_y(): return lax.ppermute(x, 'tm', [(t, t ^ 2) for t in range(tms)])]
    ppermute x2 -> x5, waiting for transfers between devices: 3.06 us -> 4.32 us  [over_cores(): return lax.ppermute(x, 'tm', swap)]
    pallas_call x11 -> x16, Pallas kernels: 10.7 us -> 10.3 us  [call(): pl.pallas_call(kernel, out_shape=[jax.ShapeDtypeStruct(shape, jnp.float32...]
  transfers between devices with their start and end apart: 18 -> 23, of which waited for: 12 -> 14; matrix products, arithmetic and copies ran while one was open for 1% -> 1% of each run, Pallas kernels for 5% -> 7%
where the time goes in v4:
time: 91.1 us; the launch traced here: 90.9 us
  waiting for transfers between devices  54.7 us (60%)
  starting transfers between devices  21.7 us (24%)
  Pallas kernels  10.3 us (11%)
  local copies, waits for them, and re-layouts  3.83 us (4%)
    ppermute x7, waiting for transfers between devices, behind_of(): return lax.ppermute(x, 'gen', forward)  42.6 us
    ppermute x7, starting transfers between devices, behind_of(): return lax.ppermute(x, 'gen', forward)  14.2 us
    pallas_call x16, Pallas kernels, call(): pl.pallas_call(kernel, out_shape=[jax.ShapeDtypeStruct(shape, jnp.float32...  10.3 us
    ppermute x4, starting transfers between devices, over_y(): return lax.ppermute(x, 'tm', [(t, t ^ 2) for t in range(tms)])  5.32 us
    ppermute x4, waiting for transfers between devices, over_y(): return lax.ppermute(x, 'tm', [(t, t ^ 2) for t in range(tms)])  4.4 us
    ppermute x5, waiting for transfers between devices, over_cores(): return lax.ppermute(x, 'tm', swap)  4.32 us
    ppermute x7, waiting for transfers between devices, ahead_of(): return lax.ppermute(x, 'gen', backward)  3.46 us
    slice x2, local copies, waits for them, and re-layouts, by_ring(): top, bottom = (effects[:cut], effects[cut:])  2.06 us
  transfers between devices with their start and end apart: 23, of which 14 were waited for; matrix products, arithmetic and copies ran while one was open for 1% of the time, Pallas kernels for 7%

profile of v4, /device:TPU:0, one launch (start us, length us, event | category | flops | bytes accessed | tf_op | source)
XLA Modules:
  0.0 90.9 jit_solution(10137879814523790670)
XLA Ops:
  0.0 1.0 %slice.7.refs_1_ = f32[832,128]{1,0:T(8,128)S(1)} slice(f32[1600,128]{1,0:T(8,128)} %param.6), slice={[768:1600], [0:128]} | slice | bytes 851968 | tf_op jit(solution)/shard_map/slice | solution.py:334
  1.0 3.1 %collective-permute-start.1 = (f32[832,128]{1,0:T(8,128)S(1)}, f32[832,128]{1,0:T(8,128)S(1)}, u32[]{:S(2)}, u32[]{:S(2)}) collective-permute-start(f32[832,128]{1,0:T(8,128)S(1)} %slice.7.refs_1_), channel_id=1, source_target_pairs={{0,8},{8,16},{16,24},{24,28},{28,20},{20,12},{12,4},{4,0},{1,9},{9... | collective-permute-start | bytes 1277960 | tf_op jit(solution)/shard_map/ppermute | solution.py:314
  4.1 1.0 %slice.6.refs_0_ = f32[768,128]{1,0:T(8,128)S(1)} slice(f32[1600,128]{1,0:T(8,128)} %param.6), slice={[0:768], [0:128]} | slice | bytes 786432 | tf_op jit(solution)/shard_map/slice | solution.py:334
  5.1 2.1 %collective-permute-start = (f32[768,128]{1,0:T(8,128)S(1)}, f32[768,128]{1,0:T(8,128)S(1)}, u32[]{:S(2)}, u32[]{:S(2)}) collective-permute-start(f32[768,128]{1,0:T(8,128)S(1)} %slice.6.refs_0_), channel_id=1, source_target_pairs={{0,8},{8,16},{16,24},{24,28},{28,20},{20,12},{12,4},{4,0},{1,9},{9... | collective-permute-start | bytes 1179656 | tf_op jit(solution)/shard_map/ppermute | solution.py:314
  7.2 7.5 %collective-permute-done.1.refs_1_ = f32[832,128]{1,0:T(8,128)S(1)} collective-permute-done((f32[832,128]{1,0:T(8,128)S(1)}, f32[832,128]{1,0:T(8,128)S(1)}, u32[]{:S(2)}, u32[]{:S(2)}) %collective-permute-start.1) | collective-permute-done | bytes 426016 | tf_op jit(solution)/shard_map/ppermute | solution.py:314
  14.7 2.1 %collective-permute-start.5 = (f32[832,128]{1,0:T(8,128)S(1)}, f32[832,128]{1,0:T(8,128)S(1)}, u32[]{:S(2)}, u32[]{:S(2)}) collective-permute-start(f32[832,128]{1,0:T(8,128)S(1)} %collective-permute-done.1.refs_1_), channel_id=1, source_target_pairs={{0,8},{8,16},{16,24},{24,28},{28,20},{20,12},{12,4},{4,0},{1,9},{9... | collective-permute-start | bytes 1277960 | tf_op jit(solution)/shard_map/ppermute | solution.py:314
  16.9 1.8 %copy-done = bf16[800,1600]{1,0:T(8,128)(2,1)S(1)} copy-done((bf16[800,1600]{1,0:T(8,128)(2,1)S(1)}, bf16[800,1600]{1,0:T(8,128)(2,1)}, u32[]{:S(2)}) %copy-start) | copy-done | bytes 2560024
  18.6 1.0 %shard_map.56 = (f32[800,128]{1,0:T(8,128)S(1)}, f32[4,896]{1,0:T(4,128)S(1)}) custom-call(bf16[800,1600]{1,0:T(8,128)(2,1)S(1)} %copy-done, f32[768,128]{1,0:T(8,128)S(1)} %slice.6.refs_0_, f32[832,128]{1,0:T(8,128)S(1)} %slice.7.refs_1_), custom_call_target="tpu_custom_call" | custom-call | flops 100000000 | tf_op jit(solution)/shard_map/pallas_call | solution.py:18
  19.6 3.5 %collective-permute-done.refs_0_ = f32[768,128]{1,0:T(8,128)S(1)} collective-permute-done((f32[768,128]{1,0:T(8,128)S(1)}, f32[768,128]{1,0:T(8,128)S(1)}, u32[]{:S(2)}, u32[]{:S(2)}) %collective-permute-start) | collective-permute-done | bytes 393248 | tf_op jit(solution)/shard_map/ppermute | solution.py:314
  23.1 2.1 %collective-permute-start.4 = (f32[768,128]{1,0:T(8,128)S(1)}, f32[768,128]{1,0:T(8,128)S(1)}, u32[]{:S(2)}, u32[]{:S(2)}) collective-permute-start(f32[768,128]{1,0:T(8,128)S(1)} %collective-permute-done.refs_0_), channel_id=1, source_target_pairs={{0,8},{8,16},{16,24},{24,28},{28,20},{20,12},{12,4},{4,0},{1,9},{9... | collective-permute-start | bytes 1179656 | tf_op jit(solution)/shard_map/ppermute | solution.py:314
  25.3 14.5 %collective-permute-done.4.refs_0_ = f32[768,128]{1,0:T(8,128)S(1)} collective-permute-done((f32[768,128]{1,0:T(8,128)S(1)}, f32[768,128]{1,0:T(8,128)S(1)}, u32[]{:S(2)}, u32[]{:S(2)}) %collective-permute-start.4) | collective-permute-done | bytes 393248 | tf_op jit(solution)/shard_map/ppermute | solution.py:314
  39.8 1.5 %collective-permute-done.6.refs_2_ = f32[768,128]{1,0:T(8,128)S(1)} collective-permute-done((f32[768,128]{1,0:T(8,128)S(1)}, f32[768,128]{1,0:T(8,128)S(1)}, u32[]{:S(2)}, u32[]{:S(2)}) %collective-permute-start.6) | collective-permute-done | bytes 393248 | tf_op jit(solution)/shard_map/ppermute | solution.py:311
  41.4 1.6 %collective-permute-start.10 = (f32[832,128]{1,0:T(8,128)S(1)}, f32[832,128]{1,0:T(8,128)S(1)}, u32[]{:S(2)}, u32[]{:S(2)}) collective-permute-start(f32[832,128]{1,0:T(8,128)S(1)} %collective-permute-done.5.refs_1_), channel_id=1, source_target_pairs={{0,8},{8,16},{16,24},{24,28},{28,20},{20,12},{12,4},{4,0},{1,9},{9... | collective-permute-start | bytes 1277960 | tf_op jit(solution)/shard_map/ppermute | solution.py:314
  43.0 0.4 collective-permute-start.12
  43.4 1.8 %shard_map.57 = (f32[800,128]{1,0:T(8,128)S(1)}, f32[4,896]{1,0:T(4,128)S(1)}, f32[800,128]{1,0:T(8,128)S(1)}, f32[4,896]{1,0:T(4,128)S(1)}) custom-call(bf16[800,1600]{1,0:T(8,128)(2,1)S(1)} %copy-done, f32[768,128]{1,0:T(8,128)S(1)} %collective-permute-done.4.refs_0_, f32[832,128]{1,0:T(8,128)S(1)} %collective-permute-done.5.refs_1_, ...), custom_call_target="tpu_custom_call" | custom-call | flops 200000000 | tf_op jit(solution)/shard_map/pallas_call | solution.py:18
  45.2 0.1 shard_map.58
  45.3 1.6 %collective-permute-start.8 = (f32[800,128]{1,0:T(8,128)S(1)}, f32[800,128]{1,0:T(8,128)S(1)}, u32[]{:S(2)}, u32[]{:S(2)}) collective-permute-start(f32[800,128]{1,0:T(8,128)S(1)} %get-tuple-element.55), channel_id=1, source_target_pairs={{0,2},{1,3},{2,0},{3,1},{4,6},{5,7},{6,4},{7,5},{8,10},{9,11},{10,... | collective-permute-start | bytes 1228808 | tf_op jit(solution)/shard_map/ppermute | solution.py:332
  46.9 1.8 %shard_map.55 = (f32[800,128]{1,0:T(8,128)S(1)}, f32[4,896]{1,0:T(4,128)S(1)}, f32[800,128]{1,0:T(8,128)S(1)}, f32[4,896]{1,0:T(4,128)S(1)}) custom-call(bf16[800,1600]{1,0:T(8,128)(2,1)S(1)} %copy-done.1, f32[768,128]{1,0:T(8,128)S(1)} %collective-permute-done.refs_0_, f32[832,128]{1,0:T(8,128)S(1)} %collective-permute-done.1.refs_1_, ...), custom_call_target="tpu_custom_call" | custom-call | flops 200000000 | tf_op jit(solution)/shard_map/pallas_call | solution.py:18
  48.6 1.6 %collective-permute-start.9 = (f32[768,128]{1,0:T(8,128)S(1)}, f32[768,128]{1,0:T(8,128)S(1)}, u32[]{:S(2)}, u32[]{:S(2)}) collective-permute-start(f32[768,128]{1,0:T(8,128)S(1)} %collective-permute-done.4.refs_0_), channel_id=1, source_target_pairs={{0,8},{8,16},{16,24},{24,28},{28,20},{20,12},{12,4},{4,0},{1,9},{9... | collective-permute-start | bytes 1179656 | tf_op jit(solution)/shard_map/ppermute | solution.py:314
  50.3 0.4 collective-permute-start.11
  50.7 9.5 %collective-permute-done.9.refs_0_ = f32[768,128]{1,0:T(8,128)S(1)} collective-permute-done((f32[768,128]{1,0:T(8,128)S(1)}, f32[768,128]{1,0:T(8,128)S(1)}, u32[]{:S(2)}, u32[]{:S(2)}) %collective-permute-start.9) | collective-permute-done | bytes 393248 | tf_op jit(solution)/shard_map/ppermute | solution.py:314
  60.2 1.3 %collective-permute-done.11.refs_2_ = f32[768,128]{1,0:T(8,128)S(1)} collective-permute-done((f32[768,128]{1,0:T(8,128)S(1)}, f32[768,128]{1,0:T(8,128)S(1)}, u32[]{:S(2)}, u32[]{:S(2)}) %collective-permute-start.11) | collective-permute-done | bytes 393248 | tf_op jit(solution)/shard_map/ppermute | solution.py:311
  61.5 0.1 shard_map.59.two_sum
  61.6 1.8 %shard_map.60 = (f32[800,128]{1,0:T(8,128)S(1)}, f32[4,896]{1,0:T(4,128)S(1)}, f32[800,128]{1,0:T(8,128)S(1)}, f32[4,896]{1,0:T(4,128)S(1)}) custom-call(bf16[800,1600]{1,0:T(8,128)(2,1)S(1)} %copy-done.1, f32[768,128]{1,0:T(8,128)S(1)} %collective-permute-done.9.refs_0_, f32[832,128]{1,0:T(8,128)S(1)} %collective-permute-done.10.refs_1_, ...), custom_call_target="tpu_custom_call" | custom-call | flops 2000000000 | tf_op jit(solution)/shard_map/pallas_call | solution.py:18
  63.3 0.3 shard_map.61
  63.6 0.1 collective-permute-start.13
  63.7 0.5 collective-permute-start.17
  64.2 1.6 %collective-permute-start.16 = (f32[768,128]{1,0:T(8,128)S(1)}, f32[768,128]{1,0:T(8,128)S(1)}, u32[]{:S(2)}, u32[]{:S(2)}) collective-permute-start(f32[768,128]{1,0:T(8,128)S(1)} %collective-permute-done.9.refs_0_), channel_id=1, source_target_pairs={{0,8},{8,16},{16,24},{24,28},{28,20},{20,12},{12,4},{4,0},{1,9},{9... | collective-permute-start | bytes 1179656 | tf_op jit(solution)/shard_map/ppermute | solution.py:314
  65.8 0.3 collective-permute-done.13.got_ref
  66.1 0.1 shard_map.62
  66.2 1.6 %collective-permute-start.14 = (f32[816,128]{1,0:T(8,128)S(1)}, f32[816,128]{1,0:T(8,128)S(1)}, u32[]{:S(2)}, u32[]{:S(2)}) collective-permute-start(f32[816,128]{1,0:T(8,128)S(1)} %get-tuple-element.75), channel_id=1, source_target_pairs={{0,2},{1,3},{2,0},{3,1},{4,6},{5,7},{6,4},{7,5},{8,10},{9,11},{10,... | collective-permute-start | bytes 1253384 | tf_op jit(solution)/shard_map/ppermute | solution.py:332
  67.8 7.6 %collective-permute-done.16.refs_0_ = f32[768,128]{1,0:T(8,128)S(1)} collective-permute-done((f32[768,128]{1,0:T(8,128)S(1)}, f32[768,128]{1,0:T(8,128)S(1)}, u32[]{:S(2)}, u32[]{:S(2)}) %collective-permute-start.16) | collective-permute-done | bytes 393248 | tf_op jit(solution)/shard_map/ppermute | solution.py:314
  75.4 0.5 collective-permute-done.17.refs_1_
  75.9 1.0 %shard_map.63 = (f32[800,128]{1,0:T(8,128)S(1)}, f32[4,896]{1,0:T(4,128)S(1)}) custom-call(bf16[800,1600]{1,0:T(8,128)(2,1)S(1)} %copy-done.1, f32[768,128]{1,0:T(8,128)S(1)} %collective-permute-done.16.refs_0_, f32[832,128]{1,0:T(8,128)S(1)} %collective-permute-done.17.refs_1_), custom_call_target="tpu_custom_call" | custom-call | flops 2000000000 | tf_op jit(solution)/shard_map/pallas_call | solution.py:18
  76.9 1.0 %collective-permute-done.14.got_odd = f32[816,128]{1,0:T(8,128)S(1)} collective-permute-done((f32[816,128]{1,0:T(8,128)S(1)}, f32[816,128]{1,0:T(8,128)S(1)}, u32[]{:S(2)}, u32[]{:S(2)}) %collective-permute-start.14) | collective-permute-done | bytes 417824 | tf_op jit(solution)/shard_map/ppermute | solution.py:332
  77.9 0.1 shard_map.64
  78.0 0.1 collective-permute-start.18
  78.1 1.7 %collective-permute-done.18.got_ref = f32[800,128]{1,0:T(8,128)S(1)} collective-permute-done((f32[800,128]{1,0:T(8,128)S(1)}, f32[800,128]{1,0:T(8,128)S(1)}, u32[]{:S(2)}, u32[]{:S(2)}) %collective-permute-start.18) | collective-permute-done | bytes 409632 | tf_op jit(solution)/shard_map/ppermute | solution.py:329
  79.9 1.6 %collective-permute-start.21 = (f32[400,128]{1,0:T(8,128)S(1)}, f32[400,128]{1,0:T(8,128)S(1)}, u32[]{:S(2)}, u32[]{:S(2)}) collective-permute-start(f32[400,128]{1,0:T(8,128)S(1)} %get-tuple-element.89), channel_id=1, source_target_pairs={{0,2},{1,3},{2,0},{3,1},{4,6},{5,7},{6,4},{7,5},{8,10},{9,11},{10,... | collective-permute-start | bytes 614408 | tf_op jit(solution)/shard_map/ppermute | solution.py:332
  81.4 0.1 shard_map.66
  81.6 0.6 collective-permute-start.19
  82.2 1.0 %collective-permute-done.19.got_ref = f32[4,896]{1,0:T(4,128)S(1)} collective-permute-done((f32[4,896]{1,0:T(4,128)S(1)}, f32[4,896]{1,0:T(4,128)S(1)}, u32[]{:S(2)}, u32[]{:S(2)}) %collective-permute-start.19) | collective-permute-done | bytes 14368 | tf_op jit(solution)/shard_map/ppermute | solution.py:329
  83.2 0.6 collective-permute-start.20
  83.8 3.4 %collective-permute-done.20.border_got = f32[2,896]{1,0:T(2,128)S(1)} collective-permute-done((f32[2,896]{1,0:T(2,128)S(1)}, f32[2,896]{1,0:T(2,128)S(1)}, u32[]{:S(2)}, u32[]{:S(2)}) %collective-permute-start.20) | collective-permute-done | bytes 7200 | tf_op jit(solution)/shard_map/ppermute | solution.py:332
  87.2 0.1 collective-permute-start.22
  87.3 0.1 shard_map.69.weights_ref
  87.5 1.3 %collective-permute-done.22.zero_got = f32[400,128]{1,0:T(8,128)S(1)} collective-permute-done((f32[400,128]{1,0:T(8,128)S(1)}, f32[400,128]{1,0:T(8,128)S(1)}, u32[]{:S(2)}, u32[]{:S(2)}) %collective-permute-start.22) | collective-permute-done | bytes 204832 | tf_op jit(solution)/shard_map/ppermute | solution.py:329
  88.7 2.1 %shard_map.70 = f32[800,256]{1,0:T(8,128)} custom-call(f32[816,128]{1,0:T(8,128)S(1)} %get-tuple-element.74.mine_odd, f32[816,128]{1,0:T(8,128)S(1)} %collective-permute-done.14.got_odd, f32[800,128]{1,0:T(8,128)S(1)} %shard_map.59.two_sum, f32[800,128]{1,0:T(8,128)S(1)} %collective-permute-done.15.two_got, f32[400,128]{1,0:T(8,128)S(1)} %shard_map.68.zero_sum, ...), custom_call_target="tpu_custom_call" | custom-call | tf_op jit(solution)/shard_map/pallas_call | solution.py:18
  (26 shorter events, 0.2 us)
Async XLA Ops:
  1.0 13.6 %collective-permute-start.1 = (f32[832,128]{1,0:T(8,128)S(1)}, f32[832,128]{1,0:T(8,128)S(1)}, u32[]{:S(2)}, u32[]{:S(2)}) collective-permute-start(f32[832,128]{1,0:T(8,128)S(1)} %slice.7.refs_1_), channel_id=1, source_target_pairs={{0,8},{8,16},{16,24},{24,28},{28,20},{20,12},{12,4},{4,0},{1,9},{9... | collective-permute-start | bytes 1277960 | tf_op jit(solution)/shard_map/ppermute | solution.py:314
  4.1 12.7 %collective-permute-start.3 = (f32[832,128]{1,0:T(8,128)S(1)}, f32[832,128]{1,0:T(8,128)S(1)}, u32[]{:S(2)}, u32[]{:S(2)}) collective-permute-start(f32[832,128]{1,0:T(8,128)S(1)} %slice.7.refs_1_), channel_id=1, source_target_pairs={{8,0},{16,8},{24,16},{28,24},{20,28},{12,20},{4,12},{0,4},{9,1},{1... | collective-permute-start | bytes 1277960 | tf_op jit(solution)/shard_map/ppermute | solution.py:311
  5.1 18.0 %collective-permute-start = (f32[768,128]{1,0:T(8,128)S(1)}, f32[768,128]{1,0:T(8,128)S(1)}, u32[]{:S(2)}, u32[]{:S(2)}) collective-permute-start(f32[768,128]{1,0:T(8,128)S(1)} %slice.6.refs_0_), channel_id=1, source_target_pairs={{0,8},{8,16},{16,24},{24,28},{28,20},{20,12},{12,4},{4,0},{1,9},{9... | collective-permute-start | bytes 1179656 | tf_op jit(solution)/shard_map/ppermute | solution.py:314
  7.2 18.1 %collective-permute-start.2 = (f32[768,128]{1,0:T(8,128)S(1)}, f32[768,128]{1,0:T(8,128)S(1)}, u32[]{:S(2)}, u32[]{:S(2)}) collective-permute-start(f32[768,128]{1,0:T(8,128)S(1)} %slice.6.refs_0_), channel_id=1, source_target_pairs={{8,0},{16,8},{24,16},{28,24},{20,28},{12,20},{4,12},{0,4},{9,1},{1... | collective-permute-start | bytes 1179656 | tf_op jit(solution)/shard_map/ppermute | solution.py:311
  14.7 26.7 %collective-permute-start.5 = (f32[832,128]{1,0:T(8,128)S(1)}, f32[832,128]{1,0:T(8,128)S(1)}, u32[]{:S(2)}, u32[]{:S(2)}) collective-permute-start(f32[832,128]{1,0:T(8,128)S(1)} %collective-permute-done.1.refs_1_), channel_id=1, source_target_pairs={{0,8},{8,16},{16,24},{24,28},{28,20},{20,12},{12,4},{4,0},{1,9},{9... | collective-permute-start | bytes 1277960 | tf_op jit(solution)/shard_map/ppermute | solution.py:314
  16.9 26.1 %collective-permute-start.7 = (f32[832,128]{1,0:T(8,128)S(1)}, f32[832,128]{1,0:T(8,128)S(1)}, u32[]{:S(2)}, u32[]{:S(2)}) collective-permute-start(f32[832,128]{1,0:T(8,128)S(1)} %collective-permute-done.3.refs_3_), channel_id=1, source_target_pairs={{8,0},{16,8},{24,16},{28,24},{20,28},{12,20},{4,12},{0,4},{9,1},{1... | collective-permute-start | bytes 1277960 | tf_op jit(solution)/shard_map/ppermute | solution.py:311
  16.9 1.8 %copy-start = (bf16[800,1600]{1,0:T(8,128)(2,1)S(1)}, bf16[800,1600]{1,0:T(8,128)(2,1)}, u32[]{:S(2)}) copy-start(bf16[800,1600]{1,0:T(8,128)(2,1)} %relation_ref.9) | copy-start | bytes 7680004
  19.6 27.3 %copy-start.1 = (bf16[800,1600]{1,0:T(8,128)(2,1)S(1)}, bf16[800,1600]{1,0:T(8,128)(2,1)}, u32[]{:S(2)}) copy-start(bf16[800,1600]{1,0:T(8,128)(2,1)} %relation_ref.9) | copy-start | bytes 7680004
  23.1 16.7 %collective-permute-start.4 = (f32[768,128]{1,0:T(8,128)S(1)}, f32[768,128]{1,0:T(8,128)S(1)}, u32[]{:S(2)}, u32[]{:S(2)}) collective-permute-start(f32[768,128]{1,0:T(8,128)S(1)} %collective-permute-done.refs_0_), channel_id=1, source_target_pairs={{0,8},{8,16},{16,24},{24,28},{28,20},{20,12},{12,4},{4,0},{1,9},{9... | collective-permute-start | bytes 1179656 | tf_op jit(solution)/shard_map/ppermute | solution.py:314
  25.3 16.1 %collective-permute-start.6 = (f32[768,128]{1,0:T(8,128)S(1)}, f32[768,128]{1,0:T(8,128)S(1)}, u32[]{:S(2)}, u32[]{:S(2)}) collective-permute-start(f32[768,128]{1,0:T(8,128)S(1)} %collective-permute-done.2.refs_2_), channel_id=1, source_target_pairs={{8,0},{16,8},{24,16},{28,24},{20,28},{12,20},{4,12},{0,4},{9,1},{1... | collective-permute-start | bytes 1179656 | tf_op jit(solution)/shard_map/ppermute | solution.py:311
  41.4 20.2 %collective-permute-start.10 = (f32[832,128]{1,0:T(8,128)S(1)}, f32[832,128]{1,0:T(8,128)S(1)}, u32[]{:S(2)}, u32[]{:S(2)}) collective-permute-start(f32[832,128]{1,0:T(8,128)S(1)} %collective-permute-done.5.refs_1_), channel_id=1, source_target_pairs={{0,8},{8,16},{16,24},{24,28},{28,20},{20,12},{12,4},{4,0},{1,9},{9... | collective-permute-start | bytes 1277960 | tf_op jit(solution)/shard_map/ppermute | solution.py:314
  43.0 18.6 %collective-permute-start.12 = (f32[832,128]{1,0:T(8,128)S(1)}, f32[832,128]{1,0:T(8,128)S(1)}, u32[]{:S(2)}, u32[]{:S(2)}) collective-permute-start(f32[832,128]{1,0:T(8,128)S(1)} %collective-permute-done.7.refs_3_), channel_id=1, source_target_pairs={{8,0},{16,8},{24,16},{28,24},{20,28},{12,20},{4,12},{0,4},{9,1},{1... | collective-permute-start | bytes 1277960 | tf_op jit(solution)/shard_map/ppermute | solution.py:311
  45.3 16.2 %collective-permute-start.8 = (f32[800,128]{1,0:T(8,128)S(1)}, f32[800,128]{1,0:T(8,128)S(1)}, u32[]{:S(2)}, u32[]{:S(2)}) collective-permute-start(f32[800,128]{1,0:T(8,128)S(1)} %get-tuple-element.55), channel_id=1, source_target_pairs={{0,2},{1,3},{2,0},{3,1},{4,6},{5,7},{6,4},{7,5},{8,10},{9,11},{10,... | collective-permute-start | bytes 1228808 | tf_op jit(solution)/shard_map/ppermute | solution.py:332
  48.6 11.5 %collective-permute-start.9 = (f32[768,128]{1,0:T(8,128)S(1)}, f32[768,128]{1,0:T(8,128)S(1)}, u32[]{:S(2)}, u32[]{:S(2)}) collective-permute-start(f32[768,128]{1,0:T(8,128)S(1)} %collective-permute-done.4.refs_0_), channel_id=1, source_target_pairs={{0,8},{8,16},{16,24},{24,28},{28,20},{20,12},{12,4},{4,0},{1,9},{9... | collective-permute-start | bytes 1179656 | tf_op jit(solution)/shard_map/ppermute | solution.py:314
  50.3 11.2 %collective-permute-start.11 = (f32[768,128]{1,0:T(8,128)S(1)}, f32[768,128]{1,0:T(8,128)S(1)}, u32[]{:S(2)}, u32[]{:S(2)}) collective-permute-start(f32[768,128]{1,0:T(8,128)S(1)} %collective-permute-done.6.refs_2_), channel_id=1, source_target_pairs={{8,0},{16,8},{24,16},{28,24},{20,28},{12,20},{4,12},{0,4},{9,1},{1... | collective-permute-start | bytes 1179656 | tf_op jit(solution)/shard_map/ppermute | solution.py:311
  63.6 2.4 %collective-permute-start.13 = (f32[1632,128]{1,0:T(8,128)S(1)}, f32[1632,128]{1,0:T(8,128)S(1)}, u32[]{:S(2)}, u32[]{:S(2)}) collective-permute-start(f32[1632,128]{1,0:T(8,128)S(1)} %get-tuple-element.73), channel_id=1, source_target_pairs={{0,1},{1,0},{2,3},{3,2},{4,5},{5,4},{6,7},{7,6},{8,9},{9,8},{10,11... | collective-permute-start | bytes 2506760 | tf_op jit(solution)/shard_map/ppermute | solution.py:329
  63.7 12.2 %collective-permute-start.17 = (f32[832,128]{1,0:T(8,128)S(1)}, f32[832,128]{1,0:T(8,128)S(1)}, u32[]{:S(2)}, u32[]{:S(2)}) collective-permute-start(f32[832,128]{1,0:T(8,128)S(1)} %collective-permute-done.12.refs_3_), channel_id=1, source_target_pairs={{8,0},{16,8},{24,16},{28,24},{20,28},{12,20},{4,12},{0,4},{9,1},{1... | collective-permute-start | bytes 1277960 | tf_op jit(solution)/shard_map/ppermute | solution.py:311
  64.2 11.2 %collective-permute-start.16 = (f32[768,128]{1,0:T(8,128)S(1)}, f32[768,128]{1,0:T(8,128)S(1)}, u32[]{:S(2)}, u32[]{:S(2)}) collective-permute-start(f32[768,128]{1,0:T(8,128)S(1)} %collective-permute-done.9.refs_0_), channel_id=1, source_target_pairs={{0,8},{8,16},{16,24},{24,28},{28,20},{20,12},{12,4},{4,0},{1,9},{9... | collective-permute-start | bytes 1179656 | tf_op jit(solution)/shard_map/ppermute | solution.py:314
  66.2 21.2 %copy-start.2 = (f32[1024]{0:T(1024)S(1)}, f32[1024]{0:T(1024)}, u32[]{:S(2)}) copy-start(f32[1024]{0:T(1024)} %one_ref.1) | copy-start | bytes 12292
  66.2 21.2 %copy-start.3 = (f32[1024]{0:T(1024)S(1)}, f32[1024]{0:T(1024)}, u32[]{:S(2)}) copy-start(f32[1024]{0:T(1024)} %two_ref.1) | copy-start | bytes 12292
  66.2 21.2 %copy-start.4 = (f32[1024]{0:T(1024)S(1)}, f32[1024]{0:T(1024)}, u32[]{:S(2)}) copy-start(f32[1024]{0:T(1024)} %scale_ref.1) | copy-start | bytes 12292
  66.2 11.7 %collective-permute-start.14 = (f32[816,128]{1,0:T(8,128)S(1)}, f32[816,128]{1,0:T(8,128)S(1)}, u32[]{:S(2)}, u32[]{:S(2)}) collective-permute-start(f32[816,128]{1,0:T(8,128)S(1)} %get-tuple-element.75), channel_id=1, source_target_pairs={{0,2},{1,3},{2,0},{3,1},{4,6},{5,7},{6,4},{7,5},{8,10},{9,11},{10,... | collective-permute-start | bytes 1253384 | tf_op jit(solution)/shard_map/ppermute | solution.py:332
  78.0 1.8 %collective-permute-start.18 = (f32[800,128]{1,0:T(8,128)S(1)}, f32[800,128]{1,0:T(8,128)S(1)}, u32[]{:S(2)}, u32[]{:S(2)}) collective-permute-start(f32[800,128]{1,0:T(8,128)S(1)} %get-tuple-element.80), channel_id=1, source_target_pairs={{0,1},{1,0},{2,3},{3,2},{4,5},{5,4},{6,7},{7,6},{8,9},{9,8},{10,11... | collective-permute-start | bytes 1228808 | tf_op jit(solution)/shard_map/ppermute | solution.py:329
  79.9 7.3 %collective-permute-start.21 = (f32[400,128]{1,0:T(8,128)S(1)}, f32[400,128]{1,0:T(8,128)S(1)}, u32[]{:S(2)}, u32[]{:S(2)}) collective-permute-start(f32[400,128]{1,0:T(8,128)S(1)} %get-tuple-element.89), channel_id=1, source_target_pairs={{0,2},{1,3},{2,0},{3,1},{4,6},{5,7},{6,4},{7,5},{8,10},{9,11},{10,... | collective-permute-start | bytes 614408 | tf_op jit(solution)/shard_map/ppermute | solution.py:332
  81.4 6.0 %collective-permute-start.15 = (f32[800,128]{1,0:T(8,128)S(1)}, f32[800,128]{1,0:T(8,128)S(1)}, u32[]{:S(2)}, u32[]{:S(2)}) collective-permute-start(f32[800,128]{1,0:T(8,128)S(1)} %shard_map.59.two_sum), channel_id=1, source_target_pairs={{0,1},{1,0},{2,3},{3,2},{4,5},{5,4},{6,7},{7,6},{8,9},{9,8},{10,11... | collective-permute-start | bytes 1228808 | tf_op jit(solution)/shard_map/ppermute | solution.py:329
  81.6 1.6 %collective-permute-start.19 = (f32[4,896]{1,0:T(4,128)S(1)}, f32[4,896]{1,0:T(4,128)S(1)}, u32[]{:S(2)}, u32[]{:S(2)}) collective-permute-start(f32[4,896]{1,0:T(4,128)S(1)} %get-tuple-element.86), channel_id=1, source_target_pairs={{0,1},{1,0},{2,3},{3,2},{4,5},{5,4},{6,7},{7,6},{8,9},{9,8},{10,11... | collective-permute-start | bytes 43016 | tf_op jit(solution)/shard_map/ppermute | solution.py:329
  83.2 4.0 %collective-permute-start.20 = (f32[2,896]{1,0:T(2,128)S(1)}, f32[2,896]{1,0:T(2,128)S(1)}, u32[]{:S(2)}, u32[]{:S(2)}) collective-permute-start(f32[2,896]{1,0:T(2,128)S(1)} %get-tuple-element.87), channel_id=1, source_target_pairs={{0,2},{1,3},{2,0},{3,1},{4,6},{5,7},{6,4},{7,5},{8,10},{9,11},{10,... | collective-permute-start | bytes 21512 | tf_op jit(solution)/shard_map/ppermute | solution.py:332
  87.2 1.5 %collective-permute-start.22 = (f32[400,128]{1,0:T(8,128)S(1)}, f32[400,128]{1,0:T(8,128)S(1)}, u32[]{:S(2)}, u32[]{:S(2)}) collective-permute-start(f32[400,128]{1,0:T(8,128)S(1)} %shard_map.68.zero_sum), channel_id=1, source_target_pairs={{0,1},{1,0},{2,3},{3,2},{4,5},{5,4},{6,7},{7,6},{8,9},{9,8},{10,11... | collective-permute-start | bytes 614408 | tf_op jit(solution)/shard_map/ppermute | solution.py:329

commit v5 on v4

--- a/solution.py
+++ b/solution.py
@@ -104,6 +104,39 @@
         edges_ref = refs[2 * count + 2 * n + 1]
         edges_ref[0:2] = turned[0:2]
         edges_ref[2:4] = turned[WIDTH - 2 :]
+
+
+def bottom_kernel(cut, relation_ref, *refs):
+    both_ref = refs[-1]
+    count = (len(refs) - 1) // 2
+    for n in range(count):
+        both_ref[...] = jnp.dot(
+            relation_ref[:, cut:], two_parts(refs[n][...]), preferred_element_type=jnp.float32
+        )
+        refs[count + n][...] = both_ref[:, :WIDTH] + both_ref[:, WIDTH:]
+
+
+def top_kernel(cut, relation_ref, *refs):
+    both_ref, padded_ref = refs[-2:]
+    count = (len(refs) - 2) // 4
+    rows = relation_ref.shape[0]
+    padded_ref[...] = jnp.zeros_like(padded_ref)
+    for n in range(count):
+        both_ref[...] = jnp.dot(
+            relation_ref[:, :cut], two_parts(refs[n][...]), preferred_element_type=jnp.float32
+        )
+        padded_ref[:rows] = both_ref[:, :WIDTH] + both_ref[:, WIDTH:] + refs[count + n][...]
+        refs[2 * count + 2 * n][...] = padded_ref[:rows]
+        turned = padded_ref[...].T
+        edges_ref = refs[2 * count + 2 * n + 1]
+        edges_ref[0:2] = turned[0:2]
+        edges_ref[2:4] = turned[WIDTH - 2 :]
+
+
+def two_parts(block):
+    high = block.astype(jnp.bfloat16)
+    low = (block - high.astype(jnp.float32)).astype(jnp.bfloat16)
+    return jnp.concatenate([high, low], axis=1)
 
 
 def odd_kernel(spot_of, fars, *refs):
@@ -208,10 +241,73 @@
             mine_ref[...] = keep_ref[here] + got_ref[here]
 
 
+def row_weights(weights, far, lanes):
+    return jnp.where(lanes, weights[2 + far : 3 + far], 0.0)
+
+
+def beside(weights, border, left):
+    span = border.shape[1]
+    row = lax.broadcasted_iota(jnp.int32, (8, span), 0)
+    nothing = jnp.zeros((WIDTH - 8, span), jnp.float32)
+    end = WIDTH - 1
+    first = weights[0:1, 0:1] * border[0:1] + weights[1:2, 0:1] * border[1:2]
+    second = weights[0:1, 1:2] * border[1:2]
+    above = jnp.where(row == 0, first, jnp.where(row == 1, second, 0.0))
+    last = weights[3:4, end:] * border[0:1] + weights[4:5, end:] * border[1:2]
+    but_last = weights[4:5, end - 1 : end] * border[0:1]
+    below = jnp.where(row == 7, last, jnp.where(row == 6, but_last, 0.0))
+    none = jnp.zeros_like(above)
+    return jnp.concatenate(
+        [jnp.where(left, above, none), nothing[: WIDTH - 16], jnp.where(left, none, below)], axis=0
+    ).T
+
+
+def shares(weights, other_weights, block, left):
+    lane = lax.broadcasted_iota(jnp.int32, (1, WIDTH), 1)
+    own = weights[2:3] * block
+    beyond = 0.0
+    for far in (1, 2):
+        back, on = pltpu.roll(block, far, 1), pltpu.roll(block, WIDTH - far, 1)
+        own += row_weights(weights, -far, lane >= far) * back
+        own += row_weights(weights, far, lane < WIDTH - far) * on
+        beyond += jnp.where(
+            left,
+            row_weights(other_weights, -far, lane < far) * back,
+            row_weights(other_weights, far, lane >= WIDTH - far) * on,
+        )
+    return own, beyond
+
+
+def odd_column(spot):
+    return jnp.where((spot.place_of(spot.share * spot.tm) + spot.place) % 2 == 0, 1, 0)
+
+
+def column_weights(spot, weights_ref, column):
+    start = (spot.tm * 2 + column) * WIDTH
+    return weights_ref[:, pl.ds(pl.multiple_of(start, WIDTH), WIDTH)]
+
+
+def odd_shares_kernel(spot_of, mine_ref, got_ref, weights_ref, own_ref, beyond_ref, sides_ref):
+    spot = spot_of()
+    odd = odd_column(spot)
+    rows, span = own_ref.shape[0], sides_ref.shape[0]
+    weights = column_weights(spot, weights_ref, odd)
+    others = column_weights(spot, weights_ref, 1 - odd)
+    extra = mine_ref[rows:] + got_ref[rows:]
+    border = jnp.concatenate([extra[2 * k : 2 * k + 2] for k in range(span // WIDTH)], axis=1)
+    sides_ref[...] = beside(weights, border, odd == 0)
+    step = rows // 5
+    for n in range(5):
+        here = slice(n * step, (n + 1) * step)
+        own, beyond = shares(weights, others, mine_ref[here] + got_ref[here], odd == 0)
+        own_ref[here] = own + sides_ref[here]
+        beyond_ref[here] = beyond
+
+
 def last_kernel(
     spot_of,
-    mine_odd,
-    got_odd,
+    odd_own,
+    odd_beyond,
     two_sum,
     two_got,
     zero_sum,
@@ -220,70 +316,40 @@
     border_got,
     weights_ref,
     out_any,
-    sums_ref,
+    even_ref,
     sides_ref,
     made_ref,
     sems,
 ):
     spot = spot_of()
-    odd = jnp.where((spot.place_of(spot.share * spot.tm) + spot.place) % 2 == 0, 1, 0)
+    odd = odd_column(spot)
     rows = out_any.shape[0]
-    span = sides_ref.shape[1]
     is_two = (spot.owner_of(2) == spot.tm) | (spot.owner_of(-2) == spot.tm)
-    sums_ref[odd] = mine_odd[:rows] + got_odd[:rows]
 
     @pl.when(is_two)
     def _():
-        sums_ref[1 - odd] = two_sum[...] + two_got[...]
+        even_ref[...] = two_sum[...] + two_got[...]
 
     @pl.when(jnp.logical_not(is_two))
     def _():
         half, core = rows // 2, spot.tm % 2
-        sums_ref[1 - odd, pl.ds(pl.multiple_of(core * half, 8), half)] = zero_sum[...]
-        sums_ref[1 - odd, pl.ds(pl.multiple_of((1 - core) * half, 8), half)] = zero_got[...]
-
-    start = pl.multiple_of(spot.tm * (2 * WIDTH), 2 * WIDTH)
-    weights = weights_ref[:, pl.ds(start, 2 * WIDTH)]
-    row = lax.broadcasted_iota(jnp.int32, (8, span), 0)
-    nothing = jnp.zeros((WIDTH - 8, span), jnp.float32)
-
-    extra = mine_odd[rows:] + got_odd[rows:]
-    odd_border = jnp.concatenate([extra[2 * k : 2 * k + 2] for k in range(span // WIDTH)], axis=1)
-    even_border = border_mine[...] + border_got[...]
-    before = jnp.where(odd == 0, odd_border, even_border)
-    after = jnp.where(odd == 0, even_border, odd_border)
-    end = 2 * WIDTH - 1
-    first = weights[0:1, 0:1] * before[0:1] + weights[1:2, 0:1] * before[1:2]
-    second = weights[0:1, 1:2] * before[1:2]
-    above = jnp.where(row == 0, first, jnp.where(row == 1, second, 0.0))
-    last = weights[3:4, end:] * after[0:1] + weights[4:5, end:] * after[1:2]
-    but_last = weights[4:5, end - 1 : end] * after[0:1]
-    below = jnp.where(row == 7, last, jnp.where(row == 6, but_last, 0.0))
-    sides_ref[0] = jnp.concatenate([above, nothing], axis=0).T
-    sides_ref[1] = jnp.concatenate([nothing, below], axis=0).T
-    lane = lax.broadcasted_iota(jnp.int32, (1, WIDTH), 1)
-    inner = [weights[:, :WIDTH], weights[:, WIDTH:]]
-    near = [jnp.where(lane >= far, inner[0][2 - far : 3 - far], 0.0) for far in (1, 2)]
-    beyond = [jnp.where(lane < WIDTH - far, inner[1][2 + far : 3 + far], 0.0) for far in (1, 2)]
-    pieces = 5
-    step = rows // pieces
+        even_ref[pl.ds(pl.multiple_of(core * half, 8), half)] = zero_sum[...]
+        even_ref[pl.ds(pl.multiple_of((1 - core) * half, 8), half)] = zero_got[...]
+
+    weights = column_weights(spot, weights_ref, 1 - odd)
+    others = column_weights(spot, weights_ref, odd)
+    sides_ref[...] = beside(weights, border_mine[...] + border_got[...], odd == 1)
+    step = rows // 5
     copies = []
-    for n in range(pieces):
+    for n in range(5):
         here = slice(n * step, (n + 1) * step)
-        left, right = sums_ref[0, here], sums_ref[1, here]
-        made_left = sides_ref[0, here] + inner[0][2:3] * left
-        made_right = sides_ref[1, here] + inner[1][2:3] * right
-        for far in (1, 2):
-            left_back, right_back = pltpu.roll(left, far, 1), pltpu.roll(right, far, 1)
-            left_on, right_on = pltpu.roll(left, WIDTH - far, 1), pltpu.roll(right, WIDTH - far, 1)
-            on = jnp.where(lane < WIDTH - far, left_on, right_on)
-            back = jnp.where(lane >= far, right_back, left_back)
-            made_left += near[far - 1] * left_back + inner[0][2 + far : 3 + far] * on
-            made_right += inner[1][2 - far : 3 - far] * back + beyond[far - 1] * right_on
-        made_ref[here, :WIDTH] = made_left
-        made_ref[here, WIDTH:] = made_right
-        copies.append(pltpu.make_async_copy(made_ref.at[here], out_any.at[here], sems.at[n]))
-        copies[n].start()
+        own, beyond = shares(weights, others, even_ref[here], odd == 1)
+        made_ref[1 - odd, here] = own + sides_ref[here] + odd_beyond[here]
+        made_ref[odd, here] = odd_own[here] + beyond
+        for column in range(2):
+            into = out_any.at[here, column * WIDTH : (column + 1) * WIDTH]
+            copies.append(pltpu.make_async_copy(made_ref.at[column, here], into, sems.at[len(copies)]))
+            copies[-1].start()
     for copy in copies:
         copy.wait()
 
@@ -331,6 +397,25 @@
     def over_y(x):
         return lax.ppermute(x, "tm", [(t, t ^ 2) for t in range(tms)])
 
+    def in_two_steps(behind, ahead, after=(), cost=1):
+        both = pltpu.VMEM((rows, 2 * WIDTH), jnp.float32)
+        parts = [tied(blocks[far][1], *after) for far in (behind, ahead)]
+        bottoms = call(
+            functools.partial(bottom_kernel, cut),
+            [(rows, WIDTH)] * 2,
+            (relation, *parts),
+            [both],
+            flops=KERNEL_FLOPS,
+        )
+        made = call(
+            functools.partial(top_kernel, cut),
+            [(rows, WIDTH), (4, wide)] * 2,
+            (relation, blocks[behind][0], blocks[ahead][0], *bottoms),
+            [both, pltpu.VMEM((wide, WIDTH), jnp.float32)],
+            flops=cost * KERNEL_FLOPS,
+        )
+        products[behind], products[ahead] = made[:2], made[2:]
+
     top, bottom = effects[:cut], effects[cut:]
     blocks, products = {0: (top, bottom)}, {}
     behind, ahead = blocks[0], blocks[0]
@@ -342,8 +427,10 @@
         ahead_top = ahead_of(ahead[0])
         behind, ahead = (behind_top, behind_bottom), (ahead_top, ahead_bottom)
         blocks[-n], blocks[n] = behind, ahead
-        if n < half - 1:
+        if n == 1:
             multiplied(-n, n)
+        if n == 2:
+            in_two_steps(-n, n, after=(), cost=1)
     blocks[half] = (behind_of(behind[0]), ahead_of(ahead[1]))
     two_send, two_keep = call(
         functools.partial(chip_pair_kernel, spot_of, 2),
@@ -353,7 +440,7 @@
     )
     two_sum = call(sum_kernel, [(rows, WIDTH)], (two_keep, over_y(two_send)), flops=KERNEL_FLOPS // 10)[0]
     two_got = over_cores(two_sum)
-    multiplied(1 - half, half - 1, cost=10)
+    in_two_steps(1 - half, half - 1, cost=10)
     odd_fars = (-1, 3, 1, -3)
     send, keep = call(
         functools.partial(odd_kernel, spot_of, odd_fars),
@@ -369,7 +456,7 @@
         flops=KERNEL_FLOPS // 2,
     )
     odd_got = over_y(odd_send)
-    multiplied(half, cost=20)
+    multiplied(half, after=(odd_mine,), cost=20)
     even_fars = (0, half, 2, -2)
     border_send, border_keep = call(
         functools.partial(borders_kernel, spot_of, even_fars),
@@ -388,13 +475,13 @@
     send, keep = call(
         functools.partial(halves_kernel, spot_of, 0),
         [(rows, WIDTH)] * 2,
-        [tied(products[far][0], odd_got) for far in (0, half)],
+        [products[far][0] for far in (0, half)],
         flops=KERNEL_FLOPS // 2,
     )
     zero_send, zero_mine = call(
         half_sums_kernel,
         [(rows // 2, WIDTH)] * 2,
-        (keep, over_cores(send)),
+        (tied(keep, odd_got), over_cores(send)),
         flops=KERNEL_FLOPS // 10,
     )
     zero_sum = call(
@@ -405,15 +492,22 @@
     )[0]
     zero_got = over_cores(zero_sum)
     weights = call(weights_kernel, [(8, phi_one.shape[0])], (phi_one, phi_two, innov_scale))[0]
+    odd_own, odd_beyond = call(
+        functools.partial(odd_shares_kernel, spot_of),
+        [(rows, WIDTH)] * 2,
+        (odd_mine, tied(odd_got, zero_mine), weights),
+        [pltpu.VMEM((wide, WIDTH), jnp.float32)],
+        flops=KERNEL_FLOPS,
+    )
     return call(
         functools.partial(last_kernel, spot_of),
         [(rows, share * WIDTH)],
-        (odd_mine, odd_got, two_sum, two_got, zero_sum, zero_got, border_mine, border_got, weights),
+        (odd_own, odd_beyond, two_sum, two_got, zero_sum, zero_got, border_mine, border_got, weights),
         [
+            pltpu.VMEM((rows, WIDTH), jnp.float32),
+            pltpu.VMEM((wide, WIDTH), jnp.float32),
             pltpu.VMEM((2, rows, WIDTH), jnp.float32),
-            pltpu.VMEM((2, wide, WIDTH), jnp.float32),
-            pltpu.VMEM((rows, share * WIDTH), jnp.float32),
-            pltpu.SemaphoreType.DMA((5,)),
+            pltpu.SemaphoreType.DMA((10,)),
         ],
         into=pl.BlockSpec(memory_space=pl.ANY),
     )[0]

time: 91.1 us -> 86.1 us (0.945)
  waiting for transfers between devices: 54.7 us -> 49.1 us
    ppermute x7, waiting for transfers between devices: 42.6 us -> 34.4 us  [behind_of(): return lax.ppermute(x, 'gen', forward)]
    ppermute x4, waiting for transfers between devices: 4.4 us -> 7.36 us  [over_y(): return lax.ppermute(x, 'tm', [(t, t ^ 2) for t in range(tms)])]
    ppermute x5, waiting for transfers between devices: 4.32 us -> 2.79 us  [over_cores(): return lax.ppermute(x, 'tm', swap)]
    ppermute x7, waiting for transfers between devices: 3.46 us -> 4.53 us  [ahead_of(): return lax.ppermute(x, 'gen', backward)]
    pallas_call x16 -> x19, Pallas kernels: 10.3 us -> 10.9 us  [call(): pl.pallas_call(kernel, out_shape=[jax.ShapeDtypeStruct(shape, jnp.float32...]
  transfers between devices with their start and end apart: 23 -> 23, of which waited for: 14 -> 16; matrix products, arithmetic and copies ran while one was open for 1% -> 1% of each run, Pallas kernels for 7% -> 9%
where the time goes in v5:
time: 86.1 us; the launch traced here: 85.8 us
  waiting for transfers between devices  49.1 us (57%)
  starting transfers between devices  21.9 us (25%)
  Pallas kernels  10.9 us (13%)
  local copies, waits for them, and re-layouts  3.83 us (4%)
    ppermute x7, waiting for transfers between devices, behind_of(): return lax.ppermute(x, 'gen', forward)  34.4 us
    ppermute x7, starting transfers between devices, behind_of(): return lax.ppermute(x, 'gen', forward)  15 us
    pallas_call x19, Pallas kernels, call(): pl.pallas_call(kernel, out_shape=[jax.ShapeDtypeStruct(shape, jnp.float32...  10.9 us
    ppermute x4, waiting for transfers between devices, over_y(): return lax.ppermute(x, 'tm', [(t, t ^ 2) for t in range(tms)])  7.36 us
    ppermute x4, starting transfers between devices, over_y(): return lax.ppermute(x, 'tm', [(t, t ^ 2) for t in range(tms)])  5.32 us
    ppermute x7, waiting for transfers between devices, ahead_of(): return lax.ppermute(x, 'gen', backward)  4.53 us
    ppermute x5, waiting for transfers between devices, over_cores(): return lax.ppermute(x, 'tm', swap)  2.79 us
    slice x2, local copies, waits for them, and re-layouts, by_ring(): top, bottom = (effects[:cut], effects[cut:])  2.06 us
  transfers between devices with their start and end apart: 23, of which 16 were waited for; matrix products, arithmetic and copies ran while one was open for 1% of the time, Pallas kernels for 9%

profile of v5, /device:TPU:0, one launch (start us, length us, event | category | flops | bytes accessed | tf_op | source)
XLA Modules:
  0.0 85.8 jit_solution(8001177606306117080)
XLA Ops:
  0.0 1.0 %slice.7.refs_1_ = f32[832,128]{1,0:T(8,128)S(1)} slice(f32[1600,128]{1,0:T(8,128)} %param.6), slice={[768:1600], [0:128]} | slice | bytes 851968 | tf_op jit(solution)/shard_map/slice | solution.py:419
  1.0 3.1 %collective-permute-start.1 = (f32[832,128]{1,0:T(8,128)S(1)}, f32[832,128]{1,0:T(8,128)S(1)}, u32[]{:S(2)}, u32[]{:S(2)}) collective-permute-start(f32[832,128]{1,0:T(8,128)S(1)} %slice.7.refs_1_), channel_id=1, source_target_pairs={{0,8},{8,16},{16,24},{24,28},{28,20},{20,12},{12,4},{4,0},{1,9},{9... | collective-permute-start | bytes 1277960 | tf_op jit(solution)/shard_map/ppermute | solution.py:380
  4.1 1.0 %slice.6.refs_0_ = f32[768,128]{1,0:T(8,128)S(1)} slice(f32[1600,128]{1,0:T(8,128)} %param.6), slice={[0:768], [0:128]} | slice | bytes 786432 | tf_op jit(solution)/shard_map/slice | solution.py:419
  5.1 2.1 %collective-permute-start = (f32[768,128]{1,0:T(8,128)S(1)}, f32[768,128]{1,0:T(8,128)S(1)}, u32[]{:S(2)}, u32[]{:S(2)}) collective-permute-start(f32[768,128]{1,0:T(8,128)S(1)} %slice.6.refs_0_), channel_id=1, source_target_pairs={{0,8},{8,16},{16,24},{24,28},{28,20},{20,12},{12,4},{4,0},{1,9},{9... | collective-permute-start | bytes 1179656 | tf_op jit(solution)/shard_map/ppermute | solution.py:380
  7.2 7.5 %collective-permute-done.1.refs_1_ = f32[832,128]{1,0:T(8,128)S(1)} collective-permute-done((f32[832,128]{1,0:T(8,128)S(1)}, f32[832,128]{1,0:T(8,128)S(1)}, u32[]{:S(2)}, u32[]{:S(2)}) %collective-permute-start.1) | collective-permute-done | bytes 426016 | tf_op jit(solution)/shard_map/ppermute | solution.py:380
  14.7 2.1 %collective-permute-start.6 = (f32[832,128]{1,0:T(8,128)S(1)}, f32[832,128]{1,0:T(8,128)S(1)}, u32[]{:S(2)}, u32[]{:S(2)}) collective-permute-start(f32[832,128]{1,0:T(8,128)S(1)} %collective-permute-done.1.refs_1_), channel_id=1, source_target_pairs={{0,8},{8,16},{16,24},{24,28},{28,20},{20,12},{12,4},{4,0},{1,9},{9... | collective-permute-start | bytes 1277960 | tf_op jit(solution)/shard_map/ppermute | solution.py:380
  16.9 1.8 %copy-done = bf16[800,1600]{1,0:T(8,128)(2,1)S(1)} copy-done((bf16[800,1600]{1,0:T(8,128)(2,1)S(1)}, bf16[800,1600]{1,0:T(8,128)(2,1)}, u32[]{:S(2)}) %copy-start) | copy-done | bytes 2560024
  18.6 1.0 %shard_map.56 = (f32[800,128]{1,0:T(8,128)S(1)}, f32[4,896]{1,0:T(4,128)S(1)}) custom-call(bf16[800,1600]{1,0:T(8,128)(2,1)S(1)} %copy-done, f32[768,128]{1,0:T(8,128)S(1)} %slice.6.refs_0_, f32[832,128]{1,0:T(8,128)S(1)} %slice.7.refs_1_), custom_call_target="tpu_custom_call" | custom-call | flops 100000000 | tf_op jit(solution)/shard_map/pallas_call | solution.py:18
  19.6 3.5 %collective-permute-done.refs_0_ = f32[768,128]{1,0:T(8,128)S(1)} collective-permute-done((f32[768,128]{1,0:T(8,128)S(1)}, f32[768,128]{1,0:T(8,128)S(1)}, u32[]{:S(2)}, u32[]{:S(2)}) %collective-permute-start) | collective-permute-done | bytes 393248 | tf_op jit(solution)/shard_map/ppermute | solution.py:380
  23.1 2.1 %collective-permute-start.4 = (f32[768,128]{1,0:T(8,128)S(1)}, f32[768,128]{1,0:T(8,128)S(1)}, u32[]{:S(2)}, u32[]{:S(2)}) collective-permute-start(f32[768,128]{1,0:T(8,128)S(1)} %collective-permute-done.refs_0_), channel_id=1, source_target_pairs={{0,8},{8,16},{16,24},{24,28},{28,20},{20,12},{12,4},{4,0},{1,9},{9... | collective-permute-start | bytes 1179656 | tf_op jit(solution)/shard_map/ppermute | solution.py:380
  25.3 6.9 %collective-permute-done.6.refs_0_ = f32[832,128]{1,0:T(8,128)S(1)} collective-permute-done((f32[832,128]{1,0:T(8,128)S(1)}, f32[832,128]{1,0:T(8,128)S(1)}, u32[]{:S(2)}, u32[]{:S(2)}) %collective-permute-start.6) | collective-permute-done | bytes 426016 | tf_op jit(solution)/shard_map/ppermute | solution.py:380
  32.2 2.1 %collective-permute-start.11 = (f32[832,128]{1,0:T(8,128)S(1)}, f32[832,128]{1,0:T(8,128)S(1)}, u32[]{:S(2)}, u32[]{:S(2)}) collective-permute-start(f32[832,128]{1,0:T(8,128)S(1)} %collective-permute-done.6.refs_0_), channel_id=1, source_target_pairs={{0,8},{8,16},{16,24},{24,28},{28,20},{20,12},{12,4},{4,0},{1,9},{9... | collective-permute-start | bytes 1277960 | tf_op jit(solution)/shard_map/ppermute | solution.py:380
  34.4 1.0 %shard_map.57 = (f32[800,128]{1,0:T(8,128)S(1)}, f32[800,128]{1,0:T(8,128)S(1)}) custom-call(bf16[800,1600]{1,0:T(8,128)(2,1)S(1)} %copy-done, f32[832,128]{1,0:T(8,128)S(1)} %collective-permute-done.6.refs_0_, f32[832,128]{1,0:T(8,128)S(1)} %collective-permute-done.7.refs_1_), custom_call_target="tpu_custom_call" | custom-call | flops 100000000 | tf_op jit(solution)/shard_map/pallas_call | solution.py:18
  35.5 5.2 %collective-permute-done.4.refs_0_ = f32[768,128]{1,0:T(8,128)S(1)} collective-permute-done((f32[768,128]{1,0:T(8,128)S(1)}, f32[768,128]{1,0:T(8,128)S(1)}, u32[]{:S(2)}, u32[]{:S(2)}) %collective-permute-start.4) | collective-permute-done | bytes 393248 | tf_op jit(solution)/shard_map/ppermute | solution.py:380
  40.7 2.2 %collective-permute-done.5.refs_1_ = f32[768,128]{1,0:T(8,128)S(1)} collective-permute-done((f32[768,128]{1,0:T(8,128)S(1)}, f32[768,128]{1,0:T(8,128)S(1)}, u32[]{:S(2)}, u32[]{:S(2)}) %collective-permute-start.5) | collective-permute-done | bytes 393248 | tf_op jit(solution)/shard_map/ppermute | solution.py:377
  42.8 0.9 %shard_map.58 = (f32[800,128]{1,0:T(8,128)S(1)}, f32[4,896]{1,0:T(4,128)S(1)}, f32[800,128]{1,0:T(8,128)S(1)}, f32[4,896]{1,0:T(4,128)S(1)}) custom-call(bf16[800,1600]{1,0:T(8,128)(2,1)S(1)} %copy-done, f32[768,128]{1,0:T(8,128)S(1)} %collective-permute-done.4.refs_0_, f32[768,128]{1,0:T(8,128)S(1)} %collective-permute-done.5.refs_1_, ...), custom_call_target="tpu_custom_call" | custom-call | flops 100000000 | tf_op jit(solution)/shard_map/pallas_call | solution.py:18
  43.8 0.1 shard_map.59
  43.9 1.6 %collective-permute-start.8 = (f32[800,128]{1,0:T(8,128)S(1)}, f32[800,128]{1,0:T(8,128)S(1)}, u32[]{:S(2)}, u32[]{:S(2)}) collective-permute-start(f32[800,128]{1,0:T(8,128)S(1)} %get-tuple-element.65), channel_id=1, source_target_pairs={{0,2},{1,3},{2,0},{3,1},{4,6},{5,7},{6,4},{7,5},{8,10},{9,11},{10,... | collective-permute-start | bytes 1228808 | tf_op jit(solution)/shard_map/ppermute | solution.py:398
  45.5 1.8 %shard_map.55 = (f32[800,128]{1,0:T(8,128)S(1)}, f32[4,896]{1,0:T(4,128)S(1)}, f32[800,128]{1,0:T(8,128)S(1)}, f32[4,896]{1,0:T(4,128)S(1)}) custom-call(bf16[800,1600]{1,0:T(8,128)(2,1)S(1)} %copy-done.1, f32[768,128]{1,0:T(8,128)S(1)} %collective-permute-done.refs_0_, f32[832,128]{1,0:T(8,128)S(1)} %collective-permute-done.1.refs_1_, ...), custom_call_target="tpu_custom_call" | custom-call | flops 200000000 | tf_op jit(solution)/shard_map/pallas_call | solution.py:18
  47.2 1.6 %collective-permute-start.9 = (f32[768,128]{1,0:T(8,128)S(1)}, f32[768,128]{1,0:T(8,128)S(1)}, u32[]{:S(2)}, u32[]{:S(2)}) collective-permute-start(f32[768,128]{1,0:T(8,128)S(1)} %collective-permute-done.4.refs_0_), channel_id=1, source_target_pairs={{0,8},{8,16},{16,24},{24,28},{28,20},{20,12},{12,4},{4,0},{1,9},{9... | collective-permute-start | bytes 1179656 | tf_op jit(solution)/shard_map/ppermute | solution.py:380
  48.9 0.4 collective-permute-start.10
  49.3 3.2 %collective-permute-done.8.other_ref = f32[800,128]{1,0:T(8,128)S(1)} collective-permute-done((f32[800,128]{1,0:T(8,128)S(1)}, f32[800,128]{1,0:T(8,128)S(1)}, u32[]{:S(2)}, u32[]{:S(2)}) %collective-permute-start.8) | collective-permute-done | bytes 409632 | tf_op jit(solution)/shard_map/ppermute | solution.py:398
  52.6 1.0 %shard_map.61 = (f32[800,128]{1,0:T(8,128)S(1)}, f32[800,128]{1,0:T(8,128)S(1)}) custom-call(bf16[800,1600]{1,0:T(8,128)(2,1)S(1)} %copy-done.1, f32[832,128]{1,0:T(8,128)S(1)} %collective-permute-done.11.refs_0_, f32[832,128]{1,0:T(8,128)S(1)} %collective-permute-done.12.refs_1_), custom_call_target="tpu_custom_call" | custom-call | flops 100000000 | tf_op jit(solution)/shard_map/pallas_call | solution.py:18
  53.6 3.8 %collective-permute-done.9.refs_0_ = f32[768,128]{1,0:T(8,128)S(1)} collective-permute-done((f32[768,128]{1,0:T(8,128)S(1)}, f32[768,128]{1,0:T(8,128)S(1)}, u32[]{:S(2)}, u32[]{:S(2)}) %collective-permute-start.9) | collective-permute-done | bytes 393248 | tf_op jit(solution)/shard_map/ppermute | solution.py:380
  57.4 1.5 %collective-permute-done.10.refs_1_ = f32[768,128]{1,0:T(8,128)S(1)} collective-permute-done((f32[768,128]{1,0:T(8,128)S(1)}, f32[768,128]{1,0:T(8,128)S(1)}, u32[]{:S(2)}, u32[]{:S(2)}) %collective-permute-start.10) | collective-permute-done | bytes 393248 | tf_op jit(solution)/shard_map/ppermute | solution.py:377
  58.9 0.9 %shard_map.62 = (f32[800,128]{1,0:T(8,128)S(1)}, f32[4,896]{1,0:T(4,128)S(1)}, f32[800,128]{1,0:T(8,128)S(1)}, f32[4,896]{1,0:T(4,128)S(1)}) custom-call(bf16[800,1600]{1,0:T(8,128)(2,1)S(1)} %copy-done.1, f32[768,128]{1,0:T(8,128)S(1)} %collective-permute-done.9.refs_0_, f32[768,128]{1,0:T(8,128)S(1)} %collective-permute-done.10.refs_1_, ...), custom_call_target="tpu_custom_call" | custom-call | flops 1000000000 | tf_op jit(solution)/shard_map/pallas_call | solution.py:18
  59.9 0.3 shard_map.63
  60.2 0.3 collective-permute-start.16
  60.6 1.7 %collective-permute-start.15 = (f32[768,128]{1,0:T(8,128)S(1)}, f32[768,128]{1,0:T(8,128)S(1)}, u32[]{:S(2)}, u32[]{:S(2)}) collective-permute-start(f32[768,128]{1,0:T(8,128)S(1)} %collective-permute-done.9.refs_0_), channel_id=1, source_target_pairs={{0,8},{8,16},{16,24},{24,28},{28,20},{20,12},{12,4},{4,0},{1,9},{9... | collective-permute-start | bytes 1179656 | tf_op jit(solution)/shard_map/ppermute | solution.py:380
  62.3 0.3 collective-permute-done.13.got_ref
  62.6 0.1 shard_map.64
  62.7 1.6 %collective-permute-start.14 = (f32[816,128]{1,0:T(8,128)S(1)}, f32[816,128]{1,0:T(8,128)S(1)}, u32[]{:S(2)}, u32[]{:S(2)}) collective-permute-start(f32[816,128]{1,0:T(8,128)S(1)} %get-tuple-element.87), channel_id=1, source_target_pairs={{0,2},{1,3},{2,0},{3,1},{4,6},{5,7},{6,4},{7,5},{8,10},{9,11},{10,... | collective-permute-start | bytes 1253384 | tf_op jit(solution)/shard_map/ppermute | solution.py:398
  64.3 7.5 %collective-permute-done.15.refs_0_ = f32[768,128]{1,0:T(8,128)S(1)} collective-permute-done((f32[768,128]{1,0:T(8,128)S(1)}, f32[768,128]{1,0:T(8,128)S(1)}, u32[]{:S(2)}, u32[]{:S(2)}) %collective-permute-start.15) | collective-permute-done | bytes 393248 | tf_op jit(solution)/shard_map/ppermute | solution.py:380
  71.8 0.7 collective-permute-done.16.refs_1_
  72.5 1.0 %shard_map.65 = (f32[800,128]{1,0:T(8,128)S(1)}, f32[4,896]{1,0:T(4,128)S(1)}) custom-call(bf16[800,1600]{1,0:T(8,128)(2,1)S(1)} %copy-done.1, f32[768,128]{1,0:T(8,128)S(1)} %collective-permute-done.15.refs_0_, f32[832,128]{1,0:T(8,128)S(1)} %collective-permute-done.16.refs_1_), custom_call_target="tpu_custom_call" | custom-call | flops 2000000000 | tf_op jit(solution)/shard_map/pallas_call | solution.py:18
  73.5 0.1 shard_map.66
  73.7 0.8 collective-permute-done.14.got_ref
  74.4 1.0 %collective-permute-done.17.got_ref = f32[800,128]{1,0:T(8,128)S(1)} collective-permute-done((f32[800,128]{1,0:T(8,128)S(1)}, f32[800,128]{1,0:T(8,128)S(1)}, u32[]{:S(2)}, u32[]{:S(2)}) %collective-permute-start.17) | collective-permute-done | bytes 409632 | tf_op jit(solution)/shard_map/ppermute | solution.py:395
  75.4 1.6 %collective-permute-start.21 = (f32[400,128]{1,0:T(8,128)S(1)}, f32[400,128]{1,0:T(8,128)S(1)}, u32[]{:S(2)}, u32[]{:S(2)}) collective-permute-start(f32[400,128]{1,0:T(8,128)S(1)} %get-tuple-element.105), channel_id=1, source_target_pairs={{0,2},{1,3},{2,0},{3,1},{4,6},{5,7},{6,4},{7,5},{8,10},{9,11},{10,... | collective-permute-start | bytes 614408 | tf_op jit(solution)/shard_map/ppermute | solution.py:398
  77.0 0.1 shard_map.70
  77.2 0.6 collective-permute-start.19
  77.7 1.0 %collective-permute-done.19.got_ref = f32[4,896]{1,0:T(4,128)S(1)} collective-permute-done((f32[4,896]{1,0:T(4,128)S(1)}, f32[4,896]{1,0:T(4,128)S(1)}, u32[]{:S(2)}, u32[]{:S(2)}) %collective-permute-start.19) | collective-permute-done | bytes 14368 | tf_op jit(solution)/shard_map/ppermute | solution.py:395
  78.8 0.6 collective-permute-start.20
  79.4 3.4 %collective-permute-done.20.border_got = f32[2,896]{1,0:T(2,128)S(1)} collective-permute-done((f32[2,896]{1,0:T(2,128)S(1)}, f32[2,896]{1,0:T(2,128)S(1)}, u32[]{:S(2)}, u32[]{:S(2)}) %collective-permute-start.20) | collective-permute-done | bytes 7200 | tf_op jit(solution)/shard_map/ppermute | solution.py:398
  82.9 0.1 shard_map.68.weights_ref
  83.0 0.8 shard_map.69
  83.8 0.5 collective-permute-done.22.zero_got
  84.3 1.5 %shard_map.73 = f32[800,256]{1,0:T(8,128)} custom-call(f32[800,128]{1,0:T(8,128)S(1)} %get-tuple-element.96.odd_own, f32[800,128]{1,0:T(8,128)S(1)} %get-tuple-element.97.odd_beyond, f32[800,128]{1,0:T(8,128)S(1)} %shard_map.60.two_sum, f32[800,128]{1,0:T(8,128)S(1)} %collective-permute-done.18.two_got, f32[400,128]{1,0:T(8,128)S(1)} %shard_map.72.zero_sum, ...), custom_call_target="tpu_custom_call" | custom-call | tf_op jit(solution)/shard_map/pallas_call | solution.py:18
  (29 shorter events, 0.5 us)
Async XLA Ops:
  1.0 13.6 %collective-permute-start.1 = (f32[832,128]{1,0:T(8,128)S(1)}, f32[832,128]{1,0:T(8,128)S(1)}, u32[]{:S(2)}, u32[]{:S(2)}) collective-permute-start(f32[832,128]{1,0:T(8,128)S(1)} %slice.7.refs_1_), channel_id=1, source_target_pairs={{0,8},{8,16},{16,24},{24,28},{28,20},{20,12},{12,4},{4,0},{1,9},{9... | collective-permute-start | bytes 1277960 | tf_op jit(solution)/shard_map/ppermute | solution.py:380
  4.1 12.7 %collective-permute-start.3 = (f32[832,128]{1,0:T(8,128)S(1)}, f32[832,128]{1,0:T(8,128)S(1)}, u32[]{:S(2)}, u32[]{:S(2)}) collective-permute-start(f32[832,128]{1,0:T(8,128)S(1)} %slice.7.refs_1_), channel_id=1, source_target_pairs={{8,0},{16,8},{24,16},{28,24},{20,28},{12,20},{4,12},{0,4},{9,1},{1... | collective-permute-start | bytes 1277960 | tf_op jit(solution)/shard_map/ppermute | solution.py:377
  5.1 18.0 %collective-permute-start = (f32[768,128]{1,0:T(8,128)S(1)}, f32[768,128]{1,0:T(8,128)S(1)}, u32[]{:S(2)}, u32[]{:S(2)}) collective-permute-start(f32[768,128]{1,0:T(8,128)S(1)} %slice.6.refs_0_), channel_id=1, source_target_pairs={{0,8},{8,16},{16,24},{24,28},{28,20},{20,12},{12,4},{4,0},{1,9},{9... | collective-permute-start | bytes 1179656 | tf_op jit(solution)/shard_map/ppermute | solution.py:380
  7.2 18.1 %collective-permute-start.2 = (f32[768,128]{1,0:T(8,128)S(1)}, f32[768,128]{1,0:T(8,128)S(1)}, u32[]{:S(2)}, u32[]{:S(2)}) collective-permute-start(f32[768,128]{1,0:T(8,128)S(1)} %slice.6.refs_0_), channel_id=1, source_target_pairs={{8,0},{16,8},{24,16},{28,24},{20,28},{12,20},{4,12},{0,4},{9,1},{1... | collective-permute-start | bytes 1179656 | tf_op jit(solution)/shard_map/ppermute | solution.py:377
  14.7 17.6 %collective-permute-start.6 = (f32[832,128]{1,0:T(8,128)S(1)}, f32[832,128]{1,0:T(8,128)S(1)}, u32[]{:S(2)}, u32[]{:S(2)}) collective-permute-start(f32[832,128]{1,0:T(8,128)S(1)} %collective-permute-done.1.refs_1_), channel_id=1, source_target_pairs={{0,8},{8,16},{16,24},{24,28},{28,20},{20,12},{12,4},{4,0},{1,9},{9... | collective-permute-start | bytes 1277960 | tf_op jit(solution)/shard_map/ppermute | solution.py:380
  16.9 17.6 %collective-permute-start.7 = (f32[832,128]{1,0:T(8,128)S(1)}, f32[832,128]{1,0:T(8,128)S(1)}, u32[]{:S(2)}, u32[]{:S(2)}) collective-permute-start(f32[832,128]{1,0:T(8,128)S(1)} %collective-permute-done.3.refs_3_), channel_id=1, source_target_pairs={{8,0},{16,8},{24,16},{28,24},{20,28},{12,20},{4,12},{0,4},{9,1},{1... | collective-permute-start | bytes 1277960 | tf_op jit(solution)/shard_map/ppermute | solution.py:377
  16.9 1.8 %copy-start = (bf16[800,1600]{1,0:T(8,128)(2,1)S(1)}, bf16[800,1600]{1,0:T(8,128)(2,1)}, u32[]{:S(2)}) copy-start(bf16[800,1600]{1,0:T(8,128)(2,1)} %relation_ref.13) | copy-start | bytes 7680004
  23.1 17.6 %collective-permute-start.4 = (f32[768,128]{1,0:T(8,128)S(1)}, f32[768,128]{1,0:T(8,128)S(1)}, u32[]{:S(2)}, u32[]{:S(2)}) collective-permute-start(f32[768,128]{1,0:T(8,128)S(1)} %collective-permute-done.refs_0_), channel_id=1, source_target_pairs={{0,8},{8,16},{16,24},{24,28},{28,20},{20,12},{12,4},{4,0},{1,9},{9... | collective-permute-start | bytes 1179656 | tf_op jit(solution)/shard_map/ppermute | solution.py:380
  25.3 17.6 %collective-permute-start.5 = (f32[768,128]{1,0:T(8,128)S(1)}, f32[768,128]{1,0:T(8,128)S(1)}, u32[]{:S(2)}, u32[]{:S(2)}) collective-permute-start(f32[768,128]{1,0:T(8,128)S(1)} %collective-permute-done.2.refs_2_), channel_id=1, source_target_pairs={{8,0},{16,8},{24,16},{28,24},{20,28},{12,20},{4,12},{0,4},{9,1},{1... | collective-permute-start | bytes 1179656 | tf_op jit(solution)/shard_map/ppermute | solution.py:377
  32.2 20.3 %collective-permute-start.11 = (f32[832,128]{1,0:T(8,128)S(1)}, f32[832,128]{1,0:T(8,128)S(1)}, u32[]{:S(2)}, u32[]{:S(2)}) collective-permute-start(f32[832,128]{1,0:T(8,128)S(1)} %collective-permute-done.6.refs_0_), channel_id=1, source_target_pairs={{0,8},{8,16},{16,24},{24,28},{28,20},{20,12},{12,4},{4,0},{1,9},{9... | collective-permute-start | bytes 1277960 | tf_op jit(solution)/shard_map/ppermute | solution.py:380
  34.4 18.2 %collective-permute-start.12 = (f32[832,128]{1,0:T(8,128)S(1)}, f32[832,128]{1,0:T(8,128)S(1)}, u32[]{:S(2)}, u32[]{:S(2)}) collective-permute-start(f32[832,128]{1,0:T(8,128)S(1)} %collective-permute-done.7.refs_1_), channel_id=1, source_target_pairs={{8,0},{16,8},{24,16},{28,24},{20,28},{12,20},{4,12},{0,4},{9,1},{1... | collective-permute-start | bytes 1277960 | tf_op jit(solution)/shard_map/ppermute | solution.py:377
  35.4 10.0 %copy-start.1 = (bf16[800,1600]{1,0:T(8,128)(2,1)S(1)}, bf16[800,1600]{1,0:T(8,128)(2,1)}, u32[]{:S(2)}) copy-start(bf16[800,1600]{1,0:T(8,128)(2,1)} %relation_ref.13) | copy-start | bytes 7680004
  43.9 8.6 %collective-permute-start.8 = (f32[800,128]{1,0:T(8,128)S(1)}, f32[800,128]{1,0:T(8,128)S(1)}, u32[]{:S(2)}, u32[]{:S(2)}) collective-permute-start(f32[800,128]{1,0:T(8,128)S(1)} %get-tuple-element.65), channel_id=1, source_target_pairs={{0,2},{1,3},{2,0},{3,1},{4,6},{5,7},{6,4},{7,5},{8,10},{9,11},{10,... | collective-permute-start | bytes 1228808 | tf_op jit(solution)/shard_map/ppermute | solution.py:398
  47.2 10.1 %collective-permute-start.9 = (f32[768,128]{1,0:T(8,128)S(1)}, f32[768,128]{1,0:T(8,128)S(1)}, u32[]{:S(2)}, u32[]{:S(2)}) collective-permute-start(f32[768,128]{1,0:T(8,128)S(1)} %collective-permute-done.4.refs_0_), channel_id=1, source_target_pairs={{0,8},{8,16},{16,24},{24,28},{28,20},{20,12},{12,4},{4,0},{1,9},{9... | collective-permute-start | bytes 1179656 | tf_op jit(solution)/shard_map/ppermute | solution.py:380
  48.9 10.1 %collective-permute-start.10 = (f32[768,128]{1,0:T(8,128)S(1)}, f32[768,128]{1,0:T(8,128)S(1)}, u32[]{:S(2)}, u32[]{:S(2)}) collective-permute-start(f32[768,128]{1,0:T(8,128)S(1)} %collective-permute-done.5.refs_1_), channel_id=1, source_target_pairs={{8,0},{16,8},{24,16},{28,24},{20,28},{12,20},{4,12},{0,4},{9,1},{1... | collective-permute-start | bytes 1179656 | tf_op jit(solution)/shard_map/ppermute | solution.py:377
  60.2 2.4 %collective-permute-start.13 = (f32[1632,128]{1,0:T(8,128)S(1)}, f32[1632,128]{1,0:T(8,128)S(1)}, u32[]{:S(2)}, u32[]{:S(2)}) collective-permute-start(f32[1632,128]{1,0:T(8,128)S(1)} %get-tuple-element.85), channel_id=1, source_target_pairs={{0,1},{1,0},{2,3},{3,2},{4,5},{5,4},{6,7},{7,6},{8,9},{9,8},{10,11... | collective-permute-start | bytes 2506760 | tf_op jit(solution)/shard_map/ppermute | solution.py:395
  60.2 12.2 %collective-permute-start.16 = (f32[832,128]{1,0:T(8,128)S(1)}, f32[832,128]{1,0:T(8,128)S(1)}, u32[]{:S(2)}, u32[]{:S(2)}) collective-permute-start(f32[832,128]{1,0:T(8,128)S(1)} %collective-permute-done.12.refs_1_), channel_id=1, source_target_pairs={{8,0},{16,8},{24,16},{28,24},{20,28},{12,20},{4,12},{0,4},{9,1},{1... | collective-permute-start | bytes 1277960 | tf_op jit(solution)/shard_map/ppermute | solution.py:377
  60.6 11.2 %collective-permute-start.15 = (f32[768,128]{1,0:T(8,128)S(1)}, f32[768,128]{1,0:T(8,128)S(1)}, u32[]{:S(2)}, u32[]{:S(2)}) collective-permute-start(f32[768,128]{1,0:T(8,128)S(1)} %collective-permute-done.9.refs_0_), channel_id=1, source_target_pairs={{0,8},{8,16},{16,24},{24,28},{28,20},{20,12},{12,4},{4,0},{1,9},{9... | collective-permute-start | bytes 1179656 | tf_op jit(solution)/shard_map/ppermute | solution.py:380
  62.7 11.7 %collective-permute-start.14 = (f32[816,128]{1,0:T(8,128)S(1)}, f32[816,128]{1,0:T(8,128)S(1)}, u32[]{:S(2)}, u32[]{:S(2)}) collective-permute-start(f32[816,128]{1,0:T(8,128)S(1)} %get-tuple-element.87), channel_id=1, source_target_pairs={{0,2},{1,3},{2,0},{3,1},{4,6},{5,7},{6,4},{7,5},{8,10},{9,11},{10,... | collective-permute-start | bytes 1253384 | tf_op jit(solution)/shard_map/ppermute | solution.py:398
  71.8 11.1 %copy-start.2 = (f32[1024]{0:T(1024)S(1)}, f32[1024]{0:T(1024)}, u32[]{:S(2)}) copy-start(f32[1024]{0:T(1024)} %one_ref.1) | copy-start | bytes 12292
  71.8 11.1 %copy-start.3 = (f32[1024]{0:T(1024)S(1)}, f32[1024]{0:T(1024)}, u32[]{:S(2)}) copy-start(f32[1024]{0:T(1024)} %two_ref.1) | copy-start | bytes 12292
  71.8 11.1 %copy-start.4 = (f32[1024]{0:T(1024)S(1)}, f32[1024]{0:T(1024)}, u32[]{:S(2)}) copy-start(f32[1024]{0:T(1024)} %scale_ref.1) | copy-start | bytes 12292
  73.6 1.8 %collective-permute-start.17 = (f32[800,128]{1,0:T(8,128)S(1)}, f32[800,128]{1,0:T(8,128)S(1)}, u32[]{:S(2)}, u32[]{:S(2)}) collective-permute-start(f32[800,128]{1,0:T(8,128)S(1)} %get-tuple-element.93), channel_id=1, source_target_pairs={{0,1},{1,0},{2,3},{3,2},{4,5},{5,4},{6,7},{7,6},{8,9},{9,8},{10,11... | collective-permute-start | bytes 1228808 | tf_op jit(solution)/shard_map/ppermute | solution.py:395
  75.4 7.3 %collective-permute-start.21 = (f32[400,128]{1,0:T(8,128)S(1)}, f32[400,128]{1,0:T(8,128)S(1)}, u32[]{:S(2)}, u32[]{:S(2)}) collective-permute-start(f32[400,128]{1,0:T(8,128)S(1)} %get-tuple-element.105), channel_id=1, source_target_pairs={{0,2},{1,3},{2,0},{3,1},{4,6},{5,7},{6,4},{7,5},{8,10},{9,11},{10,... | collective-permute-start | bytes 614408 | tf_op jit(solution)/shard_map/ppermute | solution.py:398
  77.0 6.8 %collective-permute-start.18 = (f32[800,128]{1,0:T(8,128)S(1)}, f32[800,128]{1,0:T(8,128)S(1)}, u32[]{:S(2)}, u32[]{:S(2)}) collective-permute-start(f32[800,128]{1,0:T(8,128)S(1)} %shard_map.60.two_sum), channel_id=1, source_target_pairs={{0,1},{1,0},{2,3},{3,2},{4,5},{5,4},{6,7},{7,6},{8,9},{9,8},{10,11... | collective-permute-start | bytes 1228808 | tf_op jit(solution)/shard_map/ppermute | solution.py:395
  77.2 1.6 %collective-permute-start.19 = (f32[4,896]{1,0:T(4,128)S(1)}, f32[4,896]{1,0:T(4,128)S(1)}, u32[]{:S(2)}, u32[]{:S(2)}) collective-permute-start(f32[4,896]{1,0:T(4,128)S(1)} %get-tuple-element.102), channel_id=1, source_target_pairs={{0,1},{1,0},{2,3},{3,2},{4,5},{5,4},{6,7},{7,6},{8,9},{9,8},{10,11... | collective-permute-start | bytes 43016 | tf_op jit(solution)/shard_map/ppermute | solution.py:395
  78.8 4.0 %collective-permute-start.20 = (f32[2,896]{1,0:T(2,128)S(1)}, f32[2,896]{1,0:T(2,128)S(1)}, u32[]{:S(2)}, u32[]{:S(2)}) collective-permute-start(f32[2,896]{1,0:T(2,128)S(1)} %get-tuple-element.103), channel_id=1, source_target_pairs={{0,2},{1,3},{2,0},{3,1},{4,6},{5,7},{6,4},{7,5},{8,10},{9,11},{10,... | collective-permute-start | bytes 21512 | tf_op jit(solution)/shard_map/ppermute | solution.py:398
  82.8 1.5 %collective-permute-start.22 = (f32[400,128]{1,0:T(8,128)S(1)}, f32[400,128]{1,0:T(8,128)S(1)}, u32[]{:S(2)}, u32[]{:S(2)}) collective-permute-start(f32[400,128]{1,0:T(8,128)S(1)} %shard_map.72.zero_sum), channel_id=1, source_target_pairs={{0,1},{1,0},{2,3},{3,2},{4,5},{5,4},{6,7},{7,6},{8,9},{9,8},{10,11... | collective-permute-start | bytes 614408 | tf_op jit(solution)/shard_map/ppermute | solution.py:395

commit v6 on v5

--- a/solution.py
+++ b/solution.py
@@ -14,11 +14,12 @@
 WHOLE = pl.BlockSpec(memory_space=pltpu.VMEM)
 
 
-def call(kernel, shapes, operands, scratch=(), flops=0, into=WHOLE):
+def call(kernel, shapes, operands, scratch=(), flops=0, into=WHOLE, last=0):
     return pl.pallas_call(
         kernel,
         out_shape=[jax.ShapeDtypeStruct(shape, jnp.float32) for shape in shapes],
-        in_specs=[WHOLE] * len(operands),
+        in_specs=[WHOLE] * (len(operands) - last) + [into] * last,
+        input_output_aliases={len(operands) - last + n: n for n in range(last)},
         out_specs=[into] * len(shapes),
         scratch_shapes=scratch,
         compiler_params=pltpu.CompilerParams(vmem_limit_bytes=VMEM_LIMIT),
@@ -160,7 +161,7 @@
             send_ref[here] = message_ref[near]
 
 
-def halves_kernel(spot_of, near, near_ref, far_ref, send_ref, keep_ref):
+def halves_kernel(spot_of, near, near_ref, far_ref, send_ours, send_theirs, keep_ref):
     spot = spot_of()
     rows = near_ref.shape[0] // 2
     core = spot.tm % 2
@@ -169,16 +170,25 @@
 
         @pl.when(mine == ours)
         def _():
-            for n, ref in enumerate((near_ref, far_ref) if ours else (far_ref, near_ref)):
-                here = pl.ds(n * rows, rows)
-                send_ref[here] = ref[pl.ds(pl.multiple_of((1 - core) * rows, 8), rows)]
-                keep_ref[here] = ref[pl.ds(pl.multiple_of(core * rows, 8), rows)]
-
-
-def half_sums_kernel(keep_ref, got_ref, send_ref, mine_ref):
-    rows = mine_ref.shape[0]
-    mine_ref[...] = keep_ref[:rows] + got_ref[:rows]
-    send_ref[...] = keep_ref[rows:] + got_ref[rows:]
+            pairs = ((near_ref, send_ours), (far_ref, send_theirs))
+            if not ours:
+                pairs = ((far_ref, send_ours), (near_ref, send_theirs))
+            for n, (ref, send_ref) in enumerate(pairs):
+                send_ref[...] = ref[pl.ds(pl.multiple_of((1 - core) * rows, 8), rows)]
+                keep_ref[pl.ds(n * rows, rows)] = ref[pl.ds(pl.multiple_of(core * rows, 8), rows)]
+
+
+def half_sums_kernel(keep_ref, got_ours, got_theirs, first_ref, second_ref, mine_ref):
+    rows, piece = mine_ref.shape[0], first_ref.shape[0]
+    mine_ref[...] = keep_ref[:rows] + got_ours[...]
+    first_ref[...] = keep_ref[rows : rows + piece] + got_theirs[:piece]
+    second_ref[...] = keep_ref[rows + piece :] + got_theirs[piece:]
+
+
+def pieces_sum_kernel(one_ref, first_ref, second_ref, out_ref):
+    piece = first_ref.shape[0]
+    out_ref[:piece] = one_ref[:piece] + first_ref[...]
+    out_ref[piece:] = one_ref[piece:] + second_ref[...]
 
 
 def chip_pair_kernel(spot_of, near, near_ref, far_ref, send_ref, keep_ref):
@@ -227,18 +237,24 @@
     out_ref[...] = one_ref[...] + other_ref[...]
 
 
-def part_sums_kernel(spot_of, fars, keep_ref, got_ref, send_ref, mine_ref):
+def part_sums_kernel(spot_of, fars, keep_ref, *refs):
     spot = spot_of()
     owner = jnp.where(spot.keeps(fars[0]) == 1, spot.owner_of(fars[0]), spot.owner_of(fars[1]))
     mine = jnp.where(owner // 2 == spot.tm // 2, 0, 1)
-    rows = mine_ref.shape[0]
+    rows = refs[-1].shape[0]
     for n in range(2):
 
         @pl.when(mine == n)
         def _():
             here, there = slice(n * rows, (n + 1) * rows), slice((1 - n) * rows, (2 - n) * rows)
-            send_ref[...] = keep_ref[there] + got_ref[there]
-            mine_ref[...] = keep_ref[here] + got_ref[here]
+            size = refs[0].shape[0]
+            for out_ref, block in ((refs[-2], there), (refs[-1], here)):
+                for m, got_ref in enumerate(refs[:-2]):
+                    first, end = max(block.start, m * size), min(block.stop, (m + 1) * size)
+                    if first < end:
+                        out_ref[first - block.start : end - block.start] = (
+                            keep_ref[first:end] + got_ref[first - m * size : end - m * size]
+                        )
 
 
 def row_weights(weights, far, lanes):
@@ -306,49 +322,49 @@
 
 def last_kernel(
     spot_of,
+    same,
     odd_own,
     odd_beyond,
     two_sum,
     two_got,
-    zero_sum,
-    zero_got,
+    zero_half,
     border_mine,
     border_got,
     weights_ref,
-    out_any,
-    even_ref,
-    sides_ref,
-    made_ref,
-    sems,
+    *refs,
 ):
+    out_any, even_ref, sides_ref, made_ref, sems = refs[-5:]
     spot = spot_of()
     odd = odd_column(spot)
-    rows = out_any.shape[0]
+    rows = out_any.shape[0] // 2
+    core = spot.tm % 2
+    first = pl.multiple_of((core if same else 1 - core) * rows, 8)
+    here = pl.ds(first, rows)
     is_two = (spot.owner_of(2) == spot.tm) | (spot.owner_of(-2) == spot.tm)
 
     @pl.when(is_two)
     def _():
-        even_ref[...] = two_sum[...] + two_got[...]
+        even_ref[...] = two_sum[here] + two_got[here]
 
     @pl.when(jnp.logical_not(is_two))
     def _():
-        half, core = rows // 2, spot.tm % 2
-        even_ref[pl.ds(pl.multiple_of(core * half, 8), half)] = zero_sum[...]
-        even_ref[pl.ds(pl.multiple_of((1 - core) * half, 8), half)] = zero_got[...]
+        even_ref[...] = zero_half[...]
 
     weights = column_weights(spot, weights_ref, 1 - odd)
     others = column_weights(spot, weights_ref, odd)
     sides_ref[...] = beside(weights, border_mine[...] + border_got[...], odd == 1)
-    step = rows // 5
+    pieces = 5
+    step = rows // pieces
     copies = []
-    for n in range(5):
-        here = slice(n * step, (n + 1) * step)
-        own, beyond = shares(weights, others, even_ref[here], odd == 1)
-        made_ref[1 - odd, here] = own + sides_ref[here] + odd_beyond[here]
-        made_ref[odd, here] = odd_own[here] + beyond
+    for n in range(pieces):
+        there = pl.ds(pl.multiple_of(first + n * step, 8), step)
+        own, beyond = shares(weights, others, even_ref[n * step : (n + 1) * step], odd == 1)
+        made_ref[1 - odd, n * step : (n + 1) * step] = own + sides_ref[there] + odd_beyond[there]
+        made_ref[odd, n * step : (n + 1) * step] = odd_own[there] + beyond
         for column in range(2):
-            into = out_any.at[here, column * WIDTH : (column + 1) * WIDTH]
-            copies.append(pltpu.make_async_copy(made_ref.at[column, here], into, sems.at[len(copies)]))
+            into = out_any.at[there, column * WIDTH : (column + 1) * WIDTH]
+            made = made_ref.at[column, n * step : (n + 1) * step]
+            copies.append(pltpu.make_async_copy(made, into, sems.at[len(copies)]))
             copies[-1].start()
     for copy in copies:
         copy.wait()
@@ -452,11 +468,11 @@
     odd_send, odd_mine = call(
         functools.partial(part_sums_kernel, spot_of, odd_fars),
         [(long, WIDTH)] * 2,
-        (keep, over_cores(send)),
+        (keep, *[over_cores(send[i * (2 * long // 3) : (i + 1) * (2 * long // 3)]) for i in range(3)]),
         flops=KERNEL_FLOPS // 2,
     )
     odd_got = over_y(odd_send)
-    multiplied(half, after=(odd_mine,), cost=20)
+    multiplied(half, after=(odd_mine,), cost=1)
     even_fars = (0, half, 2, -2)
     border_send, border_keep = call(
         functools.partial(borders_kernel, spot_of, even_fars),
@@ -472,45 +488,49 @@
         flops=KERNEL_FLOPS // 10,
     )
     border_got = over_y(border_send)
-    send, keep = call(
+    send_ours, send_theirs, keep = call(
         functools.partial(halves_kernel, spot_of, 0),
-        [(rows, WIDTH)] * 2,
+        [(rows // 2, WIDTH)] * 2 + [(rows, WIDTH)],
         [products[far][0] for far in (0, half)],
         flops=KERNEL_FLOPS // 2,
     )
-    zero_send, zero_mine = call(
+    first, second, zero_mine = call(
         half_sums_kernel,
-        [(rows // 2, WIDTH)] * 2,
-        (tied(keep, odd_got), over_cores(send)),
+        [(rows // 4, WIDTH)] * 2 + [(rows // 2, WIDTH)],
+        (keep, over_cores(send_ours), over_cores(send_theirs)),
         flops=KERNEL_FLOPS // 10,
     )
-    zero_sum = call(
-        sum_kernel,
-        [(rows // 2, WIDTH)],
-        (tied(zero_mine, border_got), over_y(zero_send)),
-        flops=KERNEL_FLOPS // 10,
-    )[0]
-    zero_got = over_cores(zero_sum)
     weights = call(weights_kernel, [(8, phi_one.shape[0])], (phi_one, phi_two, innov_scale))[0]
     odd_own, odd_beyond = call(
         functools.partial(odd_shares_kernel, spot_of),
         [(rows, WIDTH)] * 2,
-        (odd_mine, tied(odd_got, zero_mine), weights),
+        (odd_mine, odd_got, weights),
         [pltpu.VMEM((wide, WIDTH), jnp.float32)],
         flops=KERNEL_FLOPS,
     )
-    return call(
-        functools.partial(last_kernel, spot_of),
-        [(rows, share * WIDTH)],
-        (odd_own, odd_beyond, two_sum, two_got, zero_sum, zero_got, border_mine, border_got, weights),
-        [
-            pltpu.VMEM((rows, WIDTH), jnp.float32),
-            pltpu.VMEM((wide, WIDTH), jnp.float32),
-            pltpu.VMEM((2, rows, WIDTH), jnp.float32),
-            pltpu.SemaphoreType.DMA((10,)),
-        ],
-        into=pl.BlockSpec(memory_space=pl.ANY),
+    zero_sum = call(
+        pieces_sum_kernel,
+        [(rows // 2, WIDTH)],
+        (tied(zero_mine, border_got, odd_own), over_y(first), over_y(second)),
+        flops=KERNEL_FLOPS // 10,
     )[0]
+    zero_got = over_cores(zero_sum)
+    applied = ()
+    for same, zero_half in ((True, zero_sum), (False, zero_got)):
+        applied = call(
+            functools.partial(last_kernel, spot_of, same),
+            [(rows, share * WIDTH)],
+            (odd_own, odd_beyond, two_sum, two_got, zero_half, border_mine, border_got, weights, *applied),
+            [
+                pltpu.VMEM((rows // 2, WIDTH), jnp.float32),
+                pltpu.VMEM((wide, WIDTH), jnp.float32),
+                pltpu.VMEM((2, rows // 2, WIDTH), jnp.float32),
+                pltpu.SemaphoreType.DMA((10,)),
+            ],
+            into=pl.BlockSpec(memory_space=pl.ANY),
+            last=len(applied),
+        )
+    return applied[0]
 
 
 def extended(cells, sides, width):
@@ -570,7 +590,7 @@
 
 def on_device(relation, effects, phi_one, phi_two, innov_scale):
     gens, tms = lax.axis_size("gen"), lax.axis_size("tm")
-    fits = gens == 8 and tms == 4 and effects.shape[1] == WIDTH and effects.shape[0] % 64 == 0 and relation.shape[0] % 80 == 0
+    fits = gens == 8 and tms == 4 and effects.shape[1] == WIDTH and effects.shape[0] % 64 == 0 and relation.shape[0] % 160 == 0
     way = by_ring if fits else by_gather
     return way(relation, effects, phi_one, phi_two, innov_scale)
 

time: 86.1 us -> 85.2 us (0.990)
  waiting for transfers between devices: 49.1 us -> 44.1 us
  starting transfers between devices: 21.9 us -> 24.8 us
  Pallas kernels: 10.9 us -> 11.9 us
    ppermute x4 -> x5, waiting for transfers between devices: 7.36 us -> 1.36 us  [over_y(): return lax.ppermute(x, 'tm', [(t, t ^ 2) for t in range(tms)])]
    ppermute x4 -> x5, starting transfers between devices: 5.32 us -> 7.65 us  [over_y(): return lax.ppermute(x, 'tm', [(t, t ^ 2) for t in range(tms)])]
    ppermute x7, waiting for transfers between devices: 34.4 us -> 32.3 us  [behind_of(): return lax.ppermute(x, 'gen', forward)]
    ppermute x7, waiting for transfers between devices: 4.53 us -> 6.4 us  [ahead_of(): return lax.ppermute(x, 'gen', backward)]
    ppermute x5 -> x8, waiting for transfers between devices: 2.79 us -> 4.08 us  [over_cores(): return lax.ppermute(x, 'tm', swap)]
    pallas_call x19 -> x20, Pallas kernels: 10.9 us -> 11.9 us  [call(): pl.pallas_call(kernel, out_shape=[jax.ShapeDtypeStruct(shape, jnp.float32...]
  transfers between devices with their start and end apart: 23 -> 27, of which waited for: 16 -> 16; matrix products, arithmetic and copies ran while one was open for 1% -> 1% of each run, Pallas kernels for 9% -> 13%
where the time goes in v6:
time: 85.2 us; the launch traced here: 85 us
  waiting for transfers between devices  44.1 us (52%)
  starting transfers between devices  24.8 us (29%)
  Pallas kernels  11.9 us (14%)
  local copies, waits for them, and re-layouts  3.89 us (5%)
    ppermute x7, waiting for transfers between devices, behind_of(): return lax.ppermute(x, 'gen', forward)  32.3 us
    ppermute x7, starting transfers between devices, behind_of(): return lax.ppermute(x, 'gen', forward)  15 us
    pallas_call x20, Pallas kernels, call(): pl.pallas_call(kernel, out_shape=[jax.ShapeDtypeStruct(shape, jnp.float32...  11.9 us
    ppermute x5, starting transfers between devices, over_y(): return lax.ppermute(x, 'tm', [(t, t ^ 2) for t in range(tms)])  7.65 us
    ppermute x7, waiting for transfers between devices, ahead_of(): return lax.ppermute(x, 'gen', backward)  6.4 us
    ppermute x8, waiting for transfers between devices, over_cores(): return lax.ppermute(x, 'tm', swap)  4.08 us
    slice x2, local copies, waits for them, and re-layouts, by_ring(): top, bottom = (effects[:cut], effects[cut:])  2.06 us
    unnamed x10, local copies, waits for them, and re-layouts  1.78 us
  transfers between devices with their start and end apart: 27, of which 16 were waited for; matrix products, arithmetic and copies ran while one was open for 1% of the time, Pallas kernels for 13%

profile of v6, /device:TPU:0, one launch (start us, length us, event | category | flops | bytes accessed | tf_op | source)
XLA Modules:
  0.0 85.0 jit_solution(13727030992595834392)
XLA Ops:
  0.0 1.0 %slice.16.refs_1_ = f32[832,128]{1,0:T(8,128)S(1)} slice(f32[1600,128]{1,0:T(8,128)} %param.6), slice={[768:1600], [0:128]} | slice | bytes 851968 | tf_op jit(solution)/shard_map/slice | solution.py:435
  1.0 3.1 %collective-permute-start.1 = (f32[832,128]{1,0:T(8,128)S(1)}, f32[832,128]{1,0:T(8,128)S(1)}, u32[]{:S(2)}, u32[]{:S(2)}) collective-permute-start(f32[832,128]{1,0:T(8,128)S(1)} %slice.16.refs_1_), channel_id=1, source_target_pairs={{0,8},{8,16},{16,24},{24,28},{28,20},{20,12},{12,4},{4,0},{1,9},{9... | collective-permute-start | bytes 1277960 | tf_op jit(solution)/shard_map/ppermute | solution.py:396
  4.1 1.0 %slice.15.refs_0_ = f32[768,128]{1,0:T(8,128)S(1)} slice(f32[1600,128]{1,0:T(8,128)} %param.6), slice={[0:768], [0:128]} | slice | bytes 786432 | tf_op jit(solution)/shard_map/slice | solution.py:435
  5.1 2.1 %collective-permute-start = (f32[768,128]{1,0:T(8,128)S(1)}, f32[768,128]{1,0:T(8,128)S(1)}, u32[]{:S(2)}, u32[]{:S(2)}) collective-permute-start(f32[768,128]{1,0:T(8,128)S(1)} %slice.15.refs_0_), channel_id=1, source_target_pairs={{0,8},{8,16},{16,24},{24,28},{28,20},{20,12},{12,4},{4,0},{1,9},{9... | collective-permute-start | bytes 1179656 | tf_op jit(solution)/shard_map/ppermute | solution.py:396
  7.2 7.5 %collective-permute-done.1.refs_1_ = f32[832,128]{1,0:T(8,128)S(1)} collective-permute-done((f32[832,128]{1,0:T(8,128)S(1)}, f32[832,128]{1,0:T(8,128)S(1)}, u32[]{:S(2)}, u32[]{:S(2)}) %collective-permute-start.1) | collective-permute-done | bytes 426016 | tf_op jit(solution)/shard_map/ppermute | solution.py:396
  14.7 2.1 %collective-permute-start.6 = (f32[832,128]{1,0:T(8,128)S(1)}, f32[832,128]{1,0:T(8,128)S(1)}, u32[]{:S(2)}, u32[]{:S(2)}) collective-permute-start(f32[832,128]{1,0:T(8,128)S(1)} %collective-permute-done.1.refs_1_), channel_id=1, source_target_pairs={{0,8},{8,16},{16,24},{24,28},{28,20},{20,12},{12,4},{4,0},{1,9},{9... | collective-permute-start | bytes 1277960 | tf_op jit(solution)/shard_map/ppermute | solution.py:396
  16.9 1.8 %copy-done = bf16[800,1600]{1,0:T(8,128)(2,1)S(1)} copy-done((bf16[800,1600]{1,0:T(8,128)(2,1)S(1)}, bf16[800,1600]{1,0:T(8,128)(2,1)}, u32[]{:S(2)}) %copy-start) | copy-done | bytes 2560024
  18.6 1.0 %shard_map.56 = (f32[800,128]{1,0:T(8,128)S(1)}, f32[4,896]{1,0:T(4,128)S(1)}) custom-call(bf16[800,1600]{1,0:T(8,128)(2,1)S(1)} %copy-done, f32[768,128]{1,0:T(8,128)S(1)} %slice.15.refs_0_, f32[832,128]{1,0:T(8,128)S(1)} %slice.16.refs_1_), custom_call_target="tpu_custom_call" | custom-call | flops 100000000 | tf_op jit(solution)/shard_map/pallas_call | solution.py:18
  19.6 3.5 %collective-permute-done.refs_0_ = f32[768,128]{1,0:T(8,128)S(1)} collective-permute-done((f32[768,128]{1,0:T(8,128)S(1)}, f32[768,128]{1,0:T(8,128)S(1)}, u32[]{:S(2)}, u32[]{:S(2)}) %collective-permute-start) | collective-permute-done | bytes 393248 | tf_op jit(solution)/shard_map/ppermute | solution.py:396
  23.1 2.1 %collective-permute-start.4 = (f32[768,128]{1,0:T(8,128)S(1)}, f32[768,128]{1,0:T(8,128)S(1)}, u32[]{:S(2)}, u32[]{:S(2)}) collective-permute-start(f32[768,128]{1,0:T(8,128)S(1)} %collective-permute-done.refs_0_), channel_id=1, source_target_pairs={{0,8},{8,16},{16,24},{24,28},{28,20},{20,12},{12,4},{4,0},{1,9},{9... | collective-permute-start | bytes 1179656 | tf_op jit(solution)/shard_map/ppermute | solution.py:396
  25.3 6.9 %collective-permute-done.6.refs_0_ = f32[832,128]{1,0:T(8,128)S(1)} collective-permute-done((f32[832,128]{1,0:T(8,128)S(1)}, f32[832,128]{1,0:T(8,128)S(1)}, u32[]{:S(2)}, u32[]{:S(2)}) %collective-permute-start.6) | collective-permute-done | bytes 426016 | tf_op jit(solution)/shard_map/ppermute | solution.py:396
  32.2 2.1 %collective-permute-start.11 = (f32[832,128]{1,0:T(8,128)S(1)}, f32[832,128]{1,0:T(8,128)S(1)}, u32[]{:S(2)}, u32[]{:S(2)}) collective-permute-start(f32[832,128]{1,0:T(8,128)S(1)} %collective-permute-done.6.refs_0_), channel_id=1, source_target_pairs={{0,8},{8,16},{16,24},{24,28},{28,20},{20,12},{12,4},{4,0},{1,9},{9... | collective-permute-start | bytes 1277960 | tf_op jit(solution)/shard_map/ppermute | solution.py:396
  34.4 1.0 %shard_map.57 = (f32[800,128]{1,0:T(8,128)S(1)}, f32[800,128]{1,0:T(8,128)S(1)}) custom-call(bf16[800,1600]{1,0:T(8,128)(2,1)S(1)} %copy-done, f32[832,128]{1,0:T(8,128)S(1)} %collective-permute-done.6.refs_0_, f32[832,128]{1,0:T(8,128)S(1)} %collective-permute-done.7.refs_1_), custom_call_target="tpu_custom_call" | custom-call | flops 100000000 | tf_op jit(solution)/shard_map/pallas_call | solution.py:18
  35.5 5.2 %collective-permute-done.4.refs_0_ = f32[768,128]{1,0:T(8,128)S(1)} collective-permute-done((f32[768,128]{1,0:T(8,128)S(1)}, f32[768,128]{1,0:T(8,128)S(1)}, u32[]{:S(2)}, u32[]{:S(2)}) %collective-permute-start.4) | collective-permute-done | bytes 393248 | tf_op jit(solution)/shard_map/ppermute | solution.py:396
  40.7 2.2 %collective-permute-done.5.refs_1_ = f32[768,128]{1,0:T(8,128)S(1)} collective-permute-done((f32[768,128]{1,0:T(8,128)S(1)}, f32[768,128]{1,0:T(8,128)S(1)}, u32[]{:S(2)}, u32[]{:S(2)}) %collective-permute-start.5) | collective-permute-done | bytes 393248 | tf_op jit(solution)/shard_map/ppermute | solution.py:393
  42.8 0.9 %shard_map.58 = (f32[800,128]{1,0:T(8,128)S(1)}, f32[4,896]{1,0:T(4,128)S(1)}, f32[800,128]{1,0:T(8,128)S(1)}, f32[4,896]{1,0:T(4,128)S(1)}) custom-call(bf16[800,1600]{1,0:T(8,128)(2,1)S(1)} %copy-done, f32[768,128]{1,0:T(8,128)S(1)} %collective-permute-done.4.refs_0_, f32[768,128]{1,0:T(8,128)S(1)} %collective-permute-done.5.refs_1_, ...), custom_call_target="tpu_custom_call" | custom-call | flops 100000000 | tf_op jit(solution)/shard_map/pallas_call | solution.py:18
  43.9 1.6 %collective-permute-start.8 = (f32[800,128]{1,0:T(8,128)S(1)}, f32[800,128]{1,0:T(8,128)S(1)}, u32[]{:S(2)}, u32[]{:S(2)}) collective-permute-start(f32[800,128]{1,0:T(8,128)S(1)} %get-tuple-element.65), channel_id=1, source_target_pairs={{0,2},{1,3},{2,0},{3,1},{4,6},{5,7},{6,4},{7,5},{8,10},{9,11},{10,... | collective-permute-start | bytes 1228808 | tf_op jit(solution)/shard_map/ppermute | solution.py:414
  45.5 1.8 %shard_map.55 = (f32[800,128]{1,0:T(8,128)S(1)}, f32[4,896]{1,0:T(4,128)S(1)}, f32[800,128]{1,0:T(8,128)S(1)}, f32[4,896]{1,0:T(4,128)S(1)}) custom-call(bf16[800,1600]{1,0:T(8,128)(2,1)S(1)} %copy-done.1, f32[768,128]{1,0:T(8,128)S(1)} %collective-permute-done.refs_0_, f32[832,128]{1,0:T(8,128)S(1)} %collective-permute-done.1.refs_1_, ...), custom_call_target="tpu_custom_call" | custom-call | flops 200000000 | tf_op jit(solution)/shard_map/pallas_call | solution.py:18
  47.2 1.6 %collective-permute-start.9 = (f32[768,128]{1,0:T(8,128)S(1)}, f32[768,128]{1,0:T(8,128)S(1)}, u32[]{:S(2)}, u32[]{:S(2)}) collective-permute-start(f32[768,128]{1,0:T(8,128)S(1)} %collective-permute-done.4.refs_0_), channel_id=1, source_target_pairs={{0,8},{8,16},{16,24},{24,28},{28,20},{20,12},{12,4},{4,0},{1,9},{9... | collective-permute-start | bytes 1179656 | tf_op jit(solution)/shard_map/ppermute | solution.py:396
  48.9 0.4 collective-permute-start.10
  49.3 8.1 %collective-permute-done.9.refs_0_ = f32[768,128]{1,0:T(8,128)S(1)} collective-permute-done((f32[768,128]{1,0:T(8,128)S(1)}, f32[768,128]{1,0:T(8,128)S(1)}, u32[]{:S(2)}, u32[]{:S(2)}) %collective-permute-start.9) | collective-permute-done | bytes 393248 | tf_op jit(solution)/shard_map/ppermute | solution.py:396
  57.4 1.8 %collective-permute-start.18 = (f32[768,128]{1,0:T(8,128)S(1)}, f32[768,128]{1,0:T(8,128)S(1)}, u32[]{:S(2)}, u32[]{:S(2)}) collective-permute-start(f32[768,128]{1,0:T(8,128)S(1)} %collective-permute-done.9.refs_0_), channel_id=1, source_target_pairs={{0,8},{8,16},{16,24},{24,28},{28,20},{20,12},{12,4},{4,0},{1,9},{9... | collective-permute-start | bytes 1179656 | tf_op jit(solution)/shard_map/ppermute | solution.py:396
  59.3 1.0 %shard_map.61 = (f32[800,128]{1,0:T(8,128)S(1)}, f32[800,128]{1,0:T(8,128)S(1)}) custom-call(bf16[800,1600]{1,0:T(8,128)(2,1)S(1)} %copy-done.1, f32[832,128]{1,0:T(8,128)S(1)} %collective-permute-done.11.refs_0_, f32[832,128]{1,0:T(8,128)S(1)} %collective-permute-done.12.refs_1_), custom_call_target="tpu_custom_call" | custom-call | flops 100000000 | tf_op jit(solution)/shard_map/pallas_call | solution.py:18
  60.3 0.9 %shard_map.62 = (f32[800,128]{1,0:T(8,128)S(1)}, f32[4,896]{1,0:T(4,128)S(1)}, f32[800,128]{1,0:T(8,128)S(1)}, f32[4,896]{1,0:T(4,128)S(1)}) custom-call(bf16[800,1600]{1,0:T(8,128)(2,1)S(1)} %copy-done.1, f32[768,128]{1,0:T(8,128)S(1)} %collective-permute-done.9.refs_0_, f32[768,128]{1,0:T(8,128)S(1)} %collective-permute-done.10.refs_1_, ...), custom_call_target="tpu_custom_call" | custom-call | flops 1000000000 | tf_op jit(solution)/shard_map/pallas_call | solution.py:18
  61.3 0.3 shard_map.63
  61.6 0.3 collective-permute-start.19
  62.0 0.5 collective-permute-start.14
  62.5 1.0 %collective-permute-done.13.refs_0_ = f32[544,128]{1,0:T(8,128)S(1)} collective-permute-done((f32[544,128]{1,0:T(8,128)S(1)}, f32[544,128]{1,0:T(8,128)S(1)}, u32[]{:S(2)}, u32[]{:S(2)}) %collective-permute-start.13) | collective-permute-done | bytes 278560 | tf_op jit(solution)/shard_map/ppermute | solution.py:411
  63.5 0.4 collective-permute-done.14.refs_1_
  63.9 0.4 collective-permute-done.15.refs_2_
  64.4 1.8 %collective-permute-start.16 = (f32[816,128]{1,0:T(8,128)S(1)}, f32[816,128]{1,0:T(8,128)S(1)}, u32[]{:S(2)}, u32[]{:S(2)}) collective-permute-start(f32[816,128]{1,0:T(8,128)S(1)} %get-tuple-element.87), channel_id=1, source_target_pairs={{0,2},{1,3},{2,0},{3,1},{4,6},{5,7},{6,4},{7,5},{8,10},{9,11},{10,... | collective-permute-start | bytes 1253384 | tf_op jit(solution)/shard_map/ppermute | solution.py:414
  66.3 1.1 %collective-permute-done.18.refs_0_ = f32[768,128]{1,0:T(8,128)S(1)} collective-permute-done((f32[768,128]{1,0:T(8,128)S(1)}, f32[768,128]{1,0:T(8,128)S(1)}, u32[]{:S(2)}, u32[]{:S(2)}) %collective-permute-start.18) | collective-permute-done | bytes 393248 | tf_op jit(solution)/shard_map/ppermute | solution.py:396
  67.4 4.1 %collective-permute-done.19.refs_1_ = f32[832,128]{1,0:T(8,128)S(1)} collective-permute-done((f32[832,128]{1,0:T(8,128)S(1)}, f32[832,128]{1,0:T(8,128)S(1)}, u32[]{:S(2)}, u32[]{:S(2)}) %collective-permute-start.19) | collective-permute-done | bytes 426016 | tf_op jit(solution)/shard_map/ppermute | solution.py:393
  71.5 1.0 %shard_map.67 = (f32[800,128]{1,0:T(8,128)S(1)}, f32[4,896]{1,0:T(4,128)S(1)}) custom-call(bf16[800,1600]{1,0:T(8,128)(2,1)S(1)} %copy-done.1, f32[768,128]{1,0:T(8,128)S(1)} %collective-permute-done.18.refs_0_, f32[832,128]{1,0:T(8,128)S(1)} %collective-permute-done.19.refs_1_), custom_call_target="tpu_custom_call" | custom-call | flops 100000000 | tf_op jit(solution)/shard_map/pallas_call | solution.py:18
  72.5 0.1 shard_map.68
  72.7 0.5 collective-permute-start.21
  73.2 0.9 %collective-permute-done.20.got_ours = f32[400,128]{1,0:T(8,128)S(1)} collective-permute-done((f32[400,128]{1,0:T(8,128)S(1)}, f32[400,128]{1,0:T(8,128)S(1)}, u32[]{:S(2)}, u32[]{:S(2)}) %collective-permute-start.20) | collective-permute-done | bytes 204832 | tf_op jit(solution)/shard_map/ppermute | solution.py:411
  74.1 0.3 collective-permute-done.21.got_theirs
  74.4 2.1 %collective-permute-start.24 = (f32[200,128]{1,0:T(8,128)S(1)}, f32[200,128]{1,0:T(8,128)S(1)}, u32[]{:S(2)}, u32[]{:S(2)}) collective-permute-start(f32[200,128]{1,0:T(8,128)S(1)} %get-tuple-element.104), channel_id=1, source_target_pairs={{0,2},{1,3},{2,0},{3,1},{4,6},{5,7},{6,4},{7,5},{8,10},{9,11},{10,... | collective-permute-start | bytes 307208 | tf_op jit(solution)/shard_map/ppermute | solution.py:414
  76.7 0.1 shard_map.70
  76.9 0.1 shard_map.65.weights_ref
  77.0 1.0 %collective-permute-done.22.got_ref = f32[4,896]{1,0:T(4,128)S(1)} collective-permute-done((f32[4,896]{1,0:T(4,128)S(1)}, f32[4,896]{1,0:T(4,128)S(1)}, u32[]{:S(2)}, u32[]{:S(2)}) %collective-permute-start.22) | collective-permute-done | bytes 14368 | tf_op jit(solution)/shard_map/ppermute | solution.py:411
  78.1 2.0 %collective-permute-start.23 = (f32[2,896]{1,0:T(2,128)S(1)}, f32[2,896]{1,0:T(2,128)S(1)}, u32[]{:S(2)}, u32[]{:S(2)}) collective-permute-start(f32[2,896]{1,0:T(2,128)S(1)} %get-tuple-element.102), channel_id=1, source_target_pairs={{0,2},{1,3},{2,0},{3,1},{4,6},{5,7},{6,4},{7,5},{8,10},{9,11},{10,... | collective-permute-start | bytes 21512 | tf_op jit(solution)/shard_map/ppermute | solution.py:414
  80.1 0.7 shard_map.66
  80.8 1.4 %collective-permute-done.23.border_got = f32[2,896]{1,0:T(2,128)S(1)} collective-permute-done((f32[2,896]{1,0:T(2,128)S(1)}, f32[2,896]{1,0:T(2,128)S(1)}, u32[]{:S(2)}, u32[]{:S(2)}) %collective-permute-start.23) | collective-permute-done | bytes 7200 | tf_op jit(solution)/shard_map/ppermute | solution.py:414
  82.3 1.3 %shard_map.73.refs_0_ = f32[800,256]{1,0:T(8,128)} custom-call(f32[800,128]{1,0:T(8,128)S(1)} %get-tuple-element.88.odd_own, f32[800,128]{1,0:T(8,128)S(1)} %get-tuple-element.89.odd_beyond, f32[800,128]{1,0:T(8,128)S(1)} %shard_map.60.two_sum, f32[800,128]{1,0:T(8,128)S(1)} %collective-permute-done.17.two_got, f32[400,128]{1,0:T(8,128)S(1)} %shard_map.72.zero_half, ...), custom_call_target="tpu_custom_call" | custom-call | tf_op jit(solution)/shard_map/pallas_call | solution.py:18
  83.6 0.1 collective-permute-done.26.zero_half
  83.8 1.2 %shard_map.74 = f32[800,256]{1,0:T(8,128)} custom-call(f32[800,128]{1,0:T(8,128)S(1)} %get-tuple-element.88.odd_own, f32[800,128]{1,0:T(8,128)S(1)} %get-tuple-element.89.odd_beyond, f32[800,128]{1,0:T(8,128)S(1)} %shard_map.60.two_sum, f32[800,128]{1,0:T(8,128)S(1)} %collective-permute-done.17.two_got, ...), custom_call_target="tpu_custom_call", output_to_operand_aliasing={{}: (8, {})} | custom-call | tf_op jit(solution)/shard_map/pallas_call | solution.py:18
  (39 shorter events, 1.1 us)
Async XLA Ops:
  1.0 13.6 %collective-permute-start.1 = (f32[832,128]{1,0:T(8,128)S(1)}, f32[832,128]{1,0:T(8,128)S(1)}, u32[]{:S(2)}, u32[]{:S(2)}) collective-permute-start(f32[832,128]{1,0:T(8,128)S(1)} %slice.16.refs_1_), channel_id=1, source_target_pairs={{0,8},{8,16},{16,24},{24,28},{28,20},{20,12},{12,4},{4,0},{1,9},{9... | collective-permute-start | bytes 1277960 | tf_op jit(solution)/shard_map/ppermute | solution.py:396
  4.1 12.7 %collective-permute-start.3 = (f32[832,128]{1,0:T(8,128)S(1)}, f32[832,128]{1,0:T(8,128)S(1)}, u32[]{:S(2)}, u32[]{:S(2)}) collective-permute-start(f32[832,128]{1,0:T(8,128)S(1)} %slice.16.refs_1_), channel_id=1, source_target_pairs={{8,0},{16,8},{24,16},{28,24},{20,28},{12,20},{4,12},{0,4},{9,1},{1... | collective-permute-start | bytes 1277960 | tf_op jit(solution)/shard_map/ppermute | solution.py:393
  5.1 18.0 %collective-permute-start = (f32[768,128]{1,0:T(8,128)S(1)}, f32[768,128]{1,0:T(8,128)S(1)}, u32[]{:S(2)}, u32[]{:S(2)}) collective-permute-start(f32[768,128]{1,0:T(8,128)S(1)} %slice.15.refs_0_), channel_id=1, source_target_pairs={{0,8},{8,16},{16,24},{24,28},{28,20},{20,12},{12,4},{4,0},{1,9},{9... | collective-permute-start | bytes 1179656 | tf_op jit(solution)/shard_map/ppermute | solution.py:396
  7.2 18.1 %collective-permute-start.2 = (f32[768,128]{1,0:T(8,128)S(1)}, f32[768,128]{1,0:T(8,128)S(1)}, u32[]{:S(2)}, u32[]{:S(2)}) collective-permute-start(f32[768,128]{1,0:T(8,128)S(1)} %slice.15.refs_0_), channel_id=1, source_target_pairs={{8,0},{16,8},{24,16},{28,24},{20,28},{12,20},{4,12},{0,4},{9,1},{1... | collective-permute-start | bytes 1179656 | tf_op jit(solution)/shard_map/ppermute | solution.py:393
  14.7 17.6 %collective-permute-start.6 = (f32[832,128]{1,0:T(8,128)S(1)}, f32[832,128]{1,0:T(8,128)S(1)}, u32[]{:S(2)}, u32[]{:S(2)}) collective-permute-start(f32[832,128]{1,0:T(8,128)S(1)} %collective-permute-done.1.refs_1_), channel_id=1, source_target_pairs={{0,8},{8,16},{16,24},{24,28},{28,20},{20,12},{12,4},{4,0},{1,9},{9... | collective-permute-start | bytes 1277960 | tf_op jit(solution)/shard_map/ppermute | solution.py:396
  16.9 17.6 %collective-permute-start.7 = (f32[832,128]{1,0:T(8,128)S(1)}, f32[832,128]{1,0:T(8,128)S(1)}, u32[]{:S(2)}, u32[]{:S(2)}) collective-permute-start(f32[832,128]{1,0:T(8,128)S(1)} %collective-permute-done.3.refs_3_), channel_id=1, source_target_pairs={{8,0},{16,8},{24,16},{28,24},{20,28},{12,20},{4,12},{0,4},{9,1},{1... | collective-permute-start | bytes 1277960 | tf_op jit(solution)/shard_map/ppermute | solution.py:393
  16.9 1.8 %copy-start = (bf16[800,1600]{1,0:T(8,128)(2,1)S(1)}, bf16[800,1600]{1,0:T(8,128)(2,1)}, u32[]{:S(2)}) copy-start(bf16[800,1600]{1,0:T(8,128)(2,1)} %relation_ref.13) | copy-start | bytes 7680004
  23.1 17.6 %collective-permute-start.4 = (f32[768,128]{1,0:T(8,128)S(1)}, f32[768,128]{1,0:T(8,128)S(1)}, u32[]{:S(2)}, u32[]{:S(2)}) collective-permute-start(f32[768,128]{1,0:T(8,128)S(1)} %collective-permute-done.refs_0_), channel_id=1, source_target_pairs={{0,8},{8,16},{16,24},{24,28},{28,20},{20,12},{12,4},{4,0},{1,9},{9... | collective-permute-start | bytes 1179656 | tf_op jit(solution)/shard_map/ppermute | solution.py:396
  25.3 17.6 %collective-permute-start.5 = (f32[768,128]{1,0:T(8,128)S(1)}, f32[768,128]{1,0:T(8,128)S(1)}, u32[]{:S(2)}, u32[]{:S(2)}) collective-permute-start(f32[768,128]{1,0:T(8,128)S(1)} %collective-permute-done.2.refs_2_), channel_id=1, source_target_pairs={{8,0},{16,8},{24,16},{28,24},{20,28},{12,20},{4,12},{0,4},{9,1},{1... | collective-permute-start | bytes 1179656 | tf_op jit(solution)/shard_map/ppermute | solution.py:393
  32.2 27.0 %collective-permute-start.11 = (f32[832,128]{1,0:T(8,128)S(1)}, f32[832,128]{1,0:T(8,128)S(1)}, u32[]{:S(2)}, u32[]{:S(2)}) collective-permute-start(f32[832,128]{1,0:T(8,128)S(1)} %collective-permute-done.6.refs_0_), channel_id=1, source_target_pairs={{0,8},{8,16},{16,24},{24,28},{28,20},{20,12},{12,4},{4,0},{1,9},{9... | collective-permute-start | bytes 1277960 | tf_op jit(solution)/shard_map/ppermute | solution.py:396
  34.4 24.9 %collective-permute-start.12 = (f32[832,128]{1,0:T(8,128)S(1)}, f32[832,128]{1,0:T(8,128)S(1)}, u32[]{:S(2)}, u32[]{:S(2)}) collective-permute-start(f32[832,128]{1,0:T(8,128)S(1)} %collective-permute-done.7.refs_1_), channel_id=1, source_target_pairs={{8,0},{16,8},{24,16},{28,24},{20,28},{12,20},{4,12},{0,4},{9,1},{1... | collective-permute-start | bytes 1277960 | tf_op jit(solution)/shard_map/ppermute | solution.py:393
  35.4 10.0 %copy-start.1 = (bf16[800,1600]{1,0:T(8,128)(2,1)S(1)}, bf16[800,1600]{1,0:T(8,128)(2,1)}, u32[]{:S(2)}) copy-start(bf16[800,1600]{1,0:T(8,128)(2,1)} %relation_ref.13) | copy-start | bytes 7680004
  43.9 15.3 %collective-permute-start.8 = (f32[800,128]{1,0:T(8,128)S(1)}, f32[800,128]{1,0:T(8,128)S(1)}, u32[]{:S(2)}, u32[]{:S(2)}) collective-permute-start(f32[800,128]{1,0:T(8,128)S(1)} %get-tuple-element.65), channel_id=1, source_target_pairs={{0,2},{1,3},{2,0},{3,1},{4,6},{5,7},{6,4},{7,5},{8,10},{9,11},{10,... | collective-permute-start | bytes 1228808 | tf_op jit(solution)/shard_map/ppermute | solution.py:414
  47.2 10.1 %collective-permute-start.9 = (f32[768,128]{1,0:T(8,128)S(1)}, f32[768,128]{1,0:T(8,128)S(1)}, u32[]{:S(2)}, u32[]{:S(2)}) collective-permute-start(f32[768,128]{1,0:T(8,128)S(1)} %collective-permute-done.4.refs_0_), channel_id=1, source_target_pairs={{0,8},{8,16},{16,24},{24,28},{28,20},{20,12},{12,4},{4,0},{1,9},{9... | collective-permute-start | bytes 1179656 | tf_op jit(solution)/shard_map/ppermute | solution.py:396
  48.9 11.5 %collective-permute-start.10 = (f32[768,128]{1,0:T(8,128)S(1)}, f32[768,128]{1,0:T(8,128)S(1)}, u32[]{:S(2)}, u32[]{:S(2)}) collective-permute-start(f32[768,128]{1,0:T(8,128)S(1)} %collective-permute-done.5.refs_1_), channel_id=1, source_target_pairs={{8,0},{16,8},{24,16},{28,24},{20,28},{12,20},{4,12},{0,4},{9,1},{1... | collective-permute-start | bytes 1179656 | tf_op jit(solution)/shard_map/ppermute | solution.py:393
  57.4 10.0 %collective-permute-start.18 = (f32[768,128]{1,0:T(8,128)S(1)}, f32[768,128]{1,0:T(8,128)S(1)}, u32[]{:S(2)}, u32[]{:S(2)}) collective-permute-start(f32[768,128]{1,0:T(8,128)S(1)} %collective-permute-done.9.refs_0_), channel_id=1, source_target_pairs={{0,8},{8,16},{16,24},{24,28},{28,20},{20,12},{12,4},{4,0},{1,9},{9... | collective-permute-start | bytes 1179656 | tf_op jit(solution)/shard_map/ppermute | solution.py:396
  61.6 9.9 %collective-permute-start.19 = (f32[832,128]{1,0:T(8,128)S(1)}, f32[832,128]{1,0:T(8,128)S(1)}, u32[]{:S(2)}, u32[]{:S(2)}) collective-permute-start(f32[832,128]{1,0:T(8,128)S(1)} %collective-permute-done.12.refs_1_), channel_id=1, source_target_pairs={{8,0},{16,8},{24,16},{28,24},{20,28},{12,20},{4,12},{0,4},{9,1},{1... | collective-permute-start | bytes 1277960 | tf_op jit(solution)/shard_map/ppermute | solution.py:393
  61.9 1.6 %collective-permute-start.13 = (f32[544,128]{1,0:T(8,128)S(1)}, f32[544,128]{1,0:T(8,128)S(1)}, u32[]{:S(2)}, u32[]{:S(2)}) collective-permute-start(f32[544,128]{1,0:T(8,128)S(1)} %get-tuple-element.109), channel_id=1, source_target_pairs={{0,1},{1,0},{2,3},{3,2},{4,5},{5,4},{6,7},{7,6},{8,9},{9,8},{10,11... | collective-permute-start | bytes 835592 | tf_op jit(solution)/shard_map/ppermute | solution.py:411
  62.0 1.9 %collective-permute-start.14 = (f32[544,128]{1,0:T(8,128)S(1)}, f32[544,128]{1,0:T(8,128)S(1)}, u32[]{:S(2)}, u32[]{:S(2)}) collective-permute-start(f32[544,128]{1,0:T(8,128)S(1)} %get-tuple-element.108), channel_id=1, source_target_pairs={{0,1},{1,0},{2,3},{3,2},{4,5},{5,4},{6,7},{7,6},{8,9},{9,8},{10,11... | collective-permute-start | bytes 835592 | tf_op jit(solution)/shard_map/ppermute | solution.py:411
  62.5 1.8 %collective-permute-start.15 = (f32[544,128]{1,0:T(8,128)S(1)}, f32[544,128]{1,0:T(8,128)S(1)}, u32[]{:S(2)}, u32[]{:S(2)}) collective-permute-start(f32[544,128]{1,0:T(8,128)S(1)} %get-tuple-element.107), channel_id=1, source_target_pairs={{0,1},{1,0},{2,3},{3,2},{4,5},{5,4},{6,7},{7,6},{8,9},{9,8},{10,11... | collective-permute-start | bytes 835592 | tf_op jit(solution)/shard_map/ppermute | solution.py:411
  64.4 12.5 %copy-start.2 = (f32[1024]{0:T(1024)S(1)}, f32[1024]{0:T(1024)}, u32[]{:S(2)}) copy-start(f32[1024]{0:T(1024)} %one_ref.1) | copy-start | bytes 12292
  64.4 12.5 %copy-start.3 = (f32[1024]{0:T(1024)S(1)}, f32[1024]{0:T(1024)}, u32[]{:S(2)}) copy-start(f32[1024]{0:T(1024)} %two_ref.1) | copy-start | bytes 12292
  64.4 12.5 %copy-start.4 = (f32[1024]{0:T(1024)S(1)}, f32[1024]{0:T(1024)}, u32[]{:S(2)}) copy-start(f32[1024]{0:T(1024)} %scale_ref.1) | copy-start | bytes 12292
  64.4 15.7 %collective-permute-start.16 = (f32[816,128]{1,0:T(8,128)S(1)}, f32[816,128]{1,0:T(8,128)S(1)}, u32[]{:S(2)}, u32[]{:S(2)}) collective-permute-start(f32[816,128]{1,0:T(8,128)S(1)} %get-tuple-element.87), channel_id=1, source_target_pairs={{0,2},{1,3},{2,0},{3,1},{4,6},{5,7},{6,4},{7,5},{8,10},{9,11},{10,... | collective-permute-start | bytes 1253384 | tf_op jit(solution)/shard_map/ppermute | solution.py:414
  72.6 1.5 %collective-permute-start.20 = (f32[400,128]{1,0:T(8,128)S(1)}, f32[400,128]{1,0:T(8,128)S(1)}, u32[]{:S(2)}, u32[]{:S(2)}) collective-permute-start(f32[400,128]{1,0:T(8,128)S(1)} %get-tuple-element.94), channel_id=1, source_target_pairs={{0,1},{1,0},{2,3},{3,2},{4,5},{5,4},{6,7},{7,6},{8,9},{9,8},{10,11... | collective-permute-start | bytes 614408 | tf_op jit(solution)/shard_map/ppermute | solution.py:411
  72.7 1.7 %collective-permute-start.21 = (f32[400,128]{1,0:T(8,128)S(1)}, f32[400,128]{1,0:T(8,128)S(1)}, u32[]{:S(2)}, u32[]{:S(2)}) collective-permute-start(f32[400,128]{1,0:T(8,128)S(1)} %get-tuple-element.95), channel_id=1, source_target_pairs={{0,1},{1,0},{2,3},{3,2},{4,5},{5,4},{6,7},{7,6},{8,9},{9,8},{10,11... | collective-permute-start | bytes 614408 | tf_op jit(solution)/shard_map/ppermute | solution.py:411
  73.2 9.2 %collective-permute-start.17 = (f32[800,128]{1,0:T(8,128)S(1)}, f32[800,128]{1,0:T(8,128)S(1)}, u32[]{:S(2)}, u32[]{:S(2)}) collective-permute-start(f32[800,128]{1,0:T(8,128)S(1)} %shard_map.60.two_sum), channel_id=1, source_target_pairs={{0,1},{1,0},{2,3},{3,2},{4,5},{5,4},{6,7},{7,6},{8,9},{9,8},{10,11... | collective-permute-start | bytes 1228808 | tf_op jit(solution)/shard_map/ppermute | solution.py:411
  74.4 7.8 %collective-permute-start.24 = (f32[200,128]{1,0:T(8,128)S(1)}, f32[200,128]{1,0:T(8,128)S(1)}, u32[]{:S(2)}, u32[]{:S(2)}) collective-permute-start(f32[200,128]{1,0:T(8,128)S(1)} %get-tuple-element.104), channel_id=1, source_target_pairs={{0,2},{1,3},{2,0},{3,1},{4,6},{5,7},{6,4},{7,5},{8,10},{9,11},{10,... | collective-permute-start | bytes 307208 | tf_op jit(solution)/shard_map/ppermute | solution.py:414
  76.6 5.6 %collective-permute-start.25 = (f32[200,128]{1,0:T(8,128)S(1)}, f32[200,128]{1,0:T(8,128)S(1)}, u32[]{:S(2)}, u32[]{:S(2)}) collective-permute-start(f32[200,128]{1,0:T(8,128)S(1)} %get-tuple-element.105), channel_id=1, source_target_pairs={{0,2},{1,3},{2,0},{3,1},{4,6},{5,7},{6,4},{7,5},{8,10},{9,11},{10,... | collective-permute-start | bytes 307208 | tf_op jit(solution)/shard_map/ppermute | solution.py:414
  76.8 1.2 %collective-permute-start.22 = (f32[4,896]{1,0:T(4,128)S(1)}, f32[4,896]{1,0:T(4,128)S(1)}, u32[]{:S(2)}, u32[]{:S(2)}) collective-permute-start(f32[4,896]{1,0:T(4,128)S(1)} %get-tuple-element.101), channel_id=1, source_target_pairs={{0,1},{1,0},{2,3},{3,2},{4,5},{5,4},{6,7},{7,6},{8,9},{9,8},{10,11... | collective-permute-start | bytes 43016 | tf_op jit(solution)/shard_map/ppermute | solution.py:411
  78.1 4.1 %collective-permute-start.23 = (f32[2,896]{1,0:T(2,128)S(1)}, f32[2,896]{1,0:T(2,128)S(1)}, u32[]{:S(2)}, u32[]{:S(2)}) collective-permute-start(f32[2,896]{1,0:T(2,128)S(1)} %get-tuple-element.102), channel_id=1, source_target_pairs={{0,2},{1,3},{2,0},{3,1},{4,6},{5,7},{6,4},{7,5},{8,10},{9,11},{10,... | collective-permute-start | bytes 21512 | tf_op jit(solution)/shard_map/ppermute | solution.py:414
  82.2 1.5 %collective-permute-start.26 = (f32[400,128]{1,0:T(8,128)S(1)}, f32[400,128]{1,0:T(8,128)S(1)}, u32[]{:S(2)}, u32[]{:S(2)}) collective-permute-start(f32[400,128]{1,0:T(8,128)S(1)} %shard_map.72.zero_half), channel_id=1, source_target_pairs={{0,1},{1,0},{2,3},{3,2},{4,5},{5,4},{6,7},{7,6},{8,9},{9,8},{10,11... | collective-permute-start | bytes 614408 | tf_op jit(solution)/shard_map/ppermute | solution.py:411

commit v7 on v6

--- a/solution.py
+++ b/solution.py
@@ -107,24 +107,24 @@
         edges_ref[2:4] = turned[WIDTH - 2 :]
 
 
-def bottom_kernel(cut, relation_ref, *refs):
+def first_part_kernel(columns, relation_ref, *refs):
     both_ref = refs[-1]
     count = (len(refs) - 1) // 2
     for n in range(count):
         both_ref[...] = jnp.dot(
-            relation_ref[:, cut:], two_parts(refs[n][...]), preferred_element_type=jnp.float32
+            relation_ref[:, columns], two_parts(refs[n][...]), preferred_element_type=jnp.float32
         )
         refs[count + n][...] = both_ref[:, :WIDTH] + both_ref[:, WIDTH:]
 
 
-def top_kernel(cut, relation_ref, *refs):
+def last_part_kernel(columns, relation_ref, *refs):
     both_ref, padded_ref = refs[-2:]
     count = (len(refs) - 2) // 4
     rows = relation_ref.shape[0]
     padded_ref[...] = jnp.zeros_like(padded_ref)
     for n in range(count):
         both_ref[...] = jnp.dot(
-            relation_ref[:, :cut], two_parts(refs[n][...]), preferred_element_type=jnp.float32
+            relation_ref[:, columns], two_parts(refs[n][...]), preferred_element_type=jnp.float32
         )
         padded_ref[:rows] = both_ref[:, :WIDTH] + both_ref[:, WIDTH:] + refs[count + n][...]
         refs[2 * count + 2 * n][...] = padded_ref[:rows]
@@ -413,18 +413,19 @@
     def over_y(x):
         return lax.ppermute(x, "tm", [(t, t ^ 2) for t in range(tms)])
 
-    def in_two_steps(behind, ahead, after=(), cost=1):
+    def in_two_steps(behind, ahead, after=(), cost=1, between=lambda *made: None):
         both = pltpu.VMEM((rows, 2 * WIDTH), jnp.float32)
         parts = [tied(blocks[far][1], *after) for far in (behind, ahead)]
         bottoms = call(
-            functools.partial(bottom_kernel, cut),
+            functools.partial(first_part_kernel, slice(cut, depth)),
             [(rows, WIDTH)] * 2,
             (relation, *parts),
             [both],
             flops=KERNEL_FLOPS,
         )
+        between(*bottoms)
         made = call(
-            functools.partial(top_kernel, cut),
+            functools.partial(last_part_kernel, slice(0, cut)),
             [(rows, WIDTH), (4, wide)] * 2,
             (relation, blocks[behind][0], blocks[ahead][0], *bottoms),
             [both, pltpu.VMEM((wide, WIDTH), jnp.float32)],
@@ -447,7 +448,6 @@
             multiplied(-n, n)
         if n == 2:
             in_two_steps(-n, n, after=(), cost=1)
-    blocks[half] = (behind_of(behind[0]), ahead_of(ahead[1]))
     two_send, two_keep = call(
         functools.partial(chip_pair_kernel, spot_of, 2),
         [(rows, WIDTH)] * 2,
@@ -456,7 +456,10 @@
     )
     two_sum = call(sum_kernel, [(rows, WIDTH)], (two_keep, over_y(two_send)), flops=KERNEL_FLOPS // 10)[0]
     two_got = over_cores(two_sum)
-    in_two_steps(1 - half, half - 1, cost=10)
+    def last_step(*made):
+        blocks[half] = (behind_of(tied(behind[0], *made)), ahead_of(ahead[1]))
+
+    in_two_steps(1 - half, half - 1, cost=10, between=last_step)
     odd_fars = (-1, 3, 1, -3)
     send, keep = call(
         functools.partial(odd_kernel, spot_of, odd_fars),
@@ -472,7 +475,21 @@
         flops=KERNEL_FLOPS // 2,
     )
     odd_got = over_y(odd_send)
-    multiplied(half, after=(odd_mine,), cost=1)
+    both = pltpu.VMEM((rows, 2 * WIDTH), jnp.float32)
+    top_product = call(
+        functools.partial(first_part_kernel, slice(0, cut)),
+        [(rows, WIDTH)],
+        (relation, tied(blocks[half][0], odd_mine)),
+        [both],
+        flops=1 * KERNEL_FLOPS,
+    )[0]
+    products[half] = call(
+        functools.partial(last_part_kernel, slice(cut, depth)),
+        [(rows, WIDTH), (4, wide)],
+        (relation, tied(blocks[half][1], odd_mine), top_product),
+        [both, pltpu.VMEM((wide, WIDTH), jnp.float32)],
+        flops=10 * KERNEL_FLOPS,
+    )
     even_fars = (0, half, 2, -2)
     border_send, border_keep = call(
         functools.partial(borders_kernel, spot_of, even_fars),

time: 85.2 us -> 84.1 us (0.987)
  starting transfers between devices: 24.8 us -> 23.6 us
    ppermute x7, waiting for transfers between devices: 32.3 us -> 15.2 us  [behind_of(): return lax.ppermute(x, 'gen', forward)]
    ppermute x7, waiting for transfers between devices: 6.4 us -> 19.8 us  [ahead_of(): return lax.ppermute(x, 'gen', backward)]
    ppermute x7, starting transfers between devices: 15 us -> 3.85 us  [behind_of(): return lax.ppermute(x, 'gen', forward)]
    ppermute x7, starting transfers between devices: 0.71 us -> 11.7 us  [ahead_of(): return lax.ppermute(x, 'gen', backward)]
    ppermute x5, waiting for transfers between devices: 1.36 us -> 4.98 us  [over_y(): return lax.ppermute(x, 'tm', [(t, t ^ 2) for t in range(tms)])]
    ppermute x5, starting transfers between devices: 7.65 us -> 6.61 us  [over_y(): return lax.ppermute(x, 'tm', [(t, t ^ 2) for t in range(tms)])]
    pallas_call x20 -> x21, Pallas kernels: 11.9 us -> 12.1 us  [call(): pl.pallas_call(kernel, out_shape=[jax.ShapeDtypeStruct(shape, jnp.float32...]
  transfers between devices with their start and end apart: 27 -> 27, of which waited for: 16 -> 17; matrix products, arithmetic and copies ran while one was open for 1% -> 1% of each run, Pallas kernels for 13% -> 13%
where the time goes in v7:
time: 84.1 us; the launch traced here: 83.8 us
  waiting for transfers between devices  44 us (52%)
  starting transfers between devices  23.6 us (28%)
  Pallas kernels  12.1 us (14%)
  local copies, waits for them, and re-layouts  3.89 us (5%)
    ppermute x7, waiting for transfers between devices, ahead_of(): return lax.ppermute(x, 'gen', backward)  19.8 us
    ppermute x7, waiting for transfers between devices, behind_of(): return lax.ppermute(x, 'gen', forward)  15.2 us
    pallas_call x21, Pallas kernels, call(): pl.pallas_call(kernel, out_shape=[jax.ShapeDtypeStruct(shape, jnp.float32...  12.1 us
    ppermute x7, starting transfers between devices, ahead_of(): return lax.ppermute(x, 'gen', backward)  11.7 us
    ppermute x5, starting transfers between devices, over_y(): return lax.ppermute(x, 'tm', [(t, t ^ 2) for t in range(tms)])  6.61 us
    ppermute x5, waiting for transfers between devices, over_y(): return lax.ppermute(x, 'tm', [(t, t ^ 2) for t in range(tms)])  4.98 us
    ppermute x8, waiting for transfers between devices, over_cores(): return lax.ppermute(x, 'tm', swap)  4.08 us
    ppermute x7, starting transfers between devices, behind_of(): return lax.ppermute(x, 'gen', forward)  3.85 us
  transfers between devices with their start and end apart: 27, of which 17 were waited for; matrix products, arithmetic and copies ran while one was open for 1% of the time, Pallas kernels for 13%

profile of v7, /device:TPU:0, one launch (start us, length us, event | category | flops | bytes accessed | tf_op | source)
XLA Modules:
  0.0 83.8 jit_solution(4147372205690123268)
XLA Ops:
  0.0 1.0 %slice.16.refs_1_ = f32[832,128]{1,0:T(8,128)S(1)} slice(f32[1600,128]{1,0:T(8,128)} %param.6), slice={[768:1600], [0:128]} | slice | bytes 851968 | tf_op jit(solution)/shard_map/slice | solution.py:436
  1.0 3.0 %collective-permute-start.3 = (f32[832,128]{1,0:T(8,128)S(1)}, f32[832,128]{1,0:T(8,128)S(1)}, u32[]{:S(2)}, u32[]{:S(2)}) collective-permute-start(f32[832,128]{1,0:T(8,128)S(1)} %slice.16.refs_1_), channel_id=1, source_target_pairs={{8,0},{16,8},{24,16},{28,24},{20,28},{12,20},{4,12},{0,4},{9,1},{1... | collective-permute-start | bytes 1277960 | tf_op jit(solution)/shard_map/ppermute | solution.py:393
  4.2 1.0 %slice.15.refs_0_ = f32[768,128]{1,0:T(8,128)S(1)} slice(f32[1600,128]{1,0:T(8,128)} %param.6), slice={[0:768], [0:128]} | slice | bytes 786432 | tf_op jit(solution)/shard_map/slice | solution.py:436
  5.2 2.0 %collective-permute-start = (f32[768,128]{1,0:T(8,128)S(1)}, f32[768,128]{1,0:T(8,128)S(1)}, u32[]{:S(2)}, u32[]{:S(2)}) collective-permute-start(f32[768,128]{1,0:T(8,128)S(1)} %slice.15.refs_0_), channel_id=1, source_target_pairs={{0,8},{8,16},{16,24},{24,28},{28,20},{20,12},{12,4},{4,0},{1,9},{9... | collective-permute-start | bytes 1179656 | tf_op jit(solution)/shard_map/ppermute | solution.py:396
  7.3 7.5 %collective-permute-done.3.refs_3_ = f32[832,128]{1,0:T(8,128)S(1)} collective-permute-done((f32[832,128]{1,0:T(8,128)S(1)}, f32[832,128]{1,0:T(8,128)S(1)}, u32[]{:S(2)}, u32[]{:S(2)}) %collective-permute-start.3) | collective-permute-done | bytes 426016 | tf_op jit(solution)/shard_map/ppermute | solution.py:393
  14.8 2.0 %collective-permute-start.7 = (f32[832,128]{1,0:T(8,128)S(1)}, f32[832,128]{1,0:T(8,128)S(1)}, u32[]{:S(2)}, u32[]{:S(2)}) collective-permute-start(f32[832,128]{1,0:T(8,128)S(1)} %collective-permute-done.3.refs_3_), channel_id=1, source_target_pairs={{8,0},{16,8},{24,16},{28,24},{20,28},{12,20},{4,12},{0,4},{9,1},{1... | collective-permute-start | bytes 1277960 | tf_op jit(solution)/shard_map/ppermute | solution.py:393
  16.9 1.7 %copy-done = bf16[800,1600]{1,0:T(8,128)(2,1)S(1)} copy-done((bf16[800,1600]{1,0:T(8,128)(2,1)S(1)}, bf16[800,1600]{1,0:T(8,128)(2,1)}, u32[]{:S(2)}) %copy-start) | copy-done | bytes 2560024
  18.6 1.0 %shard_map.56 = (f32[800,128]{1,0:T(8,128)S(1)}, f32[4,896]{1,0:T(4,128)S(1)}) custom-call(bf16[800,1600]{1,0:T(8,128)(2,1)S(1)} %copy-done, f32[768,128]{1,0:T(8,128)S(1)} %slice.15.refs_0_, f32[832,128]{1,0:T(8,128)S(1)} %slice.16.refs_1_), custom_call_target="tpu_custom_call" | custom-call | flops 100000000 | tf_op jit(solution)/shard_map/pallas_call | solution.py:18
  19.6 5.6 %collective-permute-done.refs_0_ = f32[768,128]{1,0:T(8,128)S(1)} collective-permute-done((f32[768,128]{1,0:T(8,128)S(1)}, f32[768,128]{1,0:T(8,128)S(1)}, u32[]{:S(2)}, u32[]{:S(2)}) %collective-permute-start) | collective-permute-done | bytes 393248 | tf_op jit(solution)/shard_map/ppermute | solution.py:396
  25.2 1.6 %collective-permute-start.5 = (f32[768,128]{1,0:T(8,128)S(1)}, f32[768,128]{1,0:T(8,128)S(1)}, u32[]{:S(2)}, u32[]{:S(2)}) collective-permute-start(f32[768,128]{1,0:T(8,128)S(1)} %collective-permute-done.2.refs_2_), channel_id=1, source_target_pairs={{8,0},{16,8},{24,16},{28,24},{20,28},{12,20},{4,12},{0,4},{9,1},{1... | collective-permute-start | bytes 1179656 | tf_op jit(solution)/shard_map/ppermute | solution.py:393
  26.8 0.4 collective-permute-start.4
  27.2 5.1 %collective-permute-done.7.refs_1_ = f32[832,128]{1,0:T(8,128)S(1)} collective-permute-done((f32[832,128]{1,0:T(8,128)S(1)}, f32[832,128]{1,0:T(8,128)S(1)}, u32[]{:S(2)}, u32[]{:S(2)}) %collective-permute-start.7) | collective-permute-done | bytes 426016 | tf_op jit(solution)/shard_map/ppermute | solution.py:393
  32.3 2.0 %collective-permute-start.12 = (f32[832,128]{1,0:T(8,128)S(1)}, f32[832,128]{1,0:T(8,128)S(1)}, u32[]{:S(2)}, u32[]{:S(2)}) collective-permute-start(f32[832,128]{1,0:T(8,128)S(1)} %collective-permute-done.7.refs_1_), channel_id=1, source_target_pairs={{8,0},{16,8},{24,16},{28,24},{20,28},{12,20},{4,12},{0,4},{9,1},{1... | collective-permute-start | bytes 1277960 | tf_op jit(solution)/shard_map/ppermute | solution.py:393
  34.4 1.0 %shard_map.57 = (f32[800,128]{1,0:T(8,128)S(1)}, f32[800,128]{1,0:T(8,128)S(1)}) custom-call(bf16[800,1600]{1,0:T(8,128)(2,1)S(1)} %copy-done, f32[832,128]{1,0:T(8,128)S(1)} %collective-permute-done.6.refs_0_, f32[832,128]{1,0:T(8,128)S(1)} %collective-permute-done.7.refs_1_), custom_call_target="tpu_custom_call" | custom-call | flops 100000000 | tf_op jit(solution)/shard_map/pallas_call | solution.py:18
  35.5 5.3 %collective-permute-done.5.refs_1_ = f32[768,128]{1,0:T(8,128)S(1)} collective-permute-done((f32[768,128]{1,0:T(8,128)S(1)}, f32[768,128]{1,0:T(8,128)S(1)}, u32[]{:S(2)}, u32[]{:S(2)}) %collective-permute-start.5) | collective-permute-done | bytes 393248 | tf_op jit(solution)/shard_map/ppermute | solution.py:393
  40.7 2.0 %collective-permute-done.4.refs_0_ = f32[768,128]{1,0:T(8,128)S(1)} collective-permute-done((f32[768,128]{1,0:T(8,128)S(1)}, f32[768,128]{1,0:T(8,128)S(1)}, u32[]{:S(2)}, u32[]{:S(2)}) %collective-permute-start.4) | collective-permute-done | bytes 393248 | tf_op jit(solution)/shard_map/ppermute | solution.py:396
  42.8 0.9 %shard_map.58 = (f32[800,128]{1,0:T(8,128)S(1)}, f32[4,896]{1,0:T(4,128)S(1)}, f32[800,128]{1,0:T(8,128)S(1)}, f32[4,896]{1,0:T(4,128)S(1)}) custom-call(bf16[800,1600]{1,0:T(8,128)(2,1)S(1)} %copy-done, f32[768,128]{1,0:T(8,128)S(1)} %collective-permute-done.4.refs_0_, f32[768,128]{1,0:T(8,128)S(1)} %collective-permute-done.5.refs_1_, ...), custom_call_target="tpu_custom_call" | custom-call | flops 100000000 | tf_op jit(solution)/shard_map/pallas_call | solution.py:18
  43.8 1.6 %collective-permute-start.8 = (f32[800,128]{1,0:T(8,128)S(1)}, f32[800,128]{1,0:T(8,128)S(1)}, u32[]{:S(2)}, u32[]{:S(2)}) collective-permute-start(f32[800,128]{1,0:T(8,128)S(1)} %get-tuple-element.66), channel_id=1, source_target_pairs={{0,2},{1,3},{2,0},{3,1},{4,6},{5,7},{6,4},{7,5},{8,10},{9,11},{10,... | collective-permute-start | bytes 1228808 | tf_op jit(solution)/shard_map/ppermute | solution.py:414
  45.4 1.8 %shard_map.55 = (f32[800,128]{1,0:T(8,128)S(1)}, f32[4,896]{1,0:T(4,128)S(1)}, f32[800,128]{1,0:T(8,128)S(1)}, f32[4,896]{1,0:T(4,128)S(1)}) custom-call(bf16[800,1600]{1,0:T(8,128)(2,1)S(1)} %copy-done.1, f32[768,128]{1,0:T(8,128)S(1)} %collective-permute-done.refs_0_, f32[832,128]{1,0:T(8,128)S(1)} %collective-permute-done.1.refs_1_, ...), custom_call_target="tpu_custom_call" | custom-call | flops 200000000 | tf_op jit(solution)/shard_map/pallas_call | solution.py:18
  47.1 0.6 collective-permute-start.9
  47.7 1.5 %collective-permute-start.10 = (f32[768,128]{1,0:T(8,128)S(1)}, f32[768,128]{1,0:T(8,128)S(1)}, u32[]{:S(2)}, u32[]{:S(2)}) collective-permute-start(f32[768,128]{1,0:T(8,128)S(1)} %collective-permute-done.5.refs_1_), channel_id=1, source_target_pairs={{8,0},{16,8},{24,16},{28,24},{20,28},{12,20},{4,12},{0,4},{9,1},{1... | collective-permute-start | bytes 1179656 | tf_op jit(solution)/shard_map/ppermute | solution.py:393
  49.2 3.2 %collective-permute-done.8.other_ref = f32[800,128]{1,0:T(8,128)S(1)} collective-permute-done((f32[800,128]{1,0:T(8,128)S(1)}, f32[800,128]{1,0:T(8,128)S(1)}, u32[]{:S(2)}, u32[]{:S(2)}) %collective-permute-start.8) | collective-permute-done | bytes 409632 | tf_op jit(solution)/shard_map/ppermute | solution.py:414
  52.5 1.0 %shard_map.61 = (f32[800,128]{1,0:T(8,128)S(1)}, f32[800,128]{1,0:T(8,128)S(1)}) custom-call(bf16[800,1600]{1,0:T(8,128)(2,1)S(1)} %copy-done.1, f32[832,128]{1,0:T(8,128)S(1)} %collective-permute-done.11.refs_0_, f32[832,128]{1,0:T(8,128)S(1)} %collective-permute-done.12.refs_1_), custom_call_target="tpu_custom_call" | custom-call | flops 100000000 | tf_op jit(solution)/shard_map/pallas_call | solution.py:18
  53.5 5.3 %collective-permute-done.9.refs_0_ = f32[768,128]{1,0:T(8,128)S(1)} collective-permute-done((f32[768,128]{1,0:T(8,128)S(1)}, f32[768,128]{1,0:T(8,128)S(1)}, u32[]{:S(2)}, u32[]{:S(2)}) %collective-permute-start.9) | collective-permute-done | bytes 393248 | tf_op jit(solution)/shard_map/ppermute | solution.py:396
  58.8 0.4 collective-permute-start.19
  59.3 0.9 %shard_map.62 = (f32[800,128]{1,0:T(8,128)S(1)}, f32[4,896]{1,0:T(4,128)S(1)}, f32[800,128]{1,0:T(8,128)S(1)}, f32[4,896]{1,0:T(4,128)S(1)}) custom-call(bf16[800,1600]{1,0:T(8,128)(2,1)S(1)} %copy-done.1, f32[768,128]{1,0:T(8,128)S(1)} %collective-permute-done.9.refs_0_, f32[768,128]{1,0:T(8,128)S(1)} %collective-permute-done.10.refs_1_, ...), custom_call_target="tpu_custom_call" | custom-call | flops 1000000000 | tf_op jit(solution)/shard_map/pallas_call | solution.py:18
  60.2 0.3 shard_map.63
  60.5 1.7 %collective-permute-start.18 = (f32[832,128]{1,0:T(8,128)S(1)}, f32[832,128]{1,0:T(8,128)S(1)}, u32[]{:S(2)}, u32[]{:S(2)}) collective-permute-start(f32[832,128]{1,0:T(8,128)S(1)} %collective-permute-done.12.refs_1_), channel_id=1, source_target_pairs={{8,0},{16,8},{24,16},{28,24},{20,28},{12,20},{4,12},{0,4},{9,1},{1... | collective-permute-start | bytes 1277960 | tf_op jit(solution)/shard_map/ppermute | solution.py:393
  62.3 0.5 collective-permute-start.14
  62.9 1.0 %collective-permute-done.15.refs_2_ = f32[544,128]{1,0:T(8,128)S(1)} collective-permute-done((f32[544,128]{1,0:T(8,128)S(1)}, f32[544,128]{1,0:T(8,128)S(1)}, u32[]{:S(2)}, u32[]{:S(2)}) %collective-permute-start.15) | collective-permute-done | bytes 278560 | tf_op jit(solution)/shard_map/ppermute | solution.py:411
  63.9 0.4 collective-permute-done.14.refs_1_
  64.2 0.4 collective-permute-done.13.refs_0_
  64.7 1.6 %collective-permute-start.16 = (f32[816,128]{1,0:T(8,128)S(1)}, f32[816,128]{1,0:T(8,128)S(1)}, u32[]{:S(2)}, u32[]{:S(2)}) collective-permute-start(f32[816,128]{1,0:T(8,128)S(1)} %get-tuple-element.88), channel_id=1, source_target_pairs={{0,2},{1,3},{2,0},{3,1},{4,6},{5,7},{6,4},{7,5},{8,10},{9,11},{10,... | collective-permute-start | bytes 1253384 | tf_op jit(solution)/shard_map/ppermute | solution.py:414
  66.3 2.2 %collective-permute-done.19.refs_0_ = f32[768,128]{1,0:T(8,128)S(1)} collective-permute-done((f32[768,128]{1,0:T(8,128)S(1)}, f32[768,128]{1,0:T(8,128)S(1)}, u32[]{:S(2)}, u32[]{:S(2)}) %collective-permute-start.19) | collective-permute-done | bytes 393248 | tf_op jit(solution)/shard_map/ppermute | solution.py:396
  68.5 0.5 shard_map.67.refs_1_
  69.0 1.9 %collective-permute-done.18.refs_0_ = f32[832,128]{1,0:T(8,128)S(1)} collective-permute-done((f32[832,128]{1,0:T(8,128)S(1)}, f32[832,128]{1,0:T(8,128)S(1)}, u32[]{:S(2)}, u32[]{:S(2)}) %collective-permute-start.18) | collective-permute-done | bytes 426016 | tf_op jit(solution)/shard_map/ppermute | solution.py:393
  71.0 0.7 shard_map.68
  71.8 0.5 collective-permute-start.21
  72.4 0.9 %collective-permute-done.20.got_ours = f32[400,128]{1,0:T(8,128)S(1)} collective-permute-done((f32[400,128]{1,0:T(8,128)S(1)}, f32[400,128]{1,0:T(8,128)S(1)}, u32[]{:S(2)}, u32[]{:S(2)}) %collective-permute-start.20) | collective-permute-done | bytes 204832 | tf_op jit(solution)/shard_map/ppermute | solution.py:411
  73.3 0.3 collective-permute-done.21.got_theirs
  73.6 1.4 %collective-permute-start.24 = (f32[200,128]{1,0:T(8,128)S(1)}, f32[200,128]{1,0:T(8,128)S(1)}, u32[]{:S(2)}, u32[]{:S(2)}) collective-permute-start(f32[200,128]{1,0:T(8,128)S(1)} %get-tuple-element.106), channel_id=1, source_target_pairs={{0,2},{1,3},{2,0},{3,1},{4,6},{5,7},{6,4},{7,5},{8,10},{9,11},{10,... | collective-permute-start | bytes 307208 | tf_op jit(solution)/shard_map/ppermute | solution.py:414
  75.0 0.7 collective-permute-start.25
  76.1 1.0 %collective-permute-done.22.got_ref = f32[4,896]{1,0:T(4,128)S(1)} collective-permute-done((f32[4,896]{1,0:T(4,128)S(1)}, f32[4,896]{1,0:T(4,128)S(1)}, u32[]{:S(2)}, u32[]{:S(2)}) %collective-permute-start.22) | collective-permute-done | bytes 14368 | tf_op jit(solution)/shard_map/ppermute | solution.py:411
  77.1 1.4 %collective-permute-start.23 = (f32[2,896]{1,0:T(2,128)S(1)}, f32[2,896]{1,0:T(2,128)S(1)}, u32[]{:S(2)}, u32[]{:S(2)}) collective-permute-start(f32[2,896]{1,0:T(2,128)S(1)} %get-tuple-element.104), channel_id=1, source_target_pairs={{0,2},{1,3},{2,0},{3,1},{4,6},{5,7},{6,4},{7,5},{8,10},{9,11},{10,... | collective-permute-start | bytes 21512 | tf_op jit(solution)/shard_map/ppermute | solution.py:414
  78.5 0.7 shard_map.66
  79.3 1.8 %collective-permute-done.23.border_got = f32[2,896]{1,0:T(2,128)S(1)} collective-permute-done((f32[2,896]{1,0:T(2,128)S(1)}, f32[2,896]{1,0:T(2,128)S(1)}, u32[]{:S(2)}, u32[]{:S(2)}) %collective-permute-start.23) | collective-permute-done | bytes 7200 | tf_op jit(solution)/shard_map/ppermute | solution.py:414
  81.2 1.3 %shard_map.74.refs_0_ = f32[800,256]{1,0:T(8,128)} custom-call(f32[800,128]{1,0:T(8,128)S(1)} %get-tuple-element.89.odd_own, f32[800,128]{1,0:T(8,128)S(1)} %get-tuple-element.90.odd_beyond, f32[800,128]{1,0:T(8,128)S(1)} %shard_map.60.two_sum, f32[800,128]{1,0:T(8,128)S(1)} %collective-permute-done.17.two_got, f32[400,128]{1,0:T(8,128)S(1)} %shard_map.73.zero_half, ...), custom_call_target="tpu_custom_call" | custom-call | tf_op jit(solution)/shard_map/pallas_call | solution.py:18
  82.6 1.2 %shard_map.75 = f32[800,256]{1,0:T(8,128)} custom-call(f32[800,128]{1,0:T(8,128)S(1)} %get-tuple-element.89.odd_own, f32[800,128]{1,0:T(8,128)S(1)} %get-tuple-element.90.odd_beyond, f32[800,128]{1,0:T(8,128)S(1)} %shard_map.60.two_sum, f32[800,128]{1,0:T(8,128)S(1)} %collective-permute-done.17.two_got, ...), custom_call_target="tpu_custom_call", output_to_operand_aliasing={{}: (8, {})} | custom-call | tf_op jit(solution)/shard_map/pallas_call | solution.py:18
  (40 shorter events, 1.9 us)
Async XLA Ops:
  1.0 13.7 %collective-permute-start.3 = (f32[832,128]{1,0:T(8,128)S(1)}, f32[832,128]{1,0:T(8,128)S(1)}, u32[]{:S(2)}, u32[]{:S(2)}) collective-permute-start(f32[832,128]{1,0:T(8,128)S(1)} %slice.16.refs_1_), channel_id=1, source_target_pairs={{8,0},{16,8},{24,16},{28,24},{20,28},{12,20},{4,12},{0,4},{9,1},{1... | collective-permute-start | bytes 1277960 | tf_op jit(solution)/shard_map/ppermute | solution.py:393
  4.0 12.7 %collective-permute-start.1 = (f32[832,128]{1,0:T(8,128)S(1)}, f32[832,128]{1,0:T(8,128)S(1)}, u32[]{:S(2)}, u32[]{:S(2)}) collective-permute-start(f32[832,128]{1,0:T(8,128)S(1)} %slice.16.refs_1_), channel_id=1, source_target_pairs={{0,8},{8,16},{16,24},{24,28},{28,20},{20,12},{12,4},{4,0},{1,9},{9... | collective-permute-start | bytes 1277960 | tf_op jit(solution)/shard_map/ppermute | solution.py:396
  5.2 20.0 %collective-permute-start = (f32[768,128]{1,0:T(8,128)S(1)}, f32[768,128]{1,0:T(8,128)S(1)}, u32[]{:S(2)}, u32[]{:S(2)}) collective-permute-start(f32[768,128]{1,0:T(8,128)S(1)} %slice.15.refs_0_), channel_id=1, source_target_pairs={{0,8},{8,16},{16,24},{24,28},{28,20},{20,12},{12,4},{4,0},{1,9},{9... | collective-permute-start | bytes 1179656 | tf_op jit(solution)/shard_map/ppermute | solution.py:396
  7.2 18.0 %collective-permute-start.2 = (f32[768,128]{1,0:T(8,128)S(1)}, f32[768,128]{1,0:T(8,128)S(1)}, u32[]{:S(2)}, u32[]{:S(2)}) collective-permute-start(f32[768,128]{1,0:T(8,128)S(1)} %slice.15.refs_0_), channel_id=1, source_target_pairs={{8,0},{16,8},{24,16},{28,24},{20,28},{12,20},{4,12},{0,4},{9,1},{1... | collective-permute-start | bytes 1179656 | tf_op jit(solution)/shard_map/ppermute | solution.py:393
  14.8 17.6 %collective-permute-start.7 = (f32[832,128]{1,0:T(8,128)S(1)}, f32[832,128]{1,0:T(8,128)S(1)}, u32[]{:S(2)}, u32[]{:S(2)}) collective-permute-start(f32[832,128]{1,0:T(8,128)S(1)} %collective-permute-done.3.refs_3_), channel_id=1, source_target_pairs={{8,0},{16,8},{24,16},{28,24},{20,28},{12,20},{4,12},{0,4},{9,1},{1... | collective-permute-start | bytes 1277960 | tf_op jit(solution)/shard_map/ppermute | solution.py:393
  16.8 17.6 %collective-permute-start.6 = (f32[832,128]{1,0:T(8,128)S(1)}, f32[832,128]{1,0:T(8,128)S(1)}, u32[]{:S(2)}, u32[]{:S(2)}) collective-permute-start(f32[832,128]{1,0:T(8,128)S(1)} %collective-permute-done.1.refs_1_), channel_id=1, source_target_pairs={{0,8},{8,16},{16,24},{24,28},{28,20},{20,12},{12,4},{4,0},{1,9},{9... | collective-permute-start | bytes 1277960 | tf_op jit(solution)/shard_map/ppermute | solution.py:396
  16.9 1.8 %copy-start = (bf16[800,1600]{1,0:T(8,128)(2,1)S(1)}, bf16[800,1600]{1,0:T(8,128)(2,1)}, u32[]{:S(2)}) copy-start(bf16[800,1600]{1,0:T(8,128)(2,1)} %relation_ref.15) | copy-start | bytes 7680004
  25.2 15.5 %collective-permute-start.5 = (f32[768,128]{1,0:T(8,128)S(1)}, f32[768,128]{1,0:T(8,128)S(1)}, u32[]{:S(2)}, u32[]{:S(2)}) collective-permute-start(f32[768,128]{1,0:T(8,128)S(1)} %collective-permute-done.2.refs_2_), channel_id=1, source_target_pairs={{8,0},{16,8},{24,16},{28,24},{20,28},{12,20},{4,12},{0,4},{9,1},{1... | collective-permute-start | bytes 1179656 | tf_op jit(solution)/shard_map/ppermute | solution.py:393
  26.8 16.0 %collective-permute-start.4 = (f32[768,128]{1,0:T(8,128)S(1)}, f32[768,128]{1,0:T(8,128)S(1)}, u32[]{:S(2)}, u32[]{:S(2)}) collective-permute-start(f32[768,128]{1,0:T(8,128)S(1)} %collective-permute-done.refs_0_), channel_id=1, source_target_pairs={{0,8},{8,16},{16,24},{24,28},{28,20},{20,12},{12,4},{4,0},{1,9},{9... | collective-permute-start | bytes 1179656 | tf_op jit(solution)/shard_map/ppermute | solution.py:396
  32.3 20.2 %collective-permute-start.12 = (f32[832,128]{1,0:T(8,128)S(1)}, f32[832,128]{1,0:T(8,128)S(1)}, u32[]{:S(2)}, u32[]{:S(2)}) collective-permute-start(f32[832,128]{1,0:T(8,128)S(1)} %collective-permute-done.7.refs_1_), channel_id=1, source_target_pairs={{8,0},{16,8},{24,16},{28,24},{20,28},{12,20},{4,12},{0,4},{9,1},{1... | collective-permute-start | bytes 1277960 | tf_op jit(solution)/shard_map/ppermute | solution.py:393
  34.3 18.2 %collective-permute-start.11 = (f32[832,128]{1,0:T(8,128)S(1)}, f32[832,128]{1,0:T(8,128)S(1)}, u32[]{:S(2)}, u32[]{:S(2)}) collective-permute-start(f32[832,128]{1,0:T(8,128)S(1)} %collective-permute-done.6.refs_0_), channel_id=1, source_target_pairs={{0,8},{8,16},{16,24},{24,28},{28,20},{20,12},{12,4},{4,0},{1,9},{9... | collective-permute-start | bytes 1277960 | tf_op jit(solution)/shard_map/ppermute | solution.py:396
  35.5 9.9 %copy-start.1 = (bf16[800,1600]{1,0:T(8,128)(2,1)S(1)}, bf16[800,1600]{1,0:T(8,128)(2,1)}, u32[]{:S(2)}) copy-start(bf16[800,1600]{1,0:T(8,128)(2,1)} %relation_ref.15) | copy-start | bytes 7680004
  43.8 8.6 %collective-permute-start.8 = (f32[800,128]{1,0:T(8,128)S(1)}, f32[800,128]{1,0:T(8,128)S(1)}, u32[]{:S(2)}, u32[]{:S(2)}) collective-permute-start(f32[800,128]{1,0:T(8,128)S(1)} %get-tuple-element.66), channel_id=1, source_target_pairs={{0,2},{1,3},{2,0},{3,1},{4,6},{5,7},{6,4},{7,5},{8,10},{9,11},{10,... | collective-permute-start | bytes 1228808 | tf_op jit(solution)/shard_map/ppermute | solution.py:414
  47.1 11.7 %collective-permute-start.9 = (f32[768,128]{1,0:T(8,128)S(1)}, f32[768,128]{1,0:T(8,128)S(1)}, u32[]{:S(2)}, u32[]{:S(2)}) collective-permute-start(f32[768,128]{1,0:T(8,128)S(1)} %collective-permute-done.4.refs_0_), channel_id=1, source_target_pairs={{0,8},{8,16},{16,24},{24,28},{28,20},{20,12},{12,4},{4,0},{1,9},{9... | collective-permute-start | bytes 1179656 | tf_op jit(solution)/shard_map/ppermute | solution.py:396
  47.7 11.5 %collective-permute-start.10 = (f32[768,128]{1,0:T(8,128)S(1)}, f32[768,128]{1,0:T(8,128)S(1)}, u32[]{:S(2)}, u32[]{:S(2)}) collective-permute-start(f32[768,128]{1,0:T(8,128)S(1)} %collective-permute-done.5.refs_1_), channel_id=1, source_target_pairs={{8,0},{16,8},{24,16},{28,24},{20,28},{12,20},{4,12},{0,4},{9,1},{1... | collective-permute-start | bytes 1179656 | tf_op jit(solution)/shard_map/ppermute | solution.py:393
  58.8 9.7 %collective-permute-start.19 = (f32[768,128]{1,0:T(8,128)S(1)}, f32[768,128]{1,0:T(8,128)S(1)}, u32[]{:S(2)}, u32[]{:S(2)}) collective-permute-start(f32[768,128]{1,0:T(8,128)S(1)} %collective-permute-done.9.refs_0_), channel_id=1, source_target_pairs={{0,8},{8,16},{16,24},{24,28},{28,20},{20,12},{12,4},{4,0},{1,9},{9... | collective-permute-start | bytes 1179656 | tf_op jit(solution)/shard_map/ppermute | solution.py:396
  60.5 10.5 %collective-permute-start.18 = (f32[832,128]{1,0:T(8,128)S(1)}, f32[832,128]{1,0:T(8,128)S(1)}, u32[]{:S(2)}, u32[]{:S(2)}) collective-permute-start(f32[832,128]{1,0:T(8,128)S(1)} %collective-permute-done.12.refs_1_), channel_id=1, source_target_pairs={{8,0},{16,8},{24,16},{28,24},{20,28},{12,20},{4,12},{0,4},{9,1},{1... | collective-permute-start | bytes 1277960 | tf_op jit(solution)/shard_map/ppermute | solution.py:393
  62.2 1.6 %collective-permute-start.15 = (f32[544,128]{1,0:T(8,128)S(1)}, f32[544,128]{1,0:T(8,128)S(1)}, u32[]{:S(2)}, u32[]{:S(2)}) collective-permute-start(f32[544,128]{1,0:T(8,128)S(1)} %get-tuple-element.109), channel_id=1, source_target_pairs={{0,1},{1,0},{2,3},{3,2},{4,5},{5,4},{6,7},{7,6},{8,9},{9,8},{10,11... | collective-permute-start | bytes 835592 | tf_op jit(solution)/shard_map/ppermute | solution.py:411
  62.3 1.9 %collective-permute-start.14 = (f32[544,128]{1,0:T(8,128)S(1)}, f32[544,128]{1,0:T(8,128)S(1)}, u32[]{:S(2)}, u32[]{:S(2)}) collective-permute-start(f32[544,128]{1,0:T(8,128)S(1)} %get-tuple-element.110), channel_id=1, source_target_pairs={{0,1},{1,0},{2,3},{3,2},{4,5},{5,4},{6,7},{7,6},{8,9},{9,8},{10,11... | collective-permute-start | bytes 835592 | tf_op jit(solution)/shard_map/ppermute | solution.py:411
  62.8 1.8 %collective-permute-start.13 = (f32[544,128]{1,0:T(8,128)S(1)}, f32[544,128]{1,0:T(8,128)S(1)}, u32[]{:S(2)}, u32[]{:S(2)}) collective-permute-start(f32[544,128]{1,0:T(8,128)S(1)} %get-tuple-element.111), channel_id=1, source_target_pairs={{0,1},{1,0},{2,3},{3,2},{4,5},{5,4},{6,7},{7,6},{8,9},{9,8},{10,11... | collective-permute-start | bytes 835592 | tf_op jit(solution)/shard_map/ppermute | solution.py:411
  64.7 13.8 %collective-permute-start.16 = (f32[816,128]{1,0:T(8,128)S(1)}, f32[816,128]{1,0:T(8,128)S(1)}, u32[]{:S(2)}, u32[]{:S(2)}) collective-permute-start(f32[816,128]{1,0:T(8,128)S(1)} %get-tuple-element.88), channel_id=1, source_target_pairs={{0,2},{1,3},{2,0},{3,1},{4,6},{5,7},{6,4},{7,5},{8,10},{9,11},{10,... | collective-permute-start | bytes 1253384 | tf_op jit(solution)/shard_map/ppermute | solution.py:414
  69.0 6.9 %copy-start.2 = (f32[1024]{0:T(1024)S(1)}, f32[1024]{0:T(1024)}, u32[]{:S(2)}) copy-start(f32[1024]{0:T(1024)} %one_ref.1) | copy-start | bytes 12292
  69.0 6.9 %copy-start.3 = (f32[1024]{0:T(1024)S(1)}, f32[1024]{0:T(1024)}, u32[]{:S(2)}) copy-start(f32[1024]{0:T(1024)} %two_ref.1) | copy-start | bytes 12292
  69.0 6.9 %copy-start.4 = (f32[1024]{0:T(1024)S(1)}, f32[1024]{0:T(1024)}, u32[]{:S(2)}) copy-start(f32[1024]{0:T(1024)} %scale_ref.1) | copy-start | bytes 12292
  71.8 1.5 %collective-permute-start.20 = (f32[400,128]{1,0:T(8,128)S(1)}, f32[400,128]{1,0:T(8,128)S(1)}, u32[]{:S(2)}, u32[]{:S(2)}) collective-permute-start(f32[400,128]{1,0:T(8,128)S(1)} %get-tuple-element.96), channel_id=1, source_target_pairs={{0,1},{1,0},{2,3},{3,2},{4,5},{5,4},{6,7},{7,6},{8,9},{9,8},{10,11... | collective-permute-start | bytes 614408 | tf_op jit(solution)/shard_map/ppermute | solution.py:411
  71.8 1.7 %collective-permute-start.21 = (f32[400,128]{1,0:T(8,128)S(1)}, f32[400,128]{1,0:T(8,128)S(1)}, u32[]{:S(2)}, u32[]{:S(2)}) collective-permute-start(f32[400,128]{1,0:T(8,128)S(1)} %get-tuple-element.97), channel_id=1, source_target_pairs={{0,1},{1,0},{2,3},{3,2},{4,5},{5,4},{6,7},{7,6},{8,9},{9,8},{10,11... | collective-permute-start | bytes 614408 | tf_op jit(solution)/shard_map/ppermute | solution.py:411
  72.3 8.8 %collective-permute-start.17 = (f32[800,128]{1,0:T(8,128)S(1)}, f32[800,128]{1,0:T(8,128)S(1)}, u32[]{:S(2)}, u32[]{:S(2)}) collective-permute-start(f32[800,128]{1,0:T(8,128)S(1)} %shard_map.60.two_sum), channel_id=1, source_target_pairs={{0,1},{1,0},{2,3},{3,2},{4,5},{5,4},{6,7},{7,6},{8,9},{9,8},{10,11... | collective-permute-start | bytes 1228808 | tf_op jit(solution)/shard_map/ppermute | solution.py:411
  73.6 7.4 %collective-permute-start.24 = (f32[200,128]{1,0:T(8,128)S(1)}, f32[200,128]{1,0:T(8,128)S(1)}, u32[]{:S(2)}, u32[]{:S(2)}) collective-permute-start(f32[200,128]{1,0:T(8,128)S(1)} %get-tuple-element.106), channel_id=1, source_target_pairs={{0,2},{1,3},{2,0},{3,1},{4,6},{5,7},{6,4},{7,5},{8,10},{9,11},{10,... | collective-permute-start | bytes 307208 | tf_op jit(solution)/shard_map/ppermute | solution.py:414
  75.0 6.1 %collective-permute-start.25 = (f32[200,128]{1,0:T(8,128)S(1)}, f32[200,128]{1,0:T(8,128)S(1)}, u32[]{:S(2)}, u32[]{:S(2)}) collective-permute-start(f32[200,128]{1,0:T(8,128)S(1)} %get-tuple-element.107), channel_id=1, source_target_pairs={{0,2},{1,3},{2,0},{3,1},{4,6},{5,7},{6,4},{7,5},{8,10},{9,11},{10,... | collective-permute-start | bytes 307208 | tf_op jit(solution)/shard_map/ppermute | solution.py:414
  75.9 1.2 %collective-permute-start.22 = (f32[4,896]{1,0:T(4,128)S(1)}, f32[4,896]{1,0:T(4,128)S(1)}, u32[]{:S(2)}, u32[]{:S(2)}) collective-permute-start(f32[4,896]{1,0:T(4,128)S(1)} %get-tuple-element.103), channel_id=1, source_target_pairs={{0,1},{1,0},{2,3},{3,2},{4,5},{5,4},{6,7},{7,6},{8,9},{9,8},{10,11... | collective-permute-start | bytes 43016 | tf_op jit(solution)/shard_map/ppermute | solution.py:411
  77.1 3.9 %collective-permute-start.23 = (f32[2,896]{1,0:T(2,128)S(1)}, f32[2,896]{1,0:T(2,128)S(1)}, u32[]{:S(2)}, u32[]{:S(2)}) collective-permute-start(f32[2,896]{1,0:T(2,128)S(1)} %get-tuple-element.104), channel_id=1, source_target_pairs={{0,2},{1,3},{2,0},{3,1},{4,6},{5,7},{6,4},{7,5},{8,10},{9,11},{10,... | collective-permute-start | bytes 21512 | tf_op jit(solution)/shard_map/ppermute | solution.py:414
  81.1 1.5 %collective-permute-start.26 = (f32[400,128]{1,0:T(8,128)S(1)}, f32[400,128]{1,0:T(8,128)S(1)}, u32[]{:S(2)}, u32[]{:S(2)}) collective-permute-start(f32[400,128]{1,0:T(8,128)S(1)} %shard_map.73.zero_half), channel_id=1, source_target_pairs={{0,1},{1,0},{2,3},{3,2},{4,5},{5,4},{6,7},{7,6},{8,9},{9,8},{10,11... | collective-permute-start | bytes 614408 | tf_op jit(solution)/shard_map/ppermute | solution.py:411

commit v8 on v7

--- a/solution.py
+++ b/solution.py
@@ -14,13 +14,13 @@
 WHOLE = pl.BlockSpec(memory_space=pltpu.VMEM)
 
 
-def call(kernel, shapes, operands, scratch=(), flops=0, into=WHOLE, last=0):
+def call(kernel, shapes, operands, scratch=(), flops=0, into=None, last=0):
     return pl.pallas_call(
         kernel,
         out_shape=[jax.ShapeDtypeStruct(shape, jnp.float32) for shape in shapes],
-        in_specs=[WHOLE] * (len(operands) - last) + [into] * last,
+        in_specs=[WHOLE] * (len(operands) - last) + (into[:last] if last else []),
         input_output_aliases={len(operands) - last + n: n for n in range(last)},
-        out_specs=[into] * len(shapes),
+        out_specs=into or [WHOLE] * len(shapes),
         scratch_shapes=scratch,
         compiler_params=pltpu.CompilerParams(vmem_limit_bytes=VMEM_LIMIT),
         cost_estimate=pl.CostEstimate(flops=flops, bytes_accessed=0, transcendentals=0),
@@ -178,17 +178,10 @@
                 keep_ref[pl.ds(n * rows, rows)] = ref[pl.ds(pl.multiple_of(core * rows, 8), rows)]
 
 
-def half_sums_kernel(keep_ref, got_ours, got_theirs, first_ref, second_ref, mine_ref):
-    rows, piece = mine_ref.shape[0], first_ref.shape[0]
+def half_sums_kernel(keep_ref, got_ours, got_theirs, send_ref, mine_ref):
+    rows = mine_ref.shape[0]
     mine_ref[...] = keep_ref[:rows] + got_ours[...]
-    first_ref[...] = keep_ref[rows : rows + piece] + got_theirs[:piece]
-    second_ref[...] = keep_ref[rows + piece :] + got_theirs[piece:]
-
-
-def pieces_sum_kernel(one_ref, first_ref, second_ref, out_ref):
-    piece = first_ref.shape[0]
-    out_ref[:piece] = one_ref[:piece] + first_ref[...]
-    out_ref[piece:] = one_ref[piece:] + second_ref[...]
+    send_ref[...] = keep_ref[rows:] + got_theirs[...]
 
 
 def chip_pair_kernel(spot_of, near, near_ref, far_ref, send_ref, keep_ref):
@@ -333,7 +326,7 @@
     weights_ref,
     *refs,
 ):
-    out_any, even_ref, sides_ref, made_ref, sems = refs[-5:]
+    out_any, sides_ref, even_ref, made_ref, sems = refs[-5:] if same else (refs[-4], refs[0], *refs[-3:])
     spot = spot_of()
     odd = odd_column(spot)
     rows = out_any.shape[0] // 2
@@ -352,7 +345,8 @@
 
     weights = column_weights(spot, weights_ref, 1 - odd)
     others = column_weights(spot, weights_ref, odd)
-    sides_ref[...] = beside(weights, border_mine[...] + border_got[...], odd == 1)
+    if same:
+        sides_ref[...] = beside(weights, border_mine[...] + border_got[...], odd == 1)
     pieces = 5
     step = rows // pieces
     copies = []
@@ -511,9 +505,9 @@
         [products[far][0] for far in (0, half)],
         flops=KERNEL_FLOPS // 2,
     )
-    first, second, zero_mine = call(
+    zero_send, zero_mine = call(
         half_sums_kernel,
-        [(rows // 4, WIDTH)] * 2 + [(rows // 2, WIDTH)],
+        [(rows // 2, WIDTH)] * 2,
         (keep, over_cores(send_ours), over_cores(send_theirs)),
         flops=KERNEL_FLOPS // 10,
     )
@@ -526,28 +520,34 @@
         flops=KERNEL_FLOPS,
     )
     zero_sum = call(
-        pieces_sum_kernel,
+        sum_kernel,
         [(rows // 2, WIDTH)],
-        (tied(zero_mine, border_got, odd_own), over_y(first), over_y(second)),
+        (tied(zero_mine, border_got, odd_own), over_y(zero_send)),
         flops=KERNEL_FLOPS // 10,
     )[0]
     zero_got = over_cores(zero_sum)
-    applied = ()
-    for same, zero_half in ((True, zero_sum), (False, zero_got)):
-        applied = call(
-            functools.partial(last_kernel, spot_of, same),
-            [(rows, share * WIDTH)],
-            (odd_own, odd_beyond, two_sum, two_got, zero_half, border_mine, border_got, weights, *applied),
-            [
-                pltpu.VMEM((rows // 2, WIDTH), jnp.float32),
-                pltpu.VMEM((wide, WIDTH), jnp.float32),
-                pltpu.VMEM((2, rows // 2, WIDTH), jnp.float32),
-                pltpu.SemaphoreType.DMA((10,)),
-            ],
-            into=pl.BlockSpec(memory_space=pl.ANY),
-            last=len(applied),
-        )
-    return applied[0]
+    anywhere = pl.BlockSpec(memory_space=pl.ANY)
+    given = (odd_own, odd_beyond, two_sum, two_got)
+    scratch = [
+        pltpu.VMEM((rows // 2, WIDTH), jnp.float32),
+        pltpu.VMEM((2, rows // 2, WIDTH), jnp.float32),
+        pltpu.SemaphoreType.DMA((10,)),
+    ]
+    applied, sides = call(
+        functools.partial(last_kernel, spot_of, True),
+        [(rows, share * WIDTH), (wide, WIDTH)],
+        (*given, zero_sum, border_mine, border_got, weights),
+        scratch,
+        into=[anywhere, WHOLE],
+    )
+    return call(
+        functools.partial(last_kernel, spot_of, False),
+        [(rows, share * WIDTH)],
+        (*given, zero_got, border_mine, border_got, weights, sides, applied),
+        scratch,
+        into=[anywhere],
+        last=1,
+    )[0]
 
 
 def extended(cells, sides, width):

time: 84.1 us -> 83.8 us (level)
  starting transfers between devices: 23.6 us -> 22.7 us
  waiting for transfers between devices: 44 us -> 44.9 us
    ppermute x5 -> x4, starting transfers between devices: 6.61 us -> 5.31 us  [over_y(): return lax.ppermute(x, 'tm', [(t, t ^ 2) for t in range(tms)])]
    ppermute x5 -> x4, waiting for transfers between devices: 4.98 us -> 5.92 us  [over_y(): return lax.ppermute(x, 'tm', [(t, t ^ 2) for t in range(tms)])]
  transfers between devices with their start and end apart: 27 -> 26, of which waited for: 17 -> 17; matrix products, arithmetic and copies ran while one was open for 1% -> 1% of each run, Pallas kernels for 13% -> 13%
where the time goes in v8:
time: 83.8 us; the launch traced here: 83.6 us
  waiting for transfers between devices  44.9 us (54%)
  starting transfers between devices  22.7 us (27%)
  Pallas kernels  11.8 us (14%)
  local copies, waits for them, and re-layouts  3.89 us (5%)
    ppermute x7, waiting for transfers between devices, ahead_of(): return lax.ppermute(x, 'gen', backward)  19.8 us
    ppermute x7, waiting for transfers between devices, behind_of(): return lax.ppermute(x, 'gen', forward)  15.2 us
    pallas_call x21, Pallas kernels, call(): pl.pallas_call(kernel, out_shape=[jax.ShapeDtypeStruct(shape, jnp.float32...  11.8 us
    ppermute x7, starting transfers between devices, ahead_of(): return lax.ppermute(x, 'gen', backward)  11.7 us
    ppermute x4, waiting for transfers between devices, over_y(): return lax.ppermute(x, 'tm', [(t, t ^ 2) for t in range(tms)])  5.92 us
    ppermute x4, starting transfers between devices, over_y(): return lax.ppermute(x, 'tm', [(t, t ^ 2) for t in range(tms)])  5.31 us
    ppermute x8, waiting for transfers between devices, over_cores(): return lax.ppermute(x, 'tm', swap)  4.05 us
    ppermute x7, starting transfers between devices, behind_of(): return lax.ppermute(x, 'gen', forward)  3.85 us
  transfers between devices with their start and end apart: 26, of which 17 were waited for; matrix products, arithmetic and copies ran while one was open for 1% of the time, Pallas kernels for 13%

profile of v8, /device:TPU:0, one launch (start us, length us, event | category | flops | bytes accessed | tf_op | source)
XLA Modules:
  0.0 83.6 jit_solution(16644858358434050895)
XLA Ops:
  0.0 1.0 %slice.16.refs_1_ = f32[832,128]{1,0:T(8,128)S(1)} slice(f32[1600,128]{1,0:T(8,128)} %param.6), slice={[768:1600], [0:128]} | slice | bytes 851968 | tf_op jit(solution)/shard_map/slice | solution.py:430
  1.0 3.0 %collective-permute-start.3 = (f32[832,128]{1,0:T(8,128)S(1)}, f32[832,128]{1,0:T(8,128)S(1)}, u32[]{:S(2)}, u32[]{:S(2)}) collective-permute-start(f32[832,128]{1,0:T(8,128)S(1)} %slice.16.refs_1_), channel_id=1, source_target_pairs={{8,0},{16,8},{24,16},{28,24},{20,28},{12,20},{4,12},{0,4},{9,1},{1... | collective-permute-start | bytes 1277960 | tf_op jit(solution)/shard_map/ppermute | solution.py:387
  4.2 1.0 %slice.15.refs_0_ = f32[768,128]{1,0:T(8,128)S(1)} slice(f32[1600,128]{1,0:T(8,128)} %param.6), slice={[0:768], [0:128]} | slice | bytes 786432 | tf_op jit(solution)/shard_map/slice | solution.py:430
  5.2 2.0 %collective-permute-start = (f32[768,128]{1,0:T(8,128)S(1)}, f32[768,128]{1,0:T(8,128)S(1)}, u32[]{:S(2)}, u32[]{:S(2)}) collective-permute-start(f32[768,128]{1,0:T(8,128)S(1)} %slice.15.refs_0_), channel_id=1, source_target_pairs={{0,8},{8,16},{16,24},{24,28},{28,20},{20,12},{12,4},{4,0},{1,9},{9... | collective-permute-start | bytes 1179656 | tf_op jit(solution)/shard_map/ppermute | solution.py:390
  7.3 7.5 %collective-permute-done.3.refs_3_ = f32[832,128]{1,0:T(8,128)S(1)} collective-permute-done((f32[832,128]{1,0:T(8,128)S(1)}, f32[832,128]{1,0:T(8,128)S(1)}, u32[]{:S(2)}, u32[]{:S(2)}) %collective-permute-start.3) | collective-permute-done | bytes 426016 | tf_op jit(solution)/shard_map/ppermute | solution.py:387
  14.8 2.0 %collective-permute-start.7 = (f32[832,128]{1,0:T(8,128)S(1)}, f32[832,128]{1,0:T(8,128)S(1)}, u32[]{:S(2)}, u32[]{:S(2)}) collective-permute-start(f32[832,128]{1,0:T(8,128)S(1)} %collective-permute-done.3.refs_3_), channel_id=1, source_target_pairs={{8,0},{16,8},{24,16},{28,24},{20,28},{12,20},{4,12},{0,4},{9,1},{1... | collective-permute-start | bytes 1277960 | tf_op jit(solution)/shard_map/ppermute | solution.py:387
  16.9 1.7 %copy-done = bf16[800,1600]{1,0:T(8,128)(2,1)S(1)} copy-done((bf16[800,1600]{1,0:T(8,128)(2,1)S(1)}, bf16[800,1600]{1,0:T(8,128)(2,1)}, u32[]{:S(2)}) %copy-start) | copy-done | bytes 2560024
  18.6 1.0 %shard_map.56 = (f32[800,128]{1,0:T(8,128)S(1)}, f32[4,896]{1,0:T(4,128)S(1)}) custom-call(bf16[800,1600]{1,0:T(8,128)(2,1)S(1)} %copy-done, f32[768,128]{1,0:T(8,128)S(1)} %slice.15.refs_0_, f32[832,128]{1,0:T(8,128)S(1)} %slice.16.refs_1_), custom_call_target="tpu_custom_call" | custom-call | flops 100000000 | tf_op jit(solution)/shard_map/pallas_call | solution.py:18
  19.6 5.6 %collective-permute-done.refs_0_ = f32[768,128]{1,0:T(8,128)S(1)} collective-permute-done((f32[768,128]{1,0:T(8,128)S(1)}, f32[768,128]{1,0:T(8,128)S(1)}, u32[]{:S(2)}, u32[]{:S(2)}) %collective-permute-start) | collective-permute-done | bytes 393248 | tf_op jit(solution)/shard_map/ppermute | solution.py:390
  25.2 1.6 %collective-permute-start.5 = (f32[768,128]{1,0:T(8,128)S(1)}, f32[768,128]{1,0:T(8,128)S(1)}, u32[]{:S(2)}, u32[]{:S(2)}) collective-permute-start(f32[768,128]{1,0:T(8,128)S(1)} %collective-permute-done.2.refs_2_), channel_id=1, source_target_pairs={{8,0},{16,8},{24,16},{28,24},{20,28},{12,20},{4,12},{0,4},{9,1},{1... | collective-permute-start | bytes 1179656 | tf_op jit(solution)/shard_map/ppermute | solution.py:387
  26.8 0.4 collective-permute-start.4
  27.2 5.1 %collective-permute-done.7.refs_1_ = f32[832,128]{1,0:T(8,128)S(1)} collective-permute-done((f32[832,128]{1,0:T(8,128)S(1)}, f32[832,128]{1,0:T(8,128)S(1)}, u32[]{:S(2)}, u32[]{:S(2)}) %collective-permute-start.7) | collective-permute-done | bytes 426016 | tf_op jit(solution)/shard_map/ppermute | solution.py:387
  32.3 2.0 %collective-permute-start.12 = (f32[832,128]{1,0:T(8,128)S(1)}, f32[832,128]{1,0:T(8,128)S(1)}, u32[]{:S(2)}, u32[]{:S(2)}) collective-permute-start(f32[832,128]{1,0:T(8,128)S(1)} %collective-permute-done.7.refs_1_), channel_id=1, source_target_pairs={{8,0},{16,8},{24,16},{28,24},{20,28},{12,20},{4,12},{0,4},{9,1},{1... | collective-permute-start | bytes 1277960 | tf_op jit(solution)/shard_map/ppermute | solution.py:387
  34.4 1.0 %shard_map.57 = (f32[800,128]{1,0:T(8,128)S(1)}, f32[800,128]{1,0:T(8,128)S(1)}) custom-call(bf16[800,1600]{1,0:T(8,128)(2,1)S(1)} %copy-done, f32[832,128]{1,0:T(8,128)S(1)} %collective-permute-done.6.refs_0_, f32[832,128]{1,0:T(8,128)S(1)} %collective-permute-done.7.refs_1_), custom_call_target="tpu_custom_call" | custom-call | flops 100000000 | tf_op jit(solution)/shard_map/pallas_call | solution.py:18
  35.5 5.3 %collective-permute-done.5.refs_1_ = f32[768,128]{1,0:T(8,128)S(1)} collective-permute-done((f32[768,128]{1,0:T(8,128)S(1)}, f32[768,128]{1,0:T(8,128)S(1)}, u32[]{:S(2)}, u32[]{:S(2)}) %collective-permute-start.5) | collective-permute-done | bytes 393248 | tf_op jit(solution)/shard_map/ppermute | solution.py:387
  40.7 2.0 %collective-permute-done.4.refs_0_ = f32[768,128]{1,0:T(8,128)S(1)} collective-permute-done((f32[768,128]{1,0:T(8,128)S(1)}, f32[768,128]{1,0:T(8,128)S(1)}, u32[]{:S(2)}, u32[]{:S(2)}) %collective-permute-start.4) | collective-permute-done | bytes 393248 | tf_op jit(solution)/shard_map/ppermute | solution.py:390
  42.8 0.9 %shard_map.58 = (f32[800,128]{1,0:T(8,128)S(1)}, f32[4,896]{1,0:T(4,128)S(1)}, f32[800,128]{1,0:T(8,128)S(1)}, f32[4,896]{1,0:T(4,128)S(1)}) custom-call(bf16[800,1600]{1,0:T(8,128)(2,1)S(1)} %copy-done, f32[768,128]{1,0:T(8,128)S(1)} %collective-permute-done.4.refs_0_, f32[768,128]{1,0:T(8,128)S(1)} %collective-permute-done.5.refs_1_, ...), custom_call_target="tpu_custom_call" | custom-call | flops 100000000 | tf_op jit(solution)/shard_map/pallas_call | solution.py:18
  43.8 1.6 %collective-permute-start.8 = (f32[800,128]{1,0:T(8,128)S(1)}, f32[800,128]{1,0:T(8,128)S(1)}, u32[]{:S(2)}, u32[]{:S(2)}) collective-permute-start(f32[800,128]{1,0:T(8,128)S(1)} %get-tuple-element.67), channel_id=1, source_target_pairs={{0,2},{1,3},{2,0},{3,1},{4,6},{5,7},{6,4},{7,5},{8,10},{9,11},{10,... | collective-permute-start | bytes 1228808 | tf_op jit(solution)/shard_map/ppermute | solution.py:408
  45.4 1.8 %shard_map.55 = (f32[800,128]{1,0:T(8,128)S(1)}, f32[4,896]{1,0:T(4,128)S(1)}, f32[800,128]{1,0:T(8,128)S(1)}, f32[4,896]{1,0:T(4,128)S(1)}) custom-call(bf16[800,1600]{1,0:T(8,128)(2,1)S(1)} %copy-done.1, f32[768,128]{1,0:T(8,128)S(1)} %collective-permute-done.refs_0_, f32[832,128]{1,0:T(8,128)S(1)} %collective-permute-done.1.refs_1_, ...), custom_call_target="tpu_custom_call" | custom-call | flops 200000000 | tf_op jit(solution)/shard_map/pallas_call | solution.py:18
  47.1 0.6 collective-permute-start.9
  47.7 1.5 %collective-permute-start.10 = (f32[768,128]{1,0:T(8,128)S(1)}, f32[768,128]{1,0:T(8,128)S(1)}, u32[]{:S(2)}, u32[]{:S(2)}) collective-permute-start(f32[768,128]{1,0:T(8,128)S(1)} %collective-permute-done.5.refs_1_), channel_id=1, source_target_pairs={{8,0},{16,8},{24,16},{28,24},{20,28},{12,20},{4,12},{0,4},{9,1},{1... | collective-permute-start | bytes 1179656 | tf_op jit(solution)/shard_map/ppermute | solution.py:387
  49.2 3.2 %collective-permute-done.8.other_ref = f32[800,128]{1,0:T(8,128)S(1)} collective-permute-done((f32[800,128]{1,0:T(8,128)S(1)}, f32[800,128]{1,0:T(8,128)S(1)}, u32[]{:S(2)}, u32[]{:S(2)}) %collective-permute-start.8) | collective-permute-done | bytes 409632 | tf_op jit(solution)/shard_map/ppermute | solution.py:408
  52.5 1.0 %shard_map.61 = (f32[800,128]{1,0:T(8,128)S(1)}, f32[800,128]{1,0:T(8,128)S(1)}) custom-call(bf16[800,1600]{1,0:T(8,128)(2,1)S(1)} %copy-done.1, f32[832,128]{1,0:T(8,128)S(1)} %collective-permute-done.11.refs_0_, f32[832,128]{1,0:T(8,128)S(1)} %collective-permute-done.12.refs_1_), custom_call_target="tpu_custom_call" | custom-call | flops 100000000 | tf_op jit(solution)/shard_map/pallas_call | solution.py:18
  53.5 5.3 %collective-permute-done.9.refs_0_ = f32[768,128]{1,0:T(8,128)S(1)} collective-permute-done((f32[768,128]{1,0:T(8,128)S(1)}, f32[768,128]{1,0:T(8,128)S(1)}, u32[]{:S(2)}, u32[]{:S(2)}) %collective-permute-start.9) | collective-permute-done | bytes 393248 | tf_op jit(solution)/shard_map/ppermute | solution.py:390
  58.8 0.4 collective-permute-start.19
  59.3 0.9 %shard_map.62 = (f32[800,128]{1,0:T(8,128)S(1)}, f32[4,896]{1,0:T(4,128)S(1)}, f32[800,128]{1,0:T(8,128)S(1)}, f32[4,896]{1,0:T(4,128)S(1)}) custom-call(bf16[800,1600]{1,0:T(8,128)(2,1)S(1)} %copy-done.1, f32[768,128]{1,0:T(8,128)S(1)} %collective-permute-done.9.refs_0_, f32[768,128]{1,0:T(8,128)S(1)} %collective-permute-done.10.refs_1_, ...), custom_call_target="tpu_custom_call" | custom-call | flops 1000000000 | tf_op jit(solution)/shard_map/pallas_call | solution.py:18
  60.2 0.3 shard_map.63
  60.5 1.7 %collective-permute-start.18 = (f32[832,128]{1,0:T(8,128)S(1)}, f32[832,128]{1,0:T(8,128)S(1)}, u32[]{:S(2)}, u32[]{:S(2)}) collective-permute-start(f32[832,128]{1,0:T(8,128)S(1)} %collective-permute-done.12.refs_1_), channel_id=1, source_target_pairs={{8,0},{16,8},{24,16},{28,24},{20,28},{12,20},{4,12},{0,4},{9,1},{1... | collective-permute-start | bytes 1277960 | tf_op jit(solution)/shard_map/ppermute | solution.py:387
  62.3 0.5 collective-permute-start.14
  62.9 1.0 %collective-permute-done.15.refs_2_ = f32[544,128]{1,0:T(8,128)S(1)} collective-permute-done((f32[544,128]{1,0:T(8,128)S(1)}, f32[544,128]{1,0:T(8,128)S(1)}, u32[]{:S(2)}, u32[]{:S(2)}) %collective-permute-start.15) | collective-permute-done | bytes 278560 | tf_op jit(solution)/shard_map/ppermute | solution.py:405
  63.9 0.4 collective-permute-done.14.refs_1_
  64.3 0.4 collective-permute-done.13.refs_0_
  64.8 1.6 %collective-permute-start.16 = (f32[816,128]{1,0:T(8,128)S(1)}, f32[816,128]{1,0:T(8,128)S(1)}, u32[]{:S(2)}, u32[]{:S(2)}) collective-permute-start(f32[816,128]{1,0:T(8,128)S(1)} %get-tuple-element.89), channel_id=1, source_target_pairs={{0,2},{1,3},{2,0},{3,1},{4,6},{5,7},{6,4},{7,5},{8,10},{9,11},{10,... | collective-permute-start | bytes 1253384 | tf_op jit(solution)/shard_map/ppermute | solution.py:408
  66.3 2.2 %collective-permute-done.19.refs_0_ = f32[768,128]{1,0:T(8,128)S(1)} collective-permute-done((f32[768,128]{1,0:T(8,128)S(1)}, f32[768,128]{1,0:T(8,128)S(1)}, u32[]{:S(2)}, u32[]{:S(2)}) %collective-permute-start.19) | collective-permute-done | bytes 393248 | tf_op jit(solution)/shard_map/ppermute | solution.py:390
  68.5 0.5 shard_map.67.refs_1_
  69.0 1.9 %collective-permute-done.18.refs_0_ = f32[832,128]{1,0:T(8,128)S(1)} collective-permute-done((f32[832,128]{1,0:T(8,128)S(1)}, f32[832,128]{1,0:T(8,128)S(1)}, u32[]{:S(2)}, u32[]{:S(2)}) %collective-permute-start.18) | collective-permute-done | bytes 426016 | tf_op jit(solution)/shard_map/ppermute | solution.py:387
  71.0 0.7 shard_map.68
  71.8 0.5 collective-permute-start.21
  72.3 0.9 %collective-permute-done.20.got_ours = f32[400,128]{1,0:T(8,128)S(1)} collective-permute-done((f32[400,128]{1,0:T(8,128)S(1)}, f32[400,128]{1,0:T(8,128)S(1)}, u32[]{:S(2)}, u32[]{:S(2)}) %collective-permute-start.20) | collective-permute-done | bytes 204832 | tf_op jit(solution)/shard_map/ppermute | solution.py:405
  73.3 0.3 collective-permute-done.21.got_theirs
  73.6 1.4 %collective-permute-start.24 = (f32[400,128]{1,0:T(8,128)S(1)}, f32[400,128]{1,0:T(8,128)S(1)}, u32[]{:S(2)}, u32[]{:S(2)}) collective-permute-start(f32[400,128]{1,0:T(8,128)S(1)} %get-tuple-element.107), channel_id=1, source_target_pairs={{0,2},{1,3},{2,0},{3,1},{4,6},{5,7},{6,4},{7,5},{8,10},{9,11},{10,... | collective-permute-start | bytes 614408 | tf_op jit(solution)/shard_map/ppermute | solution.py:408
  75.2 0.6 collective-permute-start.22
  75.9 0.9 %collective-permute-done.22.got_ref = f32[4,896]{1,0:T(4,128)S(1)} collective-permute-done((f32[4,896]{1,0:T(4,128)S(1)}, f32[4,896]{1,0:T(4,128)S(1)}, u32[]{:S(2)}, u32[]{:S(2)}) %collective-permute-start.22) | collective-permute-done | bytes 14368 | tf_op jit(solution)/shard_map/ppermute | solution.py:405
  76.8 0.8 collective-permute-start.23
  77.6 0.7 shard_map.66
  78.3 2.7 %collective-permute-done.23.border_got = f32[2,896]{1,0:T(2,128)S(1)} collective-permute-done((f32[2,896]{1,0:T(2,128)S(1)}, f32[2,896]{1,0:T(2,128)S(1)}, u32[]{:S(2)}, u32[]{:S(2)}) %collective-permute-start.23) | collective-permute-done | bytes 7200 | tf_op jit(solution)/shard_map/ppermute | solution.py:408
  81.2 1.3 %shard_map.74 = (f32[800,256]{1,0:T(8,128)}, f32[896,128]{1,0:T(8,128)S(1)}) custom-call(f32[800,128]{1,0:T(8,128)S(1)} %get-tuple-element.90.odd_own, f32[800,128]{1,0:T(8,128)S(1)} %get-tuple-element.91.odd_beyond, f32[800,128]{1,0:T(8,128)S(1)} %shard_map.60.two_sum, f32[800,128]{1,0:T(8,128)S(1)} %collective-permute-done.17.two_got, ...), custom_call_target="tpu_custom_call" | custom-call | tf_op jit(solution)/shard_map/pallas_call | solution.py:18
  82.6 1.0 %shard_map.75 = f32[800,256]{1,0:T(8,128)} custom-call(f32[800,128]{1,0:T(8,128)S(1)} %get-tuple-element.90.odd_own, f32[800,128]{1,0:T(8,128)S(1)} %get-tuple-element.91.odd_beyond, f32[800,128]{1,0:T(8,128)S(1)} %shard_map.60.two_sum, f32[800,128]{1,0:T(8,128)S(1)} %collective-permute-done.17.two_got, ...), custom_call_target="tpu_custom_call", output_to_operand_aliasing={{}: (9, {})} | custom-call | tf_op jit(solution)/shard_map/pallas_call | solution.py:18
  (38 shorter events, 1.7 us)
Async XLA Ops:
  1.0 13.7 %collective-permute-start.3 = (f32[832,128]{1,0:T(8,128)S(1)}, f32[832,128]{1,0:T(8,128)S(1)}, u32[]{:S(2)}, u32[]{:S(2)}) collective-permute-start(f32[832,128]{1,0:T(8,128)S(1)} %slice.16.refs_1_), channel_id=1, source_target_pairs={{8,0},{16,8},{24,16},{28,24},{20,28},{12,20},{4,12},{0,4},{9,1},{1... | collective-permute-start | bytes 1277960 | tf_op jit(solution)/shard_map/ppermute | solution.py:387
  4.0 12.7 %collective-permute-start.1 = (f32[832,128]{1,0:T(8,128)S(1)}, f32[832,128]{1,0:T(8,128)S(1)}, u32[]{:S(2)}, u32[]{:S(2)}) collective-permute-start(f32[832,128]{1,0:T(8,128)S(1)} %slice.16.refs_1_), channel_id=1, source_target_pairs={{0,8},{8,16},{16,24},{24,28},{28,20},{20,12},{12,4},{4,0},{1,9},{9... | collective-permute-start | bytes 1277960 | tf_op jit(solution)/shard_map/ppermute | solution.py:390
  5.2 20.0 %collective-permute-start = (f32[768,128]{1,0:T(8,128)S(1)}, f32[768,128]{1,0:T(8,128)S(1)}, u32[]{:S(2)}, u32[]{:S(2)}) collective-permute-start(f32[768,128]{1,0:T(8,128)S(1)} %slice.15.refs_0_), channel_id=1, source_target_pairs={{0,8},{8,16},{16,24},{24,28},{28,20},{20,12},{12,4},{4,0},{1,9},{9... | collective-permute-start | bytes 1179656 | tf_op jit(solution)/shard_map/ppermute | solution.py:390
  7.2 18.0 %collective-permute-start.2 = (f32[768,128]{1,0:T(8,128)S(1)}, f32[768,128]{1,0:T(8,128)S(1)}, u32[]{:S(2)}, u32[]{:S(2)}) collective-permute-start(f32[768,128]{1,0:T(8,128)S(1)} %slice.15.refs_0_), channel_id=1, source_target_pairs={{8,0},{16,8},{24,16},{28,24},{20,28},{12,20},{4,12},{0,4},{9,1},{1... | collective-permute-start | bytes 1179656 | tf_op jit(solution)/shard_map/ppermute | solution.py:387
  14.8 17.6 %collective-permute-start.7 = (f32[832,128]{1,0:T(8,128)S(1)}, f32[832,128]{1,0:T(8,128)S(1)}, u32[]{:S(2)}, u32[]{:S(2)}) collective-permute-start(f32[832,128]{1,0:T(8,128)S(1)} %collective-permute-done.3.refs_3_), channel_id=1, source_target_pairs={{8,0},{16,8},{24,16},{28,24},{20,28},{12,20},{4,12},{0,4},{9,1},{1... | collective-permute-start | bytes 1277960 | tf_op jit(solution)/shard_map/ppermute | solution.py:387
  16.8 17.6 %collective-permute-start.6 = (f32[832,128]{1,0:T(8,128)S(1)}, f32[832,128]{1,0:T(8,128)S(1)}, u32[]{:S(2)}, u32[]{:S(2)}) collective-permute-start(f32[832,128]{1,0:T(8,128)S(1)} %collective-permute-done.1.refs_1_), channel_id=1, source_target_pairs={{0,8},{8,16},{16,24},{24,28},{28,20},{20,12},{12,4},{4,0},{1,9},{9... | collective-permute-start | bytes 1277960 | tf_op jit(solution)/shard_map/ppermute | solution.py:390
  16.9 1.8 %copy-start = (bf16[800,1600]{1,0:T(8,128)(2,1)S(1)}, bf16[800,1600]{1,0:T(8,128)(2,1)}, u32[]{:S(2)}) copy-start(bf16[800,1600]{1,0:T(8,128)(2,1)} %relation_ref.15) | copy-start | bytes 7680004
  25.2 15.5 %collective-permute-start.5 = (f32[768,128]{1,0:T(8,128)S(1)}, f32[768,128]{1,0:T(8,128)S(1)}, u32[]{:S(2)}, u32[]{:S(2)}) collective-permute-start(f32[768,128]{1,0:T(8,128)S(1)} %collective-permute-done.2.refs_2_), channel_id=1, source_target_pairs={{8,0},{16,8},{24,16},{28,24},{20,28},{12,20},{4,12},{0,4},{9,1},{1... | collective-permute-start | bytes 1179656 | tf_op jit(solution)/shard_map/ppermute | solution.py:387
  26.8 16.0 %collective-permute-start.4 = (f32[768,128]{1,0:T(8,128)S(1)}, f32[768,128]{1,0:T(8,128)S(1)}, u32[]{:S(2)}, u32[]{:S(2)}) collective-permute-start(f32[768,128]{1,0:T(8,128)S(1)} %collective-permute-done.refs_0_), channel_id=1, source_target_pairs={{0,8},{8,16},{16,24},{24,28},{28,20},{20,12},{12,4},{4,0},{1,9},{9... | collective-permute-start | bytes 1179656 | tf_op jit(solution)/shard_map/ppermute | solution.py:390
  32.3 20.2 %collective-permute-start.12 = (f32[832,128]{1,0:T(8,128)S(1)}, f32[832,128]{1,0:T(8,128)S(1)}, u32[]{:S(2)}, u32[]{:S(2)}) collective-permute-start(f32[832,128]{1,0:T(8,128)S(1)} %collective-permute-done.7.refs_1_), channel_id=1, source_target_pairs={{8,0},{16,8},{24,16},{28,24},{20,28},{12,20},{4,12},{0,4},{9,1},{1... | collective-permute-start | bytes 1277960 | tf_op jit(solution)/shard_map/ppermute | solution.py:387
  34.3 18.2 %collective-permute-start.11 = (f32[832,128]{1,0:T(8,128)S(1)}, f32[832,128]{1,0:T(8,128)S(1)}, u32[]{:S(2)}, u32[]{:S(2)}) collective-permute-start(f32[832,128]{1,0:T(8,128)S(1)} %collective-permute-done.6.refs_0_), channel_id=1, source_target_pairs={{0,8},{8,16},{16,24},{24,28},{28,20},{20,12},{12,4},{4,0},{1,9},{9... | collective-permute-start | bytes 1277960 | tf_op jit(solution)/shard_map/ppermute | solution.py:390
  35.5 9.9 %copy-start.1 = (bf16[800,1600]{1,0:T(8,128)(2,1)S(1)}, bf16[800,1600]{1,0:T(8,128)(2,1)}, u32[]{:S(2)}) copy-start(bf16[800,1600]{1,0:T(8,128)(2,1)} %relation_ref.15) | copy-start | bytes 7680004
  43.8 8.6 %collective-permute-start.8 = (f32[800,128]{1,0:T(8,128)S(1)}, f32[800,128]{1,0:T(8,128)S(1)}, u32[]{:S(2)}, u32[]{:S(2)}) collective-permute-start(f32[800,128]{1,0:T(8,128)S(1)} %get-tuple-element.67), channel_id=1, source_target_pairs={{0,2},{1,3},{2,0},{3,1},{4,6},{5,7},{6,4},{7,5},{8,10},{9,11},{10,... | collective-permute-start | bytes 1228808 | tf_op jit(solution)/shard_map/ppermute | solution.py:408
  47.1 11.7 %collective-permute-start.9 = (f32[768,128]{1,0:T(8,128)S(1)}, f32[768,128]{1,0:T(8,128)S(1)}, u32[]{:S(2)}, u32[]{:S(2)}) collective-permute-start(f32[768,128]{1,0:T(8,128)S(1)} %collective-permute-done.4.refs_0_), channel_id=1, source_target_pairs={{0,8},{8,16},{16,24},{24,28},{28,20},{20,12},{12,4},{4,0},{1,9},{9... | collective-permute-start | bytes 1179656 | tf_op jit(solution)/shard_map/ppermute | solution.py:390
  47.7 11.5 %collective-permute-start.10 = (f32[768,128]{1,0:T(8,128)S(1)}, f32[768,128]{1,0:T(8,128)S(1)}, u32[]{:S(2)}, u32[]{:S(2)}) collective-permute-start(f32[768,128]{1,0:T(8,128)S(1)} %collective-permute-done.5.refs_1_), channel_id=1, source_target_pairs={{8,0},{16,8},{24,16},{28,24},{20,28},{12,20},{4,12},{0,4},{9,1},{1... | collective-permute-start | bytes 1179656 | tf_op jit(solution)/shard_map/ppermute | solution.py:387
  58.8 9.7 %collective-permute-start.19 = (f32[768,128]{1,0:T(8,128)S(1)}, f32[768,128]{1,0:T(8,128)S(1)}, u32[]{:S(2)}, u32[]{:S(2)}) collective-permute-start(f32[768,128]{1,0:T(8,128)S(1)} %collective-permute-done.9.refs_0_), channel_id=1, source_target_pairs={{0,8},{8,16},{16,24},{24,28},{28,20},{20,12},{12,4},{4,0},{1,9},{9... | collective-permute-start | bytes 1179656 | tf_op jit(solution)/shard_map/ppermute | solution.py:390
  60.5 10.5 %collective-permute-start.18 = (f32[832,128]{1,0:T(8,128)S(1)}, f32[832,128]{1,0:T(8,128)S(1)}, u32[]{:S(2)}, u32[]{:S(2)}) collective-permute-start(f32[832,128]{1,0:T(8,128)S(1)} %collective-permute-done.12.refs_1_), channel_id=1, source_target_pairs={{8,0},{16,8},{24,16},{28,24},{20,28},{12,20},{4,12},{0,4},{9,1},{1... | collective-permute-start | bytes 1277960 | tf_op jit(solution)/shard_map/ppermute | solution.py:387
  62.2 1.6 %collective-permute-start.15 = (f32[544,128]{1,0:T(8,128)S(1)}, f32[544,128]{1,0:T(8,128)S(1)}, u32[]{:S(2)}, u32[]{:S(2)}) collective-permute-start(f32[544,128]{1,0:T(8,128)S(1)} %get-tuple-element.111), channel_id=1, source_target_pairs={{0,1},{1,0},{2,3},{3,2},{4,5},{5,4},{6,7},{7,6},{8,9},{9,8},{10,11... | collective-permute-start | bytes 835592 | tf_op jit(solution)/shard_map/ppermute | solution.py:405
  62.3 1.9 %collective-permute-start.14 = (f32[544,128]{1,0:T(8,128)S(1)}, f32[544,128]{1,0:T(8,128)S(1)}, u32[]{:S(2)}, u32[]{:S(2)}) collective-permute-start(f32[544,128]{1,0:T(8,128)S(1)} %get-tuple-element.112), channel_id=1, source_target_pairs={{0,1},{1,0},{2,3},{3,2},{4,5},{5,4},{6,7},{7,6},{8,9},{9,8},{10,11... | collective-permute-start | bytes 835592 | tf_op jit(solution)/shard_map/ppermute | solution.py:405
  62.8 1.8 %collective-permute-start.13 = (f32[544,128]{1,0:T(8,128)S(1)}, f32[544,128]{1,0:T(8,128)S(1)}, u32[]{:S(2)}, u32[]{:S(2)}) collective-permute-start(f32[544,128]{1,0:T(8,128)S(1)} %get-tuple-element.113), channel_id=1, source_target_pairs={{0,1},{1,0},{2,3},{3,2},{4,5},{5,4},{6,7},{7,6},{8,9},{9,8},{10,11... | collective-permute-start | bytes 835592 | tf_op jit(solution)/shard_map/ppermute | solution.py:405
  64.8 12.8 %collective-permute-start.16 = (f32[816,128]{1,0:T(8,128)S(1)}, f32[816,128]{1,0:T(8,128)S(1)}, u32[]{:S(2)}, u32[]{:S(2)}) collective-permute-start(f32[816,128]{1,0:T(8,128)S(1)} %get-tuple-element.89), channel_id=1, source_target_pairs={{0,2},{1,3},{2,0},{3,1},{4,6},{5,7},{6,4},{7,5},{8,10},{9,11},{10,... | collective-permute-start | bytes 1253384 | tf_op jit(solution)/shard_map/ppermute | solution.py:408
  69.0 6.7 %copy-start.2 = (f32[1024]{0:T(1024)S(1)}, f32[1024]{0:T(1024)}, u32[]{:S(2)}) copy-start(f32[1024]{0:T(1024)} %one_ref.1) | copy-start | bytes 12292
  69.0 6.7 %copy-start.3 = (f32[1024]{0:T(1024)S(1)}, f32[1024]{0:T(1024)}, u32[]{:S(2)}) copy-start(f32[1024]{0:T(1024)} %two_ref.1) | copy-start | bytes 12292
  69.0 6.7 %copy-start.4 = (f32[1024]{0:T(1024)S(1)}, f32[1024]{0:T(1024)}, u32[]{:S(2)}) copy-start(f32[1024]{0:T(1024)} %scale_ref.1) | copy-start | bytes 12292
  71.8 1.5 %collective-permute-start.20 = (f32[400,128]{1,0:T(8,128)S(1)}, f32[400,128]{1,0:T(8,128)S(1)}, u32[]{:S(2)}, u32[]{:S(2)}) collective-permute-start(f32[400,128]{1,0:T(8,128)S(1)} %get-tuple-element.97), channel_id=1, source_target_pairs={{0,1},{1,0},{2,3},{3,2},{4,5},{5,4},{6,7},{7,6},{8,9},{9,8},{10,11... | collective-permute-start | bytes 614408 | tf_op jit(solution)/shard_map/ppermute | solution.py:405
  71.8 1.7 %collective-permute-start.21 = (f32[400,128]{1,0:T(8,128)S(1)}, f32[400,128]{1,0:T(8,128)S(1)}, u32[]{:S(2)}, u32[]{:S(2)}) collective-permute-start(f32[400,128]{1,0:T(8,128)S(1)} %get-tuple-element.98), channel_id=1, source_target_pairs={{0,1},{1,0},{2,3},{3,2},{4,5},{5,4},{6,7},{7,6},{8,9},{9,8},{10,11... | collective-permute-start | bytes 614408 | tf_op jit(solution)/shard_map/ppermute | solution.py:405
  73.6 7.4 %collective-permute-start.24 = (f32[400,128]{1,0:T(8,128)S(1)}, f32[400,128]{1,0:T(8,128)S(1)}, u32[]{:S(2)}, u32[]{:S(2)}) collective-permute-start(f32[400,128]{1,0:T(8,128)S(1)} %get-tuple-element.107), channel_id=1, source_target_pairs={{0,2},{1,3},{2,0},{3,1},{4,6},{5,7},{6,4},{7,5},{8,10},{9,11},{10,... | collective-permute-start | bytes 614408 | tf_op jit(solution)/shard_map/ppermute | solution.py:408
  75.0 6.2 %collective-permute-start.17 = (f32[800,128]{1,0:T(8,128)S(1)}, f32[800,128]{1,0:T(8,128)S(1)}, u32[]{:S(2)}, u32[]{:S(2)}) collective-permute-start(f32[800,128]{1,0:T(8,128)S(1)} %shard_map.60.two_sum), channel_id=1, source_target_pairs={{0,1},{1,0},{2,3},{3,2},{4,5},{5,4},{6,7},{7,6},{8,9},{9,8},{10,11... | collective-permute-start | bytes 1228808 | tf_op jit(solution)/shard_map/ppermute | solution.py:405
  75.2 1.6 %collective-permute-start.22 = (f32[4,896]{1,0:T(4,128)S(1)}, f32[4,896]{1,0:T(4,128)S(1)}, u32[]{:S(2)}, u32[]{:S(2)}) collective-permute-start(f32[4,896]{1,0:T(4,128)S(1)} %get-tuple-element.104), channel_id=1, source_target_pairs={{0,1},{1,0},{2,3},{3,2},{4,5},{5,4},{6,7},{7,6},{8,9},{9,8},{10,11... | collective-permute-start | bytes 43016 | tf_op jit(solution)/shard_map/ppermute | solution.py:405
  76.8 4.3 %collective-permute-start.23 = (f32[2,896]{1,0:T(2,128)S(1)}, f32[2,896]{1,0:T(2,128)S(1)}, u32[]{:S(2)}, u32[]{:S(2)}) collective-permute-start(f32[2,896]{1,0:T(2,128)S(1)} %get-tuple-element.105), channel_id=1, source_target_pairs={{0,2},{1,3},{2,0},{3,1},{4,6},{5,7},{6,4},{7,5},{8,10},{9,11},{10,... | collective-permute-start | bytes 21512 | tf_op jit(solution)/shard_map/ppermute | solution.py:408
  81.1 1.5 %collective-permute-start.25 = (f32[400,128]{1,0:T(8,128)S(1)}, f32[400,128]{1,0:T(8,128)S(1)}, u32[]{:S(2)}, u32[]{:S(2)}) collective-permute-start(f32[400,128]{1,0:T(8,128)S(1)} %shard_map.73.zero_half), channel_id=1, source_target_pairs={{0,1},{1,0},{2,3},{3,2},{4,5},{5,4},{6,7},{7,6},{8,9},{9,8},{10,11... | collective-permute-start | bytes 614408 | tf_op jit(solution)/shard_map/ppermute | solution.py:405

commit v9 on v8

--- a/solution.py
+++ b/solution.py
@@ -347,7 +347,7 @@
     others = column_weights(spot, weights_ref, odd)
     if same:
         sides_ref[...] = beside(weights, border_mine[...] + border_got[...], odd == 1)
-    pieces = 5
+    pieces = 2
     step = rows // pieces
     copies = []
     for n in range(pieces):
@@ -451,7 +451,7 @@
     two_sum = call(sum_kernel, [(rows, WIDTH)], (two_keep, over_y(two_send)), flops=KERNEL_FLOPS // 10)[0]
     two_got = over_cores(two_sum)
     def last_step(*made):
-        blocks[half] = (behind_of(tied(behind[0], *made)), ahead_of(ahead[1]))
+        blocks[half] = (behind_of(tied(behind[0], *made)), ahead_of(tied(ahead[1], *made)))
 
     in_two_steps(1 - half, half - 1, cost=10, between=last_step)
     odd_fars = (-1, 3, 1, -3)
@@ -531,7 +531,7 @@
     scratch = [
         pltpu.VMEM((rows // 2, WIDTH), jnp.float32),
         pltpu.VMEM((2, rows // 2, WIDTH), jnp.float32),
-        pltpu.SemaphoreType.DMA((10,)),
+        pltpu.SemaphoreType.DMA((4,)),
     ]
     applied, sides = call(
         functools.partial(last_kernel, spot_of, True),

time: 83.8 us -> 83.8 us (level)
    ppermute x7, waiting for transfers between devices: 19.8 us -> 18.5 us  [ahead_of(): return lax.ppermute(x, 'gen', backward)]
    ppermute x4, waiting for transfers between devices: 5.92 us -> 7.18 us  [over_y(): return lax.ppermute(x, 'tm', [(t, t ^ 2) for t in range(tms)])]
  transfers between devices with their start and end apart: 26 -> 26, of which waited for: 17 -> 18; matrix products, arithmetic and copies ran while one was open for 1% -> 1% of each run, Pallas kernels for 13% -> 13%
where the time goes in v9:
time: 83.8 us; the launch traced here: 83.6 us
  waiting for transfers between devices  44.9 us (54%)
  starting transfers between devices  22.7 us (27%)
  Pallas kernels  11.8 us (14%)
  local copies, waits for them, and re-layouts  3.89 us (5%)
    ppermute x7, waiting for transfers between devices, ahead_of(): return lax.ppermute(x, 'gen', backward)  18.5 us
    ppermute x7, waiting for transfers between devices, behind_of(): return lax.ppermute(x, 'gen', forward)  15.2 us
    pallas_call x21, Pallas kernels, call(): pl.pallas_call(kernel, out_shape=[jax.ShapeDtypeStruct(shape, jnp.float32...  11.8 us
    ppermute x7, starting transfers between devices, ahead_of(): return lax.ppermute(x, 'gen', backward)  11.7 us
    ppermute x4, waiting for transfers between devices, over_y(): return lax.ppermute(x, 'tm', [(t, t ^ 2) for t in range(tms)])  7.18 us
    ppermute x4, starting transfers between devices, over_y(): return lax.ppermute(x, 'tm', [(t, t ^ 2) for t in range(tms)])  5.32 us
    ppermute x8, waiting for transfers between devices, over_cores(): return lax.ppermute(x, 'tm', swap)  4.03 us
    ppermute x7, starting transfers between devices, behind_of(): return lax.ppermute(x, 'gen', forward)  3.85 us
  transfers between devices with their start and end apart: 26, of which 18 were waited for; matrix products, arithmetic and copies ran while one was open for 1% of the time, Pallas kernels for 13%

profile of v9, /device:TPU:0, one launch (start us, length us, event | category | flops | bytes accessed | tf_op | source)
XLA Modules:
  0.0 83.6 jit_solution(12716976444632195134)
XLA Ops:
  0.0 1.0 %slice.16.refs_1_ = f32[832,128]{1,0:T(8,128)S(1)} slice(f32[1600,128]{1,0:T(8,128)} %param.6), slice={[768:1600], [0:128]} | slice | bytes 851968 | tf_op jit(solution)/shard_map/slice | solution.py:430
  1.0 3.0 %collective-permute-start.3 = (f32[832,128]{1,0:T(8,128)S(1)}, f32[832,128]{1,0:T(8,128)S(1)}, u32[]{:S(2)}, u32[]{:S(2)}) collective-permute-start(f32[832,128]{1,0:T(8,128)S(1)} %slice.16.refs_1_), channel_id=1, source_target_pairs={{8,0},{16,8},{24,16},{28,24},{20,28},{12,20},{4,12},{0,4},{9,1},{1... | collective-permute-start | bytes 1277960 | tf_op jit(solution)/shard_map/ppermute | solution.py:387
  4.2 1.0 %slice.15.refs_0_ = f32[768,128]{1,0:T(8,128)S(1)} slice(f32[1600,128]{1,0:T(8,128)} %param.6), slice={[0:768], [0:128]} | slice | bytes 786432 | tf_op jit(solution)/shard_map/slice | solution.py:430
  5.2 2.0 %collective-permute-start = (f32[768,128]{1,0:T(8,128)S(1)}, f32[768,128]{1,0:T(8,128)S(1)}, u32[]{:S(2)}, u32[]{:S(2)}) collective-permute-start(f32[768,128]{1,0:T(8,128)S(1)} %slice.15.refs_0_), channel_id=1, source_target_pairs={{0,8},{8,16},{16,24},{24,28},{28,20},{20,12},{12,4},{4,0},{1,9},{9... | collective-permute-start | bytes 1179656 | tf_op jit(solution)/shard_map/ppermute | solution.py:390
  7.3 7.5 %collective-permute-done.3.refs_3_ = f32[832,128]{1,0:T(8,128)S(1)} collective-permute-done((f32[832,128]{1,0:T(8,128)S(1)}, f32[832,128]{1,0:T(8,128)S(1)}, u32[]{:S(2)}, u32[]{:S(2)}) %collective-permute-start.3) | collective-permute-done | bytes 426016 | tf_op jit(solution)/shard_map/ppermute | solution.py:387
  14.8 2.0 %collective-permute-start.7 = (f32[832,128]{1,0:T(8,128)S(1)}, f32[832,128]{1,0:T(8,128)S(1)}, u32[]{:S(2)}, u32[]{:S(2)}) collective-permute-start(f32[832,128]{1,0:T(8,128)S(1)} %collective-permute-done.3.refs_3_), channel_id=1, source_target_pairs={{8,0},{16,8},{24,16},{28,24},{20,28},{12,20},{4,12},{0,4},{9,1},{1... | collective-permute-start | bytes 1277960 | tf_op jit(solution)/shard_map/ppermute | solution.py:387
  16.9 1.7 %copy-done = bf16[800,1600]{1,0:T(8,128)(2,1)S(1)} copy-done((bf16[800,1600]{1,0:T(8,128)(2,1)S(1)}, bf16[800,1600]{1,0:T(8,128)(2,1)}, u32[]{:S(2)}) %copy-start) | copy-done | bytes 2560024
  18.6 1.0 %shard_map.56 = (f32[800,128]{1,0:T(8,128)S(1)}, f32[4,896]{1,0:T(4,128)S(1)}) custom-call(bf16[800,1600]{1,0:T(8,128)(2,1)S(1)} %copy-done, f32[768,128]{1,0:T(8,128)S(1)} %slice.15.refs_0_, f32[832,128]{1,0:T(8,128)S(1)} %slice.16.refs_1_), custom_call_target="tpu_custom_call" | custom-call | flops 100000000 | tf_op jit(solution)/shard_map/pallas_call | solution.py:18
  19.6 5.6 %collective-permute-done.refs_0_ = f32[768,128]{1,0:T(8,128)S(1)} collective-permute-done((f32[768,128]{1,0:T(8,128)S(1)}, f32[768,128]{1,0:T(8,128)S(1)}, u32[]{:S(2)}, u32[]{:S(2)}) %collective-permute-start) | collective-permute-done | bytes 393248 | tf_op jit(solution)/shard_map/ppermute | solution.py:390
  25.2 1.6 %collective-permute-start.5 = (f32[768,128]{1,0:T(8,128)S(1)}, f32[768,128]{1,0:T(8,128)S(1)}, u32[]{:S(2)}, u32[]{:S(2)}) collective-permute-start(f32[768,128]{1,0:T(8,128)S(1)} %collective-permute-done.2.refs_2_), channel_id=1, source_target_pairs={{8,0},{16,8},{24,16},{28,24},{20,28},{12,20},{4,12},{0,4},{9,1},{1... | collective-permute-start | bytes 1179656 | tf_op jit(solution)/shard_map/ppermute | solution.py:387
  26.8 0.4 collective-permute-start.4
  27.2 5.1 %collective-permute-done.7.refs_1_ = f32[832,128]{1,0:T(8,128)S(1)} collective-permute-done((f32[832,128]{1,0:T(8,128)S(1)}, f32[832,128]{1,0:T(8,128)S(1)}, u32[]{:S(2)}, u32[]{:S(2)}) %collective-permute-start.7) | collective-permute-done | bytes 426016 | tf_op jit(solution)/shard_map/ppermute | solution.py:387
  32.3 2.0 %collective-permute-start.12 = (f32[832,128]{1,0:T(8,128)S(1)}, f32[832,128]{1,0:T(8,128)S(1)}, u32[]{:S(2)}, u32[]{:S(2)}) collective-permute-start(f32[832,128]{1,0:T(8,128)S(1)} %collective-permute-done.7.refs_1_), channel_id=1, source_target_pairs={{8,0},{16,8},{24,16},{28,24},{20,28},{12,20},{4,12},{0,4},{9,1},{1... | collective-permute-start | bytes 1277960 | tf_op jit(solution)/shard_map/ppermute | solution.py:387
  34.4 1.0 %shard_map.57 = (f32[800,128]{1,0:T(8,128)S(1)}, f32[800,128]{1,0:T(8,128)S(1)}) custom-call(bf16[800,1600]{1,0:T(8,128)(2,1)S(1)} %copy-done, f32[832,128]{1,0:T(8,128)S(1)} %collective-permute-done.6.refs_0_, f32[832,128]{1,0:T(8,128)S(1)} %collective-permute-done.7.refs_1_), custom_call_target="tpu_custom_call" | custom-call | flops 100000000 | tf_op jit(solution)/shard_map/pallas_call | solution.py:18
  35.5 5.3 %collective-permute-done.5.refs_1_ = f32[768,128]{1,0:T(8,128)S(1)} collective-permute-done((f32[768,128]{1,0:T(8,128)S(1)}, f32[768,128]{1,0:T(8,128)S(1)}, u32[]{:S(2)}, u32[]{:S(2)}) %collective-permute-start.5) | collective-permute-done | bytes 393248 | tf_op jit(solution)/shard_map/ppermute | solution.py:387
  40.7 2.0 %collective-permute-done.4.refs_0_ = f32[768,128]{1,0:T(8,128)S(1)} collective-permute-done((f32[768,128]{1,0:T(8,128)S(1)}, f32[768,128]{1,0:T(8,128)S(1)}, u32[]{:S(2)}, u32[]{:S(2)}) %collective-permute-start.4) | collective-permute-done | bytes 393248 | tf_op jit(solution)/shard_map/ppermute | solution.py:390
  42.8 0.9 %shard_map.58 = (f32[800,128]{1,0:T(8,128)S(1)}, f32[4,896]{1,0:T(4,128)S(1)}, f32[800,128]{1,0:T(8,128)S(1)}, f32[4,896]{1,0:T(4,128)S(1)}) custom-call(bf16[800,1600]{1,0:T(8,128)(2,1)S(1)} %copy-done, f32[768,128]{1,0:T(8,128)S(1)} %collective-permute-done.4.refs_0_, f32[768,128]{1,0:T(8,128)S(1)} %collective-permute-done.5.refs_1_, ...), custom_call_target="tpu_custom_call" | custom-call | flops 100000000 | tf_op jit(solution)/shard_map/pallas_call | solution.py:18
  43.8 1.6 %collective-permute-start.8 = (f32[800,128]{1,0:T(8,128)S(1)}, f32[800,128]{1,0:T(8,128)S(1)}, u32[]{:S(2)}, u32[]{:S(2)}) collective-permute-start(f32[800,128]{1,0:T(8,128)S(1)} %get-tuple-element.68), channel_id=1, source_target_pairs={{0,2},{1,3},{2,0},{3,1},{4,6},{5,7},{6,4},{7,5},{8,10},{9,11},{10,... | collective-permute-start | bytes 1228808 | tf_op jit(solution)/shard_map/ppermute | solution.py:408
  45.4 1.8 %shard_map.55 = (f32[800,128]{1,0:T(8,128)S(1)}, f32[4,896]{1,0:T(4,128)S(1)}, f32[800,128]{1,0:T(8,128)S(1)}, f32[4,896]{1,0:T(4,128)S(1)}) custom-call(bf16[800,1600]{1,0:T(8,128)(2,1)S(1)} %copy-done.1, f32[768,128]{1,0:T(8,128)S(1)} %collective-permute-done.refs_0_, f32[832,128]{1,0:T(8,128)S(1)} %collective-permute-done.1.refs_1_, ...), custom_call_target="tpu_custom_call" | custom-call | flops 200000000 | tf_op jit(solution)/shard_map/pallas_call | solution.py:18
  47.1 0.6 collective-permute-start.9
  47.7 1.5 %collective-permute-start.10 = (f32[768,128]{1,0:T(8,128)S(1)}, f32[768,128]{1,0:T(8,128)S(1)}, u32[]{:S(2)}, u32[]{:S(2)}) collective-permute-start(f32[768,128]{1,0:T(8,128)S(1)} %collective-permute-done.5.refs_1_), channel_id=1, source_target_pairs={{8,0},{16,8},{24,16},{28,24},{20,28},{12,20},{4,12},{0,4},{9,1},{1... | collective-permute-start | bytes 1179656 | tf_op jit(solution)/shard_map/ppermute | solution.py:387
  49.2 3.2 %collective-permute-done.8.other_ref = f32[800,128]{1,0:T(8,128)S(1)} collective-permute-done((f32[800,128]{1,0:T(8,128)S(1)}, f32[800,128]{1,0:T(8,128)S(1)}, u32[]{:S(2)}, u32[]{:S(2)}) %collective-permute-start.8) | collective-permute-done | bytes 409632 | tf_op jit(solution)/shard_map/ppermute | solution.py:408
  52.5 1.0 %shard_map.61 = (f32[800,128]{1,0:T(8,128)S(1)}, f32[800,128]{1,0:T(8,128)S(1)}) custom-call(bf16[800,1600]{1,0:T(8,128)(2,1)S(1)} %copy-done.1, f32[832,128]{1,0:T(8,128)S(1)} %collective-permute-done.11.refs_0_, f32[832,128]{1,0:T(8,128)S(1)} %collective-permute-done.12.refs_1_), custom_call_target="tpu_custom_call" | custom-call | flops 100000000 | tf_op jit(solution)/shard_map/pallas_call | solution.py:18
  53.5 5.3 %collective-permute-done.9.refs_0_ = f32[768,128]{1,0:T(8,128)S(1)} collective-permute-done((f32[768,128]{1,0:T(8,128)S(1)}, f32[768,128]{1,0:T(8,128)S(1)}, u32[]{:S(2)}, u32[]{:S(2)}) %collective-permute-start.9) | collective-permute-done | bytes 393248 | tf_op jit(solution)/shard_map/ppermute | solution.py:390
  58.8 0.4 collective-permute-start.19
  59.3 1.6 %collective-permute-start.18 = (f32[832,128]{1,0:T(8,128)S(1)}, f32[832,128]{1,0:T(8,128)S(1)}, u32[]{:S(2)}, u32[]{:S(2)}) collective-permute-start(f32[832,128]{1,0:T(8,128)S(1)} %collective-permute-done.12.refs_1_), channel_id=1, source_target_pairs={{8,0},{16,8},{24,16},{28,24},{20,28},{12,20},{4,12},{0,4},{9,1},{1... | collective-permute-start | bytes 1277960 | tf_op jit(solution)/shard_map/ppermute | solution.py:387
  60.9 0.9 %shard_map.62 = (f32[800,128]{1,0:T(8,128)S(1)}, f32[4,896]{1,0:T(4,128)S(1)}, f32[800,128]{1,0:T(8,128)S(1)}, f32[4,896]{1,0:T(4,128)S(1)}) custom-call(bf16[800,1600]{1,0:T(8,128)(2,1)S(1)} %copy-done.1, f32[768,128]{1,0:T(8,128)S(1)} %collective-permute-done.9.refs_0_, f32[768,128]{1,0:T(8,128)S(1)} %collective-permute-done.10.refs_1_, ...), custom_call_target="tpu_custom_call" | custom-call | flops 1000000000 | tf_op jit(solution)/shard_map/pallas_call | solution.py:18
  61.8 0.3 shard_map.63
  62.3 0.5 collective-permute-start.14
  62.8 1.0 %collective-permute-done.15.refs_2_ = f32[544,128]{1,0:T(8,128)S(1)} collective-permute-done((f32[544,128]{1,0:T(8,128)S(1)}, f32[544,128]{1,0:T(8,128)S(1)}, u32[]{:S(2)}, u32[]{:S(2)}) %collective-permute-start.15) | collective-permute-done | bytes 278560 | tf_op jit(solution)/shard_map/ppermute | solution.py:405
  63.8 0.4 collective-permute-done.14.refs_1_
  64.2 0.4 collective-permute-done.13.refs_0_
  64.7 1.6 %collective-permute-start.16 = (f32[816,128]{1,0:T(8,128)S(1)}, f32[816,128]{1,0:T(8,128)S(1)}, u32[]{:S(2)}, u32[]{:S(2)}) collective-permute-start(f32[816,128]{1,0:T(8,128)S(1)} %get-tuple-element.90), channel_id=1, source_target_pairs={{0,2},{1,3},{2,0},{3,1},{4,6},{5,7},{6,4},{7,5},{8,10},{9,11},{10,... | collective-permute-start | bytes 1253384 | tf_op jit(solution)/shard_map/ppermute | solution.py:408
  66.3 2.2 %collective-permute-done.19.refs_0_ = f32[768,128]{1,0:T(8,128)S(1)} collective-permute-done((f32[768,128]{1,0:T(8,128)S(1)}, f32[768,128]{1,0:T(8,128)S(1)}, u32[]{:S(2)}, u32[]{:S(2)}) %collective-permute-start.19) | collective-permute-done | bytes 393248 | tf_op jit(solution)/shard_map/ppermute | solution.py:390
  68.5 0.5 shard_map.67.refs_1_
  69.0 0.6 collective-permute-done.18.refs_0_
  69.7 0.7 shard_map.68
  70.5 0.5 collective-permute-start.21
  71.0 0.9 %collective-permute-done.20.got_ours = f32[400,128]{1,0:T(8,128)S(1)} collective-permute-done((f32[400,128]{1,0:T(8,128)S(1)}, f32[400,128]{1,0:T(8,128)S(1)}, u32[]{:S(2)}, u32[]{:S(2)}) %collective-permute-start.20) | collective-permute-done | bytes 204832 | tf_op jit(solution)/shard_map/ppermute | solution.py:405
  72.3 1.4 %collective-permute-start.24 = (f32[400,128]{1,0:T(8,128)S(1)}, f32[400,128]{1,0:T(8,128)S(1)}, u32[]{:S(2)}, u32[]{:S(2)}) collective-permute-start(f32[400,128]{1,0:T(8,128)S(1)} %get-tuple-element.109), channel_id=1, source_target_pairs={{0,2},{1,3},{2,0},{3,1},{4,6},{5,7},{6,4},{7,5},{8,10},{9,11},{10,... | collective-permute-start | bytes 614408 | tf_op jit(solution)/shard_map/ppermute | solution.py:408
  73.9 0.6 collective-permute-start.22
  74.6 0.9 %collective-permute-done.22.got_ref = f32[4,896]{1,0:T(4,128)S(1)} collective-permute-done((f32[4,896]{1,0:T(4,128)S(1)}, f32[4,896]{1,0:T(4,128)S(1)}, u32[]{:S(2)}, u32[]{:S(2)}) %collective-permute-start.22) | collective-permute-done | bytes 14368 | tf_op jit(solution)/shard_map/ppermute | solution.py:405
  75.5 0.8 collective-permute-start.23
  76.3 1.0 %collective-permute-done.16.got_ref = f32[816,128]{1,0:T(8,128)S(1)} collective-permute-done((f32[816,128]{1,0:T(8,128)S(1)}, f32[816,128]{1,0:T(8,128)S(1)}, u32[]{:S(2)}, u32[]{:S(2)}) %collective-permute-start.16) | collective-permute-done | bytes 417824 | tf_op jit(solution)/shard_map/ppermute | solution.py:408
  77.3 0.7 shard_map.66
  78.0 3.0 %collective-permute-done.23.border_got = f32[2,896]{1,0:T(2,128)S(1)} collective-permute-done((f32[2,896]{1,0:T(2,128)S(1)}, f32[2,896]{1,0:T(2,128)S(1)}, u32[]{:S(2)}, u32[]{:S(2)}) %collective-permute-start.23) | collective-permute-done | bytes 7200 | tf_op jit(solution)/shard_map/ppermute | solution.py:408
  81.1 1.3 %shard_map.74 = (f32[800,256]{1,0:T(8,128)}, f32[896,128]{1,0:T(8,128)S(1)}) custom-call(f32[800,128]{1,0:T(8,128)S(1)} %get-tuple-element.91.odd_own, f32[800,128]{1,0:T(8,128)S(1)} %get-tuple-element.92.odd_beyond, f32[800,128]{1,0:T(8,128)S(1)} %shard_map.60.two_sum, f32[800,128]{1,0:T(8,128)S(1)} %collective-permute-done.17.two_got, ...), custom_call_target="tpu_custom_call" | custom-call | tf_op jit(solution)/shard_map/pallas_call | solution.py:18
  82.5 1.0 %shard_map.75 = f32[800,256]{1,0:T(8,128)} custom-call(f32[800,128]{1,0:T(8,128)S(1)} %get-tuple-element.91.odd_own, f32[800,128]{1,0:T(8,128)S(1)} %get-tuple-element.92.odd_beyond, f32[800,128]{1,0:T(8,128)S(1)} %shard_map.60.two_sum, f32[800,128]{1,0:T(8,128)S(1)} %collective-permute-done.17.two_got, ...), custom_call_target="tpu_custom_call", output_to_operand_aliasing={{}: (9, {})} | custom-call | tf_op jit(solution)/shard_map/pallas_call | solution.py:18
  (38 shorter events, 2.0 us)
Async XLA Ops:
  1.0 13.7 %collective-permute-start.3 = (f32[832,128]{1,0:T(8,128)S(1)}, f32[832,128]{1,0:T(8,128)S(1)}, u32[]{:S(2)}, u32[]{:S(2)}) collective-permute-start(f32[832,128]{1,0:T(8,128)S(1)} %slice.16.refs_1_), channel_id=1, source_target_pairs={{8,0},{16,8},{24,16},{28,24},{20,28},{12,20},{4,12},{0,4},{9,1},{1... | collective-permute-start | bytes 1277960 | tf_op jit(solution)/shard_map/ppermute | solution.py:387
  4.0 12.7 %collective-permute-start.1 = (f32[832,128]{1,0:T(8,128)S(1)}, f32[832,128]{1,0:T(8,128)S(1)}, u32[]{:S(2)}, u32[]{:S(2)}) collective-permute-start(f32[832,128]{1,0:T(8,128)S(1)} %slice.16.refs_1_), channel_id=1, source_target_pairs={{0,8},{8,16},{16,24},{24,28},{28,20},{20,12},{12,4},{4,0},{1,9},{9... | collective-permute-start | bytes 1277960 | tf_op jit(solution)/shard_map/ppermute | solution.py:390
  5.2 20.0 %collective-permute-start = (f32[768,128]{1,0:T(8,128)S(1)}, f32[768,128]{1,0:T(8,128)S(1)}, u32[]{:S(2)}, u32[]{:S(2)}) collective-permute-start(f32[768,128]{1,0:T(8,128)S(1)} %slice.15.refs_0_), channel_id=1, source_target_pairs={{0,8},{8,16},{16,24},{24,28},{28,20},{20,12},{12,4},{4,0},{1,9},{9... | collective-permute-start | bytes 1179656 | tf_op jit(solution)/shard_map/ppermute | solution.py:390
  7.2 18.0 %collective-permute-start.2 = (f32[768,128]{1,0:T(8,128)S(1)}, f32[768,128]{1,0:T(8,128)S(1)}, u32[]{:S(2)}, u32[]{:S(2)}) collective-permute-start(f32[768,128]{1,0:T(8,128)S(1)} %slice.15.refs_0_), channel_id=1, source_target_pairs={{8,0},{16,8},{24,16},{28,24},{20,28},{12,20},{4,12},{0,4},{9,1},{1... | collective-permute-start | bytes 1179656 | tf_op jit(solution)/shard_map/ppermute | solution.py:387
  14.8 17.6 %collective-permute-start.7 = (f32[832,128]{1,0:T(8,128)S(1)}, f32[832,128]{1,0:T(8,128)S(1)}, u32[]{:S(2)}, u32[]{:S(2)}) collective-permute-start(f32[832,128]{1,0:T(8,128)S(1)} %collective-permute-done.3.refs_3_), channel_id=1, source_target_pairs={{8,0},{16,8},{24,16},{28,24},{20,28},{12,20},{4,12},{0,4},{9,1},{1... | collective-permute-start | bytes 1277960 | tf_op jit(solution)/shard_map/ppermute | solution.py:387
  16.8 17.6 %collective-permute-start.6 = (f32[832,128]{1,0:T(8,128)S(1)}, f32[832,128]{1,0:T(8,128)S(1)}, u32[]{:S(2)}, u32[]{:S(2)}) collective-permute-start(f32[832,128]{1,0:T(8,128)S(1)} %collective-permute-done.1.refs_1_), channel_id=1, source_target_pairs={{0,8},{8,16},{16,24},{24,28},{28,20},{20,12},{12,4},{4,0},{1,9},{9... | collective-permute-start | bytes 1277960 | tf_op jit(solution)/shard_map/ppermute | solution.py:390
  16.9 1.8 %copy-start = (bf16[800,1600]{1,0:T(8,128)(2,1)S(1)}, bf16[800,1600]{1,0:T(8,128)(2,1)}, u32[]{:S(2)}) copy-start(bf16[800,1600]{1,0:T(8,128)(2,1)} %relation_ref.15) | copy-start | bytes 7680004
  25.2 15.5 %collective-permute-start.5 = (f32[768,128]{1,0:T(8,128)S(1)}, f32[768,128]{1,0:T(8,128)S(1)}, u32[]{:S(2)}, u32[]{:S(2)}) collective-permute-start(f32[768,128]{1,0:T(8,128)S(1)} %collective-permute-done.2.refs_2_), channel_id=1, source_target_pairs={{8,0},{16,8},{24,16},{28,24},{20,28},{12,20},{4,12},{0,4},{9,1},{1... | collective-permute-start | bytes 1179656 | tf_op jit(solution)/shard_map/ppermute | solution.py:387
  26.8 16.0 %collective-permute-start.4 = (f32[768,128]{1,0:T(8,128)S(1)}, f32[768,128]{1,0:T(8,128)S(1)}, u32[]{:S(2)}, u32[]{:S(2)}) collective-permute-start(f32[768,128]{1,0:T(8,128)S(1)} %collective-permute-done.refs_0_), channel_id=1, source_target_pairs={{0,8},{8,16},{16,24},{24,28},{28,20},{20,12},{12,4},{4,0},{1,9},{9... | collective-permute-start | bytes 1179656 | tf_op jit(solution)/shard_map/ppermute | solution.py:390
  32.3 20.2 %collective-permute-start.12 = (f32[832,128]{1,0:T(8,128)S(1)}, f32[832,128]{1,0:T(8,128)S(1)}, u32[]{:S(2)}, u32[]{:S(2)}) collective-permute-start(f32[832,128]{1,0:T(8,128)S(1)} %collective-permute-done.7.refs_1_), channel_id=1, source_target_pairs={{8,0},{16,8},{24,16},{28,24},{20,28},{12,20},{4,12},{0,4},{9,1},{1... | collective-permute-start | bytes 1277960 | tf_op jit(solution)/shard_map/ppermute | solution.py:387
  34.3 18.2 %collective-permute-start.11 = (f32[832,128]{1,0:T(8,128)S(1)}, f32[832,128]{1,0:T(8,128)S(1)}, u32[]{:S(2)}, u32[]{:S(2)}) collective-permute-start(f32[832,128]{1,0:T(8,128)S(1)} %collective-permute-done.6.refs_0_), channel_id=1, source_target_pairs={{0,8},{8,16},{16,24},{24,28},{28,20},{20,12},{12,4},{4,0},{1,9},{9... | collective-permute-start | bytes 1277960 | tf_op jit(solution)/shard_map/ppermute | solution.py:390
  35.5 9.9 %copy-start.1 = (bf16[800,1600]{1,0:T(8,128)(2,1)S(1)}, bf16[800,1600]{1,0:T(8,128)(2,1)}, u32[]{:S(2)}) copy-start(bf16[800,1600]{1,0:T(8,128)(2,1)} %relation_ref.15) | copy-start | bytes 7680004
  43.8 8.6 %collective-permute-start.8 = (f32[800,128]{1,0:T(8,128)S(1)}, f32[800,128]{1,0:T(8,128)S(1)}, u32[]{:S(2)}, u32[]{:S(2)}) collective-permute-start(f32[800,128]{1,0:T(8,128)S(1)} %get-tuple-element.68), channel_id=1, source_target_pairs={{0,2},{1,3},{2,0},{3,1},{4,6},{5,7},{6,4},{7,5},{8,10},{9,11},{10,... | collective-permute-start | bytes 1228808 | tf_op jit(solution)/shard_map/ppermute | solution.py:408
  47.1 11.7 %collective-permute-start.9 = (f32[768,128]{1,0:T(8,128)S(1)}, f32[768,128]{1,0:T(8,128)S(1)}, u32[]{:S(2)}, u32[]{:S(2)}) collective-permute-start(f32[768,128]{1,0:T(8,128)S(1)} %collective-permute-done.4.refs_0_), channel_id=1, source_target_pairs={{0,8},{8,16},{16,24},{24,28},{28,20},{20,12},{12,4},{4,0},{1,9},{9... | collective-permute-start | bytes 1179656 | tf_op jit(solution)/shard_map/ppermute | solution.py:390
  47.7 13.1 %collective-permute-start.10 = (f32[768,128]{1,0:T(8,128)S(1)}, f32[768,128]{1,0:T(8,128)S(1)}, u32[]{:S(2)}, u32[]{:S(2)}) collective-permute-start(f32[768,128]{1,0:T(8,128)S(1)} %collective-permute-done.5.refs_1_), channel_id=1, source_target_pairs={{8,0},{16,8},{24,16},{28,24},{20,28},{12,20},{4,12},{0,4},{9,1},{1... | collective-permute-start | bytes 1179656 | tf_op jit(solution)/shard_map/ppermute | solution.py:387
  58.8 9.7 %collective-permute-start.19 = (f32[768,128]{1,0:T(8,128)S(1)}, f32[768,128]{1,0:T(8,128)S(1)}, u32[]{:S(2)}, u32[]{:S(2)}) collective-permute-start(f32[768,128]{1,0:T(8,128)S(1)} %collective-permute-done.9.refs_0_), channel_id=1, source_target_pairs={{0,8},{8,16},{16,24},{24,28},{28,20},{20,12},{12,4},{4,0},{1,9},{9... | collective-permute-start | bytes 1179656 | tf_op jit(solution)/shard_map/ppermute | solution.py:390
  59.3 10.4 %collective-permute-start.18 = (f32[832,128]{1,0:T(8,128)S(1)}, f32[832,128]{1,0:T(8,128)S(1)}, u32[]{:S(2)}, u32[]{:S(2)}) collective-permute-start(f32[832,128]{1,0:T(8,128)S(1)} %collective-permute-done.12.refs_1_), channel_id=1, source_target_pairs={{8,0},{16,8},{24,16},{28,24},{20,28},{12,20},{4,12},{0,4},{9,1},{1... | collective-permute-start | bytes 1277960 | tf_op jit(solution)/shard_map/ppermute | solution.py:387
  62.2 1.6 %collective-permute-start.15 = (f32[544,128]{1,0:T(8,128)S(1)}, f32[544,128]{1,0:T(8,128)S(1)}, u32[]{:S(2)}, u32[]{:S(2)}) collective-permute-start(f32[544,128]{1,0:T(8,128)S(1)} %get-tuple-element.113), channel_id=1, source_target_pairs={{0,1},{1,0},{2,3},{3,2},{4,5},{5,4},{6,7},{7,6},{8,9},{9,8},{10,11... | collective-permute-start | bytes 835592 | tf_op jit(solution)/shard_map/ppermute | solution.py:405
  62.3 1.9 %collective-permute-start.14 = (f32[544,128]{1,0:T(8,128)S(1)}, f32[544,128]{1,0:T(8,128)S(1)}, u32[]{:S(2)}, u32[]{:S(2)}) collective-permute-start(f32[544,128]{1,0:T(8,128)S(1)} %get-tuple-element.114), channel_id=1, source_target_pairs={{0,1},{1,0},{2,3},{3,2},{4,5},{5,4},{6,7},{7,6},{8,9},{9,8},{10,11... | collective-permute-start | bytes 835592 | tf_op jit(solution)/shard_map/ppermute | solution.py:405
  62.8 1.8 %collective-permute-start.13 = (f32[544,128]{1,0:T(8,128)S(1)}, f32[544,128]{1,0:T(8,128)S(1)}, u32[]{:S(2)}, u32[]{:S(2)}) collective-permute-start(f32[544,128]{1,0:T(8,128)S(1)} %get-tuple-element.115), channel_id=1, source_target_pairs={{0,1},{1,0},{2,3},{3,2},{4,5},{5,4},{6,7},{7,6},{8,9},{9,8},{10,11... | collective-permute-start | bytes 835592 | tf_op jit(solution)/shard_map/ppermute | solution.py:405
  64.7 12.6 %collective-permute-start.16 = (f32[816,128]{1,0:T(8,128)S(1)}, f32[816,128]{1,0:T(8,128)S(1)}, u32[]{:S(2)}, u32[]{:S(2)}) collective-permute-start(f32[816,128]{1,0:T(8,128)S(1)} %get-tuple-element.90), channel_id=1, source_target_pairs={{0,2},{1,3},{2,0},{3,1},{4,6},{5,7},{6,4},{7,5},{8,10},{9,11},{10,... | collective-permute-start | bytes 1253384 | tf_op jit(solution)/shard_map/ppermute | solution.py:408
  69.0 5.4 %copy-start.2 = (f32[1024]{0:T(1024)S(1)}, f32[1024]{0:T(1024)}, u32[]{:S(2)}) copy-start(f32[1024]{0:T(1024)} %one_ref.1) | copy-start | bytes 12292
  69.0 5.4 %copy-start.3 = (f32[1024]{0:T(1024)S(1)}, f32[1024]{0:T(1024)}, u32[]{:S(2)}) copy-start(f32[1024]{0:T(1024)} %two_ref.1) | copy-start | bytes 12292
  69.0 5.4 %copy-start.4 = (f32[1024]{0:T(1024)S(1)}, f32[1024]{0:T(1024)}, u32[]{:S(2)}) copy-start(f32[1024]{0:T(1024)} %scale_ref.1) | copy-start | bytes 12292
  70.5 1.5 %collective-permute-start.20 = (f32[400,128]{1,0:T(8,128)S(1)}, f32[400,128]{1,0:T(8,128)S(1)}, u32[]{:S(2)}, u32[]{:S(2)}) collective-permute-start(f32[400,128]{1,0:T(8,128)S(1)} %get-tuple-element.99), channel_id=1, source_target_pairs={{0,1},{1,0},{2,3},{3,2},{4,5},{5,4},{6,7},{7,6},{8,9},{9,8},{10,11... | collective-permute-start | bytes 614408 | tf_op jit(solution)/shard_map/ppermute | solution.py:405
  70.5 1.7 %collective-permute-start.21 = (f32[400,128]{1,0:T(8,128)S(1)}, f32[400,128]{1,0:T(8,128)S(1)}, u32[]{:S(2)}, u32[]{:S(2)}) collective-permute-start(f32[400,128]{1,0:T(8,128)S(1)} %get-tuple-element.100), channel_id=1, source_target_pairs={{0,1},{1,0},{2,3},{3,2},{4,5},{5,4},{6,7},{7,6},{8,9},{9,8},{10,11... | collective-permute-start | bytes 614408 | tf_op jit(solution)/shard_map/ppermute | solution.py:405
  72.3 8.7 %collective-permute-start.24 = (f32[400,128]{1,0:T(8,128)S(1)}, f32[400,128]{1,0:T(8,128)S(1)}, u32[]{:S(2)}, u32[]{:S(2)}) collective-permute-start(f32[400,128]{1,0:T(8,128)S(1)} %get-tuple-element.109), channel_id=1, source_target_pairs={{0,2},{1,3},{2,0},{3,1},{4,6},{5,7},{6,4},{7,5},{8,10},{9,11},{10,... | collective-permute-start | bytes 614408 | tf_op jit(solution)/shard_map/ppermute | solution.py:408
  73.7 7.4 %collective-permute-start.17 = (f32[800,128]{1,0:T(8,128)S(1)}, f32[800,128]{1,0:T(8,128)S(1)}, u32[]{:S(2)}, u32[]{:S(2)}) collective-permute-start(f32[800,128]{1,0:T(8,128)S(1)} %shard_map.60.two_sum), channel_id=1, source_target_pairs={{0,1},{1,0},{2,3},{3,2},{4,5},{5,4},{6,7},{7,6},{8,9},{9,8},{10,11... | collective-permute-start | bytes 1228808 | tf_op jit(solution)/shard_map/ppermute | solution.py:405
  73.9 1.6 %collective-permute-start.22 = (f32[4,896]{1,0:T(4,128)S(1)}, f32[4,896]{1,0:T(4,128)S(1)}, u32[]{:S(2)}, u32[]{:S(2)}) collective-permute-start(f32[4,896]{1,0:T(4,128)S(1)} %get-tuple-element.106), channel_id=1, source_target_pairs={{0,1},{1,0},{2,3},{3,2},{4,5},{5,4},{6,7},{7,6},{8,9},{9,8},{10,11... | collective-permute-start | bytes 43016 | tf_op jit(solution)/shard_map/ppermute | solution.py:405
  75.5 5.5 %collective-permute-start.23 = (f32[2,896]{1,0:T(2,128)S(1)}, f32[2,896]{1,0:T(2,128)S(1)}, u32[]{:S(2)}, u32[]{:S(2)}) collective-permute-start(f32[2,896]{1,0:T(2,128)S(1)} %get-tuple-element.107), channel_id=1, source_target_pairs={{0,2},{1,3},{2,0},{3,1},{4,6},{5,7},{6,4},{7,5},{8,10},{9,11},{10,... | collective-permute-start | bytes 21512 | tf_op jit(solution)/shard_map/ppermute | solution.py:408
  81.0 1.5 %collective-permute-start.25 = (f32[400,128]{1,0:T(8,128)S(1)}, f32[400,128]{1,0:T(8,128)S(1)}, u32[]{:S(2)}, u32[]{:S(2)}) collective-permute-start(f32[400,128]{1,0:T(8,128)S(1)} %shard_map.73.zero_half), channel_id=1, source_target_pairs={{0,1},{1,0},{2,3},{3,2},{4,5},{5,4},{6,7},{7,6},{8,9},{9,8},{10,11... | collective-permute-start | bytes 614408 | tf_op jit(solution)/shard_map/ppermute | solution.py:405
